TPU v7x, 32 devices: a whole 2x2x4 slice. The times are simulated.
32 devices in a mesh: gx: 4 (over y, core), gy: 8 (over z, x).
Axes of the slice: x: 2, y: 2, z: 4, core: 2. Of those that a mesh axis runs over, the one named last changes fastest.
Arguments:
- right_side: float32 [32, 128, 256], P('gx', 'gy'), may hold values from -8 to 8
- velocity: float32 [3, 32, 128, 256], P(None, 'gx', 'gy'), may hold values from 0.1 to 3
- deflation: bfloat16 [32, 32, 128, 256], P(None, 'gx', 'gy'), may hold values from -0.1875 to 0.1875
- inverse_rows: float32 [1024, 1024], P(('gx', 'gy')), may hold values from -0.1875 to 0.1875
Outputs:
- solution_field: float32 [32, 128, 256], P('gx', 'gy')
- residual: float32 [32, 128, 256], P('gx', 'gy')
All inputs are finite; a program needn't handle non-finite values.
Results may differ from a plain program's by a relative error of at most 0.005.
Values sent between devices are 32-bit elements; how exact they have to be, the bound alone decides.
No kernel may reach another device: no remote copies, remote signals or barrier semaphores. Data moves between devices by JAX's collectives and lax.ppermute only.
A program may use at most 64 MiB of HBM per device.

v0:
```python
import jax
import jax.numpy as jnp
from jax import lax
from jax.sharding import PartitionSpec as P

KD = 32
DEPTH = 2
CHEB = 4


cheb_center = 1.0
cheb_radius = 0.9


def with_halo(block, sides, width):
    for axis, dim in sides:
        count = lax.axis_size(axis)
        forward = [(i, i + 1) for i in range(count - 1)]
        backward = [(target, source) for source, target in forward]
        low = lax.ppermute(
            lax.slice_in_dim(block, block.shape[dim] - width, None, axis=dim), axis, forward
        )
        high = lax.ppermute(lax.slice_in_dim(block, 0, width, axis=dim), axis, backward)
        block = jnp.concatenate([low, block, high], axis=dim)
    return block


def upwind(padded, velocity):
    centre = padded[1:-1, 1:-1, 1:-1]
    diagonal = 6.0 + velocity[0] + velocity[1] + velocity[2]
    beside = padded[2:, 1:-1, 1:-1] + (1.0 + velocity[0]) * padded[:-2, 1:-1, 1:-1]
    beside = beside + padded[1:-1, 2:, 1:-1] + (1.0 + velocity[1]) * padded[1:-1, :-2, 1:-1]
    beside = beside + padded[1:-1, 1:-1, 2:] + (1.0 + velocity[2]) * padded[1:-1, 1:-1, :-2]
    return diagonal * centre - beside


def box_apply(field, velocity):
    return upwind(jnp.pad(field, 1), velocity)


def chebyshev(source, velocity, inside):
    inverse_diag = 1.0 / (6.0 + velocity[0] + velocity[1] + velocity[2])
    sigma_ratio = cheb_center / cheb_radius
    rho_now = 1.0 / sigma_ratio
    update = inverse_diag * source / cheb_center * inside
    estimate = update
    remainder = source
    for sweep_index in range(CHEB - 1):
        remainder = remainder - box_apply(update, velocity)
        rho_next = 1.0 / (2.0 * sigma_ratio - rho_now)
        update = (
            rho_next * rho_now * update + 2.0 * rho_next / cheb_radius * inverse_diag * remainder
        ) * inside
        estimate = estimate + update
        rho_now = rho_next
    return estimate


def apply_global(field, velocity):
    padded = with_halo(field, (("gx", 0), ("gy", 1)), 1)
    padded = jnp.pad(padded, ((0, 0), (0, 0), (1, 1)))
    return upwind(padded, velocity)


def precondition(residual, wide_velocity, flat_vectors, inverse_rows, inside):
    size_x, size_y, size_z = residual.shape
    coarse = jnp.dot(
        flat_vectors, residual.astype(jnp.bfloat16).reshape(-1), preferred_element_type=jnp.float32
    )
    gathered = lax.all_gather(coarse, ("gx", "gy"), axis=0, tiled=True)
    solved = jnp.dot(inverse_rows, gathered, precision=lax.Precision.HIGHEST)
    solved = solved.astype(jnp.bfloat16)
    correction = jnp.dot(solved, flat_vectors, preferred_element_type=jnp.float32).reshape(
        size_x, size_y, size_z
    )
    stacked = with_halo(jnp.stack((residual, correction)), (("gx", 1), ("gy", 2)), DEPTH + 1)
    padded_vel = jnp.pad(wide_velocity, ((0, 0), (1, 1), (1, 1), (0, 0)))
    image_corr = box_apply(stacked[1], padded_vel)[1:-1, 1:-1]
    source = (stacked[0][1:-1, 1:-1] - image_corr) * inside
    estimate = chebyshev(source, wide_velocity, inside)
    return correction + estimate[DEPTH : DEPTH + size_x, DEPTH : DEPTH + size_y]


def local(right_side, velocity, deflation, inverse_rows):
    size_x, size_y, size_z = right_side.shape
    wide_velocity = with_halo(velocity, (("gx", 1), ("gy", 2)), DEPTH)
    rows_x = lax.axis_index("gx") * size_x - DEPTH + lax.iota(jnp.int32, size_x + 2 * DEPTH)
    rows_y = lax.axis_index("gy") * size_y - DEPTH + lax.iota(jnp.int32, size_y + 2 * DEPTH)
    inside_x = ((rows_x >= 0) & (rows_x < size_x * lax.axis_size("gx"))).astype(jnp.float32)
    inside_y = ((rows_y >= 0) & (rows_y < size_y * lax.axis_size("gy"))).astype(jnp.float32)
    inside = inside_x[:, None, None] * inside_y[None, :, None]
    flat_vectors = deflation.reshape(KD, -1)
    rho_now = lax.psum(jnp.sum(right_side * right_side), ("gx", "gy"))
    search = precondition(right_side, wide_velocity, flat_vectors, inverse_rows, inside)
    image = apply_global(search, velocity)
    denominator = lax.psum(jnp.sum(right_side * image), ("gx", "gy"))
    alpha_step = rho_now / denominator
    middle = right_side - alpha_step * image
    smoothed = precondition(middle, wide_velocity, flat_vectors, inverse_rows, inside)
    turned = apply_global(smoothed, velocity)
    cross, square = lax.psum((jnp.sum(turned * middle), jnp.sum(turned * turned)), ("gx", "gy"))
    omega_step = cross / square
    solution_field = alpha_step * search + omega_step * smoothed
    return (solution_field, middle - omega_step * turned)


def solution(mesh):
    return jax.shard_map(
        local,
        mesh=mesh,
        in_specs=(
            P("gx", "gy", None),
            P(None, "gx", "gy", None),
            P(None, "gx", "gy", None),
            P(("gx", "gy"), None),
        ),
        out_specs=(P("gx", "gy", None), P("gx", "gy", None)),
        check_vma=False,
    )
```

profile of v0, /device:TPU:0, one launch (start us, length us, event | category | flops | bytes accessed | tf_op | source)
XLA Modules:
  0.0 277.3 jit_solution(12829819673077453023)
XLA Ops:
  0.7 1.0 convert_bitcast_fusion.1
  1.6 2.8 %fusion.4 = f32[32]{0:T(128)S(1)} fusion(bf16[32,8,16,256]{3,2,1,0:T(8,128)(2,1)} %param.6, bf16[8,16,256,1]{2,1,0,3:T(8,128)(2,1)S(1)} %convert_bitcast_fusion.1), kind=kOutput, calls=%fused_computation.4 | convolution fusion | flops 2097152 | bytes 2162816 | tf_op jit(solution)/shard_map/dot_general | solution.py:67
  4.6 42.0 %all-reduce.11 = f32[1024]{0:T(1024)S(1)} all-reduce(f32[1024]{0:T(1024)S(1)} %dynamic-update-slice), channel_id=1, replica_groups=mesh['gx'=4,'gy'=8] {'gx','gy'}, use_global_device_ids=true, to_apply=%add.11 | all-reduce | flops 1024 | bytes 8192
  46.6 2.8 %copy.11 = bf16[4,8,128,256]{3,1,2,0:T(8,128)(2,1)S(1)} copy(bf16[4,8,128,256]{3,2,1,0:T(8,128)(2,1)} %bitcast.163) | data formatting | bytes 4194304
  49.6 0.4 fusion.123
  50.3 1.3 collective-permute-start.4
  51.6 1.3 collective-permute-start.5
  52.9 0.7 fusion.120
  53.6 6.2 %collective-permute-start = (f32[3,2,16,256]{3,2,1,0:T(8,128)}, f32[3,2,16,256]{3,2,1,0:T(8,128)}, u32[]{:S(2)}, u32[]{:S(2)}) collective-permute-start(f32[3,2,16,256]{3,2,1,0:T(8,128)} %get-tuple-element.44), channel_id=1, source_target_pairs={{0,8},{8,16},{16,24},{1,9},{9,17},{17,25},{2,10},{10,18},{18,26},{... | collective-permute-start | bytes 294920 | tf_op jit(solution)/shard_map/ppermute | solution.py:20
  59.8 1.3 collective-permute-start.1
  61.2 0.7 reshape.94
  61.9 0.9 constant_dynamic-update-slice_fusion.2
  62.9 0.9 collective-permute-done.1
  63.9 2.5 collective-permute-start.2
  66.3 1.3 collective-permute-start.3
  67.7 5.0 %collective-permute-start.6 = (f32[2,14,3,256]{3,2,1,0:T(4,128)S(1)}, f32[2,14,3,256]{3,2,1,0:T(4,128)S(1)}, u32[]{:S(2)}, u32[]{:S(2)}) collective-permute-start(f32[2,14,3,256]{3,2,1,0:T(4,128)S(1)} %get-tuple-element.41), channel_id=1, source_target_pairs={{0,1},{1,2},{2,3},{3,4},{4,5},{5,6},{6,7},{8,9},{9,10},{10,11},{11... | collective-permute-start | bytes 258056 | tf_op jit(solution)/shard_map/ppermute | solution.py:20
  72.7 1.3 collective-permute-start.7
  74.5 1.3 collective-permute-done.6
  75.8 4.5 %collective-permute-done.7 = f32[2,14,3,256]{3,2,1,0:T(4,128)S(1)} collective-permute-done((f32[2,14,3,256]{3,2,1,0:T(4,128)S(1)}, f32[2,14,3,256]{3,2,1,0:T(4,128)S(1)}, u32[]{:S(2)}, u32[]{:S(2)}) %collective-permute-start.7) | collective-permute-done | bytes 86048 | tf_op jit(solution)/shard_map/ppermute | solution.py:23
  80.4 0.3 pad_slice_fusion.14
  80.8 0.4 multiply_multiply_fusion.1
  81.1 0.4 add_multiply_fusion.3
  81.6 0.4 bitcast_multiply_fusion.3
  82.0 0.3 fusion.41
  82.6 1.3 collective-permute-start.8
  83.9 4.1 %collective-permute-start.9 = (f32[1,16,256]{2,1,0:T(8,128)S(1)}, f32[1,16,256]{2,1,0:T(8,128)S(1)}, u32[]{:S(2)}, u32[]{:S(2)}) collective-permute-start(f32[1,16,256]{2,1,0:T(8,128)S(1)} %get-tuple-element.67), channel_id=1, source_target_pairs={{0,8},{8,16},{16,24},{1,9},{9,17},{17,25},{2,10},{10,18},{18,26},{... | collective-permute-start | bytes 49160 | tf_op jit(solution)/shard_map/ppermute | solution.py:20
  88.0 0.8 collective-permute-done.9
  88.8 1.3 collective-permute-start.10
  90.1 5.2 %collective-permute-start.11 = (f32[10,1,256]{2,1,0:T(1,128)S(1)}, f32[10,1,256]{2,1,0:T(1,128)S(1)}, u32[]{:S(2)}, u32[]{:S(2)}) collective-permute-start(f32[10,1,256]{2,1,0:T(1,128)S(1)} %get-tuple-element.63), channel_id=1, source_target_pairs={{0,1},{1,2},{2,3},{3,4},{4,5},{5,6},{6,7},{8,9},{9,10},{10,11},{11... | collective-permute-start | bytes 30728 | tf_op jit(solution)/shard_map/ppermute | solution.py:20
  95.3 1.4 collective-permute-done.11
  96.7 0.2 select_maximum_fusion.4
  96.9 1.5 multiply_reduce_fusion.2
  98.4 44.9 %all-reduce.14 = (f32[]{:T(128)}, f32[]{:T(128)}) all-reduce(f32[]{:T(128)} %get-tuple-element.5, f32[]{:T(128)} %get-tuple-element.4), channel_id=1, replica_groups=mesh['gx'=4,'gy'=8] {'gx','gy'}, use_global_device_ids=true, to_apply=%region_1.0 | all-reduce | flops 2 | bytes 16 | tf_op jit(solution)/shard_map/psum | solution.py:93
  144.6 1.6 convert_bitcast_fusion
  146.2 3.0 %fusion.7 = f32[32]{0:T(128)S(1)} fusion(bf16[32,8,16,256]{3,2,1,0:T(8,128)(2,1)} %param.6, bf16[8,16,256,1]{2,1,0,3:T(8,128)(2,1)S(1)} %get-tuple-element.18), kind=kOutput, calls=%fused_computation.5 | convolution fusion | flops 2097152 | bytes 2162816 | tf_op jit(solution)/shard_map/dot_general | solution.py:67
  149.2 0.6 broadcast.159
  149.8 1.4 dynamic-update-slice.1
  151.2 40.8 %all-reduce.12 = f32[1024]{0:T(1024)S(1)} all-reduce(f32[1024]{0:T(1024)} %dynamic-update-slice.1), channel_id=1, replica_groups=mesh['gx'=4,'gy'=8] {'gx','gy'}, use_global_device_ids=true, to_apply=%add.12 | all-reduce | flops 1024 | bytes 8192
  192.2 1.1 fusion.124
  193.3 0.9 stack_reshape.7
  194.2 1.3 collective-permute-start.12
  195.5 1.3 collective-permute-start.13
  196.8 4.4 %collective-permute-done.13 = f32[2,3,16,256]{3,2,1,0:T(8,128)S(1)} collective-permute-done((f32[2,3,16,256]{3,2,1,0:T(8,128)S(1)}, f32[2,3,16,256]{3,2,1,0:T(8,128)S(1)}, u32[]{:S(2)}, u32[]{:S(2)}) %collective-permute-start.13) | collective-permute-done | bytes 98336 | tf_op jit(solution)/shard_map/ppermute | solution.py:23
  201.3 2.1 collective-permute-start.14
  203.4 1.5 collective-permute-start.15
  204.9 1.6 reshape.95
  206.5 4.4 %collective-permute-done.15 = f32[2,14,3,256]{3,2,1,0:T(4,128)S(1)} collective-permute-done((f32[2,14,3,256]{3,2,1,0:T(4,128)S(1)}, f32[2,14,3,256]{3,2,1,0:T(4,128)S(1)}, u32[]{:S(2)}, u32[]{:S(2)}) %collective-permute-start.15) | collective-permute-done | bytes 86048 | tf_op jit(solution)/shard_map/ppermute | solution.py:23
  211.1 0.3 pad_slice_fusion.8
  211.4 0.6 copy-done.9
  212.2 0.4 multiply_multiply_fusion
  212.7 0.4 add_multiply_fusion.1
  213.1 0.4 bitcast_multiply_fusion
  213.5 0.3 fusion.69
  214.0 1.1 fusion.92
  215.0 1.3 collective-permute-start.16
  216.3 4.6 %collective-permute-start.17 = (f32[1,16,256]{2,1,0:T(8,128)S(1)}, f32[1,16,256]{2,1,0:T(8,128)S(1)}, u32[]{:S(2)}, u32[]{:S(2)}) collective-permute-start(f32[1,16,256]{2,1,0:T(8,128)S(1)} %get-tuple-element.65), channel_id=1, source_target_pairs={{0,8},{8,16},{16,24},{1,9},{9,17},{17,25},{2,10},{10,18},{18,26},{... | collective-permute-start | bytes 49160 | tf_op jit(solution)/shard_map/ppermute | solution.py:20
  221.0 0.8 collective-permute-done.17
  221.8 1.3 collective-permute-start.18
  223.1 5.2 %collective-permute-start.19 = (f32[10,1,256]{2,1,0:T(1,128)S(1)}, f32[10,1,256]{2,1,0:T(1,128)S(1)}, u32[]{:S(2)}, u32[]{:S(2)}) collective-permute-start(f32[10,1,256]{2,1,0:T(1,128)S(1)} %get-tuple-element.61), channel_id=1, source_target_pairs={{0,1},{1,2},{2,3},{3,4},{4,5},{5,6},{6,7},{8,9},{9,10},{10,11},{11... | collective-permute-start | bytes 30728 | tf_op jit(solution)/shard_map/ppermute | solution.py:20
  228.3 1.4 collective-permute-done.19
  229.6 0.2 select_maximum_fusion
  229.9 0.8 multiply_reduce_fusion
  230.6 44.6 %all-reduce.13 = (f32[]{:T(128)}, f32[]{:T(128)}) all-reduce(f32[]{:T(128)} %get-tuple-element.3, f32[]{:T(128)} %get-tuple-element.2), channel_id=1, replica_groups=mesh['gx'=4,'gy'=8] {'gx','gy'}, use_global_device_ids=true, to_apply=%region_5.6 | all-reduce | flops 2 | bytes 16 | tf_op jit(solution)/shard_map/psum | solution.py:101
  276.6 0.7 multiply_subtract_fusion
  (84 shorter events, 2.7 us)
Async XLA Ops:
  0.6 48.8 %copy-start = (f32[32,1024]{1,0:T(8,128)S(1)}, f32[32,1024]{1,0:T(8,128)}, u32[]{:S(2)}) copy-start(f32[32,1024]{1,0:T(8,128)} %param.7) | copy-start | bytes 393220
  49.4 0.9 copy-start.4
  49.4 3.5 %copy-start.1 = (f32[3,8,16,256]{3,2,1,0:T(8,128)S(1)}, f32[3,8,16,256]{3,2,1,0:T(8,128)}, u32[]{:S(2)}) copy-start(f32[3,8,16,256]{3,2,1,0:T(8,128)} %param.5) | copy-start | bytes 1179652
  50.1 23.9 %copy-start.14 = (f32[1,8,16,256]{3,2,1,0:T(8,128)}, f32[1,8,16,256]{3,2,1,0:T(8,128)S(1)}, u32[]{:S(2)}) copy-start(f32[1,8,16,256]{3,2,1,0:T(8,128)S(1)} %stack_reshape.6) | copy-start | bytes 393220
  50.3 17.3 %collective-permute-start.4 = (f32[2,3,16,256]{3,2,1,0:T(8,128)S(1)}, f32[2,3,16,256]{3,2,1,0:T(8,128)S(1)}, u32[]{:S(2)}, u32[]{:S(2)}) collective-permute-start(f32[2,3,16,256]{3,2,1,0:T(8,128)S(1)} %get-tuple-element.59), channel_id=1, source_target_pairs={{0,8},{8,16},{16,24},{1,9},{9,17},{17,25},{2,10},{10,18},{18,26},{... | collective-permute-start | bytes 294920 | tf_op jit(solution)/shard_map/ppermute | solution.py:20
  51.6 16.0 %collective-permute-start.5 = (f32[2,3,16,256]{3,2,1,0:T(8,128)S(1)}, f32[2,3,16,256]{3,2,1,0:T(8,128)S(1)}, u32[]{:S(2)}, u32[]{:S(2)}) collective-permute-start(f32[2,3,16,256]{3,2,1,0:T(8,128)S(1)} %get-tuple-element.60), channel_id=1, source_target_pairs={{8,0},{16,8},{24,16},{9,1},{17,9},{25,17},{10,2},{18,10},{26,18},{... | collective-permute-start | bytes 294920 | tf_op jit(solution)/shard_map/ppermute | solution.py:23
  53.6 8.3 %collective-permute-start = (f32[3,2,16,256]{3,2,1,0:T(8,128)}, f32[3,2,16,256]{3,2,1,0:T(8,128)}, u32[]{:S(2)}, u32[]{:S(2)}) collective-permute-start(f32[3,2,16,256]{3,2,1,0:T(8,128)} %get-tuple-element.44), channel_id=1, source_target_pairs={{0,8},{8,16},{16,24},{1,9},{9,17},{17,25},{2,10},{10,18},{18,26},{... | collective-permute-start | bytes 294920 | tf_op jit(solution)/shard_map/ppermute | solution.py:20
  59.8 4.0 %collective-permute-start.1 = (f32[3,2,16,256]{3,2,1,0:T(8,128)}, f32[3,2,16,256]{3,2,1,0:T(8,128)S(1)}, u32[]{:S(2)}, u32[]{:S(2)}) collective-permute-start(f32[3,2,16,256]{3,2,1,0:T(8,128)} %get-tuple-element.43), channel_id=1, source_target_pairs={{8,0},{16,8},{24,16},{9,1},{17,9},{25,17},{10,2},{18,10},{26,18},{... | collective-permute-start | bytes 294920 | tf_op jit(solution)/shard_map/ppermute | solution.py:23
  63.9 10.1 %collective-permute-start.2 = (f32[3,12,2,256]{3,2,1,0:T(2,128)S(1)}, f32[3,12,2,256]{3,2,1,0:T(2,128)S(1)}, u32[]{:S(2)}, u32[]{:S(2)}) collective-permute-start(f32[3,12,2,256]{3,2,1,0:T(2,128)S(1)} %get-tuple-element.37), channel_id=1, source_target_pairs={{0,1},{1,2},{2,3},{3,4},{4,5},{5,6},{6,7},{8,9},{9,10},{10,11},{11... | collective-permute-start | bytes 221192 | tf_op jit(solution)/shard_map/ppermute | solution.py:20
  66.3 7.7 %collective-permute-start.3 = (f32[3,12,2,256]{3,2,1,0:T(2,128)S(1)}, f32[3,12,2,256]{3,2,1,0:T(2,128)S(1)}, u32[]{:S(2)}, u32[]{:S(2)}) collective-permute-start(f32[3,12,2,256]{3,2,1,0:T(2,128)S(1)} %get-tuple-element.38), channel_id=1, source_target_pairs={{1,0},{2,1},{3,2},{4,3},{5,4},{6,5},{7,6},{9,8},{10,9},{11,10},{12... | collective-permute-start | bytes 221192 | tf_op jit(solution)/shard_map/ppermute | solution.py:23
  67.6 6.4 %copy-start.19 = (f32[2,3,16,256]{3,2,1,0:T(8,128)}, f32[2,3,16,256]{3,2,1,0:T(8,128)S(1)}, u32[]{:S(2)}) copy-start(f32[2,3,16,256]{3,2,1,0:T(8,128)S(1)} %collective-permute-done.4) | copy-start | bytes 294916
  67.7 6.4 %copy-start.21 = (f32[2,3,16,256]{3,2,1,0:T(8,128)}, f32[2,3,16,256]{3,2,1,0:T(8,128)S(1)}, u32[]{:S(2)}) copy-start(f32[2,3,16,256]{3,2,1,0:T(8,128)S(1)} %collective-permute-done.5) | copy-start | bytes 294916
  67.7 8.1 %collective-permute-start.6 = (f32[2,14,3,256]{3,2,1,0:T(4,128)S(1)}, f32[2,14,3,256]{3,2,1,0:T(4,128)S(1)}, u32[]{:S(2)}, u32[]{:S(2)}) collective-permute-start(f32[2,14,3,256]{3,2,1,0:T(4,128)S(1)} %get-tuple-element.41), channel_id=1, source_target_pairs={{0,1},{1,2},{2,3},{3,4},{4,5},{5,6},{6,7},{8,9},{9,10},{10,11},{11... | collective-permute-start | bytes 258056 | tf_op jit(solution)/shard_map/ppermute | solution.py:20
  72.7 7.6 %collective-permute-start.7 = (f32[2,14,3,256]{3,2,1,0:T(4,128)S(1)}, f32[2,14,3,256]{3,2,1,0:T(4,128)S(1)}, u32[]{:S(2)}, u32[]{:S(2)}) collective-permute-start(f32[2,14,3,256]{3,2,1,0:T(4,128)S(1)} %get-tuple-element.42), channel_id=1, source_target_pairs={{1,0},{2,1},{3,2},{4,3},{5,4},{6,5},{7,6},{9,8},{10,9},{11,10},{12... | collective-permute-start | bytes 258056 | tf_op jit(solution)/shard_map/ppermute | solution.py:23
  74.2 6.1 %copy-start.15 = (f32[1,8,16,256]{3,2,1,0:T(8,128)S(1)}, f32[1,8,16,256]{3,2,1,0:T(8,128)}, u32[]{:S(2)}) copy-start(f32[1,8,16,256]{3,2,1,0:T(8,128)} %copy-done.14) | copy-start | bytes 393220
  74.2 6.1 %copy-start.20 = (f32[2,3,16,256]{3,2,1,0:T(8,128)S(1)}, f32[2,3,16,256]{3,2,1,0:T(8,128)}, u32[]{:S(2)}) copy-start(f32[2,3,16,256]{3,2,1,0:T(8,128)} %copy-done.19) | copy-start | bytes 294916
  74.2 6.1 %copy-start.22 = (f32[2,3,16,256]{3,2,1,0:T(8,128)S(1)}, f32[2,3,16,256]{3,2,1,0:T(8,128)}, u32[]{:S(2)}) copy-start(f32[2,3,16,256]{3,2,1,0:T(8,128)} %copy-done.21) | copy-start | bytes 294916
  74.3 8.0 %copy-start.16 = (f32[12,20,256]{2,1,0:T(8,128)}, f32[12,20,256]{2,1,0:T(8,128)S(1)}, u32[]{:S(2)}) copy-start(f32[12,20,256]{2,1,0:T(8,128)S(1)} %get-tuple-element.21) | copy-start | bytes 737284
  74.4 6.3 %copy-start.8 = (f32[14,22,256]{2,1,0:T(8,128)}, f32[14,22,256]{2,1,0:T(8,128)S(1)}, u32[]{:S(2)}) copy-start(f32[14,22,256]{2,1,0:T(8,128)S(1)} %get-tuple-element.30) | copy-start | bytes 946180
  74.4 6.3 %copy-start.10 = (f32[14,22,256]{2,1,0:T(8,128)}, f32[14,22,256]{2,1,0:T(8,128)S(1)}, u32[]{:S(2)}) copy-start(f32[14,22,256]{2,1,0:T(8,128)S(1)} %get-tuple-element.31) | copy-start | bytes 946180
  74.4 6.3 %copy-start.12 = (f32[14,22,256]{2,1,0:T(8,128)}, f32[14,22,256]{2,1,0:T(8,128)S(1)}, u32[]{:S(2)}) copy-start(f32[14,22,256]{2,1,0:T(8,128)S(1)} %get-tuple-element.32) | copy-start | bytes 946180
  81.5 0.9 copy-start.17
  82.0 14.9 %copy-start.2 = (f32[3,8,16,256]{3,2,1,0:T(8,128)S(1)}, f32[3,8,16,256]{3,2,1,0:T(8,128)}, u32[]{:S(2)}) copy-start(f32[3,8,16,256]{3,2,1,0:T(8,128)} %param.5) | copy-start | bytes 1179652
  82.6 15.8 %copy-start.6 = (f32[8,16,256]{2,1,0:T(8,128)}, f32[8,16,256]{2,1,0:T(8,128)S(1)}, u32[]{:S(2)}) copy-start(f32[8,16,256]{2,1,0:T(8,128)S(1)} %fusion.105) | copy-start | bytes 393220
  82.6 5.4 %collective-permute-start.8 = (f32[1,16,256]{2,1,0:T(8,128)S(1)}, f32[1,16,256]{2,1,0:T(8,128)S(1)}, u32[]{:S(2)}, u32[]{:S(2)}) collective-permute-start(f32[1,16,256]{2,1,0:T(8,128)S(1)} %get-tuple-element.68), channel_id=1, source_target_pairs={{8,0},{16,8},{24,16},{9,1},{17,9},{25,17},{10,2},{18,10},{26,18},{... | collective-permute-start | bytes 49160 | tf_op jit(solution)/shard_map/ppermute | solution.py:23
  83.9 4.9 %collective-permute-start.9 = (f32[1,16,256]{2,1,0:T(8,128)S(1)}, f32[1,16,256]{2,1,0:T(8,128)S(1)}, u32[]{:S(2)}, u32[]{:S(2)}) collective-permute-start(f32[1,16,256]{2,1,0:T(8,128)S(1)} %get-tuple-element.67), channel_id=1, source_target_pairs={{0,8},{8,16},{16,24},{1,9},{9,17},{17,25},{2,10},{10,18},{18,26},{... | collective-permute-start | bytes 49160 | tf_op jit(solution)/shard_map/ppermute | solution.py:20
  88.8 6.5 %collective-permute-start.10 = (f32[10,1,256]{2,1,0:T(1,128)S(1)}, f32[10,1,256]{2,1,0:T(1,128)S(1)}, u32[]{:S(2)}, u32[]{:S(2)}) collective-permute-start(f32[10,1,256]{2,1,0:T(1,128)S(1)} %get-tuple-element.64), channel_id=1, source_target_pairs={{1,0},{2,1},{3,2},{4,3},{5,4},{6,5},{7,6},{9,8},{10,9},{11,10},{12... | collective-permute-start | bytes 30728 | tf_op jit(solution)/shard_map/ppermute | solution.py:23
  90.1 6.5 %collective-permute-start.11 = (f32[10,1,256]{2,1,0:T(1,128)S(1)}, f32[10,1,256]{2,1,0:T(1,128)S(1)}, u32[]{:S(2)}, u32[]{:S(2)}) collective-permute-start(f32[10,1,256]{2,1,0:T(1,128)S(1)} %get-tuple-element.63), channel_id=1, source_target_pairs={{0,1},{1,2},{2,3},{3,4},{4,5},{5,6},{6,7},{8,9},{9,10},{10,11},{11... | collective-permute-start | bytes 30728 | tf_op jit(solution)/shard_map/ppermute | solution.py:20
  146.2 48.0 %copy-start.5 = (f32[8,16,256]{2,1,0:T(8,128)S(1)}, f32[8,16,256]{2,1,0:T(8,128)}, u32[]{:S(2)}) copy-start(f32[8,16,256]{2,1,0:T(8,128)} %get-tuple-element.19) | copy-start | bytes 393220
  194.2 2.6 collective-permute-start.12
  195.5 5.7 %collective-permute-start.13 = (f32[2,3,16,256]{3,2,1,0:T(8,128)S(1)}, f32[2,3,16,256]{3,2,1,0:T(8,128)S(1)}, u32[]{:S(2)}, u32[]{:S(2)}) collective-permute-start(f32[2,3,16,256]{3,2,1,0:T(8,128)S(1)} %get-tuple-element.58), channel_id=1, source_target_pairs={{8,0},{16,8},{24,16},{9,1},{17,9},{25,17},{10,2},{18,10},{26,18},{... | collective-permute-start | bytes 294920 | tf_op jit(solution)/shard_map/ppermute | solution.py:23
  201.3 5.2 %collective-permute-start.14 = (f32[2,14,3,256]{3,2,1,0:T(4,128)S(1)}, f32[2,14,3,256]{3,2,1,0:T(4,128)S(1)}, u32[]{:S(2)}, u32[]{:S(2)}) collective-permute-start(f32[2,14,3,256]{3,2,1,0:T(4,128)S(1)} %get-tuple-element.39), channel_id=1, source_target_pairs={{0,1},{1,2},{2,3},{3,4},{4,5},{5,6},{6,7},{8,9},{9,10},{10,11},{11... | collective-permute-start | bytes 258056 | tf_op jit(solution)/shard_map/ppermute | solution.py:20
  203.4 7.5 %collective-permute-start.15 = (f32[2,14,3,256]{3,2,1,0:T(4,128)S(1)}, f32[2,14,3,256]{3,2,1,0:T(4,128)S(1)}, u32[]{:S(2)}, u32[]{:S(2)}) collective-permute-start(f32[2,14,3,256]{3,2,1,0:T(4,128)S(1)} %get-tuple-element.40), channel_id=1, source_target_pairs={{1,0},{2,1},{3,2},{4,3},{5,4},{6,5},{7,6},{9,8},{10,9},{11,10},{12... | collective-permute-start | bytes 258056 | tf_op jit(solution)/shard_map/ppermute | solution.py:23
  211.0 1.0 copy-start.9
  211.0 1.1 copy-start.11
  211.0 1.2 copy-start.13
  213.0 0.9 copy-start.18
  213.5 16.4 %copy-start.3 = (f32[3,8,16,256]{3,2,1,0:T(8,128)S(1)}, f32[3,8,16,256]{3,2,1,0:T(8,128)}, u32[]{:S(2)}) copy-start(f32[3,8,16,256]{3,2,1,0:T(8,128)} %param.5) | copy-start | bytes 1179652
  213.5 63.1 %copy-start.7 = (f32[8,16,256]{2,1,0:T(8,128)S(1)}, f32[8,16,256]{2,1,0:T(8,128)}, u32[]{:S(2)}) copy-start(f32[8,16,256]{2,1,0:T(8,128)} %copy-done.6) | copy-start | bytes 393220
  215.0 5.9 %collective-permute-start.16 = (f32[1,16,256]{2,1,0:T(8,128)S(1)}, f32[1,16,256]{2,1,0:T(8,128)S(1)}, u32[]{:S(2)}, u32[]{:S(2)}) collective-permute-start(f32[1,16,256]{2,1,0:T(8,128)S(1)} %get-tuple-element.66), channel_id=1, source_target_pairs={{8,0},{16,8},{24,16},{9,1},{17,9},{25,17},{10,2},{18,10},{26,18},{... | collective-permute-start | bytes 49160 | tf_op jit(solution)/shard_map/ppermute | solution.py:23
  216.3 5.5 %collective-permute-start.17 = (f32[1,16,256]{2,1,0:T(8,128)S(1)}, f32[1,16,256]{2,1,0:T(8,128)S(1)}, u32[]{:S(2)}, u32[]{:S(2)}) collective-permute-start(f32[1,16,256]{2,1,0:T(8,128)S(1)} %get-tuple-element.65), channel_id=1, source_target_pairs={{0,8},{8,16},{16,24},{1,9},{9,17},{17,25},{2,10},{10,18},{18,26},{... | collective-permute-start | bytes 49160 | tf_op jit(solution)/shard_map/ppermute | solution.py:20
  221.8 6.5 %collective-permute-start.18 = (f32[10,1,256]{2,1,0:T(1,128)S(1)}, f32[10,1,256]{2,1,0:T(1,128)S(1)}, u32[]{:S(2)}, u32[]{:S(2)}) collective-permute-start(f32[10,1,256]{2,1,0:T(1,128)S(1)} %get-tuple-element.62), channel_id=1, source_target_pairs={{1,0},{2,1},{3,2},{4,3},{5,4},{6,5},{7,6},{9,8},{10,9},{11,10},{12... | collective-permute-start | bytes 30728 | tf_op jit(solution)/shard_map/ppermute | solution.py:23
  223.1 6.5 %collective-permute-start.19 = (f32[10,1,256]{2,1,0:T(1,128)S(1)}, f32[10,1,256]{2,1,0:T(1,128)S(1)}, u32[]{:S(2)}, u32[]{:S(2)}) collective-permute-start(f32[10,1,256]{2,1,0:T(1,128)S(1)} %get-tuple-element.61), channel_id=1, source_target_pairs={{0,1},{1,2},{2,3},{3,4},{4,5},{5,6},{6,7},{8,9},{9,10},{10,11},{11... | collective-permute-start | bytes 30728 | tf_op jit(solution)/shard_map/ppermute | solution.py:20
where the time goes:
time: 279 us; the launch traced here: 277 us
  blocking collectives  172 us (62%)
  starting transfers between devices  50.4 us (18%)
  waiting for transfers between devices  19.9 us (7%)
  local copies, waits for them, and re-layouts  11.6 us (4%)
  other arithmetic  11.5 us (4%)
  matrix products  7.74 us (3%)
  between operations  4.01 us (1%)
    unnamed x2, blocking collectives  82.8 us
    psum x1, blocking collectives, local(): rho_now = lax.psum(jnp.sum(right_side * right_side), ('gx', 'gy'))  44.9 us
    psum x1, blocking collectives, local(): lax.psum((jnp.sum(turned * middle), jnp.sum(turned * turned)), ('gx', 'gy'))  44.6 us
    ppermute x10, starting transfers between devices, with_halo(): lax.ppermute(lax.slice_in_dim(block, block.shape[dim] - width, None, axis...  37.3 us
    ppermute x10, waiting for transfers between devices, with_halo(): lax.ppermute(lax.slice_in_dim(block, 0, width, axis=dim), axis, backward)  14.2 us
    ppermute x10, starting transfers between devices, with_halo(): lax.ppermute(lax.slice_in_dim(block, 0, width, axis=dim), axis, backward)  13.1 us
    unnamed x53, local copies, waits for them, and re-layouts  7.36 us
    dot_general x2, matrix products, precondition(): jnp.dot(flat_vectors, residual.astype(jnp.bfloat16).reshape(-1), preferre...  5.86 us
  transfers between devices with their start and end apart: 20, of which 9 were waited for; matrix products, arithmetic and copies ran while one was open for 2% of the time, Pallas kernels for 0%

commit v1 on v0

v1 whole, which is shorter than its diff:
```python
import functools

import jax
import jax.numpy as jnp
from jax import lax
from jax.experimental import pallas as pl
from jax.experimental.pallas import tpu as pltpu
from jax.sharding import PartitionSpec as P

DEPTH = 2
CHEB = 4
WIDE = 4
LANES = 128
AXES = ("gx", "gy")
F32 = jnp.float32
HIGHEST = lax.Precision.HIGHEST
PARAMS = pltpu.CompilerParams(vmem_limit_bytes=24 * 1024 * 1024)

cheb_center = 1.0
cheb_radius = 0.9

ODD_X, ODD_Y, LOW_X, HIGH_X, LOW_Y, HIGH_Y, SLOT = range(7)
OWN_LOW, PAST_LOW, PAST_HIGH, OWN_HIGH = 3, 4, 5, 6


def pair_permutations(count_x, count_y):
    def number(i, j):
        return i * count_y + j

    even_x, odd_x, even_y, odd_y = [], [], [], []
    for i in range(count_x):
        for j in range(count_y):
            here = number(i, j)
            even_x.append((here, number(i ^ 1, j)))
            even_y.append((here, number(i, j ^ 1)))
            other = ((i - 1) ^ 1) + 1
            odd_x.append((here, number(other, j) if 0 <= other < count_x else number(i, j ^ 1)))
            other = ((j - 1) ^ 1) + 1
            odd_y.append((here, number(i, other) if 0 <= other < count_y else number(i ^ 1, j)))
    return (even_x, odd_x), (even_y, odd_y)


def call(body, outs, scratch, *args):
    specs = [pl.BlockSpec(memory_space=pltpu.SMEM)] + [pl.BlockSpec(memory_space=pltpu.VMEM)] * (len(args) - 1)
    return pl.pallas_call(
        body,
        out_shape=[jax.ShapeDtypeStruct(shape, F32) for shape in outs],
        in_specs=specs,
        out_specs=[pl.BlockSpec(memory_space=pltpu.VMEM)] * len(outs),
        scratch_shapes=[pltpu.VMEM(shape, F32) for shape in scratch],
        compiler_params=PARAMS,
    )(*args)


def rows_of(plane):
    return lax.broadcasted_iota(jnp.int32, plane.shape, 0)


def z_before(plane):
    return pltpu.roll(plane, 1, 1)


def z_after(plane, keep_last):
    return jnp.where(keep_last, pltpu.roll(plane, plane.shape[1] - 1, 1), 0.0)


def stencil(before, here, after, diagonal, c0, c1, c2, keep_last):
    rows = here.shape[0]
    out = diagonal * here
    if after is not None:
        out = out - after
    if before is not None:
        out = out - c0 * before
    out = out - pltpu.roll(here, rows - 1, 0) - c1 * pltpu.roll(here, 1, 0)
    return out - z_after(here, keep_last) - c2 * z_before(here)


def lane_masks(shape):
    lanes = lax.broadcasted_iota(jnp.int32, shape, 1)
    return lanes > 0, lanes < shape[1] - 1


def restrict(vectors, field, sums, flags, send):
    count, size_x, size_y, size_z = vectors.shape
    stage = send[1]
    stage[...] = jnp.zeros_like(stage)

    def lanes_of(total):
        total = jnp.sum(total, axis=0, keepdims=True)
        return functools.reduce(jnp.add, [total[:, k : k + LANES] for k in range(0, size_z, LANES)])

    offset = pl.multiple_of(flags[SLOT] * count, count)
    for j in range(count):
        total = vectors[j, 0].astype(F32) * field[0]
        for x in range(1, size_x):
            total = total + vectors[j, x].astype(F32) * field[x]
        stage[pl.ds(offset + j, 1), :] = lanes_of(total)
    for k, total in enumerate(sums):
        stage[LANES + k : LANES + k + 1, :] = lanes_of(total)
    write_row(stage, send[0])


def write_row(stage, out):
    row = lax.dot_general(
        jnp.ones((8, LANES), F32), stage[...], (((1,), (1,)), ((), ())), precision=HIGHEST, preferred_element_type=F32
    )
    for k in range(0, out.shape[0], 8):
        out[k : k + 8, :] = row


def gathered(received):
    count = received.shape[0]
    return received[:, :LANES], jnp.sum(received[:, LANES:], axis=0, keepdims=True)


def solve(coarse, inverse, vectors):
    count = coarse.shape[0]
    share = LANES // vectors.shape[0]
    groups = count // share
    pick = (
        lax.broadcasted_iota(jnp.int32, (groups, count), 1) // share
        == lax.broadcasted_iota(jnp.int32, (groups, count), 0)
    ).astype(F32)
    packed = jnp.dot(pick, coarse, precision=HIGHEST, preferred_element_type=F32)
    total = inverse[:, :LANES] * packed[0:1]
    for k in range(1, groups):
        total = total + inverse[:, k * LANES : (k + 1) * LANES] * packed[k : k + 1]
    return jnp.sum(total, axis=1, keepdims=True).astype(jnp.bfloat16).astype(F32)


def prolong(solved, vectors, corr):
    count, size_x, size_y, size_z = vectors.shape
    totals = [jnp.zeros((size_y, size_z), F32) for _ in range(size_x)]
    for j in range(count):
        weight = jnp.broadcast_to(solved[j : j + 1], (size_y, size_z))
        for x in range(size_x):
            totals[x] = totals[x] + vectors[j, x].astype(F32) * weight
    for x in range(size_x):
        corr[x] = totals[x]


def subtract_own(field, corr, velocity, out):
    size_x, size_y, size_z = corr.shape
    keep_first, keep_last = lane_masks((size_y, size_z))
    rows = lax.broadcasted_iota(jnp.int32, (size_y, size_z), 0)
    for x in range(size_x):
        v0, v1, v2 = velocity[0, x], velocity[1, x], velocity[2, x]
        here = corr[x]
        image = (6.0 + v0 + v1 + v2) * here
        if x + 1 < size_x:
            image = image - corr[x + 1]
        if x > 0:
            image = image - (1.0 + v0) * corr[x - 1]
        image = image - jnp.where(rows < size_y - 1, pltpu.roll(here, size_y - 1, 0), 0.0)
        image = image - (1.0 + v1) * jnp.where(rows > 0, pltpu.roll(here, 1, 0), 0.0)
        image = image - z_after(here, keep_last) - (1.0 + v2) * jnp.where(keep_first, z_before(here), 0.0)
        out[x] = field[x] - image


def write_y_message(out, field, corr, high):
    size_x, size_y, _ = corr.shape
    start = size_y - WIDE if high else 0
    for k in range(WIDE):
        for x in range(size_x):
            out[k, x : x + 1, :] = field[x, start + k : start + k + 1, :]
    edge = size_y - 1 if high else 0
    for x in range(size_x):
        out[WIDE, x : x + 1, :] = corr[x, edge : edge + 1, :]
    out[WIDE + 1, 0:WIDE, :] = corr[0, start : start + WIDE, :]
    out[WIDE + 1, WIDE : 2 * WIDE, :] = corr[size_x - 1, start : start + WIDE, :]


def by_parity(odd, write, even_out, odd_out):
    @pl.when(odd == 0)
    def _():
        write(even_out, True)
        write(odd_out, False)

    @pl.when(odd != 0)
    def _():
        write(even_out, False)
        write(odd_out, True)


def first_kernel(flags, field, vectors, out, stage):
    square = field[0] * field[0]
    for x in range(1, field.shape[0]):
        square = square + field[x] * field[x]
    rounded = [field[x].astype(jnp.bfloat16).astype(F32) for x in range(field.shape[0])]
    restrict(vectors, rounded, [square], flags, (out, stage))


def velocity_faces_kernel(flags, velocity, even_out, odd_out):
    _, size_x, size_y, _ = velocity.shape

    def write(out, high):
        start = size_y - WIDE if high else 0
        for d in range(3):
            for k in range(WIDE):
                for x in range(size_x):
                    out[d * WIDE + k, x : x + 1, :] = velocity[d, x, start + k : start + k + 1, :]

    by_parity(flags[ODD_Y], write, even_out, odd_out)


def velocity_wide_kernel(flags, velocity, even_in, odd_in, wide, even_out, odd_out):
    _, size_x, size_y, _ = velocity.shape

    def place(low, high):
        for d in range(3):
            for x in range(size_x):
                wide[d, x, WIDE : WIDE + size_y, :] = velocity[d, x]
                for k in range(WIDE):
                    wide[d, x, k : k + 1, :] = low[d * WIDE + k, x : x + 1, :]
                    row = WIDE + size_y + k
                    wide[d, x, row : row + 1, :] = high[d * WIDE + k, x : x + 1, :]

    @pl.when(flags[ODD_Y] == 0)
    def _():
        place(odd_in, even_in)

    @pl.when(flags[ODD_Y] != 0)
    def _():
        place(even_in, odd_in)

    def write(out, high):
        start = size_x - WIDE if high else 0
        for d in range(3):
            for k in range(WIDE):
                out[d * WIDE + k] = wide[d, start + k]

    by_parity(flags[ODD_X], write, even_out, odd_out)


def coarse_kernel(flags, received, inverse, vectors, field, velocity, corr, rest, even_out, odd_out):
    coarse, _ = gathered(received)
    prolong(solve(coarse, inverse, vectors), vectors, corr)
    subtract_own(field, corr, velocity, rest)
    by_parity(flags[ODD_Y], lambda out, high: write_y_message(out, rest, corr, high), even_out, odd_out)


def second_coarse_kernel(
    flags, received, second, inverse, vectors, field, image, velocity, corr, rest, middle, alpha, even_out, odd_out
):
    coarse, squares = gathered(received)
    coarse_image, products = gathered(second)
    step = jnp.broadcast_to(squares[:, 0:1] / products[:, 0:1], alpha.shape)
    alpha[...] = step
    step = step[0:1, 0:1]
    for x in range(field.shape[0]):
        middle[x] = field[x] - step * image[x]
    prolong(solve(coarse - step * coarse_image, inverse, vectors), vectors, corr)
    subtract_own(middle, corr, velocity, rest)
    by_parity(flags[ODD_Y], lambda out, high: write_y_message(out, rest, corr, high), even_out, odd_out)


def extend_kernel(flags, rest, corr, even_in, odd_in, wide, sides, even_out, odd_out):
    size_x, size_y, size_z = rest.shape
    rows = size_y + 2 * WIDE

    def place(low, high):
        has_low, has_high = flags[LOW_Y] != 0, flags[HIGH_Y] != 0
        past_low = jnp.where(has_low, low[WIDE], 0.0)
        past_high = jnp.where(has_high, high[WIDE], 0.0)
        for x in range(size_x):
            wide[x, WIDE : WIDE + size_y, :] = rest[x]
            for k in range(WIDE):
                wide[x, k : k + 1, :] = low[k, x : x + 1, :]
                wide[x, WIDE + size_y + k : WIDE + size_y + k + 1, :] = high[k, x : x + 1, :]
            wide[x, rows : rows + 8, :] = jnp.zeros((8, size_z), F32)
            wide[x, rows + OWN_LOW : rows + OWN_LOW + 1, :] = corr[x, 0:1, :]
            wide[x, rows + PAST_LOW : rows + PAST_LOW + 1, :] = past_low[x : x + 1]
            wide[x, rows + PAST_HIGH : rows + PAST_HIGH + 1, :] = past_high[x : x + 1]
            wide[x, rows + OWN_HIGH : rows + OWN_HIGH + 1, :] = corr[x, size_y - 1 : size_y, :]
        for side, x in enumerate((0, size_x - 1)):
            first = side * WIDE
            sides[side, 0:WIDE, :] = low[WIDE + 1, first : first + WIDE, :]
            sides[side, WIDE : WIDE + size_y, :] = corr[x]
            sides[side, WIDE + size_y : rows, :] = high[WIDE + 1, first : first + WIDE, :]
            sides[side, rows : rows + 8, :] = jnp.zeros((8, size_z), F32)

    @pl.when(flags[ODD_Y] == 0)
    def _():
        place(odd_in, even_in)

    @pl.when(flags[ODD_Y] != 0)
    def _():
        place(even_in, odd_in)

    def write(out, high):
        start = size_x - WIDE if high else 0
        for k in range(WIDE):
            out[k] = wide[start + k]
        out[WIDE] = sides[1 if high else 0]

    by_parity(flags[ODD_X], write, even_out, odd_out)


def chebyshev(planes, tile, weight_of, source, left, update, coefs, keep_last, wanted):
    c0, c1, c2, diagonal = coefs
    sigma = cheb_center / cheb_radius
    rho = 1.0 / sigma
    first, last = planes[0], planes[-1]
    estimate = {}
    for x in planes:
        left[x, tile] = source[x, tile]
        value = weight_of(x) * source[x, tile]
        update[0, x, tile] = value
        if x in wanted:
            estimate[x] = value
    for sweep in range(1, CHEB):
        rest = CHEB - 1 - sweep
        low, high = max(first, wanted[0] - rest), min(last, wanted[-1] + rest)
        rho_next = 1.0 / (2.0 * sigma - rho)
        now, later = (sweep + 1) % 2, sweep % 2
        for x in range(low, high + 1):
            here = update[now, x, tile]
            before = update[now, x - 1, tile] if x > first else None
            after = update[now, x + 1, tile] if x < last else None
            remainder = left[x, tile] - stencil(
                before, here, after, diagonal[x, tile], c0[x, tile], c1[x, tile], c2[x, tile], keep_last
            )
            if rest:
                left[x, tile] = remainder
            value = rho_next * rho * here + (2.0 * rho_next / cheb_radius) * (weight_of(x) * remainder)
            if rest:
                update[later, x, tile] = value
            if x in wanted:
                estimate[x] = estimate[x] + value
        rho = rho_next
    return estimate


def smooth(flags, wide, sides, even_in, odd_in, velocity, even_vel, odd_vel, corr, field_out, image_out, scratch):
    c0, c1, c2, diagonal, inverse, source, left, update, whole = scratch
    size_x, size_y, size_z = corr.shape
    rows = size_y + 2 * WIDE
    span = size_x + 2 * WIDE
    shape = (rows, size_z)
    row = lax.broadcasted_iota(jnp.int32, shape, 0)
    keep_first, keep_last = lane_masks(shape)
    has_low_x, has_high_x = flags[LOW_X] != 0, flags[HIGH_X] != 0
    has_low_y, has_high_y = flags[LOW_Y] != 0, flags[HIGH_Y] != 0
    lowest, highest = slice(0, 8), slice(rows - 8, rows)
    tile_row = lax.broadcasted_iota(jnp.int32, (8, size_z), 0)
    last_tile = slice(rows, rows + 8)

    def coefficients(x, v0, v1, v2):
        c0[x] = 1.0 + v0
        c1[x] = 1.0 + v1
        c2[x] = jnp.where(keep_first, 1.0 + v2, 0.0)
        total = 6.0 + v0 + v1 + v2
        diagonal[x] = total
        inverse[x] = 1.0 / total

    def source_plane(x, plane):
        source[x] = plane[0:rows]
        lines = plane[last_tile]
        kept = (tile_row == OWN_LOW) | (tile_row == PAST_LOW)
        source[x, lowest] = source[x, lowest] + jnp.where(
            kept, lines * jnp.where(tile_row == PAST_LOW, c1[x, lowest], 1.0), 0.0
        )
        lines = pltpu.roll(lines, 8 - (PAST_HIGH - OWN_LOW), 0)
        source[x, highest] = source[x, highest] + jnp.where(
            kept, lines * jnp.where(tile_row == PAST_LOW, c1[x, highest], 1.0), 0.0
        )

    def halo(low, high, low_vel, high_vel):
        for k in range(WIDE):
            coefficients(k, *[low_vel[d * WIDE + k] for d in range(3)])
            source_plane(k, low[k])
            x = WIDE + size_x + k
            coefficients(x, *[high_vel[d * WIDE + k] for d in range(3)])
            source_plane(x, high[k])
        whole[0] = jnp.where(has_low_x, low[WIDE, 0:rows], 0.0)
        whole[size_x + 1] = jnp.where(has_high_x, high[WIDE, 0:rows], 0.0)

    @pl.when(flags[ODD_X] == 0)
    def _():
        halo(odd_in, even_in, odd_vel, even_vel)

    @pl.when(flags[ODD_X] != 0)
    def _():
        halo(even_in, odd_in, even_vel, odd_vel)

    for k in range(size_x):
        coefficients(WIDE + k, velocity[0, k], velocity[1, k], velocity[2, k])
        source_plane(WIDE + k, wide[k])

    low_in, high_in = WIDE, WIDE + size_x - 1
    source[low_in - 1] = source[low_in - 1] + sides[0, 0:rows]
    source[low_in] = source[low_in] + c0[low_in] * whole[0]
    source[high_in] = source[high_in] + whole[size_x + 1]
    source[high_in + 1] = source[high_in + 1] + c0[high_in + 1] * sides[1, 0:rows]

    first_row = jnp.where(has_low_y, WIDE - DEPTH, WIDE)
    end_row = jnp.where(has_high_y, WIDE + size_y + DEPTH, WIDE + size_y)
    box_rows = (row >= first_row) & (row < end_row)
    everything = slice(0, rows)

    def plane_weight(x, tile, kept):
        value = jnp.where(kept, inverse[x, tile], 0.0)
        if x < WIDE:
            value = jnp.where(has_low_x, value, 0.0)
        if x >= WIDE + size_x:
            value = jnp.where(has_high_x, value, 0.0)
        return value

    run = functools.partial(
        chebyshev, source=source, left=left, update=update, coefs=(c0, c1, c2, diagonal)
    )
    box_planes = range(WIDE - DEPTH, WIDE + size_x + DEPTH)
    own_planes = range(WIDE, WIDE + size_x)

    low_planes, high_planes = range(0, WIDE + DEPTH), range(span - WIDE - DEPTH, span)
    own_weight = lambda x: plane_weight(x, everything, box_rows)
    beside = run(low_planes, everything, own_weight, keep_last=keep_last, wanted=(WIDE - 1,))[WIDE - 1]
    inner = (row >= WIDE) & (row < WIDE + size_y)
    whole[0] = jnp.where(has_low_x & inner, whole[0] + beside, 0.0)
    x = WIDE + size_x
    beside = run(high_planes, everything, own_weight, keep_last=keep_last, wanted=(x,))[x]
    whole[size_x + 1] = jnp.where(has_high_x & inner, whole[size_x + 1] + beside, 0.0)

    own = run(box_planes, everything, own_weight, keep_last=keep_last, wanted=tuple(own_planes))
    zeros = jnp.zeros((rows - size_y, size_z), F32)
    for k in range(size_x):
        placed = pltpu.roll(jnp.concatenate([corr[k], zeros], axis=0), WIDE, 0)
        whole[k + 1] = jnp.where(inner, placed + own[WIDE + k], 0.0)

    keep_tile = lane_masks((8, size_z))[1]
    low_weight = lambda x: plane_weight(x, lowest, tile_row < WIDE + DEPTH)
    beside = run(box_planes, lowest, low_weight, keep_last=keep_tile, wanted=tuple(own_planes))
    for k in range(size_x):
        line = pltpu.roll(wide[k, last_tile], 8 + WIDE - 1 - PAST_LOW, 0) + beside[WIDE + k]
        kept = has_low_y & (tile_row == WIDE - 1)
        whole[k + 1, lowest] = jnp.where(kept, line, whole[k + 1, lowest])
    high_weight = lambda x: plane_weight(x, highest, tile_row >= 8 - WIDE - DEPTH)
    beside = run(box_planes, highest, high_weight, keep_last=keep_tile, wanted=tuple(own_planes))
    for k in range(size_x):
        line = pltpu.roll(wide[k, last_tile], (8 + 8 - WIDE - PAST_HIGH) % 8, 0) + beside[WIDE + k]
        kept = has_high_y & (tile_row == 8 - WIDE)
        whole[k + 1, highest] = jnp.where(kept, line, whole[k + 1, highest])

    for k in range(size_x):
        x = WIDE + k
        image = stencil(
            whole[k], whole[k + 1], whole[k + 2], diagonal[x], c0[x], c1[x], c2[x], keep_last
        )
        image_out[k] = pltpu.roll(image, rows - WIDE, 0)[0:size_y]
        field_out[k] = pltpu.roll(whole[k + 1], rows - WIDE, 0)[0:size_y]


def dot_planes(left, right):
    total = left[0] * right[0]
    for x in range(1, left.shape[0]):
        total = total + left[x] * right[x]
    return total


def search_kernel(
    flags, wide, sides, even_in, odd_in, velocity, even_vel, odd_vel, corr, vectors, right_side, search, image, out,
    stage, *scratch
):
    smooth(flags, wide, sides, even_in, odd_in, velocity, even_vel, odd_vel, corr, search, image, scratch)
    restrict(vectors, image, [dot_planes(right_side, image)], flags, (out, stage))


def smoothed_kernel(
    flags, wide, sides, even_in, odd_in, velocity, even_vel, odd_vel, corr, middle, smoothed, turned, out, stage, *scratch
):
    smooth(flags, wide, sides, even_in, odd_in, velocity, even_vel, odd_vel, corr, smoothed, turned, scratch)
    stage[...] = jnp.zeros_like(stage)
    for k, total in enumerate((dot_planes(turned, middle), dot_planes(turned, turned))):
        total = jnp.sum(total, axis=0, keepdims=True)
        parts = [total[:, i : i + LANES] for i in range(0, total.shape[1], LANES)]
        stage[LANES + k : LANES + k + 1, :] = functools.reduce(jnp.add, parts)
    write_row(stage, out)


def last_kernel(flags, received, alpha, search, smoothed, middle, turned, solution_field, residual):
    _, sums = gathered(received)
    omega = sums[:, 0:1] / sums[:, 1:2]
    step = alpha[0:1, 0:1]
    for x in range(search.shape[0]):
        solution_field[x] = step * search[x] + omega * smoothed[x]
        residual[x] = middle[x] - omega * turned[x]


def local(right_side, velocity, deflation, inverse_rows):
    size_x, size_y, size_z = right_side.shape
    vectors_count = deflation.shape[0]
    count_x, count_y = lax.axis_size("gx"), lax.axis_size("gy")
    count = count_x * count_y
    at_x, at_y = lax.axis_index("gx"), lax.axis_index("gy")
    flags = jnp.stack(
        [
            at_x % 2,
            at_y % 2,
            (at_x > 0).astype(jnp.int32),
            (at_x < count_x - 1).astype(jnp.int32),
            (at_y > 0).astype(jnp.int32),
            (at_y < count_y - 1).astype(jnp.int32),
            (at_x * count_y + at_y) % (LANES // vectors_count),
            at_x,
        ]
    ).astype(jnp.int32)
    x_pairs, y_pairs = pair_permutations(count_x, count_y)

    def swap(messages, pairs):
        return [lax.ppermute(message, AXES, pair) for message, pair in zip(messages, pairs)]

    def share(row):
        return lax.all_to_all(row, AXES, 0, 0, tiled=True)

    rows = size_y + 2 * WIDE
    span = size_x + 2 * WIDE
    block = (size_x, size_y, size_z)
    row = (count, 2 * LANES)
    stage = (2 * LANES, LANES)
    y_message = (WIDE + 2, size_x, size_z)
    x_message = (WIDE + 1, rows + 8, size_z)
    region = (span, rows, size_z)
    smooth_scratch = [region] * 7 + [(2,) + region, (size_x + 2, rows, size_z)]

    faces = (3 * WIDE, size_x, size_z)
    velocity_y = swap(call(velocity_faces_kernel, [faces] * 2, [], flags, velocity), y_pairs)
    (first_row,) = call(first_kernel, [row], [stage], flags, right_side, deflation)
    wide_faces = (3 * WIDE, rows, size_z)
    wide_velocity, *velocity_x = call(
        velocity_wide_kernel,
        [(3, size_x, rows, size_z), wide_faces, wide_faces],
        [],
        flags,
        velocity,
        *velocity_y,
    )
    velocity_x = swap(velocity_x, x_pairs)
    first = share(first_row)

    def exchange(corr, rest, messages):
        messages = swap(messages, y_pairs)
        wide, sides, *messages = call(
            extend_kernel,
            [(size_x, rows + 8, size_z), (2, rows + 8, size_z), x_message, x_message],
            [],
            flags,
            rest,
            corr,
            *messages,
        )
        return (wide, sides, *swap(messages, x_pairs), wide_velocity, *velocity_x, corr)

    corr, rest, *messages = call(
        coarse_kernel,
        [block, block, y_message, y_message],
        [],
        flags,
        first,
        inverse_rows,
        deflation,
        right_side,
        velocity,
    )
    search, image, second_row = call(
        search_kernel,
        [block, block, row],
        [stage] + smooth_scratch,
        flags,
        *exchange(corr, rest, messages),
        deflation,
        right_side,
    )
    second = share(second_row)
    corr, rest, middle, alpha, *messages = call(
        second_coarse_kernel,
        [block, block, block, (8, LANES), y_message, y_message],
        [],
        flags,
        first,
        second,
        inverse_rows,
        deflation,
        right_side,
        image,
        velocity,
    )
    smoothed, turned, third_row = call(
        smoothed_kernel,
        [block, block, row],
        [stage] + smooth_scratch,
        flags,
        *exchange(corr, rest, messages),
        middle,
    )
    third = share(third_row)
    return tuple(
        call(last_kernel, [block, block], [], flags, third, alpha, search, smoothed, middle, turned)
    )


def solution(mesh):
    return jax.shard_map(
        local,
        mesh=mesh,
        in_specs=(
            P("gx", "gy", None),
            P(None, "gx", "gy", None),
            P(None, "gx", "gy", None),
            P(("gx", "gy"), None),
        ),
        out_specs=(P("gx", "gy", None), P("gx", "gy", None)),
        check_vma=False,
    )
```

time: 279 us -> 80.4 us (0.29)
  blocking collectives: 172 us -> 31 us
  starting transfers between devices: 50.4 us -> 13.2 us
  Pallas kernels: 0 us -> 13.7 us
  other arithmetic: 11.5 us -> 0 us
  local copies, waits for them, and re-layouts: 11.6 us -> 3.79 us
  matrix products: 7.74 us -> 0 us
  between operations: 4.01 us -> 0.8 us
    psum x2 -> x0, blocking collectives: 89.4 us -> none  [the longest x1 44.9 us: local(): rho_now = lax.psum(jnp.sum(right_side * right_side), ('gx', 'gy'))]
    unnamed x2 -> x0, blocking collectives: 82.8 us -> none
    ppermute x20 -> x12, starting transfers between devices: 50.4 us -> 13.2 us  [swap(): lax.ppermute(message, AXES, pair)]
    all_to_all x0 -> x3, blocking collectives: none -> 31 us  [share(): return lax.all_to_all(row, AXES, 0, 0, tiled=True)]
    pallas_call x0 -> x10, Pallas kernels: none -> 13.7 us  [call(): pl.pallas_call(body, out_shape=[jax.ShapeDtypeStruct(shape, F32) for shap...]
    dot_general x6 -> x0, matrix products: 7.74 us -> none  [the longest x2 5.86 us: precondition(): jnp.dot(flat_vectors, residual.astype(jnp.bfloat16).reshape(-1), preferre...]
    unnamed x53 -> x17, local copies, waits for them, and re-layouts: 7.36 us -> 3.52 us
    ppermute x20 -> x12, waiting for transfers between devices: 19.9 us -> 17.6 us  [swap(): lax.ppermute(message, AXES, pair)]
  transfers between devices with their start and end apart: 20 -> 12, of which waited for: 9 -> 5; matrix products, arithmetic and copies ran while one was open for 2% -> 0% of each run, Pallas kernels for 0% -> 4%
where the time goes in v1:
time: 80.4 us; the launch traced here: 80.1 us
  blocking collectives  31 us (39%)
  waiting for transfers between devices  17.6 us (22%)
  Pallas kernels  13.7 us (17%)
  starting transfers between devices  13.2 us (16%)
  local copies, waits for them, and re-layouts  3.79 us (5%)
    all_to_all x3, blocking collectives, share(): return lax.all_to_all(row, AXES, 0, 0, tiled=True)  31 us
    ppermute x12, waiting for transfers between devices, swap(): lax.ppermute(message, AXES, pair)  17.6 us
    pallas_call x10, Pallas kernels, call(): pl.pallas_call(body, out_shape=[jax.ShapeDtypeStruct(shape, F32) for shap...  13.7 us
    ppermute x12, starting transfers between devices, swap(): lax.ppermute(message, AXES, pair)  13.2 us
    unnamed x17, local copies, waits for them, and re-layouts  3.52 us
  transfers between devices with their start and end apart: 12, of which 5 were waited for; matrix products, arithmetic and copies ran while one was open for 0% of the time, Pallas kernels for 4%

profile of v1, /device:TPU:0, one launch (start us, length us, event | category | flops | bytes accessed | tf_op | source)
XLA Modules:
  0.0 80.1 jit_solution(8267291126665149295)
XLA Ops:
  0.7 0.1 stack.51.flags
  0.8 0.0 copy-start.2
  0.8 1.0 %copy-done.2 = f32[3,8,16,256]{3,2,1,0:T(8,128)S(1)} copy-done((f32[3,8,16,256]{3,2,1,0:T(8,128)S(1)}, f32[3,8,16,256]{3,2,1,0:T(8,128)}, u32[]{:S(2)}) %copy-start.2) | copy-done | bytes 393240
  1.8 0.0 copy-start.3
  1.8 0.0 copy-start.6
  1.8 0.7 shard_map.62
  2.4 3.0 %collective-permute-start.4 = (f32[12,8,256]{2,1,0:T(8,128)S(1)}, f32[12,8,256]{2,1,0:T(8,128)S(1)}, u32[]{:S(2)}, u32[]{:S(2)}) collective-permute-start(f32[12,8,256]{2,1,0:T(8,128)S(1)} %get-tuple-element.39), channel_id=1, source_target_pairs={{0,1},{1,0},{2,3},{3,2},{4,5},{5,4},{6,7},{7,6},{8,9},{9,8},{10,11... | collective-permute-start | bytes 294920 | tf_op jit(solution)/shard_map/ppermute | solution.py:510
  5.4 0.0 collective-permute-start.5
  5.4 4.2 %collective-permute-done.4.even_in = f32[12,8,256]{2,1,0:T(8,128)S(1)} collective-permute-done((f32[12,8,256]{2,1,0:T(8,128)S(1)}, f32[12,8,256]{2,1,0:T(8,128)S(1)}, u32[]{:S(2)}, u32[]{:S(2)}) %collective-permute-start.4) | collective-permute-done | bytes 98336 | tf_op jit(solution)/shard_map/ppermute | solution.py:510
  9.6 0.0 collective-permute-done.5.odd_in
  9.6 0.7 shard_map.63
  10.3 0.1 collective-permute-start.6
  10.4 2.5 %collective-permute-start.7 = (f32[12,24,256]{2,1,0:T(8,128)S(1)}, f32[12,24,256]{2,1,0:T(8,128)S(1)}, u32[]{:S(2)}, u32[]{:S(2)}) collective-permute-start(f32[12,24,256]{2,1,0:T(8,128)S(1)} %get-tuple-element.43), channel_id=1, source_target_pairs={{0,1},{1,0},{2,3},{3,2},{4,5},{5,4},{6,7},{7,6},{8,16},{9,17},{10,... | collective-permute-start | bytes 884744 | tf_op jit(solution)/shard_map/ppermute | solution.py:510
  13.0 0.0 copy-start
  13.0 1.6 %copy-done = bf16[32,8,16,256]{3,2,1,0:T(8,128)(2,1)S(1)} copy-done((bf16[32,8,16,256]{3,2,1,0:T(8,128)(2,1)S(1)}, bf16[32,8,16,256]{3,2,1,0:T(8,128)(2,1)}, u32[]{:S(2)}) %copy-start) | copy-done | bytes 2097176
  14.5 0.0 copy-start.4
  14.5 0.9 %copy-done.4 = f32[8,16,256]{2,1,0:T(8,128)S(1)} copy-done((f32[8,16,256]{2,1,0:T(8,128)S(1)}, f32[8,16,256]{2,1,0:T(8,128)}, u32[]{:S(2)}) %copy-start.4) | copy-done | bytes 131096
  15.5 1.2 %shard_map.59 = f32[32,256]{1,0:T(8,128)S(1)} custom-call(s32[8]{0:T(128)S(1)} %stack.51.flags, f32[8,16,256]{2,1,0:T(8,128)S(1)} %copy-done.4, bf16[32,8,16,256]{3,2,1,0:T(8,128)(2,1)S(1)} %copy-done), custom_call_target="tpu_custom_call" | custom-call | tf_op jit(solution)/shard_map/pallas_call | solution.py:45
  16.7 0.0 copy-start.1
  16.7 0.0 copy-start.5
  16.7 0.1 copy.6
  16.7 12.0 %all_to_all.33 = f32[32,1,256]{2,1,0:T(1,128)S(1)} all-to-all(f32[32,1,256]{2,1,0:T(1,128)S(1)} %copy.6), channel_id=1, replica_groups=mesh['gx'=4,'gy'=8] {'gx','gy'}, dimensions={0} | all-to-all | bytes 65536 | tf_op jit(solution)/shard_map/all_to_all | solution.py:513
  28.7 0.0 copy-done.3
  28.7 0.0 copy-done.6
  28.7 1.4 %shard_map.60 = (f32[8,16,256]{2,1,0:T(8,128)S(1)}, f32[8,16,256]{2,1,0:T(8,128)S(1)}, f32[6,8,256]{2,1,0:T(8,128)S(1)}, f32[6,8,256]{2,1,0:T(8,128)S(1)}) custom-call(s32[8]{0:T(128)S(1)} %stack.51.flags, f32[32,256]{1,0:T(8,128)S(1)} %bitcast.20, f32[32,1024]{1,0:T(8,128)S(1)} %copy-done.6, bf16[32,8,16,256]{3,2,1,0:T(8,128)(2,1)S(1)} %copy-done, ...), custom_call_target="tpu_custom_call" | custom-call | tf_op jit(solution)/shard_map/pallas_call | solution.py:45
  30.2 0.7 collective-permute-start
  30.9 0.0 collective-permute-start.1
  30.9 3.4 %collective-permute-done.even_in = f32[6,8,256]{2,1,0:T(8,128)S(1)} collective-permute-done((f32[6,8,256]{2,1,0:T(8,128)S(1)}, f32[6,8,256]{2,1,0:T(8,128)S(1)}, u32[]{:S(2)}, u32[]{:S(2)}) %collective-permute-start) | collective-permute-done | bytes 49184 | tf_op jit(solution)/shard_map/ppermute | solution.py:510
  34.3 0.0 collective-permute-done.1.odd_in
  34.3 0.7 shard_map.61
  35.0 0.1 collective-permute-start.2
  35.1 3.0 %collective-permute-start.3 = (f32[5,32,256]{2,1,0:T(8,128)S(1)}, f32[5,32,256]{2,1,0:T(8,128)S(1)}, u32[]{:S(2)}, u32[]{:S(2)}) collective-permute-start(f32[5,32,256]{2,1,0:T(8,128)S(1)} %get-tuple-element.38), channel_id=1, source_target_pairs={{0,1},{1,0},{2,3},{3,2},{4,5},{5,4},{6,7},{7,6},{8,16},{9,17},{10,... | collective-permute-start | bytes 491528 | tf_op jit(solution)/shard_map/ppermute | solution.py:510
  38.1 0.0 collective-permute-done.2.even_in
  38.1 3.3 %collective-permute-done.3.odd_in = f32[5,32,256]{2,1,0:T(8,128)S(1)} collective-permute-done((f32[5,32,256]{2,1,0:T(8,128)S(1)}, f32[5,32,256]{2,1,0:T(8,128)S(1)}, u32[]{:S(2)}, u32[]{:S(2)}) %collective-permute-start.3) | collective-permute-done | bytes 163872 | tf_op jit(solution)/shard_map/ppermute | solution.py:510
  41.4 0.0 collective-permute-done.6.even_vel
  41.4 0.0 collective-permute-done.7.odd_vel
  41.4 0.0 copy-done.1
  41.4 0.0 copy-done.5
  41.4 3.0 %shard_map.64 = (f32[8,16,256]{2,1,0:T(8,128)S(1)}, f32[8,16,256]{2,1,0:T(8,128)S(1)}, f32[32,256]{1,0:T(8,128)S(1)}) custom-call(s32[8]{0:T(128)S(1)} %stack.51.flags, f32[8,32,256]{2,1,0:T(8,128)S(1)} %get-tuple-element.35.wide, f32[2,32,256]{2,1,0:T(8,128)S(1)} %get-tuple-element.36.sides, f32[5,32,256]{2,1,0:T(8,128)S(1)} %collective-permute-done.2.even_in, ...), custom_call_target="tpu_custom_call" | custom-call | tf_op jit(solution)/shard_map/pallas_call | solution.py:45
  44.4 0.1 copy.7
  44.4 9.5 %all_to_all.34 = f32[32,1,256]{2,1,0:T(1,128)S(1)} all-to-all(f32[32,1,256]{2,1,0:T(1,128)S(1)} %copy.7), channel_id=1, replica_groups=mesh['gx'=4,'gy'=8] {'gx','gy'}, dimensions={0} | all-to-all | bytes 65536 | tf_op jit(solution)/shard_map/all_to_all | solution.py:513
  54.0 1.5 %shard_map.65 = (f32[8,16,256]{2,1,0:T(8,128)S(1)}, f32[8,16,256]{2,1,0:T(8,128)S(1)}, f32[8,16,256]{2,1,0:T(8,128)S(1)}, f32[8,128]{1,0:T(8,128)S(1)}, f32[6,8,...) custom-call(s32[8]{0:T(128)S(1)} %stack.51.flags, f32[32,256]{1,0:T(8,128)S(1)} %bitcast.21, f32[32,256]{1,0:T(8,128)S(1)} %bitcast.22, ...), custom_call_target="tpu_custom_call" | custom-call | tf_op jit(solution)/shard_map/pallas_call | solution.py:45
  55.5 0.7 collective-permute-start.8
  56.2 0.0 collective-permute-start.9
  56.2 3.4 %collective-permute-done.8.even_in = f32[6,8,256]{2,1,0:T(8,128)S(1)} collective-permute-done((f32[6,8,256]{2,1,0:T(8,128)S(1)}, f32[6,8,256]{2,1,0:T(8,128)S(1)}, u32[]{:S(2)}, u32[]{:S(2)}) %collective-permute-start.8) | collective-permute-done | bytes 49184 | tf_op jit(solution)/shard_map/ppermute | solution.py:510
  59.6 0.0 collective-permute-done.9.odd_in
  59.6 0.7 shard_map.66
  60.3 0.1 collective-permute-start.10
  60.4 3.0 %collective-permute-start.11 = (f32[5,32,256]{2,1,0:T(8,128)S(1)}, f32[5,32,256]{2,1,0:T(8,128)S(1)}, u32[]{:S(2)}, u32[]{:S(2)}) collective-permute-start(f32[5,32,256]{2,1,0:T(8,128)S(1)} %get-tuple-element.53), channel_id=1, source_target_pairs={{0,1},{1,0},{2,3},{3,2},{4,5},{5,4},{6,7},{7,6},{8,16},{9,17},{10,... | collective-permute-start | bytes 491528 | tf_op jit(solution)/shard_map/ppermute | solution.py:510
  63.4 0.0 collective-permute-done.10.even_in
  63.4 3.3 %collective-permute-done.11.odd_in = f32[5,32,256]{2,1,0:T(8,128)S(1)} collective-permute-done((f32[5,32,256]{2,1,0:T(8,128)S(1)}, f32[5,32,256]{2,1,0:T(8,128)S(1)}, u32[]{:S(2)}, u32[]{:S(2)}) %collective-permute-start.11) | collective-permute-done | bytes 163872 | tf_op jit(solution)/shard_map/ppermute | solution.py:510
  66.7 2.5 %shard_map.67 = (f32[8,16,256]{2,1,0:T(8,128)S(1)}, f32[8,16,256]{2,1,0:T(8,128)S(1)}, f32[32,256]{1,0:T(8,128)S(1)}) custom-call(s32[8]{0:T(128)S(1)} %stack.51.flags, f32[8,32,256]{2,1,0:T(8,128)S(1)} %get-tuple-element.50.wide, f32[2,32,256]{2,1,0:T(8,128)S(1)} %get-tuple-element.51.sides, f32[5,32,256]{2,1,0:T(8,128)S(1)} %collective-permute-done.10.even_in, ...), custom_call_target="tpu_custom_call" | custom-call | tf_op jit(solution)/shard_map/pallas_call | solution.py:45
  69.2 0.1 copy.8
  69.2 9.5 %all_to_all.35 = f32[32,1,256]{2,1,0:T(1,128)S(1)} all-to-all(f32[32,1,256]{2,1,0:T(1,128)S(1)} %copy.8), channel_id=1, replica_groups=mesh['gx'=4,'gy'=8] {'gx','gy'}, dimensions={0} | all-to-all | bytes 65536 | tf_op jit(solution)/shard_map/all_to_all | solution.py:513
  78.8 1.4 %shard_map.68 = (f32[8,16,256]{2,1,0:T(8,128)}, f32[8,16,256]{2,1,0:T(8,128)}) custom-call(s32[8]{0:T(128)S(1)} %stack.51.flags, f32[32,256]{1,0:T(8,128)S(1)} %bitcast.24, f32[8,128]{1,0:T(8,128)S(1)} %get-tuple-element.56.alpha, f32[8,16,256]{2,1,0:T(8,128)S(1)} %get-tuple-element.57.search, f32[8,16,256]{2,1,0:T(8,128)S(1)} %get-tuple-element.58.smoothed, ...), custom_call_target="tpu_custom_call" | custom-call | tf_op jit(solution)/shard_map/pallas_call | solution.py:45
  (3 shorter events, 0.0 us)
Async XLA Ops:
  0.8 1.0 %copy-start.2 = (f32[3,8,16,256]{3,2,1,0:T(8,128)S(1)}, f32[3,8,16,256]{3,2,1,0:T(8,128)}, u32[]{:S(2)}) copy-start(f32[3,8,16,256]{3,2,1,0:T(8,128)} %velocity.7) | copy-start | bytes 1179652
  1.8 27.0 %copy-start.3 = (f32[3,8,16,256]{3,2,1,0:T(8,128)S(1)}, f32[3,8,16,256]{3,2,1,0:T(8,128)}, u32[]{:S(2)}) copy-start(f32[3,8,16,256]{3,2,1,0:T(8,128)} %velocity.7) | copy-start | bytes 1179652
  1.8 27.0 %copy-start.6 = (f32[32,1024]{1,0:T(8,128)S(1)}, f32[32,1024]{1,0:T(8,128)}, u32[]{:S(2)}) copy-start(f32[32,1024]{1,0:T(8,128)} %inverse.3) | copy-start | bytes 393220
  2.4 7.2 %collective-permute-start.4 = (f32[12,8,256]{2,1,0:T(8,128)S(1)}, f32[12,8,256]{2,1,0:T(8,128)S(1)}, u32[]{:S(2)}, u32[]{:S(2)}) collective-permute-start(f32[12,8,256]{2,1,0:T(8,128)S(1)} %get-tuple-element.39), channel_id=1, source_target_pairs={{0,1},{1,0},{2,3},{3,2},{4,5},{5,4},{6,7},{7,6},{8,9},{9,8},{10,11... | collective-permute-start | bytes 294920 | tf_op jit(solution)/shard_map/ppermute | solution.py:510
  5.4 4.2 %collective-permute-start.5 = (f32[12,8,256]{2,1,0:T(8,128)S(1)}, f32[12,8,256]{2,1,0:T(8,128)S(1)}, u32[]{:S(2)}, u32[]{:S(2)}) collective-permute-start(f32[12,8,256]{2,1,0:T(8,128)S(1)} %get-tuple-element.40), channel_id=1, source_target_pairs={{0,8},{1,2},{2,1},{3,4},{4,3},{5,6},{6,5},{7,15},{8,0},{9,10},{10,... | collective-permute-start | bytes 294920 | tf_op jit(solution)/shard_map/ppermute | solution.py:510
  10.3 31.0 %collective-permute-start.6 = (f32[12,24,256]{2,1,0:T(8,128)S(1)}, f32[12,24,256]{2,1,0:T(8,128)S(1)}, u32[]{:S(2)}, u32[]{:S(2)}) collective-permute-start(f32[12,24,256]{2,1,0:T(8,128)S(1)} %get-tuple-element.42), channel_id=1, source_target_pairs={{0,8},{1,9},{2,10},{3,11},{4,12},{5,13},{6,14},{7,15},{8,0},{9,1},... | collective-permute-start | bytes 884744 | tf_op jit(solution)/shard_map/ppermute | solution.py:510
  10.4 31.0 %collective-permute-start.7 = (f32[12,24,256]{2,1,0:T(8,128)S(1)}, f32[12,24,256]{2,1,0:T(8,128)S(1)}, u32[]{:S(2)}, u32[]{:S(2)}) collective-permute-start(f32[12,24,256]{2,1,0:T(8,128)S(1)} %get-tuple-element.43), channel_id=1, source_target_pairs={{0,1},{1,0},{2,3},{3,2},{4,5},{5,4},{6,7},{7,6},{8,16},{9,17},{10,... | collective-permute-start | bytes 884744 | tf_op jit(solution)/shard_map/ppermute | solution.py:510
  13.0 1.6 %copy-start = (bf16[32,8,16,256]{3,2,1,0:T(8,128)(2,1)S(1)}, bf16[32,8,16,256]{3,2,1,0:T(8,128)(2,1)}, u32[]{:S(2)}) copy-start(bf16[32,8,16,256]{3,2,1,0:T(8,128)(2,1)} %vectors.7) | copy-start | bytes 6291460
  14.5 0.9 %copy-start.4 = (f32[8,16,256]{2,1,0:T(8,128)S(1)}, f32[8,16,256]{2,1,0:T(8,128)}, u32[]{:S(2)}) copy-start(f32[8,16,256]{2,1,0:T(8,128)} %field.5) | copy-start | bytes 393220
  16.7 24.7 %copy-start.1 = (bf16[32,8,16,256]{3,2,1,0:T(8,128)(2,1)S(1)}, bf16[32,8,16,256]{3,2,1,0:T(8,128)(2,1)}, u32[]{:S(2)}) copy-start(bf16[32,8,16,256]{3,2,1,0:T(8,128)(2,1)} %vectors.7) | copy-start | bytes 6291460
  16.7 24.7 %copy-start.5 = (f32[8,16,256]{2,1,0:T(8,128)S(1)}, f32[8,16,256]{2,1,0:T(8,128)}, u32[]{:S(2)}) copy-start(f32[8,16,256]{2,1,0:T(8,128)} %field.5) | copy-start | bytes 393220
  30.2 4.2 %collective-permute-start = (f32[6,8,256]{2,1,0:T(8,128)S(1)}, f32[6,8,256]{2,1,0:T(8,128)S(1)}, u32[]{:S(2)}, u32[]{:S(2)}) collective-permute-start(f32[6,8,256]{2,1,0:T(8,128)S(1)} %get-tuple-element.33), channel_id=1, source_target_pairs={{0,1},{1,0},{2,3},{3,2},{4,5},{5,4},{6,7},{7,6},{8,9},{9,8},{10,11... | collective-permute-start | bytes 147464 | tf_op jit(solution)/shard_map/ppermute | solution.py:510
  30.9 3.4 %collective-permute-start.1 = (f32[6,8,256]{2,1,0:T(8,128)S(1)}, f32[6,8,256]{2,1,0:T(8,128)S(1)}, u32[]{:S(2)}, u32[]{:S(2)}) collective-permute-start(f32[6,8,256]{2,1,0:T(8,128)S(1)} %get-tuple-element.34), channel_id=1, source_target_pairs={{0,8},{1,2},{2,1},{3,4},{4,3},{5,6},{6,5},{7,15},{8,0},{9,10},{10,... | collective-permute-start | bytes 147464 | tf_op jit(solution)/shard_map/ppermute | solution.py:510
  35.0 3.1 %collective-permute-start.2 = (f32[5,32,256]{2,1,0:T(8,128)S(1)}, f32[5,32,256]{2,1,0:T(8,128)S(1)}, u32[]{:S(2)}, u32[]{:S(2)}) collective-permute-start(f32[5,32,256]{2,1,0:T(8,128)S(1)} %get-tuple-element.37), channel_id=1, source_target_pairs={{0,8},{1,9},{2,10},{3,11},{4,12},{5,13},{6,14},{7,15},{8,0},{9,1},... | collective-permute-start | bytes 491528 | tf_op jit(solution)/shard_map/ppermute | solution.py:510
  35.1 6.3 %collective-permute-start.3 = (f32[5,32,256]{2,1,0:T(8,128)S(1)}, f32[5,32,256]{2,1,0:T(8,128)S(1)}, u32[]{:S(2)}, u32[]{:S(2)}) collective-permute-start(f32[5,32,256]{2,1,0:T(8,128)S(1)} %get-tuple-element.38), channel_id=1, source_target_pairs={{0,1},{1,0},{2,3},{3,2},{4,5},{5,4},{6,7},{7,6},{8,16},{9,17},{10,... | collective-permute-start | bytes 491528 | tf_op jit(solution)/shard_map/ppermute | solution.py:510
  55.5 4.2 %collective-permute-start.8 = (f32[6,8,256]{2,1,0:T(8,128)S(1)}, f32[6,8,256]{2,1,0:T(8,128)S(1)}, u32[]{:S(2)}, u32[]{:S(2)}) collective-permute-start(f32[6,8,256]{2,1,0:T(8,128)S(1)} %get-tuple-element.48), channel_id=1, source_target_pairs={{0,1},{1,0},{2,3},{3,2},{4,5},{5,4},{6,7},{7,6},{8,9},{9,8},{10,11... | collective-permute-start | bytes 147464 | tf_op jit(solution)/shard_map/ppermute | solution.py:510
  56.2 3.4 %collective-permute-start.9 = (f32[6,8,256]{2,1,0:T(8,128)S(1)}, f32[6,8,256]{2,1,0:T(8,128)S(1)}, u32[]{:S(2)}, u32[]{:S(2)}) collective-permute-start(f32[6,8,256]{2,1,0:T(8,128)S(1)} %get-tuple-element.49), channel_id=1, source_target_pairs={{0,8},{1,2},{2,1},{3,4},{4,3},{5,6},{6,5},{7,15},{8,0},{9,10},{10,... | collective-permute-start | bytes 147464 | tf_op jit(solution)/shard_map/ppermute | solution.py:510
  60.3 3.1 %collective-permute-start.10 = (f32[5,32,256]{2,1,0:T(8,128)S(1)}, f32[5,32,256]{2,1,0:T(8,128)S(1)}, u32[]{:S(2)}, u32[]{:S(2)}) collective-permute-start(f32[5,32,256]{2,1,0:T(8,128)S(1)} %get-tuple-element.52), channel_id=1, source_target_pairs={{0,8},{1,9},{2,10},{3,11},{4,12},{5,13},{6,14},{7,15},{8,0},{9,1},... | collective-permute-start | bytes 491528 | tf_op jit(solution)/shard_map/ppermute | solution.py:510
  60.4 6.3 %collective-permute-start.11 = (f32[5,32,256]{2,1,0:T(8,128)S(1)}, f32[5,32,256]{2,1,0:T(8,128)S(1)}, u32[]{:S(2)}, u32[]{:S(2)}) collective-permute-start(f32[5,32,256]{2,1,0:T(8,128)S(1)} %get-tuple-element.53), channel_id=1, source_target_pairs={{0,1},{1,0},{2,3},{3,2},{4,5},{5,4},{6,7},{7,6},{8,16},{9,17},{10,... | collective-permute-start | bytes 491528 | tf_op jit(solution)/shard_map/ppermute | solution.py:510

commit v2 on v1

v2 whole, which is shorter than its diff:
```python
import functools

import jax
import jax.numpy as jnp
from jax import lax
from jax.experimental import pallas as pl
from jax.experimental.pallas import tpu as pltpu
from jax.sharding import PartitionSpec as P

DEPTH = 2
CHEB = 4
WIDE = 4
LANES = 128
AXES = ("gx", "gy")
F32 = jnp.float32
HIGHEST = lax.Precision.HIGHEST

cheb_center = 1.0
cheb_radius = 0.9

ODD_X, ODD_Y, LOW_X, HIGH_X, LOW_Y, HIGH_Y, SLOT = range(7)
OWN_LOW, PAST_LOW, PAST_HIGH, OWN_HIGH = 3, 4, 5, 6


def pair_permutations(count_x, count_y):
    def number(i, j):
        return i * count_y + j

    even_x, odd_x, even_y, odd_y = [], [], [], []
    for i in range(count_x):
        for j in range(count_y):
            here = number(i, j)
            even_x.append((here, number(i ^ 1, j)))
            even_y.append((here, number(i, j ^ 1)))
            other = ((i - 1) ^ 1) + 1
            odd_x.append((here, number(other, j) if 0 <= other < count_x else number(i, j ^ 1)))
            other = ((j - 1) ^ 1) + 1
            odd_y.append((here, number(i, other) if 0 <= other < count_y else number(i ^ 1, j)))
    return (even_x, odd_x), (even_y, odd_y)


def call(body, outs, scratch, *args, micros):
    specs = [pl.BlockSpec(memory_space=pltpu.SMEM)] + [pl.BlockSpec(memory_space=pltpu.VMEM)] * (len(args) - 1)
    return pl.pallas_call(
        body,
        out_shape=[jax.ShapeDtypeStruct(shape, F32) for shape in outs],
        in_specs=specs,
        out_specs=[pl.BlockSpec(memory_space=pltpu.VMEM)] * len(outs),
        scratch_shapes=[pltpu.VMEM(kind, F32) if isinstance(kind, tuple) else kind for kind in scratch],
        compiler_params=pltpu.CompilerParams(vmem_limit_bytes=24 * 1024 * 1024),
        cost_estimate=pl.CostEstimate(flops=0, bytes_accessed=int(micros * 3.6e6), transcendentals=0),
    )(*args)


def z_before(plane):
    return pltpu.roll(plane, 1, 1)


def z_after(plane, keep_last):
    return jnp.where(keep_last, pltpu.roll(plane, plane.shape[1] - 1, 1), 0.0)


def lane_masks(shape):
    lanes = lax.broadcasted_iota(jnp.int32, shape, 1)
    return lanes > 0, lanes < shape[1] - 1


def restrict(vectors, field, sums, flags, send, copies=()):
    count, size_x, size_y, size_z = vectors.shape
    stage = send[1]
    stage[...] = jnp.zeros_like(stage)

    def lanes_of(total):
        total = jnp.sum(total, axis=0, keepdims=True)
        return functools.reduce(jnp.add, [total[:, k : k + LANES] for k in range(0, size_z, LANES)])

    offset = pl.multiple_of(flags[SLOT] * count, count)
    for j in range(count):
        if copies and j % (count // len(copies)) == 0:
            copies[j // (count // len(copies))].wait()
        total = vectors[j, 0].astype(F32) * field[0]
        for x in range(1, size_x):
            total = total + vectors[j, x].astype(F32) * field[x]
        stage[pl.ds(offset + j, 1), :] = lanes_of(total)
    for k, total in enumerate(sums):
        stage[LANES + k : LANES + k + 1, :] = lanes_of(total)
    write_row(stage, send[0])


def write_row(stage, out):
    row = lax.dot_general(
        jnp.ones((8, LANES), F32), stage[...], (((1,), (1,)), ((), ())), precision=HIGHEST, preferred_element_type=F32
    )
    for k in range(0, out.shape[0], 8):
        out[k : k + 8, :] = row


def gathered(received):
    count = received.shape[0]
    return received[:, :LANES], jnp.sum(received[:, LANES:], axis=0, keepdims=True)


def solve(coarse, inverse, vectors):
    count = coarse.shape[0]
    share = LANES // vectors.shape[0]
    groups = count // share
    pick = (
        lax.broadcasted_iota(jnp.int32, (groups, count), 1) // share
        == lax.broadcasted_iota(jnp.int32, (groups, count), 0)
    ).astype(F32)
    packed = jnp.dot(pick, coarse, precision=HIGHEST, preferred_element_type=F32)
    total = inverse[:, :LANES] * packed[0:1]
    for k in range(1, groups):
        total = total + inverse[:, k * LANES : (k + 1) * LANES] * packed[k : k + 1]
    return jnp.sum(total, axis=1, keepdims=True).astype(jnp.bfloat16).astype(F32)


def prolong(solved, vectors, corr):
    count, size_x, size_y, size_z = vectors.shape
    totals = [jnp.zeros((size_y, size_z), F32) for _ in range(size_x)]
    for j in range(count):
        weight = jnp.broadcast_to(solved[j : j + 1], (size_y, size_z))
        for x in range(size_x):
            totals[x] = totals[x] + vectors[j, x].astype(F32) * weight
    for x in range(size_x):
        corr[x] = totals[x]


def subtract_own(field, corr, velocity, out):
    size_x, size_y, size_z = corr.shape
    keep_first, keep_last = lane_masks((size_y, size_z))
    rows = lax.broadcasted_iota(jnp.int32, (size_y, size_z), 0)
    for x in range(size_x):
        v0, v1, v2 = velocity[0, x], velocity[1, x], velocity[2, x]
        here = corr[x]
        image = (6.0 + v0 + v1 + v2) * here
        if x + 1 < size_x:
            image = image - corr[x + 1]
        if x > 0:
            image = image - (1.0 + v0) * corr[x - 1]
        image = image - jnp.where(rows < size_y - 1, pltpu.roll(here, size_y - 1, 0), 0.0)
        image = image - (1.0 + v1) * jnp.where(rows > 0, pltpu.roll(here, 1, 0), 0.0)
        image = image - z_after(here, keep_last) - (1.0 + v2) * jnp.where(keep_first, z_before(here), 0.0)
        out[x] = field[x] - image


def write_y_message(out, field, corr, high):
    size_x, size_y, _ = corr.shape
    start = size_y - WIDE if high else 0
    edge = size_y - 1 if high else 0
    for x in range(size_x):
        out[x] = field[x, start : start + WIDE, :]
        out[size_x + x // WIDE, x % WIDE : x % WIDE + 1, :] = corr[x, edge : edge + 1, :]
    last = size_x + size_x // WIDE
    out[last] = corr[0, start : start + WIDE, :]
    out[last + 1] = corr[size_x - 1, start : start + WIDE, :]


def by_parity(odd, write, even_out, odd_out):
    @pl.when(odd == 0)
    def _():
        write(even_out, True)
        write(odd_out, False)

    @pl.when(odd != 0)
    def _():
        write(even_out, False)
        write(odd_out, True)


def velocity_faces_kernel(flags, velocity, after, even_y, odd_y, even_x, odd_x):
    _, size_x, size_y, _ = velocity.shape

    def write_y(out, high):
        start = size_y - WIDE if high else 0
        for d in range(3):
            for x in range(size_x):
                out[d, x] = velocity[d, x, start : start + WIDE, :]

    def write_x(out, high):
        start = size_x - WIDE if high else 0
        for d in range(3):
            for k in range(WIDE):
                out[d, k, 0:size_y, :] = velocity[d, start + k]
                out[d, k, size_y:, :] = jnp.zeros((2 * WIDE, velocity.shape[3]), F32)

    by_parity(flags[ODD_Y], write_y, even_y, odd_y)
    by_parity(flags[ODD_X], write_x, even_x, odd_x)


def coefficients(x, v0, v1, v2, kept, keep_first, outs):
    inverse, b0, b1, b2 = outs
    total = 6.0 + v0 + v1 + v2
    value = jnp.where(kept, 1.0 / total, 0.0)
    inverse[x] = value
    b0[x] = value * (1.0 + v0)
    b1[x] = value * (1.0 + v1)
    b2[x] = jnp.where(keep_first, value * (1.0 + v2), 0.0)
    return total


def rows_in_grid(flags, shape):
    row = lax.broadcasted_iota(jnp.int32, shape, 0)
    first_row = jnp.where(flags[LOW_Y] != 0, 0, WIDE)
    end_row = jnp.where(flags[HIGH_Y] != 0, shape[0], shape[0] - WIDE)
    return (row >= first_row) & (row < end_row)


def coefficients_kernel(flags, velocity, even_in, odd_in, diagonal, inverse, b0, b1, b2, wide):
    _, size_x, size_y, size_z = velocity.shape
    rows = size_y + 2 * WIDE

    def place(low, high):
        for d in range(3):
            for x in range(size_x):
                wide[d, x, 0:WIDE, :] = low[d, x]
                wide[d, x, WIDE : WIDE + size_y, :] = velocity[d, x]
                wide[d, x, WIDE + size_y : rows, :] = high[d, x]

    @pl.when(flags[ODD_Y] == 0)
    def _():
        place(odd_in, even_in)

    @pl.when(flags[ODD_Y] != 0)
    def _():
        place(even_in, odd_in)

    kept = rows_in_grid(flags, (rows, size_z))
    keep_first, _ = lane_masks((rows, size_z))
    for x in range(size_x):
        diagonal[x] = coefficients(x, wide[0, x], wide[1, x], wide[2, x], kept, keep_first, (inverse, b0, b1, b2))


def halo_coefficients(flags, even_in, odd_in, even_vel, odd_vel, outs, wide):
    rows, size_z = even_vel.shape[2:]
    size_y = rows - 2 * WIDE
    kept = rows_in_grid(flags, (rows, size_z))
    keep_first, _ = lane_masks((rows, size_z))

    def side(start, message, faces, present):
        for k in range(WIDE):
            for d in range(3):
                wide[d, 0:WIDE, :] = message[WIDE + 1 + d, 8 * k : 8 * k + WIDE, :]
                wide[d, WIDE : WIDE + size_y, :] = faces[d, k, 0:size_y, :]
                wide[d, WIDE + size_y : rows, :] = message[WIDE + 1 + d, 8 * k + WIDE : 8 * k + 2 * WIDE, :]
            coefficients(start + k, wide[0], wide[1], wide[2], kept & (flags[present] != 0), keep_first, outs)

    @pl.when(flags[ODD_X] == 0)
    def _():
        side(0, odd_in, odd_vel, LOW_X)
        side(WIDE, even_in, even_vel, HIGH_X)

    @pl.when(flags[ODD_X] != 0)
    def _():
        side(0, even_in, even_vel, LOW_X)
        side(WIDE, odd_in, odd_vel, HIGH_X)


class Region:
    def __init__(self, own, halo):
        self.own, self.halo = own, halo

    def __getitem__(self, index):
        x, tile = index if isinstance(index, tuple) else (index, slice(None))
        size_x = self.own.shape[0]
        if x < WIDE:
            return self.halo[x, tile]
        return self.own[x - WIDE, tile] if x < WIDE + size_x else self.halo[x - size_x, tile]


def coarse_kernel(flags, received, inverse, vectors, field, velocity, after, corr, rest, even_out, odd_out):
    coarse, _ = gathered(received)
    prolong(solve(coarse, inverse, vectors), vectors, corr)
    subtract_own(field, corr, velocity, rest)
    by_parity(flags[ODD_Y], lambda out, high: write_y_message(out, rest, corr, high), even_out, odd_out)


def second_coarse_kernel(
    flags, received, second, inverse, vectors, field, image, velocity, corr, rest, middle, alpha, even_out, odd_out
):
    coarse, _ = gathered(received)
    coarse_image, products = gathered(second)
    step = jnp.broadcast_to(products[:, 0:1] / products[:, 1:2], alpha.shape)
    alpha[...] = step
    step = step[0:1, 0:1]
    for x in range(field.shape[0]):
        middle[x] = field[x] - step * image[x]
    prolong(solve(coarse - step * coarse_image, inverse, vectors), vectors, corr)
    subtract_own(middle, corr, velocity, rest)
    by_parity(flags[ODD_Y], lambda out, high: write_y_message(out, rest, corr, high), even_out, odd_out)


def extend_kernel(flags, rest, corr, even_in, odd_in, even_vel, odd_vel, wide, sides, even_out, odd_out):
    size_x, size_y, size_z = rest.shape
    rows = size_y + 2 * WIDE

    def place(low, high):
        has_low, has_high = flags[LOW_Y] != 0, flags[HIGH_Y] != 0
        for x in range(size_x):
            at, line = size_x + x // WIDE, slice(x % WIDE, x % WIDE + 1)
            wide[x, 0:WIDE, :] = low[x]
            wide[x, WIDE : WIDE + size_y, :] = rest[x]
            wide[x, WIDE + size_y : rows, :] = high[x]
            wide[x, rows : rows + 8, :] = jnp.zeros((8, size_z), F32)
            wide[x, rows + OWN_LOW : rows + OWN_LOW + 1, :] = corr[x, 0:1, :]
            wide[x, rows + PAST_LOW : rows + PAST_LOW + 1, :] = jnp.where(has_low, low[at, line, :], 0.0)
            wide[x, rows + PAST_HIGH : rows + PAST_HIGH + 1, :] = jnp.where(has_high, high[at, line, :], 0.0)
            wide[x, rows + OWN_HIGH : rows + OWN_HIGH + 1, :] = corr[x, size_y - 1 : size_y, :]
        last = size_x + size_x // WIDE
        for side, x in enumerate((0, size_x - 1)):
            sides[side, 0:WIDE, :] = low[last + side]
            sides[side, WIDE : WIDE + size_y, :] = corr[x]
            sides[side, WIDE + size_y : rows, :] = high[last + side]
            sides[side, rows : rows + 8, :] = jnp.zeros((8, size_z), F32)

    @pl.when(flags[ODD_Y] == 0)
    def _():
        place(odd_in, even_in)

    @pl.when(flags[ODD_Y] != 0)
    def _():
        place(even_in, odd_in)

    def write(out, high):
        start = size_x - WIDE if high else 0
        for k in range(WIDE):
            out[k] = wide[start + k]
        out[WIDE] = sides[1 if high else 0]

    by_parity(flags[ODD_X], write, even_out, odd_out)
    if even_vel is None:
        return

    def corners(low, high):
        def write(out, upper):
            start = size_x - WIDE if upper else 0
            for d in range(3):
                for k in range(WIDE):
                    out[WIDE + 1 + d, 8 * k : 8 * k + WIDE, :] = low[d, start + k]
                    out[WIDE + 1 + d, 8 * k + WIDE : 8 * k + 2 * WIDE, :] = high[d, start + k]

        by_parity(flags[ODD_X], write, even_out, odd_out)

    @pl.when(flags[ODD_Y] == 0)
    def _():
        corners(odd_vel, even_vel)

    @pl.when(flags[ODD_Y] != 0)
    def _():
        corners(even_vel, odd_vel)


def extend_again_kernel(flags, rest, corr, even_in, odd_in, wide, sides, even_out, odd_out):
    extend_kernel(flags, rest, corr, even_in, odd_in, None, None, wide, sides, even_out, odd_out)


def beside_terms(before, here, after, x, tile, coefs, keep_last):
    inverse, b0, b1, b2 = coefs
    rows = here.shape[0]
    ahead = pltpu.roll(here, rows - 1, 0) + z_after(here, keep_last)
    if after is not None:
        ahead = ahead + after
    total = inverse[x, tile] * ahead + b1[x, tile] * pltpu.roll(here, 1, 0) + b2[x, tile] * z_before(here)
    if before is not None:
        total = total + b0[x, tile] * before
    return total


def chebyshev(planes, tile, inside, source, left, update, coefs, keep_last, wanted):
    sigma = cheb_center / cheb_radius
    rho = 1.0 / sigma
    first, last = planes[0], planes[-1]
    for x in planes:
        update[0, x, tile] = jnp.where(inside, source(x), 0.0)
    estimate = {}
    for sweep in range(1, CHEB):
        rest = CHEB - 1 - sweep
        low, high = max(first, wanted[0] - rest), min(last, wanted[-1] + rest)
        rho_next = 1.0 / (2.0 * sigma - rho)
        for x in range(low, high + 1):
            here = update[sweep - 1, x, tile]
            before = update[sweep - 1, x - 1, tile] if x > first else None
            after = update[sweep - 1, x + 1, tile] if x < last else None
            remainder = (here if sweep == 1 else left[x, tile]) - here
            remainder = remainder + beside_terms(before, here, after, x, tile, coefs, keep_last)
            if rest:
                left[x, tile] = remainder
            value = rho_next * rho * here + (2.0 * rho_next / cheb_radius) * jnp.where(inside, remainder, 0.0)
            if rest:
                update[sweep, x, tile] = value
            else:
                for k in range(CHEB - 1):
                    value = value + update[k, x, tile]
                estimate[x] = value
        rho = rho_next
    return estimate


def smooth(
    flags, wide, sides, even_in, odd_in, diagonal, coefs, corr, field_out, image_out, scratch
):
    source, left, update, whole = scratch
    inverse, b0, b1, _ = coefs
    size_x, size_y, size_z = corr.shape
    rows = size_y + 2 * WIDE
    span = size_x + 2 * WIDE
    row = lax.broadcasted_iota(jnp.int32, (rows, size_z), 0)
    keep_last = lane_masks((rows, size_z))[1]
    has_low_x, has_high_x = flags[LOW_X] != 0, flags[HIGH_X] != 0
    has_low_y, has_high_y = flags[LOW_Y] != 0, flags[HIGH_Y] != 0
    lowest, highest = slice(0, 8), slice(rows - 8, rows)
    tile_row = lax.broadcasted_iota(jnp.int32, (8, size_z), 0)
    last_tile = slice(rows, rows + 8)
    kept = (tile_row == OWN_LOW) | (tile_row == PAST_LOW)

    def source_plane(x, plane):
        source[x] = inverse[x] * plane[0:rows]
        lines = plane[last_tile]
        for tile, shift in ((lowest, 0), (highest, 8 - (PAST_HIGH - OWN_LOW))):
            moved = pltpu.roll(lines, shift, 0) if shift else lines
            factor = jnp.where(tile_row == PAST_LOW, b1[x, tile], inverse[x, tile])
            source[x, tile] = source[x, tile] + jnp.where(kept, moved * factor, 0.0)

    def halo(low, high):
        for k in range(WIDE):
            source_plane(k, low.at[k])
            source_plane(WIDE + size_x + k, high.at[k])
        whole[0] = jnp.where(has_low_x, low[WIDE, 0:rows], 0.0)
        whole[size_x + 1] = jnp.where(has_high_x, high[WIDE, 0:rows], 0.0)

    @pl.when(flags[ODD_X] == 0)
    def _():
        halo(odd_in, even_in)

    @pl.when(flags[ODD_X] != 0)
    def _():
        halo(even_in, odd_in)

    for k in range(size_x):
        source_plane(WIDE + k, wide.at[k])

    low_in, high_in = WIDE, WIDE + size_x - 1
    source[low_in - 1] = source[low_in - 1] + inverse[low_in - 1] * sides[0, 0:rows]
    source[low_in] = source[low_in] + b0[low_in] * whole[0]
    source[high_in] = source[high_in] + inverse[high_in] * whole[size_x + 1]
    source[high_in + 1] = source[high_in + 1] + b0[high_in + 1] * sides[1, 0:rows]

    def run(planes, tile, inside, wanted):
        return chebyshev(
            planes,
            tile,
            inside,
            lambda x: source[x, tile],
            left,
            update,
            coefs,
            lane_masks(inside.shape)[1],
            wanted,
        )

    everything = slice(0, rows)
    box_rows = (row >= WIDE - DEPTH) & (row < WIDE + size_y + DEPTH)
    box_planes = range(WIDE - DEPTH, WIDE + size_x + DEPTH)
    own_planes = range(WIDE, WIDE + size_x)
    inner = (row >= WIDE) & (row < WIDE + size_y)

    beside = run(range(0, WIDE + DEPTH), everything, box_rows, (WIDE - 1,))[WIDE - 1]
    whole[0] = jnp.where(has_low_x & inner, whole[0] + beside, 0.0)
    x = WIDE + size_x
    beside = run(range(span - WIDE - DEPTH, span), everything, box_rows, (x,))[x]
    whole[size_x + 1] = jnp.where(has_high_x & inner, whole[size_x + 1] + beside, 0.0)

    own = run(box_planes, everything, box_rows, tuple(own_planes))
    zeros = jnp.zeros((rows - size_y, size_z), F32)
    for k in range(size_x):
        placed = pltpu.roll(jnp.concatenate([corr[k], zeros], axis=0), WIDE, 0)
        whole[k + 1] = jnp.where(inner, placed + own[WIDE + k], 0.0)

    beside = run(box_planes, lowest, tile_row < WIDE + DEPTH, tuple(own_planes))
    for k in range(size_x):
        line = pltpu.roll(wide[k, last_tile], 8 + WIDE - 1 - PAST_LOW, 0) + beside[WIDE + k]
        here = has_low_y & (tile_row == WIDE - 1)
        whole[k + 1, lowest] = jnp.where(here, line, whole[k + 1, lowest])
    beside = run(box_planes, highest, tile_row >= 8 - WIDE - DEPTH, tuple(own_planes))
    for k in range(size_x):
        line = pltpu.roll(wide[k, last_tile], (8 + 8 - WIDE - PAST_HIGH) % 8, 0) + beside[WIDE + k]
        here = has_high_y & (tile_row == 8 - WIDE)
        whole[k + 1, highest] = jnp.where(here, line, whole[k + 1, highest])

    for k in range(size_x):
        x = WIDE + k
        terms = beside_terms(whole[k], whole[k + 1], whole[k + 2], x, everything, coefs, keep_last)
        image = diagonal[k] * (whole[k + 1] - terms)
        image_out[k] = pltpu.roll(image, rows - WIDE, 0)[0:size_y]
        field_out[k] = pltpu.roll(whole[k + 1], rows - WIDE, 0)[0:size_y]


def dot_planes(left, right):
    total = left[0] * right[0]
    for x in range(1, left.shape[0]):
        total = total + left[x] * right[x]
    return total


def search_kernel(
    flags, wide, sides, even_in, odd_in, diagonal, own0, own1, own2, own3, corr, even_vel, odd_vel, vectors, right_side,
    search, image, out, halo0, halo1, halo2, halo3, stage, wide_vel, *scratch
):
    halos = (halo0, halo1, halo2, halo3)
    halo_coefficients(flags, even_in, odd_in, even_vel, odd_vel, halos, wide_vel)
    coefs = [Region(*pair) for pair in zip((own0, own1, own2, own3), halos)]
    smooth(flags, wide, sides, even_in, odd_in, diagonal, coefs, corr, search, image, scratch)
    products = [dot_planes(right_side, right_side), dot_planes(right_side, image)]
    restrict(vectors, image, products, flags, (out, stage))


def smoothed_kernel(
    flags, wide, sides, even_in, odd_in, diagonal, own0, own1, own2, own3, corr, halo0, halo1, halo2, halo3, middle,
    smoothed, turned, out, stage, *scratch
):
    coefs = [Region(*pair) for pair in zip((own0, own1, own2, own3), (halo0, halo1, halo2, halo3))]
    smooth(flags, wide, sides, even_in, odd_in, diagonal, coefs, corr, smoothed, turned, scratch)
    stage[...] = jnp.zeros_like(stage)
    for k, total in enumerate((dot_planes(turned, middle), dot_planes(turned, turned))):
        total = jnp.sum(total, axis=0, keepdims=True)
        parts = [total[:, i : i + LANES] for i in range(0, total.shape[1], LANES)]
        stage[LANES + k : LANES + k + 1, :] = functools.reduce(jnp.add, parts)
    write_row(stage, out)


def last_kernel(flags, received, alpha, search, smoothed, middle, turned, solution_field, residual):
    _, sums = gathered(received)
    omega = sums[:, 0:1] / sums[:, 1:2]
    step = alpha[0:1, 0:1]
    for x in range(search.shape[0]):
        solution_field[x] = step * search[x] + omega * smoothed[x]
        residual[x] = middle[x] - omega * turned[x]


def local(right_side, velocity, deflation, inverse_rows):
    size_x, size_y, size_z = right_side.shape
    vectors_count = deflation.shape[0]
    count_x, count_y = lax.axis_size("gx"), lax.axis_size("gy")
    count = count_x * count_y
    at_x, at_y = lax.axis_index("gx"), lax.axis_index("gy")
    flags = jnp.stack(
        [
            at_x % 2,
            at_y % 2,
            (at_x > 0).astype(jnp.int32),
            (at_x < count_x - 1).astype(jnp.int32),
            (at_y > 0).astype(jnp.int32),
            (at_y < count_y - 1).astype(jnp.int32),
            (at_x * count_y + at_y) % (LANES // vectors_count),
            at_x,
        ]
    ).astype(jnp.int32)
    x_pairs, y_pairs = pair_permutations(count_x, count_y)

    def swap(messages, pairs):
        return [lax.ppermute(message, AXES, pair) for message, pair in zip(messages, pairs)]

    def share(row):
        return lax.all_to_all(row, AXES, 0, 0, tiled=True)

    rows = size_y + 2 * WIDE
    span = size_x + 2 * WIDE
    block = (size_x, size_y, size_z)
    row = (count, 2 * LANES)
    stage = (2 * LANES, LANES)
    y_message = (size_x + size_x // WIDE + 2, WIDE, size_z)
    region = (span, rows, size_z)
    smooth_scratch = [region, region, (CHEB - 1,) + region, (size_x + 2, rows, size_z)]

    rounded = lax.reduce_precision(right_side, 8, 7)
    partial = lax.optimization_barrier(jnp.sum(deflation.astype(F32) * rounded, axis=(1, 2)))
    share_count = LANES // vectors_count
    first_row = jnp.where(jnp.arange(2 * share_count)[:, None] == flags[SLOT], jnp.sum(partial, axis=1)[None, :], 0.0)
    first_row = jnp.broadcast_to(first_row.reshape(1, 2 * LANES), row)

    first = share(first_row)
    faces_y, faces_x = (3, size_x, WIDE, size_z), (3, WIDE, rows, size_z)
    faces = call(
        velocity_faces_kernel, [faces_y] * 2 + [faces_x] * 2, [], flags, velocity, first_row[0, :8], micros=0.01
    )
    after = faces[0]
    velocity_y, velocity_x = swap(faces[:2], y_pairs), swap(faces[2:], x_pairs)

    def exchange(corr, rest, messages, extend, message, *vel):
        wide, sides, *messages = call(
            extend,
            [(size_x, rows + 8, size_z), (2, rows + 8, size_z), message, message],
            [],
            flags,
            rest,
            corr,
            *swap(messages, y_pairs),
            *vel,
            micros=0.01,
        )
        return (wide, sides, *swap(messages, x_pairs), *coefs, corr)

    corr, rest, *messages = call(
        coarse_kernel,
        [block, block, y_message, y_message],
        [],
        flags,
        first,
        inverse_rows,
        deflation,
        right_side,
        velocity,
        after,
        micros=1.4,
    )
    wide_own, wide_halo = (size_x, rows, size_z), (2 * WIDE, rows, size_z)
    coefs = call(
        coefficients_kernel,
        [wide_own] * 5,
        [(3, size_x, rows, size_z)],
        flags,
        velocity,
        *velocity_y,
        micros=0.01,
    )
    search, image, second_row, *halo_coefs = call(
        search_kernel,
        [block, block, row] + [wide_halo] * 4,
        [stage, (3, rows, size_z)] + smooth_scratch,
        flags,
        *exchange(corr, rest, messages, extend_kernel, (WIDE + 4, rows + 8, size_z), *velocity_y),
        *velocity_x,
        deflation,
        right_side,
        micros=3.0,
    )
    second = share(second_row)
    corr, rest, middle, alpha, *messages = call(
        second_coarse_kernel,
        [block, block, block, (8, LANES), y_message, y_message],
        [],
        flags,
        first,
        second,
        inverse_rows,
        deflation,
        right_side,
        image,
        velocity,
        micros=1.4,
    )
    smoothed, turned, third_row = call(
        smoothed_kernel,
        [block, block, row],
        [stage] + smooth_scratch,
        flags,
        *exchange(corr, rest, messages, extend_again_kernel, (WIDE + 1, rows + 8, size_z)),
        *halo_coefs,
        middle,
        micros=2.5,
    )
    third = share(third_row)
    return tuple(
        call(last_kernel, [block, block], [], flags, third, alpha, search, smoothed, middle, turned, micros=1.4)
    )


def solution(mesh):
    return jax.shard_map(
        local,
        mesh=mesh,
        in_specs=(
            P("gx", "gy", None),
            P(None, "gx", "gy", None),
            P(None, "gx", "gy", None),
            P(("gx", "gy"), None),
        ),
        out_specs=(P("gx", "gy", None), P("gx", "gy", None)),
        check_vma=False,
    )
```

time: 80.4 us -> 74.2 us (0.923)
  blocking collectives: 31 us -> 19 us
  starting transfers between devices: 13.2 us -> 19.5 us
  other arithmetic: 0 us -> 3.36 us
  local copies, waits for them, and re-layouts: 3.79 us -> 1.76 us
  Pallas kernels: 13.7 us -> 12.5 us
    all_to_all x3 -> x2, blocking collectives: 31 us -> 19 us  [share(): return lax.all_to_all(row, AXES, 0, 0, tiled=True)]
    all_to_all x0 -> x1, starting transfers between devices: none -> 7.38 us  [share(): return lax.all_to_all(row, AXES, 0, 0, tiled=True)]
    ppermute x12, waiting for transfers between devices: 17.6 us -> 11.6 us  [swap(): lax.ppermute(message, AXES, pair)]
    all_to_all x0 -> x1, waiting for transfers between devices: none -> 5.35 us  [share(): return lax.all_to_all(row, AXES, 0, 0, tiled=True)]
    unnamed x17 -> x15, local copies, waits for them, and re-layouts: 3.52 us -> 0.75 us
    reduce_sum x0 -> x2, other arithmetic: none -> 2.18 us  [the longest x1 2.07 us: local(): jnp.sum(deflation.astype(F32) * rounded, axis=(1, 2))]
    pallas_call x10 -> x9, Pallas kernels: 13.7 us -> 12.5 us  [call(): pl.pallas_call(body, out_shape=[jax.ShapeDtypeStruct(shape, F32) for shap...]
    ppermute x12, starting transfers between devices: 13.2 us -> 12.1 us  [swap(): lax.ppermute(message, AXES, pair)]
  transfers between devices with their start and end apart: 12 -> 13, of which waited for: 5 -> 5; matrix products, arithmetic and copies ran while one was open for 0% -> 1% of each run, Pallas kernels for 4% -> 4%
where the time goes in v2:
time: 74.2 us; the launch traced here: 74 us
  starting transfers between devices  19.5 us (26%)
  blocking collectives  19 us (26%)
  waiting for transfers between devices  17 us (23%)
  Pallas kernels  12.5 us (17%)
  other arithmetic  3.36 us (5%)
  local copies, waits for them, and re-layouts  1.76 us (2%)
  between operations  0.86 us (1%)
    all_to_all x2, blocking collectives, share(): return lax.all_to_all(row, AXES, 0, 0, tiled=True)  19 us
    pallas_call x9, Pallas kernels, call(): pl.pallas_call(body, out_shape=[jax.ShapeDtypeStruct(shape, F32) for shap...  12.5 us
    ppermute x12, starting transfers between devices, swap(): lax.ppermute(message, AXES, pair)  12.1 us
    ppermute x12, waiting for transfers between devices, swap(): lax.ppermute(message, AXES, pair)  11.6 us
    all_to_all x1, starting transfers between devices, share(): return lax.all_to_all(row, AXES, 0, 0, tiled=True)  7.38 us
    all_to_all x1, waiting for transfers between devices, share(): return lax.all_to_all(row, AXES, 0, 0, tiled=True)  5.35 us
    reduce_sum x1, other arithmetic, local(): jnp.sum(deflation.astype(F32) * rounded, axis=(1, 2))  2.07 us
  transfers between devices with their start and end apart: 13, of which 5 were waited for; matrix products, arithmetic and copies ran while one was open for 1% of the time, Pallas kernels for 4%

profile of v2, /device:TPU:0, one launch (start us, length us, event | category | flops | bytes accessed | tf_op | source)
XLA Modules:
  0.0 74.0 jit_solution(5924680244481810396)
XLA Ops:
  0.6 0.0 copy-start.2
  0.6 0.0 copy-start
  0.7 0.0 copy-start.1
  0.7 0.0 copy-start.3
  0.7 1.1 %reduce_precision.3 = f32[8,16,256]{2,1,0:T(8,128)S(1)} reduce-precision(f32[8,16,256]{2,1,0:T(8,128)} %field.3), exponent_bits=8, mantissa_bits=7 | non-fusion elementwise | flops 32768 | bytes 262144 | tf_op jit(solution)/shard_map/reduce_precision | solution.py:575
  1.8 2.1 %multiply_reduce_fusion = f32[32,256]{1,0:T(8,128)S(1)} fusion(bf16[32,8,16,256]{3,2,1,0:T(8,128)(2,1)} %vectors.5, f32[8,16,256]{2,1,0:T(8,128)S(1)} %reduce_precision.3), kind=kLoop, calls=%fused_computation | loop fusion | flops 3137536 | bytes 2260992 | tf_op jit(solution)/shard_map/reduce_sum | solution.py:576
  3.9 0.1 reduce_sum.19
  4.0 0.1 broadcast_select_fusion
  4.1 0.1 select_n.38
  4.2 0.1 stack.51.flags
  4.3 0.0 copy-done.1
  4.3 0.6 shard_map.59
  4.9 0.0 copy-start.4
  4.9 0.7 copy-done.4
  5.6 0.5 collective-permute-start.3
  6.1 0.1 select_n.37
  6.1 0.6 broadcast_in_dim.31
  6.8 7.4 %all-to-all-start = ((f32[32,1,256]{2,1,0:T(1,128)}), f32[32,1,256]{2,1,0:T(1,128)S(1)}, u32[]{:S(2)}, u32[]{:S(2)}) async-start(f32[32,1,256]{2,1,0:T(1,128)} %broadcast_in_dim.31), calls=%async_computation | async-start | bytes 65536 | tf_op jit(solution)/shard_map/all_to_all | solution.py:564
  14.2 1.8 %collective-permute-start.2 = (f32[3,8,4,256]{3,2,1,0:T(4,128)S(1)}, f32[3,8,4,256]{3,2,1,0:T(4,128)S(1)}, u32[]{:S(2)}, u32[]{:S(2)}) collective-permute-start(f32[3,8,4,256]{3,2,1,0:T(4,128)S(1)} %get-tuple-element.39.after), channel_id=1, source_target_pairs={{0,1},{1,0},{2,3},{3,2},{4,5},{5,4},{6,7},{7,6},{8,9},{9,8},{10,11... | collective-permute-start | bytes 294920 | tf_op jit(solution)/shard_map/ppermute | solution.py:561
  16.0 5.4 %all-to-all-done = f32[32,1,256]{2,1,0:T(1,128)S(1)} async-done(((f32[32,1,256]{2,1,0:T(1,128)}), f32[32,1,256]{2,1,0:T(1,128)S(1)}, u32[]{:S(2)}, u32[]{:S(2)}) %all-to-all-start) | async-done | bytes 32800 | tf_op jit(solution)/shard_map/all_to_all | solution.py:564
  21.3 0.0 copy-start.5
  21.3 0.0 copy-done.2
  21.4 0.0 copy-done
  21.4 0.0 copy-done.3
  21.4 1.4 %shard_map.60 = (f32[8,16,256]{2,1,0:T(8,128)S(1)}, f32[8,16,256]{2,1,0:T(8,128)S(1)}, f32[12,4,256]{2,1,0:T(4,128)S(1)}, f32[12,4,256]{2,1,0:T(4,128)S(1)}) custom-call(s32[8]{0:T(128)S(1)} %stack.51.flags, f32[32,256]{1,0:T(8,128)S(1)} %bitcast.21, f32[32,1024]{1,0:T(8,128)S(1)} %copy-done.3, bf16[32,8,16,256]{3,2,1,0:T(8,128)(2,1)S(1)} %copy-done, ...), custom_call_target="tpu_custom_call" | custom-call | bytes 5040000 | tf_op jit(solution)/shard_map/pallas_call | solution.py:44
  22.7 0.7 %collective-permute-start = (f32[12,4,256]{2,1,0:T(4,128)S(1)}, f32[12,4,256]{2,1,0:T(4,128)S(1)}, u32[]{:S(2)}, u32[]{:S(2)}) collective-permute-start(f32[12,4,256]{2,1,0:T(4,128)S(1)} %get-tuple-element.42), channel_id=1, source_target_pairs={{0,1},{1,0},{2,3},{3,2},{4,5},{5,4},{6,7},{7,6},{8,9},{9,8},{10,11... | collective-permute-start | bytes 147464 | tf_op jit(solution)/shard_map/ppermute | solution.py:561
  23.5 0.0 collective-permute-start.1
  23.5 0.0 copy-done.5
  23.5 0.5 collective-permute-start.6
  24.0 0.0 collective-permute-done.3.odd_vel.odd_in
  24.0 1.6 %collective-permute-start.7 = (f32[3,4,24,256]{3,2,1,0:T(8,128)S(1)}, f32[3,4,24,256]{3,2,1,0:T(8,128)S(1)}, u32[]{:S(2)}, u32[]{:S(2)}) collective-permute-start(f32[3,4,24,256]{3,2,1,0:T(8,128)S(1)} %get-tuple-element.55), channel_id=1, source_target_pairs={{0,1},{1,0},{2,3},{3,2},{4,5},{5,4},{6,7},{7,6},{8,16},{9,17},{10,... | collective-permute-start | bytes 884744 | tf_op jit(solution)/shard_map/ppermute | solution.py:561
  25.6 0.0 collective-permute-done.2.even_vel.even_in
  25.6 1.3 %collective-permute-done.even_in = f32[12,4,256]{2,1,0:T(4,128)S(1)} collective-permute-done((f32[12,4,256]{2,1,0:T(4,128)S(1)}, f32[12,4,256]{2,1,0:T(4,128)S(1)}, u32[]{:S(2)}, u32[]{:S(2)}) %collective-permute-start) | collective-permute-done | bytes 49184 | tf_op jit(solution)/shard_map/ppermute | solution.py:561
  26.9 0.0 collective-permute-done.1.odd_in
  26.9 0.7 shard_map.61
  27.6 0.1 collective-permute-start.4
  27.7 3.1 %collective-permute-start.5 = (f32[8,32,256]{2,1,0:T(8,128)S(1)}, f32[8,32,256]{2,1,0:T(8,128)S(1)}, u32[]{:S(2)}, u32[]{:S(2)}) collective-permute-start(f32[8,32,256]{2,1,0:T(8,128)S(1)} %get-tuple-element.48), channel_id=1, source_target_pairs={{0,1},{1,0},{2,3},{3,2},{4,5},{5,4},{6,7},{7,6},{8,16},{9,17},{10,... | collective-permute-start | bytes 786440 | tf_op jit(solution)/shard_map/ppermute | solution.py:561
  30.8 0.7 shard_map.62
  31.5 0.0 collective-permute-done.6.even_vel
  31.5 0.0 collective-permute-done.7.odd_vel
  31.5 0.0 collective-permute-done.4.even_in
  31.5 3.6 %collective-permute-done.5.odd_in = f32[8,32,256]{2,1,0:T(8,128)S(1)} collective-permute-done((f32[8,32,256]{2,1,0:T(8,128)S(1)}, f32[8,32,256]{2,1,0:T(8,128)S(1)}, u32[]{:S(2)}, u32[]{:S(2)}) %collective-permute-start.5) | collective-permute-done | bytes 262176 | tf_op jit(solution)/shard_map/ppermute | solution.py:561
  35.1 3.1 %shard_map.63 = (f32[8,16,256]{2,1,0:T(8,128)S(1)}, f32[8,16,256]{2,1,0:T(8,128)S(1)}, f32[32,256]{1,0:T(8,128)S(1)}, f32[8,24,256]{2,1,0:T(8,128)S(1)}, f32[8,2...) custom-call(s32[8]{0:T(128)S(1)} %stack.51.flags, ...), custom_call_target="tpu_custom_call" | custom-call | bytes 10800000 | tf_op jit(solution)/shard_map/pallas_call | solution.py:44
  38.2 0.1 copy.6
  38.3 9.5 %all_to_all.30 = f32[32,1,256]{2,1,0:T(1,128)S(1)} all-to-all(f32[32,1,256]{2,1,0:T(1,128)S(1)} %copy.6), channel_id=1, replica_groups=mesh['gx'=4,'gy'=8] {'gx','gy'}, dimensions={0} | all-to-all | bytes 65536 | tf_op jit(solution)/shard_map/all_to_all | solution.py:564
  47.9 1.5 %shard_map.64 = (f32[8,16,256]{2,1,0:T(8,128)S(1)}, f32[8,16,256]{2,1,0:T(8,128)S(1)}, f32[8,16,256]{2,1,0:T(8,128)S(1)}, f32[8,128]{1,0:T(8,128)S(1)}, f32[12,4...) custom-call(s32[8]{0:T(128)S(1)} %stack.51.flags, f32[32,256]{1,0:T(8,128)S(1)} %bitcast.22, f32[32,256]{1,0:T(8,128)S(1)} %bitcast.23, ...), custom_call_target="tpu_custom_call" | custom-call | bytes 5040000 | tf_op jit(solution)/shard_map/pallas_call | solution.py:44
  49.3 0.7 collective-permute-start.8
  50.1 0.0 collective-permute-start.9
  50.1 3.4 %collective-permute-done.8.even_in = f32[12,4,256]{2,1,0:T(4,128)S(1)} collective-permute-done((f32[12,4,256]{2,1,0:T(4,128)S(1)}, f32[12,4,256]{2,1,0:T(4,128)S(1)}, u32[]{:S(2)}, u32[]{:S(2)}) %collective-permute-start.8) | collective-permute-done | bytes 49184 | tf_op jit(solution)/shard_map/ppermute | solution.py:561
  53.5 0.0 collective-permute-done.9.odd_in
  53.5 0.6 shard_map.65
  54.1 0.1 collective-permute-start.10
  54.2 3.0 %collective-permute-start.11 = (f32[5,32,256]{2,1,0:T(8,128)S(1)}, f32[5,32,256]{2,1,0:T(8,128)S(1)}, u32[]{:S(2)}, u32[]{:S(2)}) collective-permute-start(f32[5,32,256]{2,1,0:T(8,128)S(1)} %get-tuple-element.65), channel_id=1, source_target_pairs={{0,1},{1,0},{2,3},{3,2},{4,5},{5,4},{6,7},{7,6},{8,16},{9,17},{10,... | collective-permute-start | bytes 491528 | tf_op jit(solution)/shard_map/ppermute | solution.py:561
  57.2 0.0 collective-permute-done.10.even_in
  57.2 3.3 %collective-permute-done.11.odd_in = f32[5,32,256]{2,1,0:T(8,128)S(1)} collective-permute-done((f32[5,32,256]{2,1,0:T(8,128)S(1)}, f32[5,32,256]{2,1,0:T(8,128)S(1)}, u32[]{:S(2)}, u32[]{:S(2)}) %collective-permute-start.11) | collective-permute-done | bytes 163872 | tf_op jit(solution)/shard_map/ppermute | solution.py:561
  60.5 2.5 %shard_map.66 = (f32[8,16,256]{2,1,0:T(8,128)S(1)}, f32[8,16,256]{2,1,0:T(8,128)S(1)}, f32[32,256]{1,0:T(8,128)S(1)}) custom-call(s32[8]{0:T(128)S(1)} %stack.51.flags, f32[8,32,256]{2,1,0:T(8,128)S(1)} %get-tuple-element.62.wide, f32[2,32,256]{2,1,0:T(8,128)S(1)} %get-tuple-element.63.sides, f32[5,32,256]{2,1,0:T(8,128)S(1)} %collective-permute-done.10.even_in, ...), custom_call_target="tpu_custom_call" | custom-call | bytes 9000000 | tf_op jit(solution)/shard_map/pallas_call | solution.py:44
  63.0 0.1 copy.7
  63.1 9.5 %all_to_all.31 = f32[32,1,256]{2,1,0:T(1,128)S(1)} all-to-all(f32[32,1,256]{2,1,0:T(1,128)S(1)} %copy.7), channel_id=1, replica_groups=mesh['gx'=4,'gy'=8] {'gx','gy'}, dimensions={0} | all-to-all | bytes 65536 | tf_op jit(solution)/shard_map/all_to_all | solution.py:564
  72.6 1.4 %shard_map.67 = (f32[8,16,256]{2,1,0:T(8,128)}, f32[8,16,256]{2,1,0:T(8,128)}) custom-call(s32[8]{0:T(128)S(1)} %stack.51.flags, f32[32,256]{1,0:T(8,128)S(1)} %bitcast.24, f32[8,128]{1,0:T(8,128)S(1)} %get-tuple-element.72.alpha, f32[8,16,256]{2,1,0:T(8,128)S(1)} %get-tuple-element.73.search, f32[8,16,256]{2,1,0:T(8,128)S(1)} %get-tuple-element.74.smoothed, ...), custom_call_target="tpu_custom_call" | custom-call | bytes 5040000 | tf_op jit(solution)/shard_map/pallas_call | solution.py:44
  (5 shorter events, 0.0 us)
Async XLA Ops:
  0.6 20.7 %copy-start.2 = (f32[8,16,256]{2,1,0:T(8,128)S(1)}, f32[8,16,256]{2,1,0:T(8,128)}, u32[]{:S(2)}) copy-start(f32[8,16,256]{2,1,0:T(8,128)} %field.3) | copy-start | bytes 393220
  0.6 20.7 %copy-start = (bf16[32,8,16,256]{3,2,1,0:T(8,128)(2,1)S(1)}, bf16[32,8,16,256]{3,2,1,0:T(8,128)(2,1)}, u32[]{:S(2)}) copy-start(bf16[32,8,16,256]{3,2,1,0:T(8,128)(2,1)} %vectors.5) | copy-start | bytes 6291460
  0.7 3.6 %copy-start.1 = (f32[3,8,16,256]{3,2,1,0:T(8,128)S(1)}, f32[3,8,16,256]{3,2,1,0:T(8,128)}, u32[]{:S(2)}) copy-start(f32[3,8,16,256]{3,2,1,0:T(8,128)} %velocity.7) | copy-start | bytes 1179652
  0.7 20.7 %copy-start.3 = (f32[32,1024]{1,0:T(8,128)S(1)}, f32[32,1024]{1,0:T(8,128)}, u32[]{:S(2)}) copy-start(f32[32,1024]{1,0:T(8,128)} %inverse.3) | copy-start | bytes 393220
  4.9 0.7 copy-start.4
  5.6 18.4 %collective-permute-start.3 = (f32[3,8,4,256]{3,2,1,0:T(4,128)S(1)}, f32[3,8,4,256]{3,2,1,0:T(4,128)S(1)}, u32[]{:S(2)}, u32[]{:S(2)}) collective-permute-start(f32[3,8,4,256]{3,2,1,0:T(4,128)S(1)} %get-tuple-element.44), channel_id=1, source_target_pairs={{0,8},{1,2},{2,1},{3,4},{4,3},{5,6},{6,5},{7,15},{8,0},{9,10},{10,... | collective-permute-start | bytes 294920 | tf_op jit(solution)/shard_map/ppermute | solution.py:561
  6.8 14.6 %all-to-all-start = ((f32[32,1,256]{2,1,0:T(1,128)}), f32[32,1,256]{2,1,0:T(1,128)S(1)}, u32[]{:S(2)}, u32[]{:S(2)}) async-start(f32[32,1,256]{2,1,0:T(1,128)} %broadcast_in_dim.31), calls=%async_computation | async-start | bytes 65536 | tf_op jit(solution)/shard_map/all_to_all | solution.py:564
  14.2 11.4 %collective-permute-start.2 = (f32[3,8,4,256]{3,2,1,0:T(4,128)S(1)}, f32[3,8,4,256]{3,2,1,0:T(4,128)S(1)}, u32[]{:S(2)}, u32[]{:S(2)}) collective-permute-start(f32[3,8,4,256]{3,2,1,0:T(4,128)S(1)} %get-tuple-element.39.after), channel_id=1, source_target_pairs={{0,1},{1,0},{2,3},{3,2},{4,5},{5,4},{6,7},{7,6},{8,9},{9,8},{10,11... | collective-permute-start | bytes 294920 | tf_op jit(solution)/shard_map/ppermute | solution.py:561
  21.3 2.1 %copy-start.5 = (f32[3,4,24,256]{3,2,1,0:T(8,128)S(1)}, f32[3,4,24,256]{3,2,1,0:T(8,128)}, u32[]{:S(2)}) copy-start(f32[3,4,24,256]{3,2,1,0:T(8,128)} %copy-done.4) | copy-start | bytes 884740
  22.7 4.2 %collective-permute-start = (f32[12,4,256]{2,1,0:T(4,128)S(1)}, f32[12,4,256]{2,1,0:T(4,128)S(1)}, u32[]{:S(2)}, u32[]{:S(2)}) collective-permute-start(f32[12,4,256]{2,1,0:T(4,128)S(1)} %get-tuple-element.42), channel_id=1, source_target_pairs={{0,1},{1,0},{2,3},{3,2},{4,5},{5,4},{6,7},{7,6},{8,9},{9,8},{10,11... | collective-permute-start | bytes 147464 | tf_op jit(solution)/shard_map/ppermute | solution.py:561
  23.5 3.4 %collective-permute-start.1 = (f32[12,4,256]{2,1,0:T(4,128)S(1)}, f32[12,4,256]{2,1,0:T(4,128)S(1)}, u32[]{:S(2)}, u32[]{:S(2)}) collective-permute-start(f32[12,4,256]{2,1,0:T(4,128)S(1)} %get-tuple-element.43), channel_id=1, source_target_pairs={{0,8},{1,2},{2,1},{3,4},{4,3},{5,6},{6,5},{7,15},{8,0},{9,10},{10,... | collective-permute-start | bytes 147464 | tf_op jit(solution)/shard_map/ppermute | solution.py:561
  23.5 8.0 %collective-permute-start.6 = (f32[3,4,24,256]{3,2,1,0:T(8,128)S(1)}, f32[3,4,24,256]{3,2,1,0:T(8,128)S(1)}, u32[]{:S(2)}, u32[]{:S(2)}) collective-permute-start(f32[3,4,24,256]{3,2,1,0:T(8,128)S(1)} %copy-done.5), channel_id=1, source_target_pairs={{0,8},{1,9},{2,10},{3,11},{4,12},{5,13},{6,14},{7,15},{8,0},{9,1},... | collective-permute-start | bytes 884744 | tf_op jit(solution)/shard_map/ppermute | solution.py:561
  24.0 7.5 %collective-permute-start.7 = (f32[3,4,24,256]{3,2,1,0:T(8,128)S(1)}, f32[3,4,24,256]{3,2,1,0:T(8,128)S(1)}, u32[]{:S(2)}, u32[]{:S(2)}) collective-permute-start(f32[3,4,24,256]{3,2,1,0:T(8,128)S(1)} %get-tuple-element.55), channel_id=1, source_target_pairs={{0,1},{1,0},{2,3},{3,2},{4,5},{5,4},{6,7},{7,6},{8,16},{9,17},{10,... | collective-permute-start | bytes 884744 | tf_op jit(solution)/shard_map/ppermute | solution.py:561
  27.6 3.9 %collective-permute-start.4 = (f32[8,32,256]{2,1,0:T(8,128)S(1)}, f32[8,32,256]{2,1,0:T(8,128)S(1)}, u32[]{:S(2)}, u32[]{:S(2)}) collective-permute-start(f32[8,32,256]{2,1,0:T(8,128)S(1)} %get-tuple-element.47), channel_id=1, source_target_pairs={{0,8},{1,9},{2,10},{3,11},{4,12},{5,13},{6,14},{7,15},{8,0},{9,1},... | collective-permute-start | bytes 786440 | tf_op jit(solution)/shard_map/ppermute | solution.py:561
  27.7 7.4 %collective-permute-start.5 = (f32[8,32,256]{2,1,0:T(8,128)S(1)}, f32[8,32,256]{2,1,0:T(8,128)S(1)}, u32[]{:S(2)}, u32[]{:S(2)}) collective-permute-start(f32[8,32,256]{2,1,0:T(8,128)S(1)} %get-tuple-element.48), channel_id=1, source_target_pairs={{0,1},{1,0},{2,3},{3,2},{4,5},{5,4},{6,7},{7,6},{8,16},{9,17},{10,... | collective-permute-start | bytes 786440 | tf_op jit(solution)/shard_map/ppermute | solution.py:561
  49.3 4.2 %collective-permute-start.8 = (f32[12,4,256]{2,1,0:T(4,128)S(1)}, f32[12,4,256]{2,1,0:T(4,128)S(1)}, u32[]{:S(2)}, u32[]{:S(2)}) collective-permute-start(f32[12,4,256]{2,1,0:T(4,128)S(1)} %get-tuple-element.60), channel_id=1, source_target_pairs={{0,1},{1,0},{2,3},{3,2},{4,5},{5,4},{6,7},{7,6},{8,9},{9,8},{10,11... | collective-permute-start | bytes 147464 | tf_op jit(solution)/shard_map/ppermute | solution.py:561
  50.1 3.4 %collective-permute-start.9 = (f32[12,4,256]{2,1,0:T(4,128)S(1)}, f32[12,4,256]{2,1,0:T(4,128)S(1)}, u32[]{:S(2)}, u32[]{:S(2)}) collective-permute-start(f32[12,4,256]{2,1,0:T(4,128)S(1)} %get-tuple-element.61), channel_id=1, source_target_pairs={{0,8},{1,2},{2,1},{3,4},{4,3},{5,6},{6,5},{7,15},{8,0},{9,10},{10,... | collective-permute-start | bytes 147464 | tf_op jit(solution)/shard_map/ppermute | solution.py:561
  54.1 3.1 %collective-permute-start.10 = (f32[5,32,256]{2,1,0:T(8,128)S(1)}, f32[5,32,256]{2,1,0:T(8,128)S(1)}, u32[]{:S(2)}, u32[]{:S(2)}) collective-permute-start(f32[5,32,256]{2,1,0:T(8,128)S(1)} %get-tuple-element.64), channel_id=1, source_target_pairs={{0,8},{1,9},{2,10},{3,11},{4,12},{5,13},{6,14},{7,15},{8,0},{9,1},... | collective-permute-start | bytes 491528 | tf_op jit(solution)/shard_map/ppermute | solution.py:561
  54.2 6.3 %collective-permute-start.11 = (f32[5,32,256]{2,1,0:T(8,128)S(1)}, f32[5,32,256]{2,1,0:T(8,128)S(1)}, u32[]{:S(2)}, u32[]{:S(2)}) collective-permute-start(f32[5,32,256]{2,1,0:T(8,128)S(1)} %get-tuple-element.65), channel_id=1, source_target_pairs={{0,1},{1,0},{2,3},{3,2},{4,5},{5,4},{6,7},{7,6},{8,16},{9,17},{10,... | collective-permute-start | bytes 491528 | tf_op jit(solution)/shard_map/ppermute | solution.py:561

commit v3 on v2

--- a/solution.py
+++ b/solution.py
@@ -19,8 +19,6 @@
 cheb_radius = 0.9
 
 ODD_X, ODD_Y, LOW_X, HIGH_X, LOW_Y, HIGH_Y, SLOT = range(7)
-OWN_LOW, PAST_LOW, PAST_HIGH, OWN_HIGH = 3, 4, 5, 6
-
 
 def pair_permutations(count_x, count_y):
     def number(i, j):
@@ -168,7 +166,7 @@
         write(odd_out, True)
 
 
-def velocity_faces_kernel(flags, velocity, after, even_y, odd_y, even_x, odd_x):
+def velocity_y_kernel(flags, velocity, after, even_out, odd_out):
     _, size_x, size_y, _ = velocity.shape
 
     def write_y(out, high):
@@ -177,15 +175,21 @@
             for x in range(size_x):
                 out[d, x] = velocity[d, x, start : start + WIDE, :]
 
-    def write_x(out, high):
+    by_parity(flags[ODD_Y], write_y, even_out, odd_out)
+
+
+def write_velocity_x(flags, velocity, even_out, odd_out):
+    size_x = velocity.shape[1]
+
+    def write(out, high):
         start = size_x - WIDE if high else 0
         for d in range(3):
             for k in range(WIDE):
-                out[d, k, 0:size_y, :] = velocity[d, start + k]
-                out[d, k, size_y:, :] = jnp.zeros((2 * WIDE, velocity.shape[3]), F32)
-
-    by_parity(flags[ODD_Y], write_y, even_y, odd_y)
-    by_parity(flags[ODD_X], write_x, even_x, odd_x)
+                out[d * WIDE + k] = velocity[d, start + k]
+        for k in range(3 * WIDE, out.shape[0]):
+            out[k] = jnp.zeros(out.shape[1:], F32)
+
+    by_parity(flags[ODD_X], write, even_out, odd_out)
 
 
 def coefficients(x, v0, v1, v2, kept, keep_first, outs):
@@ -232,17 +236,17 @@
 
 
 def halo_coefficients(flags, even_in, odd_in, even_vel, odd_vel, outs, wide):
-    rows, size_z = even_vel.shape[2:]
-    size_y = rows - 2 * WIDE
+    size_y, size_z = even_vel.shape[1:]
+    rows = size_y + 2 * WIDE
     kept = rows_in_grid(flags, (rows, size_z))
     keep_first, _ = lane_masks((rows, size_z))
 
     def side(start, message, faces, present):
         for k in range(WIDE):
             for d in range(3):
-                wide[d, 0:WIDE, :] = message[WIDE + 1 + d, 8 * k : 8 * k + WIDE, :]
-                wide[d, WIDE : WIDE + size_y, :] = faces[d, k, 0:size_y, :]
-                wide[d, WIDE + size_y : rows, :] = message[WIDE + 1 + d, 8 * k + WIDE : 8 * k + 2 * WIDE, :]
+                wide[d, 0:WIDE, :] = message[WIDE + 1 + k, 8 * d : 8 * d + WIDE, :]
+                wide[d, WIDE : WIDE + size_y, :] = faces[d * WIDE + k]
+                wide[d, WIDE + size_y : rows, :] = message[WIDE + 1 + k, 8 * d + WIDE : 8 * d + 2 * WIDE, :]
             coefficients(start + k, wide[0], wide[1], wide[2], kept & (flags[present] != 0), keep_first, outs)
 
     @pl.when(flags[ODD_X] == 0)
@@ -268,11 +272,14 @@
         return self.own[x - WIDE, tile] if x < WIDE + size_x else self.halo[x - size_x, tile]
 
 
-def coarse_kernel(flags, received, inverse, vectors, field, velocity, after, corr, rest, even_out, odd_out):
+def coarse_kernel(
+    flags, received, inverse, vectors, field, velocity, after, corr, rest, even_out, odd_out, even_vel, odd_vel
+):
     coarse, _ = gathered(received)
     prolong(solve(coarse, inverse, vectors), vectors, corr)
     subtract_own(field, corr, velocity, rest)
     by_parity(flags[ODD_Y], lambda out, high: write_y_message(out, rest, corr, high), even_out, odd_out)
+    write_velocity_x(flags, velocity, even_vel, odd_vel)
 
 
 def second_coarse_kernel(
@@ -290,36 +297,42 @@
     by_parity(flags[ODD_Y], lambda out, high: write_y_message(out, rest, corr, high), even_out, odd_out)
 
 
-def extend_kernel(flags, rest, corr, even_in, odd_in, even_vel, odd_vel, wide, sides, even_out, odd_out):
+def extend_kernel(
+    flags, rest, corr, even_in, odd_in, velocity, even_vel, odd_vel, wide, sides, past, even_out, odd_out, corners=True
+):
     size_x, size_y, size_z = rest.shape
     rows = size_y + 2 * WIDE
-
-    def place(low, high):
+    end = WIDE + size_y
+
+    def place(low, high, high_vel):
         has_low, has_high = flags[LOW_Y] != 0, flags[HIGH_Y] != 0
         for x in range(size_x):
             at, line = size_x + x // WIDE, slice(x % WIDE, x % WIDE + 1)
-            wide[x, 0:WIDE, :] = low[x]
-            wide[x, WIDE : WIDE + size_y, :] = rest[x]
-            wide[x, WIDE + size_y : rows, :] = high[x]
-            wide[x, rows : rows + 8, :] = jnp.zeros((8, size_z), F32)
-            wide[x, rows + OWN_LOW : rows + OWN_LOW + 1, :] = corr[x, 0:1, :]
-            wide[x, rows + PAST_LOW : rows + PAST_LOW + 1, :] = jnp.where(has_low, low[at, line, :], 0.0)
-            wide[x, rows + PAST_HIGH : rows + PAST_HIGH + 1, :] = jnp.where(has_high, high[at, line, :], 0.0)
-            wide[x, rows + OWN_HIGH : rows + OWN_HIGH + 1, :] = corr[x, size_y - 1 : size_y, :]
+            past_low = jnp.where(has_low, low[at, line, :], 0.0)
+            past_high = jnp.where(has_high, high[at, line, :], 0.0)
+            past[0, x : x + 1, :] = past_low
+            past[1, x : x + 1, :] = past_high
+            wide[x, 0 : WIDE - 1, :] = low[x, 0 : WIDE - 1, :]
+            wide[x, WIDE - 1 : WIDE, :] = low[x, WIDE - 1 : WIDE, :] + corr[x, 0:1, :]
+            wide[x, WIDE:end, :] = rest[x]
+            wide[x, WIDE : WIDE + 1, :] = rest[x, 0:1, :] + (1.0 + velocity[1, x, 0:1, :]) * past_low
+            wide[x, end - 1 : end, :] = rest[x, size_y - 1 : size_y, :] + past_high
+            weight = 1.0 + high_vel[1, x, 0:1, :]
+            wide[x, end : end + 1, :] = high[x, 0:1, :] + weight * corr[x, size_y - 1 : size_y, :]
+            wide[x, end + 1 : rows, :] = high[x, 1:WIDE, :]
         last = size_x + size_x // WIDE
         for side, x in enumerate((0, size_x - 1)):
             sides[side, 0:WIDE, :] = low[last + side]
-            sides[side, WIDE : WIDE + size_y, :] = corr[x]
-            sides[side, WIDE + size_y : rows, :] = high[last + side]
-            sides[side, rows : rows + 8, :] = jnp.zeros((8, size_z), F32)
+            sides[side, WIDE:end, :] = corr[x]
+            sides[side, end:rows, :] = high[last + side]
 
     @pl.when(flags[ODD_Y] == 0)
     def _():
-        place(odd_in, even_in)
+        place(odd_in, even_in, even_vel)
 
     @pl.when(flags[ODD_Y] != 0)
     def _():
-        place(even_in, odd_in)
+        place(even_in, odd_in, odd_vel)
 
     def write(out, high):
         start = size_x - WIDE if high else 0
@@ -328,30 +341,26 @@
         out[WIDE] = sides[1 if high else 0]
 
     by_parity(flags[ODD_X], write, even_out, odd_out)
-    if even_vel is None:
+    if not corners:
         return
 
-    def corners(low, high):
+    def write_corners(low, high):
         def write(out, upper):
             start = size_x - WIDE if upper else 0
-            for d in range(3):
-                for k in range(WIDE):
-                    out[WIDE + 1 + d, 8 * k : 8 * k + WIDE, :] = low[d, start + k]
-                    out[WIDE + 1 + d, 8 * k + WIDE : 8 * k + 2 * WIDE, :] = high[d, start + k]
+            for k in range(WIDE):
+                for d in range(3):
+                    out[WIDE + 1 + k, 8 * d : 8 * d + WIDE, :] = low[d, start + k]
+                    out[WIDE + 1 + k, 8 * d + WIDE : 8 * d + 2 * WIDE, :] = high[d, start + k]
 
         by_parity(flags[ODD_X], write, even_out, odd_out)
 
     @pl.when(flags[ODD_Y] == 0)
     def _():
-        corners(odd_vel, even_vel)
+        write_corners(odd_vel, even_vel)
 
     @pl.when(flags[ODD_Y] != 0)
     def _():
-        corners(even_vel, odd_vel)
-
-
-def extend_again_kernel(flags, rest, corr, even_in, odd_in, wide, sides, even_out, odd_out):
-    extend_kernel(flags, rest, corr, even_in, odd_in, None, None, wide, sides, even_out, odd_out)
+        write_corners(even_vel, odd_vel)
 
 
 def beside_terms(before, here, after, x, tile, coefs, keep_last):
@@ -397,10 +406,10 @@
 
 
 def smooth(
-    flags, wide, sides, even_in, odd_in, diagonal, coefs, corr, field_out, image_out, scratch
+    flags, wide, sides, past, even_in, odd_in, diagonal, coefs, corr, field_out, image_out, scratch
 ):
     source, left, update, whole = scratch
-    inverse, b0, b1, _ = coefs
+    inverse, b0, _, _ = coefs
     size_x, size_y, size_z = corr.shape
     rows = size_y + 2 * WIDE
     span = size_x + 2 * WIDE
@@ -410,23 +419,12 @@
     has_low_y, has_high_y = flags[LOW_Y] != 0, flags[HIGH_Y] != 0
     lowest, highest = slice(0, 8), slice(rows - 8, rows)
     tile_row = lax.broadcasted_iota(jnp.int32, (8, size_z), 0)
-    last_tile = slice(rows, rows + 8)
-    kept = (tile_row == OWN_LOW) | (tile_row == PAST_LOW)
-
-    def source_plane(x, plane):
-        source[x] = inverse[x] * plane[0:rows]
-        lines = plane[last_tile]
-        for tile, shift in ((lowest, 0), (highest, 8 - (PAST_HIGH - OWN_LOW))):
-            moved = pltpu.roll(lines, shift, 0) if shift else lines
-            factor = jnp.where(tile_row == PAST_LOW, b1[x, tile], inverse[x, tile])
-            source[x, tile] = source[x, tile] + jnp.where(kept, moved * factor, 0.0)
-
     def halo(low, high):
         for k in range(WIDE):
-            source_plane(k, low.at[k])
-            source_plane(WIDE + size_x + k, high.at[k])
-        whole[0] = jnp.where(has_low_x, low[WIDE, 0:rows], 0.0)
-        whole[size_x + 1] = jnp.where(has_high_x, high[WIDE, 0:rows], 0.0)
+            source[k] = inverse[k] * low[k]
+            source[WIDE + size_x + k] = inverse[WIDE + size_x + k] * high[k]
+        whole[0] = jnp.where(has_low_x, low[WIDE], 0.0)
+        whole[size_x + 1] = jnp.where(has_high_x, high[WIDE], 0.0)
 
     @pl.when(flags[ODD_X] == 0)
     def _():
@@ -437,13 +435,13 @@
         halo(even_in, odd_in)
 
     for k in range(size_x):
-        source_plane(WIDE + k, wide.at[k])
+        source[WIDE + k] = inverse[WIDE + k] * wide[k]
 
     low_in, high_in = WIDE, WIDE + size_x - 1
-    source[low_in - 1] = source[low_in - 1] + inverse[low_in - 1] * sides[0, 0:rows]
+    source[low_in - 1] = source[low_in - 1] + inverse[low_in - 1] * sides[0]
     source[low_in] = source[low_in] + b0[low_in] * whole[0]
     source[high_in] = source[high_in] + inverse[high_in] * whole[size_x + 1]
-    source[high_in + 1] = source[high_in + 1] + b0[high_in + 1] * sides[1, 0:rows]
+    source[high_in + 1] = source[high_in + 1] + b0[high_in + 1] * sides[1]
 
     def run(planes, tile, inside, wanted):
         return chebyshev(
@@ -478,12 +476,12 @@
 
     beside = run(box_planes, lowest, tile_row < WIDE + DEPTH, tuple(own_planes))
     for k in range(size_x):
-        line = pltpu.roll(wide[k, last_tile], 8 + WIDE - 1 - PAST_LOW, 0) + beside[WIDE + k]
+        line = past[0, k : k + 1, :] + beside[WIDE + k]
         here = has_low_y & (tile_row == WIDE - 1)
         whole[k + 1, lowest] = jnp.where(here, line, whole[k + 1, lowest])
     beside = run(box_planes, highest, tile_row >= 8 - WIDE - DEPTH, tuple(own_planes))
     for k in range(size_x):
-        line = pltpu.roll(wide[k, last_tile], (8 + 8 - WIDE - PAST_HIGH) % 8, 0) + beside[WIDE + k]
+        line = past[1, k : k + 1, :] + beside[WIDE + k]
         here = has_high_y & (tile_row == 8 - WIDE)
         whole[k + 1, highest] = jnp.where(here, line, whole[k + 1, highest])
 
@@ -503,23 +501,23 @@
 
 
 def search_kernel(
-    flags, wide, sides, even_in, odd_in, diagonal, own0, own1, own2, own3, corr, even_vel, odd_vel, vectors, right_side,
+    flags, wide, sides, past, even_in, odd_in, diagonal, own0, own1, own2, own3, corr, even_vel, odd_vel, vectors, right_side,
     search, image, out, halo0, halo1, halo2, halo3, stage, wide_vel, *scratch
 ):
     halos = (halo0, halo1, halo2, halo3)
     halo_coefficients(flags, even_in, odd_in, even_vel, odd_vel, halos, wide_vel)
     coefs = [Region(*pair) for pair in zip((own0, own1, own2, own3), halos)]
-    smooth(flags, wide, sides, even_in, odd_in, diagonal, coefs, corr, search, image, scratch)
+    smooth(flags, wide, sides, past, even_in, odd_in, diagonal, coefs, corr, search, image, scratch)
     products = [dot_planes(right_side, right_side), dot_planes(right_side, image)]
     restrict(vectors, image, products, flags, (out, stage))
 
 
 def smoothed_kernel(
-    flags, wide, sides, even_in, odd_in, diagonal, own0, own1, own2, own3, corr, halo0, halo1, halo2, halo3, middle,
+    flags, wide, sides, past, even_in, odd_in, diagonal, own0, own1, own2, own3, corr, halo0, halo1, halo2, halo3, middle,
     smoothed, turned, out, stage, *scratch
 ):
     coefs = [Region(*pair) for pair in zip((own0, own1, own2, own3), (halo0, halo1, halo2, halo3))]
-    smooth(flags, wide, sides, even_in, odd_in, diagonal, coefs, corr, smoothed, turned, scratch)
+    smooth(flags, wide, sides, past, even_in, odd_in, diagonal, coefs, corr, smoothed, turned, scratch)
     stage[...] = jnp.zeros_like(stage)
     for k, total in enumerate((dot_planes(turned, middle), dot_planes(turned, turned))):
         total = jnp.sum(total, axis=0, keepdims=True)
@@ -579,30 +577,32 @@
     first_row = jnp.broadcast_to(first_row.reshape(1, 2 * LANES), row)
 
     first = share(first_row)
-    faces_y, faces_x = (3, size_x, WIDE, size_z), (3, WIDE, rows, size_z)
-    faces = call(
-        velocity_faces_kernel, [faces_y] * 2 + [faces_x] * 2, [], flags, velocity, first_row[0, :8], micros=0.01
-    )
-    after = faces[0]
-    velocity_y, velocity_x = swap(faces[:2], y_pairs), swap(faces[2:], x_pairs)
-
-    def exchange(corr, rest, messages, extend, message, *vel):
-        wide, sides, *messages = call(
-            extend,
-            [(size_x, rows + 8, size_z), (2, rows + 8, size_z), message, message],
+    faces_y, faces_x = (3, size_x, WIDE, size_z), (3 * WIDE + 2, size_y, size_z)
+    velocity_y = call(velocity_y_kernel, [faces_y] * 2, [], flags, velocity, first_row[0, :8], micros=0.01)
+    after = velocity_y[0]
+    velocity_y = swap(velocity_y, y_pairs)
+
+    wide_own, wide_halo = (size_x, rows, size_z), (2 * WIDE, rows, size_z)
+
+    def exchange(corr, rest, messages, corners):
+        message = (WIDE + 1 + (WIDE if corners else 0), rows, size_z)
+        *own, even, odd = call(
+            functools.partial(extend_kernel, corners=corners),
+            [wide_own, (2, rows, size_z), (2, size_x, size_z), message, message],
             [],
             flags,
             rest,
             corr,
             *swap(messages, y_pairs),
-            *vel,
+            velocity,
+            *velocity_y,
             micros=0.01,
         )
-        return (wide, sides, *swap(messages, x_pairs), *coefs, corr)
-
-    corr, rest, *messages = call(
+        return (*own, *swap((even, odd), x_pairs), *coefs, corr)
+
+    corr, rest, *messages, even_vel, odd_vel = call(
         coarse_kernel,
-        [block, block, y_message, y_message],
+        [block, block, y_message, y_message, faces_x, faces_x],
         [],
         flags,
         first,
@@ -613,7 +613,7 @@
         after,
         micros=1.4,
     )
-    wide_own, wide_halo = (size_x, rows, size_z), (2 * WIDE, rows, size_z)
+    velocity_x = swap((even_vel, odd_vel), x_pairs)
     coefs = call(
         coefficients_kernel,
         [wide_own] * 5,
@@ -628,7 +628,7 @@
         [block, block, row] + [wide_halo] * 4,
         [stage, (3, rows, size_z)] + smooth_scratch,
         flags,
-        *exchange(corr, rest, messages, extend_kernel, (WIDE + 4, rows + 8, size_z), *velocity_y),
+        *exchange(corr, rest, messages, True),
         *velocity_x,
         deflation,
         right_side,
@@ -654,7 +654,7 @@
         [block, block, row],
         [stage] + smooth_scratch,
         flags,
-        *exchange(corr, rest, messages, extend_again_kernel, (WIDE + 1, rows + 8, size_z)),
+        *exchange(corr, rest, messages, False),
         *halo_coefs,
         middle,
         micros=2.5,

time: 74.2 us -> 71.3 us (0.961)
  waiting for transfers between devices: 17 us -> 14 us
  starting transfers between devices: 19.5 us -> 20.3 us
    all_to_all x1, waiting for transfers between devices: 5.35 us -> 3.14 us  [share(): return lax.all_to_all(row, AXES, 0, 0, tiled=True)]
    ppermute x12, starting transfers between devices: 12.1 us -> 13 us  [swap(): lax.ppermute(message, AXES, pair)]
    ppermute x12, waiting for transfers between devices: 11.6 us -> 10.8 us  [swap(): lax.ppermute(message, AXES, pair)]
  transfers between devices with their start and end apart: 13 -> 13, of which waited for: 5 -> 5; matrix products, arithmetic and copies ran while one was open for 1% -> 0% of each run, Pallas kernels for 4% -> 5%
where the time goes in v3:
time: 71.3 us; the launch traced here: 71 us
  starting transfers between devices  20.3 us (28%)
  blocking collectives  19 us (27%)
  waiting for transfers between devices  14 us (20%)
  Pallas kernels  12.5 us (18%)
  other arithmetic  3.35 us (5%)
  local copies, waits for them, and re-layouts  1.05 us (1%)
  between operations  0.83 us (1%)
    all_to_all x2, blocking collectives, share(): return lax.all_to_all(row, AXES, 0, 0, tiled=True)  19 us
    ppermute x12, starting transfers between devices, swap(): lax.ppermute(message, AXES, pair)  13 us
    pallas_call x9, Pallas kernels, call(): pl.pallas_call(body, out_shape=[jax.ShapeDtypeStruct(shape, F32) for shap...  12.5 us
    ppermute x12, waiting for transfers between devices, swap(): lax.ppermute(message, AXES, pair)  10.8 us
    all_to_all x1, starting transfers between devices, share(): return lax.all_to_all(row, AXES, 0, 0, tiled=True)  7.3 us
    all_to_all x1, waiting for transfers between devices, share(): return lax.all_to_all(row, AXES, 0, 0, tiled=True)  3.14 us
    reduce_sum x1, other arithmetic, local(): jnp.sum(deflation.astype(F32) * rounded, axis=(1, 2))  2.06 us
  transfers between devices with their start and end apart: 13, of which 5 were waited for; matrix products, arithmetic and copies ran while one was open for 0% of the time, Pallas kernels for 5%

profile of v3, /device:TPU:0, one launch (start us, length us, event | category | flops | bytes accessed | tf_op | source)
XLA Modules:
  0.0 71.0 jit_solution(13703532416888689875)
XLA Ops:
  0.6 0.0 copy-start.2
  0.6 0.0 copy-start
  0.7 0.0 copy-start.1
  0.7 0.0 copy-start.3
  0.7 1.1 %reduce_precision.3 = f32[8,16,256]{2,1,0:T(8,128)S(1)} reduce-precision(f32[8,16,256]{2,1,0:T(8,128)} %field.3), exponent_bits=8, mantissa_bits=7 | non-fusion elementwise | flops 32768 | bytes 262144 | tf_op jit(solution)/shard_map/reduce_precision | solution.py:573
  1.8 2.1 %multiply_reduce_fusion = f32[32,256]{1,0:T(8,128)S(1)} fusion(bf16[32,8,16,256]{3,2,1,0:T(8,128)(2,1)} %vectors.5, f32[8,16,256]{2,1,0:T(8,128)S(1)} %reduce_precision.3), kind=kLoop, calls=%fused_computation | loop fusion | flops 3137536 | bytes 2260992 | tf_op jit(solution)/shard_map/reduce_sum | solution.py:574
  3.9 0.1 reduce_sum.19
  4.0 0.1 broadcast_select_fusion
  4.1 0.1 select_n.37
  4.1 0.6 broadcast_in_dim.31
  4.8 7.3 %all-to-all-start = ((f32[32,1,256]{2,1,0:T(1,128)}), f32[32,1,256]{2,1,0:T(1,128)S(1)}, u32[]{:S(2)}, u32[]{:S(2)}) async-start(f32[32,1,256]{2,1,0:T(1,128)} %broadcast_in_dim.31), calls=%async_computation | async-start | bytes 65536 | tf_op jit(solution)/shard_map/all_to_all | solution.py:562
  12.1 0.1 select_n.38
  12.2 0.1 stack.51.flags
  12.3 0.0 copy-done.1
  12.3 0.6 shard_map.59
  12.8 0.3 collective-permute-start.3
  13.1 3.0 %collective-permute-start.2 = (f32[3,8,4,256]{3,2,1,0:T(4,128)S(1)}, f32[3,8,4,256]{3,2,1,0:T(4,128)S(1)}, u32[]{:S(2)}, u32[]{:S(2)}) collective-permute-start(f32[3,8,4,256]{3,2,1,0:T(4,128)S(1)} %get-tuple-element.41.after), channel_id=1, source_target_pairs={{0,1},{1,0},{2,3},{3,2},{4,5},{5,4},{6,7},{7,6},{8,9},{9,8},{10,11... | collective-permute-start | bytes 294920 | tf_op jit(solution)/shard_map/ppermute | solution.py:559
  16.1 3.1 %all-to-all-done = f32[32,1,256]{2,1,0:T(1,128)S(1)} async-done(((f32[32,1,256]{2,1,0:T(1,128)}), f32[32,1,256]{2,1,0:T(1,128)S(1)}, u32[]{:S(2)}, u32[]{:S(2)}) %all-to-all-start) | async-done | bytes 32800 | tf_op jit(solution)/shard_map/all_to_all | solution.py:562
  19.3 0.0 copy-done.2
  19.3 0.0 copy-done
  19.3 0.0 copy-done.3
  19.3 1.4 %shard_map.60 = (f32[8,16,256]{2,1,0:T(8,128)S(1)}, f32[8,16,256]{2,1,0:T(8,128)S(1)}, f32[12,4,256]{2,1,0:T(4,128)S(1)}, f32[12,4,256]{2,1,0:T(4,128)S(1)}, f32...) custom-call(s32[8]{0:T(128)S(1)} %stack.51.flags, f32[32,256]{1,0:T(8,128)S(1)} %bitcast.21, ...), custom_call_target="tpu_custom_call" | custom-call | bytes 5040000 | tf_op jit(solution)/shard_map/pallas_call | solution.py:42
  20.7 0.7 %collective-permute-start = (f32[12,4,256]{2,1,0:T(4,128)S(1)}, f32[12,4,256]{2,1,0:T(4,128)S(1)}, u32[]{:S(2)}, u32[]{:S(2)}) collective-permute-start(f32[12,4,256]{2,1,0:T(4,128)S(1)} %get-tuple-element.44), channel_id=1, source_target_pairs={{0,1},{1,0},{2,3},{3,2},{4,5},{5,4},{6,7},{7,6},{8,9},{9,8},{10,11... | collective-permute-start | bytes 147464 | tf_op jit(solution)/shard_map/ppermute | solution.py:559
  21.4 0.0 collective-permute-start.1
  21.4 0.5 collective-permute-start.6
  21.9 0.0 collective-permute-done.3.odd_vel.odd_in
  22.0 1.5 %collective-permute-start.7 = (f32[14,16,256]{2,1,0:T(8,128)S(1)}, f32[14,16,256]{2,1,0:T(8,128)S(1)}, u32[]{:S(2)}, u32[]{:S(2)}) collective-permute-start(f32[14,16,256]{2,1,0:T(8,128)S(1)} %get-tuple-element.58), channel_id=1, source_target_pairs={{0,1},{1,0},{2,3},{3,2},{4,5},{5,4},{6,7},{7,6},{8,16},{9,17},{10,... | collective-permute-start | bytes 688136 | tf_op jit(solution)/shard_map/ppermute | solution.py:559
  23.5 0.0 collective-permute-done.2.even_vel.even_in
  23.5 1.4 %collective-permute-done.even_in = f32[12,4,256]{2,1,0:T(4,128)S(1)} collective-permute-done((f32[12,4,256]{2,1,0:T(4,128)S(1)}, f32[12,4,256]{2,1,0:T(4,128)S(1)}, u32[]{:S(2)}, u32[]{:S(2)}) %collective-permute-start) | collective-permute-done | bytes 49184 | tf_op jit(solution)/shard_map/ppermute | solution.py:559
  24.9 0.0 collective-permute-done.1.odd_in
  24.9 0.7 shard_map.61
  25.6 0.1 collective-permute-start.4
  25.6 3.1 %collective-permute-start.5 = (f32[9,24,256]{2,1,0:T(8,128)S(1)}, f32[9,24,256]{2,1,0:T(8,128)S(1)}, u32[]{:S(2)}, u32[]{:S(2)}) collective-permute-start(f32[9,24,256]{2,1,0:T(8,128)S(1)} %get-tuple-element.51), channel_id=1, source_target_pairs={{0,1},{1,0},{2,3},{3,2},{4,5},{5,4},{6,7},{7,6},{8,16},{9,17},{10,... | collective-permute-start | bytes 663560 | tf_op jit(solution)/shard_map/ppermute | solution.py:559
  28.7 0.7 shard_map.62
  29.4 0.0 collective-permute-done.6.even_vel
  29.4 0.0 collective-permute-done.7.odd_vel
  29.5 0.0 collective-permute-done.4.even_in
  29.5 3.2 %collective-permute-done.5.odd_in = f32[9,24,256]{2,1,0:T(8,128)S(1)} collective-permute-done((f32[9,24,256]{2,1,0:T(8,128)S(1)}, f32[9,24,256]{2,1,0:T(8,128)S(1)}, u32[]{:S(2)}, u32[]{:S(2)}) %collective-permute-start.5) | collective-permute-done | bytes 221216 | tf_op jit(solution)/shard_map/ppermute | solution.py:559
  32.6 3.1 %shard_map.63 = (f32[8,16,256]{2,1,0:T(8,128)S(1)}, f32[8,16,256]{2,1,0:T(8,128)S(1)}, f32[32,256]{1,0:T(8,128)S(1)}, f32[8,24,256]{2,1,0:T(8,128)S(1)}, f32[8,2...) custom-call(s32[8]{0:T(128)S(1)} %stack.51.flags, ...), custom_call_target="tpu_custom_call" | custom-call | bytes 10800000 | tf_op jit(solution)/shard_map/pallas_call | solution.py:42
  35.8 0.1 copy.6
  35.9 9.5 %all_to_all.30 = f32[32,1,256]{2,1,0:T(1,128)S(1)} all-to-all(f32[32,1,256]{2,1,0:T(1,128)S(1)} %copy.6), channel_id=1, replica_groups=mesh['gx'=4,'gy'=8] {'gx','gy'}, dimensions={0} | all-to-all | bytes 65536 | tf_op jit(solution)/shard_map/all_to_all | solution.py:562
  45.4 1.5 %shard_map.64 = (f32[8,16,256]{2,1,0:T(8,128)S(1)}, f32[8,16,256]{2,1,0:T(8,128)S(1)}, f32[8,16,256]{2,1,0:T(8,128)S(1)}, f32[8,128]{1,0:T(8,128)S(1)}, f32[12,4...) custom-call(s32[8]{0:T(128)S(1)} %stack.51.flags, f32[32,256]{1,0:T(8,128)S(1)} %bitcast.22, f32[32,256]{1,0:T(8,128)S(1)} %bitcast.23, ...), custom_call_target="tpu_custom_call" | custom-call | bytes 5040000 | tf_op jit(solution)/shard_map/pallas_call | solution.py:42
  46.9 0.7 %collective-permute-start.8 = (f32[12,4,256]{2,1,0:T(4,128)S(1)}, f32[12,4,256]{2,1,0:T(4,128)S(1)}, u32[]{:S(2)}, u32[]{:S(2)}) collective-permute-start(f32[12,4,256]{2,1,0:T(4,128)S(1)} %get-tuple-element.63), channel_id=1, source_target_pairs={{0,1},{1,0},{2,3},{3,2},{4,5},{5,4},{6,7},{7,6},{8,9},{9,8},{10,11... | collective-permute-start | bytes 147464 | tf_op jit(solution)/shard_map/ppermute | solution.py:559
  47.6 0.0 collective-permute-start.9
  47.6 3.4 %collective-permute-done.8.even_in = f32[12,4,256]{2,1,0:T(4,128)S(1)} collective-permute-done((f32[12,4,256]{2,1,0:T(4,128)S(1)}, f32[12,4,256]{2,1,0:T(4,128)S(1)}, u32[]{:S(2)}, u32[]{:S(2)}) %collective-permute-start.8) | collective-permute-done | bytes 49184 | tf_op jit(solution)/shard_map/ppermute | solution.py:559
  51.0 0.0 collective-permute-done.9.odd_in
  51.0 0.6 shard_map.65
  51.7 0.1 collective-permute-start.10
  51.7 3.0 %collective-permute-start.11 = (f32[5,24,256]{2,1,0:T(8,128)S(1)}, f32[5,24,256]{2,1,0:T(8,128)S(1)}, u32[]{:S(2)}, u32[]{:S(2)}) collective-permute-start(f32[5,24,256]{2,1,0:T(8,128)S(1)} %get-tuple-element.69), channel_id=1, source_target_pairs={{0,1},{1,0},{2,3},{3,2},{4,5},{5,4},{6,7},{7,6},{8,16},{9,17},{10,... | collective-permute-start | bytes 368648 | tf_op jit(solution)/shard_map/ppermute | solution.py:559
  54.7 0.0 collective-permute-done.10.even_in
  54.7 2.9 %collective-permute-done.11.odd_in = f32[5,24,256]{2,1,0:T(8,128)S(1)} collective-permute-done((f32[5,24,256]{2,1,0:T(8,128)S(1)}, f32[5,24,256]{2,1,0:T(8,128)S(1)}, u32[]{:S(2)}, u32[]{:S(2)}) %collective-permute-start.11) | collective-permute-done | bytes 122912 | tf_op jit(solution)/shard_map/ppermute | solution.py:559
  57.6 2.5 %shard_map.66 = (f32[8,16,256]{2,1,0:T(8,128)S(1)}, f32[8,16,256]{2,1,0:T(8,128)S(1)}, f32[32,256]{1,0:T(8,128)S(1)}) custom-call(s32[8]{0:T(128)S(1)} %stack.51.flags, f32[8,24,256]{2,1,0:T(8,128)S(1)} %get-tuple-element.65.wide, f32[2,24,256]{2,1,0:T(8,128)S(1)} %get-tuple-element.66.sides, f32[2,8,256]{2,1,0:T(8,128)S(1)} %get-tuple-element.67.past, ...), custom_call_target="tpu_custom_call" | custom-call | bytes 9000000 | tf_op jit(solution)/shard_map/pallas_call | solution.py:42
  60.1 0.1 copy.7
  60.2 9.5 %all_to_all.31 = f32[32,1,256]{2,1,0:T(1,128)S(1)} all-to-all(f32[32,1,256]{2,1,0:T(1,128)S(1)} %copy.7), channel_id=1, replica_groups=mesh['gx'=4,'gy'=8] {'gx','gy'}, dimensions={0} | all-to-all | bytes 65536 | tf_op jit(solution)/shard_map/all_to_all | solution.py:562
  69.7 1.4 %shard_map.67 = (f32[8,16,256]{2,1,0:T(8,128)}, f32[8,16,256]{2,1,0:T(8,128)}) custom-call(s32[8]{0:T(128)S(1)} %stack.51.flags, f32[32,256]{1,0:T(8,128)S(1)} %bitcast.24, f32[8,128]{1,0:T(8,128)S(1)} %get-tuple-element.76.alpha, f32[8,16,256]{2,1,0:T(8,128)S(1)} %get-tuple-element.77.search, f32[8,16,256]{2,1,0:T(8,128)S(1)} %get-tuple-element.78.smoothed, ...), custom_call_target="tpu_custom_call" | custom-call | bytes 5040000 | tf_op jit(solution)/shard_map/pallas_call | solution.py:42
  (5 shorter events, 0.0 us)
Async XLA Ops:
  0.6 18.6 %copy-start.2 = (f32[8,16,256]{2,1,0:T(8,128)S(1)}, f32[8,16,256]{2,1,0:T(8,128)}, u32[]{:S(2)}) copy-start(f32[8,16,256]{2,1,0:T(8,128)} %field.3) | copy-start | bytes 393220
  0.6 18.6 %copy-start = (bf16[32,8,16,256]{3,2,1,0:T(8,128)(2,1)S(1)}, bf16[32,8,16,256]{3,2,1,0:T(8,128)(2,1)}, u32[]{:S(2)}) copy-start(bf16[32,8,16,256]{3,2,1,0:T(8,128)(2,1)} %vectors.5) | copy-start | bytes 6291460
  0.7 11.6 %copy-start.1 = (f32[3,8,16,256]{3,2,1,0:T(8,128)S(1)}, f32[3,8,16,256]{3,2,1,0:T(8,128)}, u32[]{:S(2)}) copy-start(f32[3,8,16,256]{3,2,1,0:T(8,128)} %velocity.11) | copy-start | bytes 1179652
  0.7 18.6 %copy-start.3 = (f32[32,1024]{1,0:T(8,128)S(1)}, f32[32,1024]{1,0:T(8,128)}, u32[]{:S(2)}) copy-start(f32[32,1024]{1,0:T(8,128)} %inverse.3) | copy-start | bytes 393220
  4.8 14.5 %all-to-all-start = ((f32[32,1,256]{2,1,0:T(1,128)}), f32[32,1,256]{2,1,0:T(1,128)S(1)}, u32[]{:S(2)}, u32[]{:S(2)}) async-start(f32[32,1,256]{2,1,0:T(1,128)} %broadcast_in_dim.31), calls=%async_computation | async-start | bytes 65536 | tf_op jit(solution)/shard_map/all_to_all | solution.py:562
  12.8 9.1 %collective-permute-start.3 = (f32[3,8,4,256]{3,2,1,0:T(4,128)S(1)}, f32[3,8,4,256]{3,2,1,0:T(4,128)S(1)}, u32[]{:S(2)}, u32[]{:S(2)}) collective-permute-start(f32[3,8,4,256]{3,2,1,0:T(4,128)S(1)} %get-tuple-element.46), channel_id=1, source_target_pairs={{0,8},{1,2},{2,1},{3,4},{4,3},{5,6},{6,5},{7,15},{8,0},{9,10},{10,... | collective-permute-start | bytes 294920 | tf_op jit(solution)/shard_map/ppermute | solution.py:559
  13.1 10.3 %collective-permute-start.2 = (f32[3,8,4,256]{3,2,1,0:T(4,128)S(1)}, f32[3,8,4,256]{3,2,1,0:T(4,128)S(1)}, u32[]{:S(2)}, u32[]{:S(2)}) collective-permute-start(f32[3,8,4,256]{3,2,1,0:T(4,128)S(1)} %get-tuple-element.41.after), channel_id=1, source_target_pairs={{0,1},{1,0},{2,3},{3,2},{4,5},{5,4},{6,7},{7,6},{8,9},{9,8},{10,11... | collective-permute-start | bytes 294920 | tf_op jit(solution)/shard_map/ppermute | solution.py:559
  20.7 4.2 %collective-permute-start = (f32[12,4,256]{2,1,0:T(4,128)S(1)}, f32[12,4,256]{2,1,0:T(4,128)S(1)}, u32[]{:S(2)}, u32[]{:S(2)}) collective-permute-start(f32[12,4,256]{2,1,0:T(4,128)S(1)} %get-tuple-element.44), channel_id=1, source_target_pairs={{0,1},{1,0},{2,3},{3,2},{4,5},{5,4},{6,7},{7,6},{8,9},{9,8},{10,11... | collective-permute-start | bytes 147464 | tf_op jit(solution)/shard_map/ppermute | solution.py:559
  21.4 3.4 %collective-permute-start.1 = (f32[12,4,256]{2,1,0:T(4,128)S(1)}, f32[12,4,256]{2,1,0:T(4,128)S(1)}, u32[]{:S(2)}, u32[]{:S(2)}) collective-permute-start(f32[12,4,256]{2,1,0:T(4,128)S(1)} %get-tuple-element.45), channel_id=1, source_target_pairs={{0,8},{1,2},{2,1},{3,4},{4,3},{5,6},{6,5},{7,15},{8,0},{9,10},{10,... | collective-permute-start | bytes 147464 | tf_op jit(solution)/shard_map/ppermute | solution.py:559
  21.4 8.0 %collective-permute-start.6 = (f32[14,16,256]{2,1,0:T(8,128)S(1)}, f32[14,16,256]{2,1,0:T(8,128)S(1)}, u32[]{:S(2)}, u32[]{:S(2)}) collective-permute-start(f32[14,16,256]{2,1,0:T(8,128)S(1)} %get-tuple-element.57), channel_id=1, source_target_pairs={{0,8},{1,9},{2,10},{3,11},{4,12},{5,13},{6,14},{7,15},{8,0},{9,1},... | collective-permute-start | bytes 688136 | tf_op jit(solution)/shard_map/ppermute | solution.py:559
  22.0 7.5 %collective-permute-start.7 = (f32[14,16,256]{2,1,0:T(8,128)S(1)}, f32[14,16,256]{2,1,0:T(8,128)S(1)}, u32[]{:S(2)}, u32[]{:S(2)}) collective-permute-start(f32[14,16,256]{2,1,0:T(8,128)S(1)} %get-tuple-element.58), channel_id=1, source_target_pairs={{0,1},{1,0},{2,3},{3,2},{4,5},{5,4},{6,7},{7,6},{8,16},{9,17},{10,... | collective-permute-start | bytes 688136 | tf_op jit(solution)/shard_map/ppermute | solution.py:559
  25.6 3.9 %collective-permute-start.4 = (f32[9,24,256]{2,1,0:T(8,128)S(1)}, f32[9,24,256]{2,1,0:T(8,128)S(1)}, u32[]{:S(2)}, u32[]{:S(2)}) collective-permute-start(f32[9,24,256]{2,1,0:T(8,128)S(1)} %get-tuple-element.50), channel_id=1, source_target_pairs={{0,8},{1,9},{2,10},{3,11},{4,12},{5,13},{6,14},{7,15},{8,0},{9,1},... | collective-permute-start | bytes 663560 | tf_op jit(solution)/shard_map/ppermute | solution.py:559
  25.6 7.0 %collective-permute-start.5 = (f32[9,24,256]{2,1,0:T(8,128)S(1)}, f32[9,24,256]{2,1,0:T(8,128)S(1)}, u32[]{:S(2)}, u32[]{:S(2)}) collective-permute-start(f32[9,24,256]{2,1,0:T(8,128)S(1)} %get-tuple-element.51), channel_id=1, source_target_pairs={{0,1},{1,0},{2,3},{3,2},{4,5},{5,4},{6,7},{7,6},{8,16},{9,17},{10,... | collective-permute-start | bytes 663560 | tf_op jit(solution)/shard_map/ppermute | solution.py:559
  46.9 4.2 %collective-permute-start.8 = (f32[12,4,256]{2,1,0:T(4,128)S(1)}, f32[12,4,256]{2,1,0:T(4,128)S(1)}, u32[]{:S(2)}, u32[]{:S(2)}) collective-permute-start(f32[12,4,256]{2,1,0:T(4,128)S(1)} %get-tuple-element.63), channel_id=1, source_target_pairs={{0,1},{1,0},{2,3},{3,2},{4,5},{5,4},{6,7},{7,6},{8,9},{9,8},{10,11... | collective-permute-start | bytes 147464 | tf_op jit(solution)/shard_map/ppermute | solution.py:559
  47.6 3.4 %collective-permute-start.9 = (f32[12,4,256]{2,1,0:T(4,128)S(1)}, f32[12,4,256]{2,1,0:T(4,128)S(1)}, u32[]{:S(2)}, u32[]{:S(2)}) collective-permute-start(f32[12,4,256]{2,1,0:T(4,128)S(1)} %get-tuple-element.64), channel_id=1, source_target_pairs={{0,8},{1,2},{2,1},{3,4},{4,3},{5,6},{6,5},{7,15},{8,0},{9,10},{10,... | collective-permute-start | bytes 147464 | tf_op jit(solution)/shard_map/ppermute | solution.py:559
  51.7 3.1 %collective-permute-start.10 = (f32[5,24,256]{2,1,0:T(8,128)S(1)}, f32[5,24,256]{2,1,0:T(8,128)S(1)}, u32[]{:S(2)}, u32[]{:S(2)}) collective-permute-start(f32[5,24,256]{2,1,0:T(8,128)S(1)} %get-tuple-element.68), channel_id=1, source_target_pairs={{0,8},{1,9},{2,10},{3,11},{4,12},{5,13},{6,14},{7,15},{8,0},{9,1},... | collective-permute-start | bytes 368648 | tf_op jit(solution)/shard_map/ppermute | solution.py:559
  51.7 5.8 %collective-permute-start.11 = (f32[5,24,256]{2,1,0:T(8,128)S(1)}, f32[5,24,256]{2,1,0:T(8,128)S(1)}, u32[]{:S(2)}, u32[]{:S(2)}) collective-permute-start(f32[5,24,256]{2,1,0:T(8,128)S(1)} %get-tuple-element.69), channel_id=1, source_target_pairs={{0,1},{1,0},{2,3},{3,2},{4,5},{5,4},{6,7},{7,6},{8,16},{9,17},{10,... | collective-permute-start | bytes 368648 | tf_op jit(solution)/shard_map/ppermute | solution.py:559

commit v4 on v3

--- a/solution.py
+++ b/solution.py
@@ -37,14 +37,30 @@
     return (even_x, odd_x), (even_y, odd_y)
 
 
-def call(body, outs, scratch, *args, micros):
-    specs = [pl.BlockSpec(memory_space=pltpu.SMEM)] + [pl.BlockSpec(memory_space=pltpu.VMEM)] * (len(args) - 1)
+def place_flags(vectors_count):
+    count_x, count_y = lax.axis_size("gx"), lax.axis_size("gy")
+    at_x, at_y = lax.axis_index("gx"), lax.axis_index("gy")
+    return (
+        lax.rem(at_x, 2),
+        lax.rem(at_y, 2),
+        (at_x > 0).astype(jnp.int32),
+        (at_x < count_x - 1).astype(jnp.int32),
+        (at_y > 0).astype(jnp.int32),
+        (at_y < count_y - 1).astype(jnp.int32),
+        lax.rem(at_x * count_y + at_y, LANES // vectors_count),
+    )
+
+
+def call(vectors, body, outs, scratch, *args, micros):
+    def kernel(*refs):
+        body(place_flags(vectors), *refs)
+
     return pl.pallas_call(
-        body,
+        kernel,
         out_shape=[jax.ShapeDtypeStruct(shape, F32) for shape in outs],
-        in_specs=specs,
+        in_specs=[pl.BlockSpec(memory_space=pltpu.VMEM)] * len(args),
         out_specs=[pl.BlockSpec(memory_space=pltpu.VMEM)] * len(outs),
-        scratch_shapes=[pltpu.VMEM(kind, F32) if isinstance(kind, tuple) else kind for kind in scratch],
+        scratch_shapes=[pltpu.VMEM(shape, F32) for shape in scratch],
         compiler_params=pltpu.CompilerParams(vmem_limit_bytes=24 * 1024 * 1024),
         cost_estimate=pl.CostEstimate(flops=0, bytes_accessed=int(micros * 3.6e6), transcendentals=0),
     )(*args)
@@ -541,18 +557,8 @@
     count_x, count_y = lax.axis_size("gx"), lax.axis_size("gy")
     count = count_x * count_y
     at_x, at_y = lax.axis_index("gx"), lax.axis_index("gy")
-    flags = jnp.stack(
-        [
-            at_x % 2,
-            at_y % 2,
-            (at_x > 0).astype(jnp.int32),
-            (at_x < count_x - 1).astype(jnp.int32),
-            (at_y > 0).astype(jnp.int32),
-            (at_y < count_y - 1).astype(jnp.int32),
-            (at_x * count_y + at_y) % (LANES // vectors_count),
-            at_x,
-        ]
-    ).astype(jnp.int32)
+    flags = place_flags(vectors_count)
+    kernel_call = functools.partial(call, vectors_count)
     x_pairs, y_pairs = pair_permutations(count_x, count_y)
 
     def swap(messages, pairs):
@@ -578,7 +584,7 @@
 
     first = share(first_row)
     faces_y, faces_x = (3, size_x, WIDE, size_z), (3 * WIDE + 2, size_y, size_z)
-    velocity_y = call(velocity_y_kernel, [faces_y] * 2, [], flags, velocity, first_row[0, :8], micros=0.01)
+    velocity_y = kernel_call(velocity_y_kernel, [faces_y] * 2, [], velocity, first_row[0, :8], micros=0.01)
     after = velocity_y[0]
     velocity_y = swap(velocity_y, y_pairs)
 
@@ -586,11 +592,10 @@
 
     def exchange(corr, rest, messages, corners):
         message = (WIDE + 1 + (WIDE if corners else 0), rows, size_z)
-        *own, even, odd = call(
+        *own, even, odd = kernel_call(
             functools.partial(extend_kernel, corners=corners),
             [wide_own, (2, rows, size_z), (2, size_x, size_z), message, message],
             [],
-            flags,
             rest,
             corr,
             *swap(messages, y_pairs),
@@ -600,11 +605,10 @@
         )
         return (*own, *swap((even, odd), x_pairs), *coefs, corr)
 
-    corr, rest, *messages, even_vel, odd_vel = call(
+    corr, rest, *messages, even_vel, odd_vel = kernel_call(
         coarse_kernel,
         [block, block, y_message, y_message, faces_x, faces_x],
         [],
-        flags,
         first,
         inverse_rows,
         deflation,
@@ -614,20 +618,18 @@
         micros=1.4,
     )
     velocity_x = swap((even_vel, odd_vel), x_pairs)
-    coefs = call(
+    coefs = kernel_call(
         coefficients_kernel,
         [wide_own] * 5,
         [(3, size_x, rows, size_z)],
-        flags,
         velocity,
         *velocity_y,
         micros=0.01,
     )
-    search, image, second_row, *halo_coefs = call(
+    search, image, second_row, *halo_coefs = kernel_call(
         search_kernel,
         [block, block, row] + [wide_halo] * 4,
         [stage, (3, rows, size_z)] + smooth_scratch,
-        flags,
         *exchange(corr, rest, messages, True),
         *velocity_x,
         deflation,
@@ -635,11 +637,10 @@
         micros=3.0,
     )
     second = share(second_row)
-    corr, rest, middle, alpha, *messages = call(
+    corr, rest, middle, alpha, *messages = kernel_call(
         second_coarse_kernel,
         [block, block, block, (8, LANES), y_message, y_message],
         [],
-        flags,
         first,
         second,
         inverse_rows,
@@ -649,11 +650,10 @@
         velocity,
         micros=1.4,
     )
-    smoothed, turned, third_row = call(
+    smoothed, turned, third_row = kernel_call(
         smoothed_kernel,
         [block, block, row],
         [stage] + smooth_scratch,
-        flags,
         *exchange(corr, rest, messages, False),
         *halo_coefs,
         middle,
@@ -661,7 +661,7 @@
     )
     third = share(third_row)
     return tuple(
-        call(last_kernel, [block, block], [], flags, third, alpha, search, smoothed, middle, turned, micros=1.4)
+        kernel_call(last_kernel, [block, block], [], third, alpha, search, smoothed, middle, turned, micros=1.4)
     )
 
 

time: 71.3 us -> 67 us (0.940)
  Pallas kernels: 12.5 us -> 7.06 us
  waiting for transfers between devices: 14 us -> 15.1 us
    pallas_call x9, Pallas kernels: 12.5 us -> 7.06 us  [call(): pl.pallas_call(kernel, out_shape=[jax.ShapeDtypeStruct(shape, F32) for sh...]
  transfers between devices with their start and end apart: 13 -> 13, of which waited for: 5 -> 5; matrix products, arithmetic and copies ran while one was open for 0% -> 0% of each run, Pallas kernels for 5% -> 2%
where the time goes in v4:
time: 67 us; the launch traced here: 66.8 us
  starting transfers between devices  20.3 us (30%)
  blocking collectives  19.1 us (29%)
  waiting for transfers between devices  15.1 us (23%)
  Pallas kernels  7.06 us (11%)
  other arithmetic  3.35 us (5%)
  local copies, waits for them, and re-layouts  0.96 us (1%)
  between operations  0.82 us (1%)
    all_to_all x2, blocking collectives, share(): return lax.all_to_all(row, AXES, 0, 0, tiled=True)  19.1 us
    ppermute x12, starting transfers between devices, swap(): lax.ppermute(message, AXES, pair)  13.1 us
    ppermute x12, waiting for transfers between devices, swap(): lax.ppermute(message, AXES, pair)  11.4 us
    all_to_all x1, starting transfers between devices, share(): return lax.all_to_all(row, AXES, 0, 0, tiled=True)  7.3 us
    pallas_call x9, Pallas kernels, call(): pl.pallas_call(kernel, out_shape=[jax.ShapeDtypeStruct(shape, F32) for sh...  7.06 us
    all_to_all x1, waiting for transfers between devices, share(): return lax.all_to_all(row, AXES, 0, 0, tiled=True)  3.78 us
    reduce_sum x1, other arithmetic, local(): jnp.sum(deflation.astype(F32) * rounded, axis=(1, 2))  2.06 us
  transfers between devices with their start and end apart: 13, of which 5 were waited for; matrix products, arithmetic and copies ran while one was open for 0% of the time, Pallas kernels for 2%

profile of v4, /device:TPU:0, one launch (start us, length us, event | category | flops | bytes accessed | tf_op | source)
XLA Modules:
  0.0 66.8 jit_solution(11816107052785040616)
XLA Ops:
  0.6 0.0 copy-start.2
  0.6 0.0 copy-start
  0.7 0.0 copy-start.1
  0.7 0.0 copy-start.3
  0.7 1.1 %reduce_precision.3 = f32[8,16,256]{2,1,0:T(8,128)S(1)} reduce-precision(f32[8,16,256]{2,1,0:T(8,128)} %refs_4_.6), exponent_bits=8, mantissa_bits=7 | non-fusion elementwise | flops 32768 | bytes 262144 | tf_op jit(solution)/shard_map/reduce_precision | solution.py:579
  1.8 2.1 %multiply_reduce_fusion = f32[32,256]{1,0:T(8,128)S(1)} fusion(bf16[32,8,16,256]{3,2,1,0:T(8,128)(2,1)} %refs_3_.3, f32[8,16,256]{2,1,0:T(8,128)S(1)} %reduce_precision.3), kind=kLoop, calls=%fused_computation | loop fusion | flops 3137536 | bytes 2260992 | tf_op jit(solution)/shard_map/reduce_sum | solution.py:580
  3.9 0.1 reduce_sum.19
  4.0 0.1 broadcast_select_fusion
  4.0 0.1 select_n.19
  4.1 0.6 broadcast_in_dim.31
  4.8 7.3 %all-to-all-start = ((f32[32,1,256]{2,1,0:T(1,128)}), f32[32,1,256]{2,1,0:T(1,128)S(1)}, u32[]{:S(2)}, u32[]{:S(2)}) async-start(f32[32,1,256]{2,1,0:T(1,128)} %broadcast_in_dim.31), calls=%async_computation | async-start | bytes 65536 | tf_op jit(solution)/shard_map/all_to_all | solution.py:568
  12.1 0.1 select_n.20
  12.2 0.0 copy-done.1
  12.2 0.3 collective-permute-start.3
  12.5 3.0 %collective-permute-start.2 = (f32[3,8,4,256]{3,2,1,0:T(4,128)S(1)}, f32[3,8,4,256]{3,2,1,0:T(4,128)S(1)}, u32[]{:S(2)}, u32[]{:S(2)}) collective-permute-start(f32[3,8,4,256]{3,2,1,0:T(4,128)S(1)} %get-tuple-element.41.refs_5_), channel_id=1, source_target_pairs={{0,1},{1,0},{2,3},{3,2},{4,5},{5,4},{6,7},{7,6},{8,9},{9,8},{10,11... | collective-permute-start | bytes 294920 | tf_op jit(solution)/shard_map/ppermute | solution.py:565
  15.5 3.8 %all-to-all-done = f32[32,1,256]{2,1,0:T(1,128)S(1)} async-done(((f32[32,1,256]{2,1,0:T(1,128)}), f32[32,1,256]{2,1,0:T(1,128)S(1)}, u32[]{:S(2)}, u32[]{:S(2)}) %all-to-all-start) | async-done | bytes 32800 | tf_op jit(solution)/shard_map/all_to_all | solution.py:568
  19.3 0.0 copy-done.2
  19.3 0.0 copy-done
  19.3 0.0 copy-done.3
  19.3 0.8 %shard_map.60 = (f32[8,16,256]{2,1,0:T(8,128)S(1)}, f32[8,16,256]{2,1,0:T(8,128)S(1)}, f32[12,4,256]{2,1,0:T(4,128)S(1)}, f32[12,4,256]{2,1,0:T(4,128)S(1)}, f32...) custom-call(f32[32,256]{1,0:T(8,128)S(1)} %bitcast.13, f32[32,1024]{1,0:T(8,128)S(1)} %copy-done.3, ...), custom_call_target="tpu_custom_call" | custom-call | bytes 5040000 | tf_op jit(solution)/shard_map/pallas_call | solution.py:58
  20.1 0.7 %collective-permute-start = (f32[12,4,256]{2,1,0:T(4,128)S(1)}, f32[12,4,256]{2,1,0:T(4,128)S(1)}, u32[]{:S(2)}, u32[]{:S(2)}) collective-permute-start(f32[12,4,256]{2,1,0:T(4,128)S(1)} %get-tuple-element.44), channel_id=1, source_target_pairs={{0,1},{1,0},{2,3},{3,2},{4,5},{5,4},{6,7},{7,6},{8,9},{9,8},{10,11... | collective-permute-start | bytes 147464 | tf_op jit(solution)/shard_map/ppermute | solution.py:565
  20.9 0.0 collective-permute-start.1
  20.9 0.5 collective-permute-start.6
  21.4 0.0 collective-permute-done.3.refs_6_.refs_2_
  21.4 1.6 %collective-permute-start.7 = (f32[14,16,256]{2,1,0:T(8,128)S(1)}, f32[14,16,256]{2,1,0:T(8,128)S(1)}, u32[]{:S(2)}, u32[]{:S(2)}) collective-permute-start(f32[14,16,256]{2,1,0:T(8,128)S(1)} %get-tuple-element.58), channel_id=1, source_target_pairs={{0,1},{1,0},{2,3},{3,2},{4,5},{5,4},{6,7},{7,6},{8,16},{9,17},{10,... | collective-permute-start | bytes 688136 | tf_op jit(solution)/shard_map/ppermute | solution.py:565
  22.9 0.0 collective-permute-done.2.refs_5_.refs_1_
  22.9 1.3 %collective-permute-done.refs_2_ = f32[12,4,256]{2,1,0:T(4,128)S(1)} collective-permute-done((f32[12,4,256]{2,1,0:T(4,128)S(1)}, f32[12,4,256]{2,1,0:T(4,128)S(1)}, u32[]{:S(2)}, u32[]{:S(2)}) %collective-permute-start) | collective-permute-done | bytes 49184 | tf_op jit(solution)/shard_map/ppermute | solution.py:565
  24.3 0.0 collective-permute-done.1.refs_3_
  24.3 0.1 shard_map.61
  24.4 0.1 collective-permute-start.4
  24.5 3.1 %collective-permute-start.5 = (f32[9,24,256]{2,1,0:T(8,128)S(1)}, f32[9,24,256]{2,1,0:T(8,128)S(1)}, u32[]{:S(2)}, u32[]{:S(2)}) collective-permute-start(f32[9,24,256]{2,1,0:T(8,128)S(1)} %get-tuple-element.51), channel_id=1, source_target_pairs={{0,1},{1,0},{2,3},{3,2},{4,5},{5,4},{6,7},{7,6},{8,16},{9,17},{10,... | collective-permute-start | bytes 663560 | tf_op jit(solution)/shard_map/ppermute | solution.py:565
  27.6 0.1 shard_map.62
  27.7 0.0 collective-permute-done.6.refs_11_
  27.8 0.0 collective-permute-done.7.refs_12_
  27.8 0.0 collective-permute-done.4.refs_3_
  27.8 3.7 %collective-permute-done.5.refs_4_ = f32[9,24,256]{2,1,0:T(8,128)S(1)} collective-permute-done((f32[9,24,256]{2,1,0:T(8,128)S(1)}, f32[9,24,256]{2,1,0:T(8,128)S(1)}, u32[]{:S(2)}, u32[]{:S(2)}) %collective-permute-start.5) | collective-permute-done | bytes 221216 | tf_op jit(solution)/shard_map/ppermute | solution.py:565
  31.5 2.3 %shard_map.63 = (f32[8,16,256]{2,1,0:T(8,128)S(1)}, f32[8,16,256]{2,1,0:T(8,128)S(1)}, f32[32,256]{1,0:T(8,128)S(1)}, f32[8,24,256]{2,1,0:T(8,128)S(1)}, f32[8,2...) custom-call(f32[8,24,256]{2,1,0:T(8,128)S(1)} %get-tuple-element.47.refs_0_, ...), custom_call_target="tpu_custom_call" | custom-call | bytes 10800000 | tf_op jit(solution)/shard_map/pallas_call | solution.py:58
  33.8 0.1 copy.6
  33.9 9.6 %all_to_all.30 = f32[32,1,256]{2,1,0:T(1,128)S(1)} all-to-all(f32[32,1,256]{2,1,0:T(1,128)S(1)} %copy.6), channel_id=1, replica_groups=mesh['gx'=4,'gy'=8] {'gx','gy'}, dimensions={0} | all-to-all | bytes 65536 | tf_op jit(solution)/shard_map/all_to_all | solution.py:568
  43.5 0.9 %shard_map.64 = (f32[8,16,256]{2,1,0:T(8,128)S(1)}, f32[8,16,256]{2,1,0:T(8,128)S(1)}, f32[8,16,256]{2,1,0:T(8,128)S(1)}, f32[8,128]{1,0:T(8,128)S(1)}, f32[12,4...) custom-call(f32[32,256]{1,0:T(8,128)S(1)} %bitcast.14, f32[32,256]{1,0:T(8,128)S(1)} %bitcast.15, f32[32,1024]{1,0:T(8,128)S(1)} %copy-done.3, ...), custom_call_target="tpu_custom_call" | custom-call | bytes 5040000 | tf_op jit(solution)/shard_map/pallas_call | solution.py:58
  44.4 0.7 %collective-permute-start.8 = (f32[12,4,256]{2,1,0:T(4,128)S(1)}, f32[12,4,256]{2,1,0:T(4,128)S(1)}, u32[]{:S(2)}, u32[]{:S(2)}) collective-permute-start(f32[12,4,256]{2,1,0:T(4,128)S(1)} %get-tuple-element.63), channel_id=1, source_target_pairs={{0,1},{1,0},{2,3},{3,2},{4,5},{5,4},{6,7},{7,6},{8,9},{9,8},{10,11... | collective-permute-start | bytes 147464 | tf_op jit(solution)/shard_map/ppermute | solution.py:565
  45.2 0.0 collective-permute-start.9
  45.2 3.4 %collective-permute-done.8.refs_2_ = f32[12,4,256]{2,1,0:T(4,128)S(1)} collective-permute-done((f32[12,4,256]{2,1,0:T(4,128)S(1)}, f32[12,4,256]{2,1,0:T(4,128)S(1)}, u32[]{:S(2)}, u32[]{:S(2)}) %collective-permute-start.8) | collective-permute-done | bytes 49184 | tf_op jit(solution)/shard_map/ppermute | solution.py:565
  48.6 0.0 collective-permute-done.9.refs_3_
  48.6 0.1 shard_map.65
  48.7 0.1 collective-permute-start.10
  48.8 3.0 %collective-permute-start.11 = (f32[5,24,256]{2,1,0:T(8,128)S(1)}, f32[5,24,256]{2,1,0:T(8,128)S(1)}, u32[]{:S(2)}, u32[]{:S(2)}) collective-permute-start(f32[5,24,256]{2,1,0:T(8,128)S(1)} %get-tuple-element.69), channel_id=1, source_target_pairs={{0,1},{1,0},{2,3},{3,2},{4,5},{5,4},{6,7},{7,6},{8,16},{9,17},{10,... | collective-permute-start | bytes 368648 | tf_op jit(solution)/shard_map/ppermute | solution.py:565
  51.7 0.0 collective-permute-done.10.refs_3_
  51.7 2.9 %collective-permute-done.11.refs_4_ = f32[5,24,256]{2,1,0:T(8,128)S(1)} collective-permute-done((f32[5,24,256]{2,1,0:T(8,128)S(1)}, f32[5,24,256]{2,1,0:T(8,128)S(1)}, u32[]{:S(2)}, u32[]{:S(2)}) %collective-permute-start.11) | collective-permute-done | bytes 122912 | tf_op jit(solution)/shard_map/ppermute | solution.py:565
  54.6 1.7 %shard_map.66 = (f32[8,16,256]{2,1,0:T(8,128)S(1)}, f32[8,16,256]{2,1,0:T(8,128)S(1)}, f32[32,256]{1,0:T(8,128)S(1)}) custom-call(f32[8,24,256]{2,1,0:T(8,128)S(1)} %get-tuple-element.65.refs_0_, f32[2,24,256]{2,1,0:T(8,128)S(1)} %get-tuple-element.66.refs_1_, f32[2,8,256]{2,1,0:T(8,128)S(1)} %get-tuple-element.67.refs_2_, ...), custom_call_target="tpu_custom_call" | custom-call | bytes 9000000 | tf_op jit(solution)/shard_map/pallas_call | solution.py:58
  56.3 0.1 copy.7
  56.4 9.5 %all_to_all.31 = f32[32,1,256]{2,1,0:T(1,128)S(1)} all-to-all(f32[32,1,256]{2,1,0:T(1,128)S(1)} %copy.7), channel_id=1, replica_groups=mesh['gx'=4,'gy'=8] {'gx','gy'}, dimensions={0} | all-to-all | bytes 65536 | tf_op jit(solution)/shard_map/all_to_all | solution.py:568
  65.9 0.8 %shard_map.67 = (f32[8,16,256]{2,1,0:T(8,128)}, f32[8,16,256]{2,1,0:T(8,128)}) custom-call(f32[32,256]{1,0:T(8,128)S(1)} %bitcast.16, f32[8,128]{1,0:T(8,128)S(1)} %get-tuple-element.76.refs_1_, f32[8,16,256]{2,1,0:T(8,128)S(1)} %get-tuple-element.77.refs_2_, f32[8,16,256]{2,1,0:T(8,128)S(1)} %get-tuple-element.78.refs_3_, ...), custom_call_target="tpu_custom_call" | custom-call | bytes 5040000 | tf_op jit(solution)/shard_map/pallas_call | solution.py:58
  (6 shorter events, 0.0 us)
Async XLA Ops:
  0.6 18.6 %copy-start.2 = (f32[8,16,256]{2,1,0:T(8,128)S(1)}, f32[8,16,256]{2,1,0:T(8,128)}, u32[]{:S(2)}) copy-start(f32[8,16,256]{2,1,0:T(8,128)} %refs_4_.6) | copy-start | bytes 393220
  0.6 18.6 %copy-start = (bf16[32,8,16,256]{3,2,1,0:T(8,128)(2,1)S(1)}, bf16[32,8,16,256]{3,2,1,0:T(8,128)(2,1)}, u32[]{:S(2)}) copy-start(bf16[32,8,16,256]{3,2,1,0:T(8,128)(2,1)} %refs_3_.3) | copy-start | bytes 6291460
  0.7 11.5 %copy-start.1 = (f32[3,8,16,256]{3,2,1,0:T(8,128)S(1)}, f32[3,8,16,256]{3,2,1,0:T(8,128)}, u32[]{:S(2)}) copy-start(f32[3,8,16,256]{3,2,1,0:T(8,128)} %refs_4_.7) | copy-start | bytes 1179652
  0.7 18.6 %copy-start.3 = (f32[32,1024]{1,0:T(8,128)S(1)}, f32[32,1024]{1,0:T(8,128)}, u32[]{:S(2)}) copy-start(f32[32,1024]{1,0:T(8,128)} %refs_2_.3) | copy-start | bytes 393220
  4.8 14.5 %all-to-all-start = ((f32[32,1,256]{2,1,0:T(1,128)}), f32[32,1,256]{2,1,0:T(1,128)S(1)}, u32[]{:S(2)}, u32[]{:S(2)}) async-start(f32[32,1,256]{2,1,0:T(1,128)} %broadcast_in_dim.31), calls=%async_computation | async-start | bytes 65536 | tf_op jit(solution)/shard_map/all_to_all | solution.py:568
  12.2 9.2 %collective-permute-start.3 = (f32[3,8,4,256]{3,2,1,0:T(4,128)S(1)}, f32[3,8,4,256]{3,2,1,0:T(4,128)S(1)}, u32[]{:S(2)}, u32[]{:S(2)}) collective-permute-start(f32[3,8,4,256]{3,2,1,0:T(4,128)S(1)} %get-tuple-element.46), channel_id=1, source_target_pairs={{0,8},{1,2},{2,1},{3,4},{4,3},{5,6},{6,5},{7,15},{8,0},{9,10},{10,... | collective-permute-start | bytes 294920 | tf_op jit(solution)/shard_map/ppermute | solution.py:565
  12.5 10.4 %collective-permute-start.2 = (f32[3,8,4,256]{3,2,1,0:T(4,128)S(1)}, f32[3,8,4,256]{3,2,1,0:T(4,128)S(1)}, u32[]{:S(2)}, u32[]{:S(2)}) collective-permute-start(f32[3,8,4,256]{3,2,1,0:T(4,128)S(1)} %get-tuple-element.41.refs_5_), channel_id=1, source_target_pairs={{0,1},{1,0},{2,3},{3,2},{4,5},{5,4},{6,7},{7,6},{8,9},{9,8},{10,11... | collective-permute-start | bytes 294920 | tf_op jit(solution)/shard_map/ppermute | solution.py:565
  20.1 4.2 %collective-permute-start = (f32[12,4,256]{2,1,0:T(4,128)S(1)}, f32[12,4,256]{2,1,0:T(4,128)S(1)}, u32[]{:S(2)}, u32[]{:S(2)}) collective-permute-start(f32[12,4,256]{2,1,0:T(4,128)S(1)} %get-tuple-element.44), channel_id=1, source_target_pairs={{0,1},{1,0},{2,3},{3,2},{4,5},{5,4},{6,7},{7,6},{8,9},{9,8},{10,11... | collective-permute-start | bytes 147464 | tf_op jit(solution)/shard_map/ppermute | solution.py:565
  20.9 3.4 %collective-permute-start.1 = (f32[12,4,256]{2,1,0:T(4,128)S(1)}, f32[12,4,256]{2,1,0:T(4,128)S(1)}, u32[]{:S(2)}, u32[]{:S(2)}) collective-permute-start(f32[12,4,256]{2,1,0:T(4,128)S(1)} %get-tuple-element.45), channel_id=1, source_target_pairs={{0,8},{1,2},{2,1},{3,4},{4,3},{5,6},{6,5},{7,15},{8,0},{9,10},{10,... | collective-permute-start | bytes 147464 | tf_op jit(solution)/shard_map/ppermute | solution.py:565
  20.9 6.9 %collective-permute-start.6 = (f32[14,16,256]{2,1,0:T(8,128)S(1)}, f32[14,16,256]{2,1,0:T(8,128)S(1)}, u32[]{:S(2)}, u32[]{:S(2)}) collective-permute-start(f32[14,16,256]{2,1,0:T(8,128)S(1)} %get-tuple-element.57), channel_id=1, source_target_pairs={{0,8},{1,9},{2,10},{3,11},{4,12},{5,13},{6,14},{7,15},{8,0},{9,1},... | collective-permute-start | bytes 688136 | tf_op jit(solution)/shard_map/ppermute | solution.py:565
  21.4 6.4 %collective-permute-start.7 = (f32[14,16,256]{2,1,0:T(8,128)S(1)}, f32[14,16,256]{2,1,0:T(8,128)S(1)}, u32[]{:S(2)}, u32[]{:S(2)}) collective-permute-start(f32[14,16,256]{2,1,0:T(8,128)S(1)} %get-tuple-element.58), channel_id=1, source_target_pairs={{0,1},{1,0},{2,3},{3,2},{4,5},{5,4},{6,7},{7,6},{8,16},{9,17},{10,... | collective-permute-start | bytes 688136 | tf_op jit(solution)/shard_map/ppermute | solution.py:565
  24.4 3.3 %collective-permute-start.4 = (f32[9,24,256]{2,1,0:T(8,128)S(1)}, f32[9,24,256]{2,1,0:T(8,128)S(1)}, u32[]{:S(2)}, u32[]{:S(2)}) collective-permute-start(f32[9,24,256]{2,1,0:T(8,128)S(1)} %get-tuple-element.50), channel_id=1, source_target_pairs={{0,8},{1,9},{2,10},{3,11},{4,12},{5,13},{6,14},{7,15},{8,0},{9,1},... | collective-permute-start | bytes 663560 | tf_op jit(solution)/shard_map/ppermute | solution.py:565
  24.5 7.0 %collective-permute-start.5 = (f32[9,24,256]{2,1,0:T(8,128)S(1)}, f32[9,24,256]{2,1,0:T(8,128)S(1)}, u32[]{:S(2)}, u32[]{:S(2)}) collective-permute-start(f32[9,24,256]{2,1,0:T(8,128)S(1)} %get-tuple-element.51), channel_id=1, source_target_pairs={{0,1},{1,0},{2,3},{3,2},{4,5},{5,4},{6,7},{7,6},{8,16},{9,17},{10,... | collective-permute-start | bytes 663560 | tf_op jit(solution)/shard_map/ppermute | solution.py:565
  44.4 4.2 %collective-permute-start.8 = (f32[12,4,256]{2,1,0:T(4,128)S(1)}, f32[12,4,256]{2,1,0:T(4,128)S(1)}, u32[]{:S(2)}, u32[]{:S(2)}) collective-permute-start(f32[12,4,256]{2,1,0:T(4,128)S(1)} %get-tuple-element.63), channel_id=1, source_target_pairs={{0,1},{1,0},{2,3},{3,2},{4,5},{5,4},{6,7},{7,6},{8,9},{9,8},{10,11... | collective-permute-start | bytes 147464 | tf_op jit(solution)/shard_map/ppermute | solution.py:565
  45.2 3.4 %collective-permute-start.9 = (f32[12,4,256]{2,1,0:T(4,128)S(1)}, f32[12,4,256]{2,1,0:T(4,128)S(1)}, u32[]{:S(2)}, u32[]{:S(2)}) collective-permute-start(f32[12,4,256]{2,1,0:T(4,128)S(1)} %get-tuple-element.64), channel_id=1, source_target_pairs={{0,8},{1,2},{2,1},{3,4},{4,3},{5,6},{6,5},{7,15},{8,0},{9,10},{10,... | collective-permute-start | bytes 147464 | tf_op jit(solution)/shard_map/ppermute | solution.py:565
  48.7 3.1 %collective-permute-start.10 = (f32[5,24,256]{2,1,0:T(8,128)S(1)}, f32[5,24,256]{2,1,0:T(8,128)S(1)}, u32[]{:S(2)}, u32[]{:S(2)}) collective-permute-start(f32[5,24,256]{2,1,0:T(8,128)S(1)} %get-tuple-element.68), channel_id=1, source_target_pairs={{0,8},{1,9},{2,10},{3,11},{4,12},{5,13},{6,14},{7,15},{8,0},{9,1},... | collective-permute-start | bytes 368648 | tf_op jit(solution)/shard_map/ppermute | solution.py:565
  48.8 5.8 %collective-permute-start.11 = (f32[5,24,256]{2,1,0:T(8,128)S(1)}, f32[5,24,256]{2,1,0:T(8,128)S(1)}, u32[]{:S(2)}, u32[]{:S(2)}) collective-permute-start(f32[5,24,256]{2,1,0:T(8,128)S(1)} %get-tuple-element.69), channel_id=1, source_target_pairs={{0,1},{1,0},{2,3},{3,2},{4,5},{5,4},{6,7},{7,6},{8,16},{9,17},{10,... | collective-permute-start | bytes 368648 | tf_op jit(solution)/shard_map/ppermute | solution.py:565

commit v5 on v4

--- a/solution.py
+++ b/solution.py
@@ -10,6 +10,8 @@
 DEPTH = 2
 CHEB = 4
 WIDE = 4
+EARLY_FIRST = 1
+SPARE = 3
 LANES = 128
 AXES = ("gx", "gy")
 F32 = jnp.float32
@@ -182,6 +184,18 @@
         write(odd_out, True)
 
 
+def by_side(odd, use, *pairs):
+    evens, odds = [pair[0] for pair in pairs], [pair[1] for pair in pairs]
+
+    @pl.when(odd == 0)
+    def _():
+        use(odds, evens)
+
+    @pl.when(odd != 0)
+    def _():
+        use(evens, odds)
+
+
 def velocity_y_kernel(flags, velocity, after, even_out, odd_out):
     _, size_x, size_y, _ = velocity.shape
 
@@ -194,16 +208,18 @@
     by_parity(flags[ODD_Y], write_y, even_out, odd_out)
 
 
-def write_velocity_x(flags, velocity, even_out, odd_out):
-    size_x = velocity.shape[1]
+def write_x_early(flags, planes, rest, corr, velocity, even_out, odd_out):
+    size_x = rest.shape[0]
 
     def write(out, high):
         start = size_x - WIDE if high else 0
-        for d in range(3):
-            for k in range(WIDE):
-                out[d * WIDE + k] = velocity[d, start + k]
-        for k in range(3 * WIDE, out.shape[0]):
-            out[k] = jnp.zeros(out.shape[1:], F32)
+        out[0] = corr[size_x - 1 if high else 0]
+        for k in range(planes):
+            out[1 + k] = rest[start + k]
+        if velocity is not None:
+            for d in range(3):
+                for k in range(WIDE):
+                    out[1 + planes + d * WIDE + k] = velocity[d, start + k]
 
     by_parity(flags[ODD_X], write, even_out, odd_out)
 
@@ -251,29 +267,22 @@
         diagonal[x] = coefficients(x, wide[0, x], wide[1, x], wide[2, x], kept, keep_first, (inverse, b0, b1, b2))
 
 
-def halo_coefficients(flags, even_in, odd_in, even_vel, odd_vel, outs, wide):
-    size_y, size_z = even_vel.shape[1:]
+def halo_coefficients(flags, early, late, outs, wide):
+    size_y, size_z = early[0].shape[1:]
     rows = size_y + 2 * WIDE
     kept = rows_in_grid(flags, (rows, size_z))
     keep_first, _ = lane_masks((rows, size_z))
 
-    def side(start, message, faces, present):
+    def side(start, message, corners, present):
         for k in range(WIDE):
             for d in range(3):
-                wide[d, 0:WIDE, :] = message[WIDE + 1 + k, 8 * d : 8 * d + WIDE, :]
-                wide[d, WIDE : WIDE + size_y, :] = faces[d * WIDE + k]
-                wide[d, WIDE + size_y : rows, :] = message[WIDE + 1 + k, 8 * d + WIDE : 8 * d + 2 * WIDE, :]
+                tile = WIDE + 2 + d * WIDE + k
+                wide[d, 0:WIDE, :] = corners[tile, 0:WIDE, :]
+                wide[d, WIDE : WIDE + size_y, :] = message[1 + EARLY_FIRST + d * WIDE + k]
+                wide[d, WIDE + size_y : rows, :] = corners[tile, WIDE : 2 * WIDE, :]
             coefficients(start + k, wide[0], wide[1], wide[2], kept & (flags[present] != 0), keep_first, outs)
 
-    @pl.when(flags[ODD_X] == 0)
-    def _():
-        side(0, odd_in, odd_vel, LOW_X)
-        side(WIDE, even_in, even_vel, HIGH_X)
-
-    @pl.when(flags[ODD_X] != 0)
-    def _():
-        side(0, even_in, even_vel, LOW_X)
-        side(WIDE, odd_in, odd_vel, HIGH_X)
+    by_side(flags[ODD_X], lambda low, high: (side(0, *low, LOW_X), side(WIDE, *high, HIGH_X)), early, late)
 
 
 class Region:
@@ -289,17 +298,18 @@
 
 
 def coarse_kernel(
-    flags, received, inverse, vectors, field, velocity, after, corr, rest, even_out, odd_out, even_vel, odd_vel
+    flags, received, inverse, vectors, field, velocity, after, corr, rest, even_out, odd_out, even_x, odd_x
 ):
     coarse, _ = gathered(received)
     prolong(solve(coarse, inverse, vectors), vectors, corr)
     subtract_own(field, corr, velocity, rest)
     by_parity(flags[ODD_Y], lambda out, high: write_y_message(out, rest, corr, high), even_out, odd_out)
-    write_velocity_x(flags, velocity, even_vel, odd_vel)
+    write_x_early(flags, EARLY_FIRST, rest, corr, velocity, even_x, odd_x)
 
 
 def second_coarse_kernel(
-    flags, received, second, inverse, vectors, field, image, velocity, corr, rest, middle, alpha, even_out, odd_out
+    flags, received, second, inverse, vectors, field, image, velocity, corr, rest, middle, alpha, even_out, odd_out,
+    even_x, odd_x
 ):
     coarse, _ = gathered(received)
     coarse_image, products = gathered(second)
@@ -311,10 +321,11 @@
     prolong(solve(coarse - step * coarse_image, inverse, vectors), vectors, corr)
     subtract_own(middle, corr, velocity, rest)
     by_parity(flags[ODD_Y], lambda out, high: write_y_message(out, rest, corr, high), even_out, odd_out)
+    write_x_early(flags, WIDE, rest, corr, None, even_x, odd_x)
 
 
 def extend_kernel(
-    flags, rest, corr, even_in, odd_in, velocity, even_vel, odd_vel, wide, sides, past, even_out, odd_out, corners=True
+    flags, rest, corr, odd_in, even_in, velocity, even_vel, odd_vel, wide, sides, past, even_out, odd_out, corners, early_planes
 ):
     size_x, size_y, size_z = rest.shape
     rows = size_y + 2 * WIDE
@@ -353,8 +364,19 @@
     def write(out, high):
         start = size_x - WIDE if high else 0
         for k in range(WIDE):
-            out[k] = wide[start + k]
-        out[WIDE] = sides[1 if high else 0]
+            out[k, 0:WIDE, :] = wide[start + k, 0:WIDE, :]
+            out[k, WIDE : 2 * WIDE, :] = wide[start + k, end:rows, :]
+        side = 1 if high else 0
+        out[WIDE, 0:WIDE, :] = sides[side, 0:WIDE, :]
+        out[WIDE, WIDE : 2 * WIDE, :] = sides[side, end:rows, :]
+        out[WIDE + 1, 0:WIDE, :] = past[0, start : start + WIDE, :]
+        out[WIDE + 1, WIDE : 2 * WIDE, :] = past[1, start : start + WIDE, :]
+
+        tile = WIDE + 2 + (3 * WIDE if corners else 0)
+        for k in range(early_planes, WIDE):
+            for row in range(0, size_y, 8):
+                out[tile] = rest[start + k, row : row + 8, :]
+                tile += 1
 
     by_parity(flags[ODD_X], write, even_out, odd_out)
     if not corners:
@@ -363,20 +385,15 @@
     def write_corners(low, high):
         def write(out, upper):
             start = size_x - WIDE if upper else 0
-            for k in range(WIDE):
-                for d in range(3):
-                    out[WIDE + 1 + k, 8 * d : 8 * d + WIDE, :] = low[d, start + k]
-                    out[WIDE + 1 + k, 8 * d + WIDE : 8 * d + 2 * WIDE, :] = high[d, start + k]
+            for d in range(3):
+                for k in range(WIDE):
+                    tile = WIDE + 2 + d * WIDE + k
+                    out[tile, 0:WIDE, :] = low[0][d, start + k]
+                    out[tile, WIDE : 2 * WIDE, :] = high[0][d, start + k]
 
         by_parity(flags[ODD_X], write, even_out, odd_out)
 
-    @pl.when(flags[ODD_Y] == 0)
-    def _():
-        write_corners(odd_vel, even_vel)
-
-    @pl.when(flags[ODD_Y] != 0)
-    def _():
-        write_corners(even_vel, odd_vel)
+    by_side(flags[ODD_Y], write_corners, (even_vel, odd_vel))
 
 
 def beside_terms(before, here, after, x, tile, coefs, keep_last):
@@ -422,10 +439,10 @@
 
 
 def smooth(
-    flags, wide, sides, past, even_in, odd_in, diagonal, coefs, corr, field_out, image_out, scratch
+    flags, early_planes, wide, sides, past, early, late, diagonal, coefs, corr, field_out, image_out, scratch
 ):
     source, left, update, whole = scratch
-    inverse, b0, _, _ = coefs
+    inverse, b0, b1, _ = coefs
     size_x, size_y, size_z = corr.shape
     rows = size_y + 2 * WIDE
     span = size_x + 2 * WIDE
@@ -435,20 +452,36 @@
     has_low_y, has_high_y = flags[LOW_Y] != 0, flags[HIGH_Y] != 0
     lowest, highest = slice(0, 8), slice(rows - 8, rows)
     tile_row = lax.broadcasted_iota(jnp.int32, (8, size_z), 0)
-    def halo(low, high):
+    end = WIDE + size_y
+
+    def put(out, x, middle, ends):
+        out[x, 0:WIDE, :] = ends[0:WIDE, :]
+        for row_ in range(0, size_y, 8):
+            out[x, WIDE + row_ : WIDE + row_ + 8, :] = middle(row_)
+        out[x, end:rows, :] = ends[WIDE : 2 * WIDE, :]
+
+    def halo(side, first, edge, present):
+        message, ends = side
         for k in range(WIDE):
-            source[k] = inverse[k] * low[k]
-            source[WIDE + size_x + k] = inverse[WIDE + size_x + k] * high[k]
-        whole[0] = jnp.where(has_low_x, low[WIDE], 0.0)
-        whole[size_x + 1] = jnp.where(has_high_x, high[WIDE], 0.0)
-
-    @pl.when(flags[ODD_X] == 0)
-    def _():
-        halo(odd_in, even_in)
-
-    @pl.when(flags[ODD_X] != 0)
-    def _():
-        halo(even_in, odd_in)
+            x = first + k
+            if k < early_planes:
+                middle = lambda row_: message[1 + k, row_ : row_ + 8, :]
+            else:
+                tile = ends.shape[0] - SPARE - (WIDE - k) * (size_y // 8)
+                middle = lambda row_: ends[tile + row_ // 8]
+            put(source, x, middle, ends.at[k])
+            source[x] = inverse[x] * source[x]
+            for row_, weight, line in ((WIDE, b1, k), (end - 1, inverse, WIDE + k)):
+                at = slice(row_, row_ + 1)
+                source[x, at] = source[x, at] + weight[x, at] * ends[WIDE + 1, line : line + 1, :]
+        put(whole, edge, lambda row_: message[0, row_ : row_ + 8, :], ends.at[WIDE])
+        whole[edge] = jnp.where(present, whole[edge], 0.0)
+
+    def halos(low, high):
+        halo(low, 0, 0, has_low_x)
+        halo(high, WIDE + size_x, size_x + 1, has_high_x)
+
+    by_side(flags[ODD_X], halos, early, late)
 
     for k in range(size_x):
         source[WIDE + k] = inverse[WIDE + k] * wide[k]
@@ -517,23 +550,25 @@
 
 
 def search_kernel(
-    flags, wide, sides, past, even_in, odd_in, diagonal, own0, own1, own2, own3, corr, even_vel, odd_vel, vectors, right_side,
-    search, image, out, halo0, halo1, halo2, halo3, stage, wide_vel, *scratch
+    flags, wide, sides, past, odd_late, even_late, diagonal, own0, own1, own2, own3, corr, odd_early, even_early, vectors,
+    right_side, search, image, out, halo0, halo1, halo2, halo3, stage, wide_vel, *scratch
 ):
     halos = (halo0, halo1, halo2, halo3)
-    halo_coefficients(flags, even_in, odd_in, even_vel, odd_vel, halos, wide_vel)
+    early, late = (even_early, odd_early), (even_late, odd_late)
+    halo_coefficients(flags, early, late, halos, wide_vel)
     coefs = [Region(*pair) for pair in zip((own0, own1, own2, own3), halos)]
-    smooth(flags, wide, sides, past, even_in, odd_in, diagonal, coefs, corr, search, image, scratch)
+    smooth(flags, EARLY_FIRST, wide, sides, past, early, late, diagonal, coefs, corr, search, image, scratch)
     products = [dot_planes(right_side, right_side), dot_planes(right_side, image)]
     restrict(vectors, image, products, flags, (out, stage))
 
 
 def smoothed_kernel(
-    flags, wide, sides, past, even_in, odd_in, diagonal, own0, own1, own2, own3, corr, halo0, halo1, halo2, halo3, middle,
-    smoothed, turned, out, stage, *scratch
+    flags, wide, sides, past, odd_late, even_late, diagonal, own0, own1, own2, own3, corr, odd_early, even_early, halo0,
+    halo1, halo2, halo3, middle, smoothed, turned, out, stage, *scratch
 ):
+    early, late = (even_early, odd_early), (even_late, odd_late)
     coefs = [Region(*pair) for pair in zip((own0, own1, own2, own3), (halo0, halo1, halo2, halo3))]
-    smooth(flags, wide, sides, past, even_in, odd_in, diagonal, coefs, corr, smoothed, turned, scratch)
+    smooth(flags, WIDE, wide, sides, past, early, late, diagonal, coefs, corr, smoothed, turned, scratch)
     stage[...] = jnp.zeros_like(stage)
     for k, total in enumerate((dot_planes(turned, middle), dot_planes(turned, turned))):
         total = jnp.sum(total, axis=0, keepdims=True)
@@ -562,7 +597,8 @@
     x_pairs, y_pairs = pair_permutations(count_x, count_y)
 
     def swap(messages, pairs):
-        return [lax.ppermute(message, AXES, pair) for message, pair in zip(messages, pairs)]
+        odd = lax.ppermute(messages[1], AXES, pairs[1])
+        return [lax.ppermute(messages[0], AXES, pairs[0]), odd]
 
     def share(row):
         return lax.all_to_all(row, AXES, 0, 0, tiled=True)
@@ -583,31 +619,35 @@
     first_row = jnp.broadcast_to(first_row.reshape(1, 2 * LANES), row)
 
     first = share(first_row)
-    faces_y, faces_x = (3, size_x, WIDE, size_z), (3 * WIDE + 2, size_y, size_z)
+    faces_y = (3, size_x, WIDE, size_z)
+    x_early = (WIDE + 1, size_y, size_z)
+    x_early_first = (1 + EARLY_FIRST + 3 * WIDE, size_y, size_z)
     velocity_y = kernel_call(velocity_y_kernel, [faces_y] * 2, [], velocity, first_row[0, :8], micros=0.01)
     after = velocity_y[0]
     velocity_y = swap(velocity_y, y_pairs)
 
     wide_own, wide_halo = (size_x, rows, size_z), (2 * WIDE, rows, size_z)
 
-    def exchange(corr, rest, messages, corners):
-        message = (WIDE + 1 + (WIDE if corners else 0), rows, size_z)
+    def exchange(corr, rest, messages, corners, early_planes):
+        tiles = WIDE + 2 + (3 * WIDE if corners else 0) + (WIDE - early_planes) * (size_y // 8)
+        message = (tiles + (SPARE if corners else 0), 2 * WIDE, size_z)
+        y_messages, early = swap(messages[:2], y_pairs), swap(messages[2:], x_pairs)
         *own, even, odd = kernel_call(
-            functools.partial(extend_kernel, corners=corners),
+            functools.partial(extend_kernel, corners=corners, early_planes=early_planes),
             [wide_own, (2, rows, size_z), (2, size_x, size_z), message, message],
             [],
             rest,
             corr,
-            *swap(messages, y_pairs),
+            *y_messages[::-1],
             velocity,
             *velocity_y,
             micros=0.01,
         )
-        return (*own, *swap((even, odd), x_pairs), *coefs, corr)
-
-    corr, rest, *messages, even_vel, odd_vel = kernel_call(
+        return (*own, *swap((even, odd), x_pairs)[::-1], *coefs, corr, *early[::-1])
+
+    corr, rest, *messages = kernel_call(
         coarse_kernel,
-        [block, block, y_message, y_message, faces_x, faces_x],
+        [block, block, y_message, y_message, x_early_first, x_early_first],
         [],
         first,
         inverse_rows,
@@ -617,7 +657,6 @@
         after,
         micros=1.4,
     )
-    velocity_x = swap((even_vel, odd_vel), x_pairs)
     coefs = kernel_call(
         coefficients_kernel,
         [wide_own] * 5,
@@ -630,8 +669,7 @@
         search_kernel,
         [block, block, row] + [wide_halo] * 4,
         [stage, (3, rows, size_z)] + smooth_scratch,
-        *exchange(corr, rest, messages, True),
-        *velocity_x,
+        *exchange(corr, rest, messages, True, EARLY_FIRST),
         deflation,
         right_side,
         micros=3.0,
@@ -639,7 +677,7 @@
     second = share(second_row)
     corr, rest, middle, alpha, *messages = kernel_call(
         second_coarse_kernel,
-        [block, block, block, (8, LANES), y_message, y_message],
+        [block, block, block, (8, LANES), y_message, y_message, x_early, x_early],
         [],
         first,
         second,
@@ -654,7 +692,7 @@
         smoothed_kernel,
         [block, block, row],
         [stage] + smooth_scratch,
-        *exchange(corr, rest, messages, False),
+        *exchange(corr, rest, messages, False, WIDE),
         *halo_coefs,
         middle,
         micros=2.5,

time: 67 us -> 64.6 us (0.964)
  waiting for transfers between devices: 15.1 us -> 12.5 us
    ppermute x12 -> x14, waiting for transfers between devices: 11.4 us -> 8.71 us  [the longest x7 5.82 us: swap(): odd = lax.ppermute(messages[1], AXES, pairs[1])]
    ppermute x12 -> x14, starting transfers between devices: 13.1 us -> 13.4 us  [the longest x7 8.04 us: swap(): return [lax.ppermute(messages[0], AXES, pairs[0]), odd]]
  transfers between devices with their start and end apart: 13 -> 15, of which waited for: 5 -> 6; matrix products, arithmetic and copies ran while one was open for 0% -> 0% of each run, Pallas kernels for 2% -> 2%
where the time goes in v5:
time: 64.6 us; the launch traced here: 64.4 us
  starting transfers between devices  20.7 us (32%)
  blocking collectives  18.8 us (29%)
  waiting for transfers between devices  12.5 us (19%)
  Pallas kernels  7.22 us (11%)
  other arithmetic  3.35 us (5%)
  local copies, waits for them, and re-layouts  0.96 us (1%)
  between operations  0.79 us (1%)
    all_to_all x2, blocking collectives, share(): return lax.all_to_all(row, AXES, 0, 0, tiled=True)  18.8 us
    ppermute x7, starting transfers between devices, swap(): return [lax.ppermute(messages[0], AXES, pairs[0]), odd]  8.04 us
    all_to_all x1, starting transfers between devices, share(): return lax.all_to_all(row, AXES, 0, 0, tiled=True)  7.3 us
    pallas_call x9, Pallas kernels, call(): pl.pallas_call(kernel, out_shape=[jax.ShapeDtypeStruct(shape, F32) for sh...  7.22 us
    ppermute x7, waiting for transfers between devices, swap(): odd = lax.ppermute(messages[1], AXES, pairs[1])  5.82 us
    ppermute x7, starting transfers between devices, swap(): odd = lax.ppermute(messages[1], AXES, pairs[1])  5.39 us
    all_to_all x1, waiting for transfers between devices, share(): return lax.all_to_all(row, AXES, 0, 0, tiled=True)  3.78 us
    ppermute x7, waiting for transfers between devices, swap(): return [lax.ppermute(messages[0], AXES, pairs[0]), odd]  2.89 us
  transfers between devices with their start and end apart: 15, of which 6 were waited for; matrix products, arithmetic and copies ran while one was open for 0% of the time, Pallas kernels for 2%

profile of v5, /device:TPU:0, one launch (start us, length us, event | category | flops | bytes accessed | tf_op | source)
XLA Modules:
  0.0 64.4 jit_solution(8639006581326941099)
XLA Ops:
  0.6 0.0 copy-start.2
  0.6 0.0 copy-start
  0.7 0.0 copy-start.1
  0.7 0.0 copy-start.3
  0.7 1.1 %reduce_precision.3 = f32[8,16,256]{2,1,0:T(8,128)S(1)} reduce-precision(f32[8,16,256]{2,1,0:T(8,128)} %refs_4_.6), exponent_bits=8, mantissa_bits=7 | non-fusion elementwise | flops 32768 | bytes 262144 | tf_op jit(solution)/shard_map/reduce_precision | solution.py:615
  1.8 2.1 %multiply_reduce_fusion = f32[32,256]{1,0:T(8,128)S(1)} fusion(bf16[32,8,16,256]{3,2,1,0:T(8,128)(2,1)} %refs_3_.3, f32[8,16,256]{2,1,0:T(8,128)S(1)} %reduce_precision.3), kind=kLoop, calls=%fused_computation | loop fusion | flops 3137536 | bytes 2260992 | tf_op jit(solution)/shard_map/reduce_sum | solution.py:616
  3.9 0.1 reduce_sum.19
  4.0 0.1 broadcast_select_fusion
  4.0 0.1 select_n.19
  4.1 0.6 broadcast_in_dim.31
  4.8 7.3 %all-to-all-start = ((f32[32,1,256]{2,1,0:T(1,128)}), f32[32,1,256]{2,1,0:T(1,128)S(1)}, u32[]{:S(2)}, u32[]{:S(2)}) async-start(f32[32,1,256]{2,1,0:T(1,128)} %broadcast_in_dim.31), calls=%async_computation | async-start | bytes 65536 | tf_op jit(solution)/shard_map/all_to_all | solution.py:604
  12.1 0.1 select_n.20
  12.2 0.0 copy-done.1
  12.2 0.3 collective-permute-start.3
  12.5 3.0 %collective-permute-start.2 = (f32[3,8,4,256]{3,2,1,0:T(4,128)S(1)}, f32[3,8,4,256]{3,2,1,0:T(4,128)S(1)}, u32[]{:S(2)}, u32[]{:S(2)}) collective-permute-start(f32[3,8,4,256]{3,2,1,0:T(4,128)S(1)} %get-tuple-element.43.refs_5_), channel_id=1, source_target_pairs={{0,1},{1,0},{2,3},{3,2},{4,5},{5,4},{6,7},{7,6},{8,9},{9,8},{10,11... | collective-permute-start | bytes 294920 | tf_op jit(solution)/shard_map/ppermute | solution.py:601
  15.5 3.8 %all-to-all-done = f32[32,1,256]{2,1,0:T(1,128)S(1)} async-done(((f32[32,1,256]{2,1,0:T(1,128)}), f32[32,1,256]{2,1,0:T(1,128)S(1)}, u32[]{:S(2)}, u32[]{:S(2)}) %all-to-all-start) | async-done | bytes 32800 | tf_op jit(solution)/shard_map/all_to_all | solution.py:604
  19.3 0.0 copy-done.2
  19.3 0.0 copy-done
  19.3 0.0 copy-done.3
  19.3 0.8 %shard_map.60 = (f32[8,16,256]{2,1,0:T(8,128)S(1)}, f32[8,16,256]{2,1,0:T(8,128)S(1)}, f32[12,4,256]{2,1,0:T(4,128)S(1)}, f32[12,4,256]{2,1,0:T(4,128)S(1)}, f32...) custom-call(f32[32,256]{1,0:T(8,128)S(1)} %bitcast.13, f32[32,1024]{1,0:T(8,128)S(1)} %copy-done.3, ...), custom_call_target="tpu_custom_call" | custom-call | bytes 5040000 | tf_op jit(solution)/shard_map/pallas_call | solution.py:60
  20.1 0.2 collective-permute-start
  20.3 2.0 %collective-permute-start.1 = (f32[12,4,256]{2,1,0:T(4,128)S(1)}, f32[12,4,256]{2,1,0:T(4,128)S(1)}, u32[]{:S(2)}, u32[]{:S(2)}) collective-permute-start(f32[12,4,256]{2,1,0:T(4,128)S(1)} %get-tuple-element.47), channel_id=1, source_target_pairs={{0,1},{1,0},{2,3},{3,2},{4,5},{5,4},{6,7},{7,6},{8,9},{9,8},{10,11... | collective-permute-start | bytes 147464 | tf_op jit(solution)/shard_map/ppermute | solution.py:601
  22.3 0.0 collective-permute-start.6
  22.3 0.0 collective-permute-done.3.refs_6_.refs_2_
  22.3 0.7 %collective-permute-start.7 = (f32[14,16,256]{2,1,0:T(8,128)S(1)}, f32[14,16,256]{2,1,0:T(8,128)S(1)}, u32[]{:S(2)}, u32[]{:S(2)}) collective-permute-start(f32[14,16,256]{2,1,0:T(8,128)S(1)} %get-tuple-element.60), channel_id=1, source_target_pairs={{0,8},{1,9},{2,10},{3,11},{4,12},{5,13},{6,14},{7,15},{8,0},{9,1},... | collective-permute-start | bytes 688136 | tf_op jit(solution)/shard_map/ppermute | solution.py:601
  23.1 0.0 collective-permute-done.2.refs_5_.refs_1_
  23.1 0.0 collective-permute-done.refs_2_
  23.1 1.3 %collective-permute-done.1.refs_3_ = f32[12,4,256]{2,1,0:T(4,128)S(1)} collective-permute-done((f32[12,4,256]{2,1,0:T(4,128)S(1)}, f32[12,4,256]{2,1,0:T(4,128)S(1)}, u32[]{:S(2)}, u32[]{:S(2)}) %collective-permute-start.1) | collective-permute-done | bytes 49184 | tf_op jit(solution)/shard_map/ppermute | solution.py:601
  24.4 0.1 shard_map.61
  24.5 2.2 %collective-permute-start.4 = (f32[27,8,256]{2,1,0:T(8,128)S(1)}, f32[27,8,256]{2,1,0:T(8,128)S(1)}, u32[]{:S(2)}, u32[]{:S(2)}) collective-permute-start(f32[27,8,256]{2,1,0:T(8,128)S(1)} %get-tuple-element.52), channel_id=1, source_target_pairs={{0,1},{1,0},{2,3},{3,2},{4,5},{5,4},{6,7},{7,6},{8,16},{9,17},{10,... | collective-permute-start | bytes 663560 | tf_op jit(solution)/shard_map/ppermute | solution.py:600
  26.8 0.0 collective-permute-start.5
  26.8 0.1 shard_map.62
  26.9 1.4 %collective-permute-done.6.refs_11_ = f32[14,16,256]{2,1,0:T(8,128)S(1)} collective-permute-done((f32[14,16,256]{2,1,0:T(8,128)S(1)}, f32[14,16,256]{2,1,0:T(8,128)S(1)}, u32[]{:S(2)}, u32[]{:S(2)}) %collective-permute-start.6) | collective-permute-done | bytes 229408 | tf_op jit(solution)/shard_map/ppermute | solution.py:600
  28.3 0.0 collective-permute-done.7.refs_12_
  28.3 2.4 %collective-permute-done.4.refs_3_ = f32[27,8,256]{2,1,0:T(8,128)S(1)} collective-permute-done((f32[27,8,256]{2,1,0:T(8,128)S(1)}, f32[27,8,256]{2,1,0:T(8,128)S(1)}, u32[]{:S(2)}, u32[]{:S(2)}) %collective-permute-start.4) | collective-permute-done | bytes 221216 | tf_op jit(solution)/shard_map/ppermute | solution.py:600
  30.7 0.0 collective-permute-done.5.refs_4_
  30.7 2.4 %shard_map.63 = (f32[8,16,256]{2,1,0:T(8,128)S(1)}, f32[8,16,256]{2,1,0:T(8,128)S(1)}, f32[32,256]{1,0:T(8,128)S(1)}, f32[8,24,256]{2,1,0:T(8,128)S(1)}, f32[8,2...) custom-call(f32[8,24,256]{2,1,0:T(8,128)S(1)} %get-tuple-element.49.refs_0_, ...), custom_call_target="tpu_custom_call" | custom-call | bytes 10800000 | tf_op jit(solution)/shard_map/pallas_call | solution.py:60
  33.1 0.1 copy.6
  33.2 9.4 %all_to_all.30 = f32[32,1,256]{2,1,0:T(1,128)S(1)} all-to-all(f32[32,1,256]{2,1,0:T(1,128)S(1)} %copy.6), channel_id=1, replica_groups=mesh['gx'=4,'gy'=8] {'gx','gy'}, dimensions={0} | all-to-all | bytes 65536 | tf_op jit(solution)/shard_map/all_to_all | solution.py:604
  42.6 1.0 %shard_map.64 = (f32[8,16,256]{2,1,0:T(8,128)S(1)}, f32[8,16,256]{2,1,0:T(8,128)S(1)}, f32[8,16,256]{2,1,0:T(8,128)S(1)}, f32[8,128]{1,0:T(8,128)S(1)}, f32[12,4...) custom-call(f32[32,256]{1,0:T(8,128)S(1)} %bitcast.14, ...), custom_call_target="tpu_custom_call" | custom-call | bytes 5040000 | tf_op jit(solution)/shard_map/pallas_call | solution.py:60
  43.6 0.2 collective-permute-start.8
  43.7 1.8 %collective-permute-start.9 = (f32[12,4,256]{2,1,0:T(4,128)S(1)}, f32[12,4,256]{2,1,0:T(4,128)S(1)}, u32[]{:S(2)}, u32[]{:S(2)}) collective-permute-start(f32[12,4,256]{2,1,0:T(4,128)S(1)} %get-tuple-element.66), channel_id=1, source_target_pairs={{0,1},{1,0},{2,3},{3,2},{4,5},{5,4},{6,7},{7,6},{8,9},{9,8},{10,11... | collective-permute-start | bytes 147464 | tf_op jit(solution)/shard_map/ppermute | solution.py:601
  45.6 0.2 collective-permute-start.12
  45.8 0.5 collective-permute-start.13
  46.3 0.0 collective-permute-done.8.refs_2_
  46.3 1.5 %collective-permute-done.9.refs_3_ = f32[12,4,256]{2,1,0:T(4,128)S(1)} collective-permute-done((f32[12,4,256]{2,1,0:T(4,128)S(1)}, f32[12,4,256]{2,1,0:T(4,128)S(1)}, u32[]{:S(2)}, u32[]{:S(2)}) %collective-permute-start.9) | collective-permute-done | bytes 49184 | tf_op jit(solution)/shard_map/ppermute | solution.py:601
  47.9 0.1 shard_map.65
  48.0 2.2 %collective-permute-start.10 = (f32[6,8,256]{2,1,0:T(8,128)S(1)}, f32[6,8,256]{2,1,0:T(8,128)S(1)}, u32[]{:S(2)}, u32[]{:S(2)}) collective-permute-start(f32[6,8,256]{2,1,0:T(8,128)S(1)} %get-tuple-element.70), channel_id=1, source_target_pairs={{0,1},{1,0},{2,3},{3,2},{4,5},{5,4},{6,7},{7,6},{8,16},{9,17},{10,... | collective-permute-start | bytes 147464 | tf_op jit(solution)/shard_map/ppermute | solution.py:600
  50.2 0.0 collective-permute-start.11
  50.2 0.0 collective-permute-done.12.refs_11_
  50.2 0.0 collective-permute-done.13.refs_12_
  50.2 2.1 %collective-permute-done.10.refs_3_ = f32[6,8,256]{2,1,0:T(8,128)S(1)} collective-permute-done((f32[6,8,256]{2,1,0:T(8,128)S(1)}, f32[6,8,256]{2,1,0:T(8,128)S(1)}, u32[]{:S(2)}, u32[]{:S(2)}) %collective-permute-start.10) | collective-permute-done | bytes 49184 | tf_op jit(solution)/shard_map/ppermute | solution.py:600
  52.3 0.0 collective-permute-done.11.refs_4_
  52.3 1.8 %shard_map.66 = (f32[8,16,256]{2,1,0:T(8,128)S(1)}, f32[8,16,256]{2,1,0:T(8,128)S(1)}, f32[32,256]{1,0:T(8,128)S(1)}) custom-call(f32[8,24,256]{2,1,0:T(8,128)S(1)} %get-tuple-element.67.refs_0_, f32[2,24,256]{2,1,0:T(8,128)S(1)} %get-tuple-element.68.refs_1_, f32[2,8,256]{2,1,0:T(8,128)S(1)} %get-tuple-element.69.refs_2_, ...), custom_call_target="tpu_custom_call" | custom-call | bytes 9000000 | tf_op jit(solution)/shard_map/pallas_call | solution.py:60
  54.0 0.1 copy.7
  54.1 9.4 %all_to_all.31 = f32[32,1,256]{2,1,0:T(1,128)S(1)} all-to-all(f32[32,1,256]{2,1,0:T(1,128)S(1)} %copy.7), channel_id=1, replica_groups=mesh['gx'=4,'gy'=8] {'gx','gy'}, dimensions={0} | all-to-all | bytes 65536 | tf_op jit(solution)/shard_map/all_to_all | solution.py:604
  63.5 0.8 %shard_map.67 = (f32[8,16,256]{2,1,0:T(8,128)}, f32[8,16,256]{2,1,0:T(8,128)}) custom-call(f32[32,256]{1,0:T(8,128)S(1)} %bitcast.16, f32[8,128]{1,0:T(8,128)S(1)} %get-tuple-element.80.refs_1_, f32[8,16,256]{2,1,0:T(8,128)S(1)} %get-tuple-element.81.refs_2_, f32[8,16,256]{2,1,0:T(8,128)S(1)} %get-tuple-element.82.refs_3_, ...), custom_call_target="tpu_custom_call" | custom-call | bytes 5040000 | tf_op jit(solution)/shard_map/pallas_call | solution.py:60
  (6 shorter events, 0.0 us)
Async XLA Ops:
  0.6 18.6 %copy-start.2 = (f32[8,16,256]{2,1,0:T(8,128)S(1)}, f32[8,16,256]{2,1,0:T(8,128)}, u32[]{:S(2)}) copy-start(f32[8,16,256]{2,1,0:T(8,128)} %refs_4_.6) | copy-start | bytes 393220
  0.6 18.6 %copy-start = (bf16[32,8,16,256]{3,2,1,0:T(8,128)(2,1)S(1)}, bf16[32,8,16,256]{3,2,1,0:T(8,128)(2,1)}, u32[]{:S(2)}) copy-start(bf16[32,8,16,256]{3,2,1,0:T(8,128)(2,1)} %refs_3_.3) | copy-start | bytes 6291460
  0.7 11.5 %copy-start.1 = (f32[3,8,16,256]{3,2,1,0:T(8,128)S(1)}, f32[3,8,16,256]{3,2,1,0:T(8,128)}, u32[]{:S(2)}) copy-start(f32[3,8,16,256]{3,2,1,0:T(8,128)} %refs_4_.7) | copy-start | bytes 1179652
  0.7 18.6 %copy-start.3 = (f32[32,1024]{1,0:T(8,128)S(1)}, f32[32,1024]{1,0:T(8,128)}, u32[]{:S(2)}) copy-start(f32[32,1024]{1,0:T(8,128)} %refs_2_.3) | copy-start | bytes 393220
  4.8 14.5 %all-to-all-start = ((f32[32,1,256]{2,1,0:T(1,128)}), f32[32,1,256]{2,1,0:T(1,128)S(1)}, u32[]{:S(2)}, u32[]{:S(2)}) async-start(f32[32,1,256]{2,1,0:T(1,128)} %broadcast_in_dim.31), calls=%async_computation | async-start | bytes 65536 | tf_op jit(solution)/shard_map/all_to_all | solution.py:604
  12.2 10.2 %collective-permute-start.3 = (f32[3,8,4,256]{3,2,1,0:T(4,128)S(1)}, f32[3,8,4,256]{3,2,1,0:T(4,128)S(1)}, u32[]{:S(2)}, u32[]{:S(2)}) collective-permute-start(f32[3,8,4,256]{3,2,1,0:T(4,128)S(1)} %get-tuple-element.48), channel_id=1, source_target_pairs={{0,8},{1,2},{2,1},{3,4},{4,3},{5,6},{6,5},{7,15},{8,0},{9,10},{10,... | collective-permute-start | bytes 294920 | tf_op jit(solution)/shard_map/ppermute | solution.py:600
  12.5 10.6 %collective-permute-start.2 = (f32[3,8,4,256]{3,2,1,0:T(4,128)S(1)}, f32[3,8,4,256]{3,2,1,0:T(4,128)S(1)}, u32[]{:S(2)}, u32[]{:S(2)}) collective-permute-start(f32[3,8,4,256]{3,2,1,0:T(4,128)S(1)} %get-tuple-element.43.refs_5_), channel_id=1, source_target_pairs={{0,1},{1,0},{2,3},{3,2},{4,5},{5,4},{6,7},{7,6},{8,9},{9,8},{10,11... | collective-permute-start | bytes 294920 | tf_op jit(solution)/shard_map/ppermute | solution.py:601
  20.1 2.9 %collective-permute-start = (f32[12,4,256]{2,1,0:T(4,128)S(1)}, f32[12,4,256]{2,1,0:T(4,128)S(1)}, u32[]{:S(2)}, u32[]{:S(2)}) collective-permute-start(f32[12,4,256]{2,1,0:T(4,128)S(1)} %get-tuple-element.46), channel_id=1, source_target_pairs={{0,8},{1,2},{2,1},{3,4},{4,3},{5,6},{6,5},{7,15},{8,0},{9,10},{10,... | collective-permute-start | bytes 147464 | tf_op jit(solution)/shard_map/ppermute | solution.py:600
  20.3 4.1 %collective-permute-start.1 = (f32[12,4,256]{2,1,0:T(4,128)S(1)}, f32[12,4,256]{2,1,0:T(4,128)S(1)}, u32[]{:S(2)}, u32[]{:S(2)}) collective-permute-start(f32[12,4,256]{2,1,0:T(4,128)S(1)} %get-tuple-element.47), channel_id=1, source_target_pairs={{0,1},{1,0},{2,3},{3,2},{4,5},{5,4},{6,7},{7,6},{8,9},{9,8},{10,11... | collective-permute-start | bytes 147464 | tf_op jit(solution)/shard_map/ppermute | solution.py:601
  22.3 6.0 %collective-permute-start.6 = (f32[14,16,256]{2,1,0:T(8,128)S(1)}, f32[14,16,256]{2,1,0:T(8,128)S(1)}, u32[]{:S(2)}, u32[]{:S(2)}) collective-permute-start(f32[14,16,256]{2,1,0:T(8,128)S(1)} %get-tuple-element.59), channel_id=1, source_target_pairs={{0,1},{1,0},{2,3},{3,2},{4,5},{5,4},{6,7},{7,6},{8,16},{9,17},{10,... | collective-permute-start | bytes 688136 | tf_op jit(solution)/shard_map/ppermute | solution.py:600
  22.3 6.0 %collective-permute-start.7 = (f32[14,16,256]{2,1,0:T(8,128)S(1)}, f32[14,16,256]{2,1,0:T(8,128)S(1)}, u32[]{:S(2)}, u32[]{:S(2)}) collective-permute-start(f32[14,16,256]{2,1,0:T(8,128)S(1)} %get-tuple-element.60), channel_id=1, source_target_pairs={{0,8},{1,9},{2,10},{3,11},{4,12},{5,13},{6,14},{7,15},{8,0},{9,1},... | collective-permute-start | bytes 688136 | tf_op jit(solution)/shard_map/ppermute | solution.py:601
  24.5 6.2 %collective-permute-start.4 = (f32[27,8,256]{2,1,0:T(8,128)S(1)}, f32[27,8,256]{2,1,0:T(8,128)S(1)}, u32[]{:S(2)}, u32[]{:S(2)}) collective-permute-start(f32[27,8,256]{2,1,0:T(8,128)S(1)} %get-tuple-element.52), channel_id=1, source_target_pairs={{0,1},{1,0},{2,3},{3,2},{4,5},{5,4},{6,7},{7,6},{8,16},{9,17},{10,... | collective-permute-start | bytes 663560 | tf_op jit(solution)/shard_map/ppermute | solution.py:600
  26.8 3.9 %collective-permute-start.5 = (f32[27,8,256]{2,1,0:T(8,128)S(1)}, f32[27,8,256]{2,1,0:T(8,128)S(1)}, u32[]{:S(2)}, u32[]{:S(2)}) collective-permute-start(f32[27,8,256]{2,1,0:T(8,128)S(1)} %get-tuple-element.53), channel_id=1, source_target_pairs={{0,8},{1,9},{2,10},{3,11},{4,12},{5,13},{6,14},{7,15},{8,0},{9,1},... | collective-permute-start | bytes 663560 | tf_op jit(solution)/shard_map/ppermute | solution.py:601
  43.6 2.8 %collective-permute-start.8 = (f32[12,4,256]{2,1,0:T(4,128)S(1)}, f32[12,4,256]{2,1,0:T(4,128)S(1)}, u32[]{:S(2)}, u32[]{:S(2)}) collective-permute-start(f32[12,4,256]{2,1,0:T(4,128)S(1)} %get-tuple-element.65), channel_id=1, source_target_pairs={{0,8},{1,2},{2,1},{3,4},{4,3},{5,6},{6,5},{7,15},{8,0},{9,10},{10,... | collective-permute-start | bytes 147464 | tf_op jit(solution)/shard_map/ppermute | solution.py:600
  43.7 4.1 %collective-permute-start.9 = (f32[12,4,256]{2,1,0:T(4,128)S(1)}, f32[12,4,256]{2,1,0:T(4,128)S(1)}, u32[]{:S(2)}, u32[]{:S(2)}) collective-permute-start(f32[12,4,256]{2,1,0:T(4,128)S(1)} %get-tuple-element.66), channel_id=1, source_target_pairs={{0,1},{1,0},{2,3},{3,2},{4,5},{5,4},{6,7},{7,6},{8,9},{9,8},{10,11... | collective-permute-start | bytes 147464 | tf_op jit(solution)/shard_map/ppermute | solution.py:601
  45.6 4.6 %collective-permute-start.12 = (f32[5,16,256]{2,1,0:T(8,128)S(1)}, f32[5,16,256]{2,1,0:T(8,128)S(1)}, u32[]{:S(2)}, u32[]{:S(2)}) collective-permute-start(f32[5,16,256]{2,1,0:T(8,128)S(1)} %get-tuple-element.72), channel_id=1, source_target_pairs={{0,1},{1,0},{2,3},{3,2},{4,5},{5,4},{6,7},{7,6},{8,16},{9,17},{10,... | collective-permute-start | bytes 245768 | tf_op jit(solution)/shard_map/ppermute | solution.py:600
  45.8 4.4 %collective-permute-start.13 = (f32[5,16,256]{2,1,0:T(8,128)S(1)}, f32[5,16,256]{2,1,0:T(8,128)S(1)}, u32[]{:S(2)}, u32[]{:S(2)}) collective-permute-start(f32[5,16,256]{2,1,0:T(8,128)S(1)} %get-tuple-element.73), channel_id=1, source_target_pairs={{0,8},{1,9},{2,10},{3,11},{4,12},{5,13},{6,14},{7,15},{8,0},{9,1},... | collective-permute-start | bytes 245768 | tf_op jit(solution)/shard_map/ppermute | solution.py:601
  48.0 4.3 %collective-permute-start.10 = (f32[6,8,256]{2,1,0:T(8,128)S(1)}, f32[6,8,256]{2,1,0:T(8,128)S(1)}, u32[]{:S(2)}, u32[]{:S(2)}) collective-permute-start(f32[6,8,256]{2,1,0:T(8,128)S(1)} %get-tuple-element.70), channel_id=1, source_target_pairs={{0,1},{1,0},{2,3},{3,2},{4,5},{5,4},{6,7},{7,6},{8,16},{9,17},{10,... | collective-permute-start | bytes 147464 | tf_op jit(solution)/shard_map/ppermute | solution.py:600
  50.2 2.1 %collective-permute-start.11 = (f32[6,8,256]{2,1,0:T(8,128)S(1)}, f32[6,8,256]{2,1,0:T(8,128)S(1)}, u32[]{:S(2)}, u32[]{:S(2)}) collective-permute-start(f32[6,8,256]{2,1,0:T(8,128)S(1)} %get-tuple-element.71), channel_id=1, source_target_pairs={{0,8},{1,9},{2,10},{3,11},{4,12},{5,13},{6,14},{7,15},{8,0},{9,1},... | collective-permute-start | bytes 147464 | tf_op jit(solution)/shard_map/ppermute | solution.py:601

commit v6 on v5

--- a/solution.py
+++ b/solution.py
@@ -53,32 +53,28 @@
     )
 
 
-def call(vectors, body, outs, scratch, *args, micros):
+def call(vectors, body, outs, scratch, *args, micros, streamed=False):
     def kernel(*refs):
         body(place_flags(vectors), *refs)
 
     return pl.pallas_call(
         kernel,
-        out_shape=[jax.ShapeDtypeStruct(shape, F32) for shape in outs],
-        in_specs=[pl.BlockSpec(memory_space=pltpu.VMEM)] * len(args),
+        out_shape=[jax.ShapeDtypeStruct(kind, F32) if isinstance(kind, tuple) else kind for kind in outs],
+        in_specs=[pl.BlockSpec(memory_space=pltpu.HBM if streamed else pltpu.VMEM)] * len(args),
         out_specs=[pl.BlockSpec(memory_space=pltpu.VMEM)] * len(outs),
-        scratch_shapes=[pltpu.VMEM(shape, F32) for shape in scratch],
+        scratch_shapes=[pltpu.VMEM(kind, F32) if isinstance(kind, tuple) else kind for kind in scratch],
         compiler_params=pltpu.CompilerParams(vmem_limit_bytes=24 * 1024 * 1024),
         cost_estimate=pl.CostEstimate(flops=0, bytes_accessed=int(micros * 3.6e6), transcendentals=0),
     )(*args)
 
 
-def z_before(plane):
-    return pltpu.roll(plane, 1, 1)
-
-
-def z_after(plane, keep_last):
-    return jnp.where(keep_last, pltpu.roll(plane, plane.shape[1] - 1, 1), 0.0)
-
-
-def lane_masks(shape):
-    lanes = lax.broadcasted_iota(jnp.int32, shape, 1)
-    return lanes > 0, lanes < shape[1] - 1
+def shift_z(plane, ahead):
+    width = plane.shape[1]
+    lane = lax.broadcasted_iota(jnp.int32, (plane.shape[0], LANES), 1)
+    edge = LANES - 1 if ahead else 0
+    turned = [pltpu.roll(plane[:, i : i + LANES], LANES - 1 if ahead else 1, 1) for i in range(0, width, LANES)]
+    beside = turned[1:] + [0.0] if ahead else [0.0] + turned[:-1]
+    return jnp.concatenate([jnp.where(lane == edge, far, near) for near, far in zip(turned, beside)], axis=1)
 
 
 def restrict(vectors, field, sums, flags, send, copies=()):
@@ -107,27 +103,26 @@
     row = lax.dot_general(
         jnp.ones((8, LANES), F32), stage[...], (((1,), (1,)), ((), ())), precision=HIGHEST, preferred_element_type=F32
     )
-    for k in range(0, out.shape[0], 8):
-        out[k : k + 8, :] = row
-
-
-def gathered(received):
-    count = received.shape[0]
-    return received[:, :LANES], jnp.sum(received[:, LANES:], axis=0, keepdims=True)
-
-
-def solve(coarse, inverse, vectors):
-    count = coarse.shape[0]
+    for k in range(out.shape[0]):
+        out[k] = row[0:1]
+
+
+def gathered(received, vectors):
     share = LANES // vectors.shape[0]
-    groups = count // share
-    pick = (
-        lax.broadcasted_iota(jnp.int32, (groups, count), 1) // share
-        == lax.broadcasted_iota(jnp.int32, (groups, count), 0)
-    ).astype(F32)
-    packed = jnp.dot(pick, coarse, precision=HIGHEST, preferred_element_type=F32)
-    total = inverse[:, :LANES] * packed[0:1]
-    for k in range(1, groups):
-        total = total + inverse[:, k * LANES : (k + 1) * LANES] * packed[k : k + 1]
+    return [
+        functools.reduce(jnp.add, [received[k + i, :, :LANES] for i in range(share)])
+        for k in range(0, received.shape[0], share)
+    ]
+
+
+def summed(received):
+    return functools.reduce(jnp.add, [received[k, :, LANES:] for k in range(received.shape[0])])
+
+
+def solve(coarse, inverse):
+    total = inverse[:, :LANES] * coarse[0]
+    for k in range(1, len(coarse)):
+        total = total + inverse[:, k * LANES : (k + 1) * LANES] * coarse[k]
     return jnp.sum(total, axis=1, keepdims=True).astype(jnp.bfloat16).astype(F32)
 
 
@@ -144,7 +139,6 @@
 
 def subtract_own(field, corr, velocity, out):
     size_x, size_y, size_z = corr.shape
-    keep_first, keep_last = lane_masks((size_y, size_z))
     rows = lax.broadcasted_iota(jnp.int32, (size_y, size_z), 0)
     for x in range(size_x):
         v0, v1, v2 = velocity[0, x], velocity[1, x], velocity[2, x]
@@ -156,7 +150,7 @@
             image = image - (1.0 + v0) * corr[x - 1]
         image = image - jnp.where(rows < size_y - 1, pltpu.roll(here, size_y - 1, 0), 0.0)
         image = image - (1.0 + v1) * jnp.where(rows > 0, pltpu.roll(here, 1, 0), 0.0)
-        image = image - z_after(here, keep_last) - (1.0 + v2) * jnp.where(keep_first, z_before(here), 0.0)
+        image = image - shift_z(here, True) - (1.0 + v2) * shift_z(here, False)
         out[x] = field[x] - image
 
 
@@ -184,6 +178,24 @@
         write(odd_out, True)
 
 
+def first_kernel(
+    flags, field, vectors, velocity, inverse, out, held_field, held_vectors, held_velocity, held_inverse, stage, sems
+):
+    parts = sems.shape[0] - 3
+    step = vectors.shape[0] // parts
+    chunks = [pl.ds(part * step, step) for part in range(parts)]
+    pairs = [(field, held_field)] + [(vectors.at[chunk], held_vectors.at[chunk]) for chunk in chunks]
+    pairs += [(velocity, held_velocity), (inverse, held_inverse)]
+    copies = [pltpu.make_async_copy(here, there, sems.at[k]) for k, (here, there) in enumerate(pairs)]
+    for copy in copies:
+        copy.start()
+    copies[0].wait()
+    rounded = [held_field[x].astype(jnp.bfloat16).astype(F32) for x in range(field.shape[0])]
+    restrict(held_vectors, rounded, [], flags, (out, stage), copies[1 : 1 + parts])
+    for copy in copies[1 + parts :]:
+        copy.wait()
+
+
 def by_side(odd, use, *pairs):
     evens, odds = [pair[0] for pair in pairs], [pair[1] for pair in pairs]
 
@@ -196,7 +208,7 @@
         use(evens, odds)
 
 
-def velocity_y_kernel(flags, velocity, after, even_out, odd_out):
+def velocity_y_kernel(flags, velocity, even_out, odd_out):
     _, size_x, size_y, _ = velocity.shape
 
     def write_y(out, high):
@@ -224,14 +236,14 @@
     by_parity(flags[ODD_X], write, even_out, odd_out)
 
 
-def coefficients(x, v0, v1, v2, kept, keep_first, outs):
+def coefficients(x, v0, v1, v2, kept, outs):
     inverse, b0, b1, b2 = outs
     total = 6.0 + v0 + v1 + v2
     value = jnp.where(kept, 1.0 / total, 0.0)
     inverse[x] = value
     b0[x] = value * (1.0 + v0)
     b1[x] = value * (1.0 + v1)
-    b2[x] = jnp.where(keep_first, value * (1.0 + v2), 0.0)
+    b2[x] = value * (1.0 + v2)
     return total
 
 
@@ -262,16 +274,14 @@
         place(even_in, odd_in)
 
     kept = rows_in_grid(flags, (rows, size_z))
-    keep_first, _ = lane_masks((rows, size_z))
     for x in range(size_x):
-        diagonal[x] = coefficients(x, wide[0, x], wide[1, x], wide[2, x], kept, keep_first, (inverse, b0, b1, b2))
+        diagonal[x] = coefficients(x, wide[0, x], wide[1, x], wide[2, x], kept, (inverse, b0, b1, b2))
 
 
 def halo_coefficients(flags, early, late, outs, wide):
     size_y, size_z = early[0].shape[1:]
     rows = size_y + 2 * WIDE
     kept = rows_in_grid(flags, (rows, size_z))
-    keep_first, _ = lane_masks((rows, size_z))
 
     def side(start, message, corners, present):
         for k in range(WIDE):
@@ -280,7 +290,7 @@
                 wide[d, 0:WIDE, :] = corners[tile, 0:WIDE, :]
                 wide[d, WIDE : WIDE + size_y, :] = message[1 + EARLY_FIRST + d * WIDE + k]
                 wide[d, WIDE + size_y : rows, :] = corners[tile, WIDE : 2 * WIDE, :]
-            coefficients(start + k, wide[0], wide[1], wide[2], kept & (flags[present] != 0), keep_first, outs)
+            coefficients(start + k, wide[0], wide[1], wide[2], kept & (flags[present] != 0), outs)
 
     by_side(flags[ODD_X], lambda low, high: (side(0, *low, LOW_X), side(WIDE, *high, HIGH_X)), early, late)
 
@@ -300,8 +310,7 @@
 def coarse_kernel(
     flags, received, inverse, vectors, field, velocity, after, corr, rest, even_out, odd_out, even_x, odd_x
 ):
-    coarse, _ = gathered(received)
-    prolong(solve(coarse, inverse, vectors), vectors, corr)
+    prolong(solve(gathered(received, vectors), inverse), vectors, corr)
     subtract_own(field, corr, velocity, rest)
     by_parity(flags[ODD_Y], lambda out, high: write_y_message(out, rest, corr, high), even_out, odd_out)
     write_x_early(flags, EARLY_FIRST, rest, corr, velocity, even_x, odd_x)
@@ -311,14 +320,14 @@
     flags, received, second, inverse, vectors, field, image, velocity, corr, rest, middle, alpha, even_out, odd_out,
     even_x, odd_x
 ):
-    coarse, _ = gathered(received)
-    coarse_image, products = gathered(second)
+    products = summed(second)
     step = jnp.broadcast_to(products[:, 0:1] / products[:, 1:2], alpha.shape)
     alpha[...] = step
     step = step[0:1, 0:1]
     for x in range(field.shape[0]):
         middle[x] = field[x] - step * image[x]
-    prolong(solve(coarse - step * coarse_image, inverse, vectors), vectors, corr)
+    pairs = zip(gathered(received, vectors), gathered(second, vectors))
+    prolong(solve([coarse - step * of_image for coarse, of_image in pairs], inverse), vectors, corr)
     subtract_own(middle, corr, velocity, rest)
     by_parity(flags[ODD_Y], lambda out, high: write_y_message(out, rest, corr, high), even_out, odd_out)
     write_x_early(flags, WIDE, rest, corr, None, even_x, odd_x)
@@ -396,19 +405,19 @@
     by_side(flags[ODD_Y], write_corners, (even_vel, odd_vel))
 
 
-def beside_terms(before, here, after, x, tile, coefs, keep_last):
+def beside_terms(before, here, after, x, tile, coefs):
     inverse, b0, b1, b2 = coefs
     rows = here.shape[0]
-    ahead = pltpu.roll(here, rows - 1, 0) + z_after(here, keep_last)
+    ahead = pltpu.roll(here, rows - 1, 0) + shift_z(here, True)
     if after is not None:
         ahead = ahead + after
-    total = inverse[x, tile] * ahead + b1[x, tile] * pltpu.roll(here, 1, 0) + b2[x, tile] * z_before(here)
+    total = inverse[x, tile] * ahead + b1[x, tile] * pltpu.roll(here, 1, 0) + b2[x, tile] * shift_z(here, False)
     if before is not None:
         total = total + b0[x, tile] * before
     return total
 
 
-def chebyshev(planes, tile, inside, source, left, update, coefs, keep_last, wanted):
+def chebyshev(planes, tile, inside, source, left, update, coefs, wanted):
     sigma = cheb_center / cheb_radius
     rho = 1.0 / sigma
     first, last = planes[0], planes[-1]
@@ -423,8 +432,9 @@
             here = update[sweep - 1, x, tile]
             before = update[sweep - 1, x - 1, tile] if x > first else None
             after = update[sweep - 1, x + 1, tile] if x < last else None
-            remainder = (here if sweep == 1 else left[x, tile]) - here
-            remainder = remainder + beside_terms(before, here, after, x, tile, coefs, keep_last)
+            remainder = beside_terms(before, here, after, x, tile, coefs)
+            if sweep > 1:
+                remainder = remainder + (left[x, tile] - here)
             if rest:
                 left[x, tile] = remainder
             value = rho_next * rho * here + (2.0 * rho_next / cheb_radius) * jnp.where(inside, remainder, 0.0)
@@ -447,7 +457,6 @@
     rows = size_y + 2 * WIDE
     span = size_x + 2 * WIDE
     row = lax.broadcasted_iota(jnp.int32, (rows, size_z), 0)
-    keep_last = lane_masks((rows, size_z))[1]
     has_low_x, has_high_x = flags[LOW_X] != 0, flags[HIGH_X] != 0
     has_low_y, has_high_y = flags[LOW_Y] != 0, flags[HIGH_Y] != 0
     lowest, highest = slice(0, 8), slice(rows - 8, rows)
@@ -501,7 +510,6 @@
             left,
             update,
             coefs,
-            lane_masks(inside.shape)[1],
             wanted,
         )
 
@@ -536,7 +544,7 @@
 
     for k in range(size_x):
         x = WIDE + k
-        terms = beside_terms(whole[k], whole[k + 1], whole[k + 2], x, everything, coefs, keep_last)
+        terms = beside_terms(whole[k], whole[k + 1], whole[k + 2], x, everything, coefs)
         image = diagonal[k] * (whole[k + 1] - terms)
         image_out[k] = pltpu.roll(image, rows - WIDE, 0)[0:size_y]
         field_out[k] = pltpu.roll(whole[k + 1], rows - WIDE, 0)[0:size_y]
@@ -578,7 +586,7 @@
 
 
 def last_kernel(flags, received, alpha, search, smoothed, middle, turned, solution_field, residual):
-    _, sums = gathered(received)
+    sums = summed(received)
     omega = sums[:, 0:1] / sums[:, 1:2]
     step = alpha[0:1, 0:1]
     for x in range(search.shape[0]):
@@ -592,7 +600,6 @@
     count_x, count_y = lax.axis_size("gx"), lax.axis_size("gy")
     count = count_x * count_y
     at_x, at_y = lax.axis_index("gx"), lax.axis_index("gy")
-    flags = place_flags(vectors_count)
     kernel_call = functools.partial(call, vectors_count)
     x_pairs, y_pairs = pair_permutations(count_x, count_y)
 
@@ -601,28 +608,32 @@
         return [lax.ppermute(messages[0], AXES, pairs[0]), odd]
 
     def share(row):
-        return lax.all_to_all(row, AXES, 0, 0, tiled=True)
+        return lax.all_to_all(row, AXES, 0, 0)
 
     rows = size_y + 2 * WIDE
     span = size_x + 2 * WIDE
     block = (size_x, size_y, size_z)
-    row = (count, 2 * LANES)
+    row = pltpu.VMEM((count, 1, 2 * LANES), F32)
     stage = (2 * LANES, LANES)
     y_message = (size_x + size_x // WIDE + 2, WIDE, size_z)
     region = (span, rows, size_z)
     smooth_scratch = [region, region, (CHEB - 1,) + region, (size_x + 2, rows, size_z)]
 
-    rounded = lax.reduce_precision(right_side, 8, 7)
-    partial = lax.optimization_barrier(jnp.sum(deflation.astype(F32) * rounded, axis=(1, 2)))
-    share_count = LANES // vectors_count
-    first_row = jnp.where(jnp.arange(2 * share_count)[:, None] == flags[SLOT], jnp.sum(partial, axis=1)[None, :], 0.0)
-    first_row = jnp.broadcast_to(first_row.reshape(1, 2 * LANES), row)
-
+    chunks = 4
+    arguments = (right_side, deflation, velocity, inverse_rows)
+    first_row, right_side, deflation, velocity, inverse_rows = kernel_call(
+        first_kernel,
+        [row] + [pltpu.VMEM(argument.shape, argument.dtype) for argument in arguments],
+        [stage, pltpu.SemaphoreType.DMA((chunks + 3,))],
+        *[pltpu.with_memory_space_constraint(argument, pltpu.HBM) for argument in arguments],
+        micros=2.0,
+        streamed=True,
+    )
     first = share(first_row)
     faces_y = (3, size_x, WIDE, size_z)
     x_early = (WIDE + 1, size_y, size_z)
     x_early_first = (1 + EARLY_FIRST + 3 * WIDE, size_y, size_z)
-    velocity_y = kernel_call(velocity_y_kernel, [faces_y] * 2, [], velocity, first_row[0, :8], micros=0.01)
+    velocity_y = kernel_call(velocity_y_kernel, [faces_y] * 2, [], velocity, micros=0.01)
     after = velocity_y[0]
     velocity_y = swap(velocity_y, y_pairs)
 

time: 64.6 us -> 62.7 us (0.971)
  other arithmetic: 3.35 us -> 0 us
  Pallas kernels: 7.22 us -> 9.63 us
  local copies, waits for them, and re-layouts: 0.96 us -> 0 us
    pallas_call x9 -> x10, Pallas kernels: 7.22 us -> 9.63 us  [call(): pl.pallas_call(kernel, out_shape=[jax.ShapeDtypeStruct(kind, F32) if isin...]
    reduce_sum x2 -> x0, other arithmetic: 2.17 us -> none  [the longest x1 2.06 us: local(): jnp.sum(deflation.astype(F32) * rounded, axis=(1, 2))]
    reduce_precision x1 -> x0, other arithmetic: 1.09 us -> none  [local(): rounded = lax.reduce_precision(right_side, 8, 7)]
where the time goes in v6:
time: 62.7 us; the launch traced here: 62.5 us
  starting transfers between devices  20.7 us (33%)
  blocking collectives  18.8 us (30%)
  waiting for transfers between devices  12.6 us (20%)
  Pallas kernels  9.63 us (15%)
  between operations  0.73 us (1%)
    all_to_all x2, blocking collectives, share(): return lax.all_to_all(row, AXES, 0, 0)  18.8 us
    pallas_call x10, Pallas kernels, call(): pl.pallas_call(kernel, out_shape=[jax.ShapeDtypeStruct(kind, F32) if isin...  9.63 us
    ppermute x7, starting transfers between devices, swap(): return [lax.ppermute(messages[0], AXES, pairs[0]), odd]  8.04 us
    all_to_all x1, starting transfers between devices, share(): return lax.all_to_all(row, AXES, 0, 0)  7.3 us
    ppermute x7, waiting for transfers between devices, swap(): odd = lax.ppermute(messages[1], AXES, pairs[1])  5.82 us
    ppermute x7, starting transfers between devices, swap(): odd = lax.ppermute(messages[1], AXES, pairs[1])  5.39 us
    all_to_all x1, waiting for transfers between devices, share(): return lax.all_to_all(row, AXES, 0, 0)  3.85 us
    ppermute x7, waiting for transfers between devices, swap(): return [lax.ppermute(messages[0], AXES, pairs[0]), odd]  2.9 us
  transfers between devices with their start and end apart: 15, of which 6 were waited for; matrix products, arithmetic and copies ran while one was open for 0% of the time, Pallas kernels for 2%

profile of v6, /device:TPU:0, one launch (start us, length us, event | category | flops | bytes accessed | tf_op | source)
XLA Modules:
  0.0 62.5 jit_solution(7739268226482877305)
XLA Ops:
  0.6 2.6 %shard_map.59 = (f32[32,1,256]{2,1,0:T(1,128)}, f32[8,16,256]{2,1,0:T(8,128)S(1)}, bf16[32,8,16,256]{3,2,1,0:T(8,128)(2,1)S(1)}, f32[3,8,16,256]{3,2,1,0:T(8,128)S(1)}, f32[32,1024]{1,0:T(8,128)S(1)}) custom-call(f32[8,16,256]{2,1,0:T(8,128)} %refs_0_.1, bf16[32,8,16,256]{3,2,1,0:T(8,128)(2,1)} %refs_1_.1, f32[3,8,16,256]{3,2,1,0:T(8,128)} %refs_2_.1, ...), custom_call_target="tpu_custom_call" | custom-call | bytes 7200000 | tf_op jit(solution)/shard_map/pallas_call | solution.py:60
  3.3 7.3 %all-to-all-start = ((f32[32,1,256]{2,1,0:T(1,128)}), f32[32,1,256]{2,1,0:T(1,128)S(1)}, u32[]{:S(2)}, u32[]{:S(2)}) async-start(f32[32,1,256]{2,1,0:T(1,128)} %get-tuple-element.48), calls=%async_computation | async-start | bytes 65536 | tf_op jit(solution)/shard_map/all_to_all | solution.py:611
  10.6 0.3 collective-permute-start.3
  10.9 3.0 %collective-permute-start.2 = (f32[3,8,4,256]{3,2,1,0:T(4,128)S(1)}, f32[3,8,4,256]{3,2,1,0:T(4,128)S(1)}, u32[]{:S(2)}, u32[]{:S(2)}) collective-permute-start(f32[3,8,4,256]{3,2,1,0:T(4,128)S(1)} %get-tuple-element.53.refs_5_), channel_id=1, source_target_pairs={{0,1},{1,0},{2,3},{3,2},{4,5},{5,4},{6,7},{7,6},{8,9},{9,8},{10,11... | collective-permute-start | bytes 294920 | tf_op jit(solution)/shard_map/ppermute | solution.py:608
  13.9 3.8 %all-to-all-done.refs_0_ = f32[32,1,256]{2,1,0:T(1,128)S(1)} async-done(((f32[32,1,256]{2,1,0:T(1,128)}), f32[32,1,256]{2,1,0:T(1,128)S(1)}, u32[]{:S(2)}, u32[]{:S(2)}) %all-to-all-start) | async-done | bytes 32800 | tf_op jit(solution)/shard_map/all_to_all | solution.py:611
  17.8 0.7 %shard_map.61 = (f32[8,16,256]{2,1,0:T(8,128)S(1)}, f32[8,16,256]{2,1,0:T(8,128)S(1)}, f32[12,4,256]{2,1,0:T(4,128)S(1)}, f32[12,4,256]{2,1,0:T(4,128)S(1)}, f32...) custom-call(f32[32,1,256]{2,1,0:T(1,128)S(1)} %all-to-all-done.refs_0_, ...), custom_call_target="tpu_custom_call" | custom-call | bytes 5040000 | tf_op jit(solution)/shard_map/pallas_call | solution.py:60
  18.5 0.2 collective-permute-start
  18.7 2.0 %collective-permute-start.1 = (f32[12,4,256]{2,1,0:T(4,128)S(1)}, f32[12,4,256]{2,1,0:T(4,128)S(1)}, u32[]{:S(2)}, u32[]{:S(2)}) collective-permute-start(f32[12,4,256]{2,1,0:T(4,128)S(1)} %get-tuple-element.57), channel_id=1, source_target_pairs={{0,1},{1,0},{2,3},{3,2},{4,5},{5,4},{6,7},{7,6},{8,9},{9,8},{10,11... | collective-permute-start | bytes 147464 | tf_op jit(solution)/shard_map/ppermute | solution.py:608
  20.6 0.0 collective-permute-start.6
  20.7 0.0 collective-permute-done.3.refs_6_.refs_2_
  20.7 0.7 %collective-permute-start.7 = (f32[14,16,256]{2,1,0:T(8,128)S(1)}, f32[14,16,256]{2,1,0:T(8,128)S(1)}, u32[]{:S(2)}, u32[]{:S(2)}) collective-permute-start(f32[14,16,256]{2,1,0:T(8,128)S(1)} %get-tuple-element.70), channel_id=1, source_target_pairs={{0,8},{1,9},{2,10},{3,11},{4,12},{5,13},{6,14},{7,15},{8,0},{9,1},... | collective-permute-start | bytes 688136 | tf_op jit(solution)/shard_map/ppermute | solution.py:608
  21.4 0.0 collective-permute-done.2.refs_5_.refs_1_
  21.4 0.0 collective-permute-done.refs_2_
  21.4 1.3 %collective-permute-done.1.refs_3_ = f32[12,4,256]{2,1,0:T(4,128)S(1)} collective-permute-done((f32[12,4,256]{2,1,0:T(4,128)S(1)}, f32[12,4,256]{2,1,0:T(4,128)S(1)}, u32[]{:S(2)}, u32[]{:S(2)}) %collective-permute-start.1) | collective-permute-done | bytes 49184 | tf_op jit(solution)/shard_map/ppermute | solution.py:608
  22.7 0.1 shard_map.62
  22.9 2.2 %collective-permute-start.4 = (f32[27,8,256]{2,1,0:T(8,128)S(1)}, f32[27,8,256]{2,1,0:T(8,128)S(1)}, u32[]{:S(2)}, u32[]{:S(2)}) collective-permute-start(f32[27,8,256]{2,1,0:T(8,128)S(1)} %get-tuple-element.62), channel_id=1, source_target_pairs={{0,1},{1,0},{2,3},{3,2},{4,5},{5,4},{6,7},{7,6},{8,16},{9,17},{10,... | collective-permute-start | bytes 663560 | tf_op jit(solution)/shard_map/ppermute | solution.py:607
  25.1 0.0 collective-permute-start.5
  25.1 0.1 shard_map.63
  25.3 1.4 %collective-permute-done.6.refs_11_ = f32[14,16,256]{2,1,0:T(8,128)S(1)} collective-permute-done((f32[14,16,256]{2,1,0:T(8,128)S(1)}, f32[14,16,256]{2,1,0:T(8,128)S(1)}, u32[]{:S(2)}, u32[]{:S(2)}) %collective-permute-start.6) | collective-permute-done | bytes 229408 | tf_op jit(solution)/shard_map/ppermute | solution.py:607
  26.7 0.0 collective-permute-done.7.refs_12_
  26.7 2.4 %collective-permute-done.4.refs_3_ = f32[27,8,256]{2,1,0:T(8,128)S(1)} collective-permute-done((f32[27,8,256]{2,1,0:T(8,128)S(1)}, f32[27,8,256]{2,1,0:T(8,128)S(1)}, u32[]{:S(2)}, u32[]{:S(2)}) %collective-permute-start.4) | collective-permute-done | bytes 221216 | tf_op jit(solution)/shard_map/ppermute | solution.py:607
  29.0 0.0 collective-permute-done.5.refs_4_
  29.0 2.4 %shard_map.64 = (f32[8,16,256]{2,1,0:T(8,128)S(1)}, f32[8,16,256]{2,1,0:T(8,128)S(1)}, f32[32,1,256]{2,1,0:T(1,128)S(1)}, f32[8,24,256]{2,1,0:T(8,128)S(1)}, f32...) custom-call(f32[8,24,256]{2,1,0:T(8,128)S(1)} %get-tuple-element.59.refs_0_, ...), custom_call_target="tpu_custom_call" | custom-call | bytes 10800000 | tf_op jit(solution)/shard_map/pallas_call | solution.py:60
  31.4 9.4 %all_to_all.15.refs_1_ = f32[32,1,256]{2,1,0:T(1,128)S(1)} all-to-all(f32[32,1,256]{2,1,0:T(1,128)S(1)} %get-tuple-element.71), channel_id=1, replica_groups=mesh['gx'=4,'gy'=8] {'gx','gy'}, dimensions={0} | all-to-all | bytes 65536 | tf_op jit(solution)/shard_map/all_to_all | solution.py:611
  40.8 0.9 %shard_map.65 = (f32[8,16,256]{2,1,0:T(8,128)S(1)}, f32[8,16,256]{2,1,0:T(8,128)S(1)}, f32[8,16,256]{2,1,0:T(8,128)S(1)}, f32[8,128]{1,0:T(8,128)S(1)}, f32[12,4...) custom-call(f32[32,1,256]{2,1,0:T(1,128)S(1)} %all-to-all-done.refs_0_, ...), custom_call_target="tpu_custom_call" | custom-call | bytes 5040000 | tf_op jit(solution)/shard_map/pallas_call | solution.py:60
  41.7 0.2 collective-permute-start.8
  41.9 1.8 %collective-permute-start.9 = (f32[12,4,256]{2,1,0:T(4,128)S(1)}, f32[12,4,256]{2,1,0:T(4,128)S(1)}, u32[]{:S(2)}, u32[]{:S(2)}) collective-permute-start(f32[12,4,256]{2,1,0:T(4,128)S(1)} %get-tuple-element.76), channel_id=1, source_target_pairs={{0,1},{1,0},{2,3},{3,2},{4,5},{5,4},{6,7},{7,6},{8,9},{9,8},{10,11... | collective-permute-start | bytes 147464 | tf_op jit(solution)/shard_map/ppermute | solution.py:608
  43.8 0.2 collective-permute-start.12
  44.0 0.5 collective-permute-start.13
  44.5 0.0 collective-permute-done.8.refs_2_
  44.5 1.5 %collective-permute-done.9.refs_3_ = f32[12,4,256]{2,1,0:T(4,128)S(1)} collective-permute-done((f32[12,4,256]{2,1,0:T(4,128)S(1)}, f32[12,4,256]{2,1,0:T(4,128)S(1)}, u32[]{:S(2)}, u32[]{:S(2)}) %collective-permute-start.9) | collective-permute-done | bytes 49184 | tf_op jit(solution)/shard_map/ppermute | solution.py:608
  46.0 0.1 shard_map.66
  46.1 2.2 %collective-permute-start.10 = (f32[6,8,256]{2,1,0:T(8,128)S(1)}, f32[6,8,256]{2,1,0:T(8,128)S(1)}, u32[]{:S(2)}, u32[]{:S(2)}) collective-permute-start(f32[6,8,256]{2,1,0:T(8,128)S(1)} %get-tuple-element.80), channel_id=1, source_target_pairs={{0,1},{1,0},{2,3},{3,2},{4,5},{5,4},{6,7},{7,6},{8,16},{9,17},{10,... | collective-permute-start | bytes 147464 | tf_op jit(solution)/shard_map/ppermute | solution.py:607
  48.3 0.0 collective-permute-start.11
  48.3 0.0 collective-permute-done.12.refs_11_
  48.3 0.0 collective-permute-done.13.refs_12_
  48.4 2.1 %collective-permute-done.10.refs_3_ = f32[6,8,256]{2,1,0:T(8,128)S(1)} collective-permute-done((f32[6,8,256]{2,1,0:T(8,128)S(1)}, f32[6,8,256]{2,1,0:T(8,128)S(1)}, u32[]{:S(2)}, u32[]{:S(2)}) %collective-permute-start.10) | collective-permute-done | bytes 49184 | tf_op jit(solution)/shard_map/ppermute | solution.py:607
  50.4 0.0 collective-permute-done.11.refs_4_
  50.4 1.8 %shard_map.67 = (f32[8,16,256]{2,1,0:T(8,128)S(1)}, f32[8,16,256]{2,1,0:T(8,128)S(1)}, f32[32,1,256]{2,1,0:T(1,128)S(1)}) custom-call(f32[8,24,256]{2,1,0:T(8,128)S(1)} %get-tuple-element.77.refs_0_, f32[2,24,256]{2,1,0:T(8,128)S(1)} %get-tuple-element.78.refs_1_, f32[2,8,256]{2,1,0:T(8,128)S(1)} %get-tuple-element.79.refs_2_, ...), custom_call_target="tpu_custom_call" | custom-call | bytes 9000000 | tf_op jit(solution)/shard_map/pallas_call | solution.py:60
  52.2 9.4 %all_to_all.16.refs_0_ = f32[32,1,256]{2,1,0:T(1,128)S(1)} all-to-all(f32[32,1,256]{2,1,0:T(1,128)S(1)} %get-tuple-element.89), channel_id=1, replica_groups=mesh['gx'=4,'gy'=8] {'gx','gy'}, dimensions={0} | all-to-all | bytes 65536 | tf_op jit(solution)/shard_map/all_to_all | solution.py:611
  61.6 0.9 %shard_map.68 = (f32[8,16,256]{2,1,0:T(8,128)}, f32[8,16,256]{2,1,0:T(8,128)}) custom-call(f32[32,1,256]{2,1,0:T(1,128)S(1)} %all_to_all.16.refs_0_, f32[8,128]{1,0:T(8,128)S(1)} %get-tuple-element.90.refs_1_, f32[8,16,256]{2,1,0:T(8,128)S(1)} %get-tuple-element.91.refs_2_, f32[8,16,256]{2,1,0:T(8,128)S(1)} %get-tuple-element.92.refs_3_, ...), custom_call_target="tpu_custom_call" | custom-call | bytes 5040000 | tf_op jit(solution)/shard_map/pallas_call | solution.py:60
  (1 shorter events, 0.0 us)
Async XLA Ops:
  3.3 14.5 %all-to-all-start = ((f32[32,1,256]{2,1,0:T(1,128)}), f32[32,1,256]{2,1,0:T(1,128)S(1)}, u32[]{:S(2)}, u32[]{:S(2)}) async-start(f32[32,1,256]{2,1,0:T(1,128)} %get-tuple-element.48), calls=%async_computation | async-start | bytes 65536 | tf_op jit(solution)/shard_map/all_to_all | solution.py:611
  10.6 10.1 %collective-permute-start.3 = (f32[3,8,4,256]{3,2,1,0:T(4,128)S(1)}, f32[3,8,4,256]{3,2,1,0:T(4,128)S(1)}, u32[]{:S(2)}, u32[]{:S(2)}) collective-permute-start(f32[3,8,4,256]{3,2,1,0:T(4,128)S(1)} %get-tuple-element.58), channel_id=1, source_target_pairs={{0,8},{1,2},{2,1},{3,4},{4,3},{5,6},{6,5},{7,15},{8,0},{9,10},{10,... | collective-permute-start | bytes 294920 | tf_op jit(solution)/shard_map/ppermute | solution.py:607
  10.9 10.5 %collective-permute-start.2 = (f32[3,8,4,256]{3,2,1,0:T(4,128)S(1)}, f32[3,8,4,256]{3,2,1,0:T(4,128)S(1)}, u32[]{:S(2)}, u32[]{:S(2)}) collective-permute-start(f32[3,8,4,256]{3,2,1,0:T(4,128)S(1)} %get-tuple-element.53.refs_5_), channel_id=1, source_target_pairs={{0,1},{1,0},{2,3},{3,2},{4,5},{5,4},{6,7},{7,6},{8,9},{9,8},{10,11... | collective-permute-start | bytes 294920 | tf_op jit(solution)/shard_map/ppermute | solution.py:608
  18.5 2.9 %collective-permute-start = (f32[12,4,256]{2,1,0:T(4,128)S(1)}, f32[12,4,256]{2,1,0:T(4,128)S(1)}, u32[]{:S(2)}, u32[]{:S(2)}) collective-permute-start(f32[12,4,256]{2,1,0:T(4,128)S(1)} %get-tuple-element.56), channel_id=1, source_target_pairs={{0,8},{1,2},{2,1},{3,4},{4,3},{5,6},{6,5},{7,15},{8,0},{9,10},{10,... | collective-permute-start | bytes 147464 | tf_op jit(solution)/shard_map/ppermute | solution.py:607
  18.7 4.1 %collective-permute-start.1 = (f32[12,4,256]{2,1,0:T(4,128)S(1)}, f32[12,4,256]{2,1,0:T(4,128)S(1)}, u32[]{:S(2)}, u32[]{:S(2)}) collective-permute-start(f32[12,4,256]{2,1,0:T(4,128)S(1)} %get-tuple-element.57), channel_id=1, source_target_pairs={{0,1},{1,0},{2,3},{3,2},{4,5},{5,4},{6,7},{7,6},{8,9},{9,8},{10,11... | collective-permute-start | bytes 147464 | tf_op jit(solution)/shard_map/ppermute | solution.py:608
  20.6 6.0 %collective-permute-start.6 = (f32[14,16,256]{2,1,0:T(8,128)S(1)}, f32[14,16,256]{2,1,0:T(8,128)S(1)}, u32[]{:S(2)}, u32[]{:S(2)}) collective-permute-start(f32[14,16,256]{2,1,0:T(8,128)S(1)} %get-tuple-element.69), channel_id=1, source_target_pairs={{0,1},{1,0},{2,3},{3,2},{4,5},{5,4},{6,7},{7,6},{8,16},{9,17},{10,... | collective-permute-start | bytes 688136 | tf_op jit(solution)/shard_map/ppermute | solution.py:607
  20.7 6.0 %collective-permute-start.7 = (f32[14,16,256]{2,1,0:T(8,128)S(1)}, f32[14,16,256]{2,1,0:T(8,128)S(1)}, u32[]{:S(2)}, u32[]{:S(2)}) collective-permute-start(f32[14,16,256]{2,1,0:T(8,128)S(1)} %get-tuple-element.70), channel_id=1, source_target_pairs={{0,8},{1,9},{2,10},{3,11},{4,12},{5,13},{6,14},{7,15},{8,0},{9,1},... | collective-permute-start | bytes 688136 | tf_op jit(solution)/shard_map/ppermute | solution.py:608
  22.9 6.2 %collective-permute-start.4 = (f32[27,8,256]{2,1,0:T(8,128)S(1)}, f32[27,8,256]{2,1,0:T(8,128)S(1)}, u32[]{:S(2)}, u32[]{:S(2)}) collective-permute-start(f32[27,8,256]{2,1,0:T(8,128)S(1)} %get-tuple-element.62), channel_id=1, source_target_pairs={{0,1},{1,0},{2,3},{3,2},{4,5},{5,4},{6,7},{7,6},{8,16},{9,17},{10,... | collective-permute-start | bytes 663560 | tf_op jit(solution)/shard_map/ppermute | solution.py:607
  25.1 3.9 %collective-permute-start.5 = (f32[27,8,256]{2,1,0:T(8,128)S(1)}, f32[27,8,256]{2,1,0:T(8,128)S(1)}, u32[]{:S(2)}, u32[]{:S(2)}) collective-permute-start(f32[27,8,256]{2,1,0:T(8,128)S(1)} %get-tuple-element.63), channel_id=1, source_target_pairs={{0,8},{1,9},{2,10},{3,11},{4,12},{5,13},{6,14},{7,15},{8,0},{9,1},... | collective-permute-start | bytes 663560 | tf_op jit(solution)/shard_map/ppermute | solution.py:608
  41.7 2.8 %collective-permute-start.8 = (f32[12,4,256]{2,1,0:T(4,128)S(1)}, f32[12,4,256]{2,1,0:T(4,128)S(1)}, u32[]{:S(2)}, u32[]{:S(2)}) collective-permute-start(f32[12,4,256]{2,1,0:T(4,128)S(1)} %get-tuple-element.75), channel_id=1, source_target_pairs={{0,8},{1,2},{2,1},{3,4},{4,3},{5,6},{6,5},{7,15},{8,0},{9,10},{10,... | collective-permute-start | bytes 147464 | tf_op jit(solution)/shard_map/ppermute | solution.py:607
  41.9 4.1 %collective-permute-start.9 = (f32[12,4,256]{2,1,0:T(4,128)S(1)}, f32[12,4,256]{2,1,0:T(4,128)S(1)}, u32[]{:S(2)}, u32[]{:S(2)}) collective-permute-start(f32[12,4,256]{2,1,0:T(4,128)S(1)} %get-tuple-element.76), channel_id=1, source_target_pairs={{0,1},{1,0},{2,3},{3,2},{4,5},{5,4},{6,7},{7,6},{8,9},{9,8},{10,11... | collective-permute-start | bytes 147464 | tf_op jit(solution)/shard_map/ppermute | solution.py:608
  43.8 4.6 %collective-permute-start.12 = (f32[5,16,256]{2,1,0:T(8,128)S(1)}, f32[5,16,256]{2,1,0:T(8,128)S(1)}, u32[]{:S(2)}, u32[]{:S(2)}) collective-permute-start(f32[5,16,256]{2,1,0:T(8,128)S(1)} %get-tuple-element.82), channel_id=1, source_target_pairs={{0,1},{1,0},{2,3},{3,2},{4,5},{5,4},{6,7},{7,6},{8,16},{9,17},{10,... | collective-permute-start | bytes 245768 | tf_op jit(solution)/shard_map/ppermute | solution.py:607
  44.0 4.4 %collective-permute-start.13 = (f32[5,16,256]{2,1,0:T(8,128)S(1)}, f32[5,16,256]{2,1,0:T(8,128)S(1)}, u32[]{:S(2)}, u32[]{:S(2)}) collective-permute-start(f32[5,16,256]{2,1,0:T(8,128)S(1)} %get-tuple-element.83), channel_id=1, source_target_pairs={{0,8},{1,9},{2,10},{3,11},{4,12},{5,13},{6,14},{7,15},{8,0},{9,1},... | collective-permute-start | bytes 245768 | tf_op jit(solution)/shard_map/ppermute | solution.py:608
  46.1 4.3 %collective-permute-start.10 = (f32[6,8,256]{2,1,0:T(8,128)S(1)}, f32[6,8,256]{2,1,0:T(8,128)S(1)}, u32[]{:S(2)}, u32[]{:S(2)}) collective-permute-start(f32[6,8,256]{2,1,0:T(8,128)S(1)} %get-tuple-element.80), channel_id=1, source_target_pairs={{0,1},{1,0},{2,3},{3,2},{4,5},{5,4},{6,7},{7,6},{8,16},{9,17},{10,... | collective-permute-start | bytes 147464 | tf_op jit(solution)/shard_map/ppermute | solution.py:607
  48.3 2.1 %collective-permute-start.11 = (f32[6,8,256]{2,1,0:T(8,128)S(1)}, f32[6,8,256]{2,1,0:T(8,128)S(1)}, u32[]{:S(2)}, u32[]{:S(2)}) collective-permute-start(f32[6,8,256]{2,1,0:T(8,128)S(1)} %get-tuple-element.81), channel_id=1, source_target_pairs={{0,8},{1,9},{2,10},{3,11},{4,12},{5,13},{6,14},{7,15},{8,0},{9,1},... | collective-permute-start | bytes 147464 | tf_op jit(solution)/shard_map/ppermute | solution.py:608

commit v7 on v6

--- a/solution.py
+++ b/solution.py
@@ -10,8 +10,7 @@
 DEPTH = 2
 CHEB = 4
 WIDE = 4
-EARLY_FIRST = 1
-SPARE = 3
+EARLY_FIRST = 0
 LANES = 128
 AXES = ("gx", "gy")
 F32 = jnp.float32
@@ -476,7 +475,7 @@
             if k < early_planes:
                 middle = lambda row_: message[1 + k, row_ : row_ + 8, :]
             else:
-                tile = ends.shape[0] - SPARE - (WIDE - k) * (size_y // 8)
+                tile = ends.shape[0] - (WIDE - k) * (size_y // 8)
                 middle = lambda row_: ends[tile + row_ // 8]
             put(source, x, middle, ends.at[k])
             source[x] = inverse[x] * source[x]
@@ -572,17 +571,19 @@
 
 def smoothed_kernel(
     flags, wide, sides, past, odd_late, even_late, diagonal, own0, own1, own2, own3, corr, odd_early, even_early, halo0,
-    halo1, halo2, halo3, middle, smoothed, turned, out, stage, *scratch
+    halo1, halo2, halo3, middle, smoothed, turned, out, *scratch
 ):
     early, late = (even_early, odd_early), (even_late, odd_late)
     coefs = [Region(*pair) for pair in zip((own0, own1, own2, own3), (halo0, halo1, halo2, halo3))]
     smooth(flags, WIDE, wide, sides, past, early, late, diagonal, coefs, corr, smoothed, turned, scratch)
-    stage[...] = jnp.zeros_like(stage)
+    lane = lax.broadcasted_iota(jnp.int32, (1, LANES), 1)
+    sums = jnp.zeros((1, LANES), F32)
     for k, total in enumerate((dot_planes(turned, middle), dot_planes(turned, turned))):
-        total = jnp.sum(total, axis=0, keepdims=True)
-        parts = [total[:, i : i + LANES] for i in range(0, total.shape[1], LANES)]
-        stage[LANES + k : LANES + k + 1, :] = functools.reduce(jnp.add, parts)
-    write_row(stage, out)
+        total = jnp.sum(jnp.sum(total, axis=0, keepdims=True), axis=1, keepdims=True)
+        sums = jnp.where(lane == k, total, sums)
+    row = jnp.concatenate([jnp.zeros((1, LANES), F32), sums], axis=1)
+    for k in range(out.shape[0]):
+        out[k] = row
 
 
 def last_kernel(flags, received, alpha, search, smoothed, middle, turned, solution_field, residual):
@@ -619,7 +620,7 @@
     region = (span, rows, size_z)
     smooth_scratch = [region, region, (CHEB - 1,) + region, (size_x + 2, rows, size_z)]
 
-    chunks = 4
+    chunks = 8
     arguments = (right_side, deflation, velocity, inverse_rows)
     first_row, right_side, deflation, velocity, inverse_rows = kernel_call(
         first_kernel,
@@ -641,7 +642,7 @@
 
     def exchange(corr, rest, messages, corners, early_planes):
         tiles = WIDE + 2 + (3 * WIDE if corners else 0) + (WIDE - early_planes) * (size_y // 8)
-        message = (tiles + (SPARE if corners else 0), 2 * WIDE, size_z)
+        message = (tiles, 2 * WIDE, size_z)
         y_messages, early = swap(messages[:2], y_pairs), swap(messages[2:], x_pairs)
         *own, even, odd = kernel_call(
             functools.partial(extend_kernel, corners=corners, early_planes=early_planes),
@@ -702,7 +703,7 @@
     smoothed, turned, third_row = kernel_call(
         smoothed_kernel,
         [block, block, row],
-        [stage] + smooth_scratch,
+        smooth_scratch,
         *exchange(corr, rest, messages, False, WIDE),
         *halo_coefs,
         middle,

time: 62.7 us -> 62.5 us (level)
  no operation moved by 1% of the time
where the time goes in v7:
time: 62.5 us; the launch traced here: 62.3 us
  starting transfers between devices  20.7 us (33%)
  blocking collectives  18.8 us (30%)
  waiting for transfers between devices  12.5 us (20%)
  Pallas kernels  9.52 us (15%)
  between operations  0.73 us (1%)
    all_to_all x2, blocking collectives, share(): return lax.all_to_all(row, AXES, 0, 0)  18.8 us
    pallas_call x10, Pallas kernels, call(): pl.pallas_call(kernel, out_shape=[jax.ShapeDtypeStruct(kind, F32) if isin...  9.52 us
    ppermute x7, starting transfers between devices, swap(): return [lax.ppermute(messages[0], AXES, pairs[0]), odd]  8.04 us
    all_to_all x1, starting transfers between devices, share(): return lax.all_to_all(row, AXES, 0, 0)  7.3 us
    ppermute x7, waiting for transfers between devices, swap(): odd = lax.ppermute(messages[1], AXES, pairs[1])  5.73 us
    ppermute x7, starting transfers between devices, swap(): odd = lax.ppermute(messages[1], AXES, pairs[1])  5.39 us
    all_to_all x1, waiting for transfers between devices, share(): return lax.all_to_all(row, AXES, 0, 0)  3.85 us
    ppermute x7, waiting for transfers between devices, swap(): return [lax.ppermute(messages[0], AXES, pairs[0]), odd]  2.9 us
  transfers between devices with their start and end apart: 15, of which 6 were waited for; matrix products, arithmetic and copies ran while one was open for 0% of the time, Pallas kernels for 2%

profile of v7, /device:TPU:0, one launch (start us, length us, event | category | flops | bytes accessed | tf_op | source)
XLA Modules:
  0.0 62.3 jit_solution(9145640559826266080)
XLA Ops:
  0.6 2.6 %shard_map.59 = (f32[32,1,256]{2,1,0:T(1,128)}, f32[8,16,256]{2,1,0:T(8,128)S(1)}, bf16[32,8,16,256]{3,2,1,0:T(8,128)(2,1)S(1)}, f32[3,8,16,256]{3,2,1,0:T(8,128)S(1)}, f32[32,1024]{1,0:T(8,128)S(1)}) custom-call(f32[8,16,256]{2,1,0:T(8,128)} %refs_0_.1, bf16[32,8,16,256]{3,2,1,0:T(8,128)(2,1)} %refs_1_.1, f32[3,8,16,256]{3,2,1,0:T(8,128)} %refs_2_.1, ...), custom_call_target="tpu_custom_call" | custom-call | bytes 7200000 | tf_op jit(solution)/shard_map/pallas_call | solution.py:59
  3.2 7.3 %all-to-all-start = ((f32[32,1,256]{2,1,0:T(1,128)}), f32[32,1,256]{2,1,0:T(1,128)S(1)}, u32[]{:S(2)}, u32[]{:S(2)}) async-start(f32[32,1,256]{2,1,0:T(1,128)} %get-tuple-element.48), calls=%async_computation | async-start | bytes 65536 | tf_op jit(solution)/shard_map/all_to_all | solution.py:612
  10.6 0.3 collective-permute-start.3
  10.9 3.0 %collective-permute-start.2 = (f32[3,8,4,256]{3,2,1,0:T(4,128)S(1)}, f32[3,8,4,256]{3,2,1,0:T(4,128)S(1)}, u32[]{:S(2)}, u32[]{:S(2)}) collective-permute-start(f32[3,8,4,256]{3,2,1,0:T(4,128)S(1)} %get-tuple-element.53.refs_5_), channel_id=1, source_target_pairs={{0,1},{1,0},{2,3},{3,2},{4,5},{5,4},{6,7},{7,6},{8,9},{9,8},{10,11... | collective-permute-start | bytes 294920 | tf_op jit(solution)/shard_map/ppermute | solution.py:609
  13.9 3.8 %all-to-all-done.refs_0_ = f32[32,1,256]{2,1,0:T(1,128)S(1)} async-done(((f32[32,1,256]{2,1,0:T(1,128)}), f32[32,1,256]{2,1,0:T(1,128)S(1)}, u32[]{:S(2)}, u32[]{:S(2)}) %all-to-all-start) | async-done | bytes 32800 | tf_op jit(solution)/shard_map/all_to_all | solution.py:612
  17.7 0.7 %shard_map.61 = (f32[8,16,256]{2,1,0:T(8,128)S(1)}, f32[8,16,256]{2,1,0:T(8,128)S(1)}, f32[12,4,256]{2,1,0:T(4,128)S(1)}, f32[12,4,256]{2,1,0:T(4,128)S(1)}, f32...) custom-call(f32[32,1,256]{2,1,0:T(1,128)S(1)} %all-to-all-done.refs_0_, ...), custom_call_target="tpu_custom_call" | custom-call | bytes 5040000 | tf_op jit(solution)/shard_map/pallas_call | solution.py:59
  18.4 0.2 collective-permute-start
  18.6 2.0 %collective-permute-start.1 = (f32[12,4,256]{2,1,0:T(4,128)S(1)}, f32[12,4,256]{2,1,0:T(4,128)S(1)}, u32[]{:S(2)}, u32[]{:S(2)}) collective-permute-start(f32[12,4,256]{2,1,0:T(4,128)S(1)} %get-tuple-element.57), channel_id=1, source_target_pairs={{0,1},{1,0},{2,3},{3,2},{4,5},{5,4},{6,7},{7,6},{8,9},{9,8},{10,11... | collective-permute-start | bytes 147464 | tf_op jit(solution)/shard_map/ppermute | solution.py:609
  20.6 0.0 collective-permute-start.6
  20.6 0.0 collective-permute-done.3.refs_6_.refs_2_
  20.6 0.7 %collective-permute-start.7 = (f32[13,16,256]{2,1,0:T(8,128)S(1)}, f32[13,16,256]{2,1,0:T(8,128)S(1)}, u32[]{:S(2)}, u32[]{:S(2)}) collective-permute-start(f32[13,16,256]{2,1,0:T(8,128)S(1)} %get-tuple-element.70), channel_id=1, source_target_pairs={{0,8},{1,9},{2,10},{3,11},{4,12},{5,13},{6,14},{7,15},{8,0},{9,1},... | collective-permute-start | bytes 638984 | tf_op jit(solution)/shard_map/ppermute | solution.py:609
  21.4 0.0 collective-permute-done.2.refs_5_.refs_1_
  21.4 0.0 collective-permute-done.refs_2_
  21.4 1.3 %collective-permute-done.1.refs_3_ = f32[12,4,256]{2,1,0:T(4,128)S(1)} collective-permute-done((f32[12,4,256]{2,1,0:T(4,128)S(1)}, f32[12,4,256]{2,1,0:T(4,128)S(1)}, u32[]{:S(2)}, u32[]{:S(2)}) %collective-permute-start.1) | collective-permute-done | bytes 49184 | tf_op jit(solution)/shard_map/ppermute | solution.py:609
  22.7 0.1 shard_map.62
  22.8 2.2 %collective-permute-start.4 = (f32[26,8,256]{2,1,0:T(8,128)S(1)}, f32[26,8,256]{2,1,0:T(8,128)S(1)}, u32[]{:S(2)}, u32[]{:S(2)}) collective-permute-start(f32[26,8,256]{2,1,0:T(8,128)S(1)} %get-tuple-element.62), channel_id=1, source_target_pairs={{0,1},{1,0},{2,3},{3,2},{4,5},{5,4},{6,7},{7,6},{8,16},{9,17},{10,... | collective-permute-start | bytes 638984 | tf_op jit(solution)/shard_map/ppermute | solution.py:608
  25.1 0.0 collective-permute-start.5
  25.1 0.1 shard_map.63
  25.2 1.2 %collective-permute-done.6.refs_11_ = f32[13,16,256]{2,1,0:T(8,128)S(1)} collective-permute-done((f32[13,16,256]{2,1,0:T(8,128)S(1)}, f32[13,16,256]{2,1,0:T(8,128)S(1)}, u32[]{:S(2)}, u32[]{:S(2)}) %collective-permute-start.6) | collective-permute-done | bytes 213024 | tf_op jit(solution)/shard_map/ppermute | solution.py:608
  26.4 0.0 collective-permute-done.7.refs_12_
  26.4 2.5 %collective-permute-done.4.refs_3_ = f32[26,8,256]{2,1,0:T(8,128)S(1)} collective-permute-done((f32[26,8,256]{2,1,0:T(8,128)S(1)}, f32[26,8,256]{2,1,0:T(8,128)S(1)}, u32[]{:S(2)}, u32[]{:S(2)}) %collective-permute-start.4) | collective-permute-done | bytes 213024 | tf_op jit(solution)/shard_map/ppermute | solution.py:608
  28.9 0.0 collective-permute-done.5.refs_4_
  28.9 2.4 %shard_map.64 = (f32[8,16,256]{2,1,0:T(8,128)S(1)}, f32[8,16,256]{2,1,0:T(8,128)S(1)}, f32[32,1,256]{2,1,0:T(1,128)S(1)}, f32[8,24,256]{2,1,0:T(8,128)S(1)}, f32...) custom-call(f32[8,24,256]{2,1,0:T(8,128)S(1)} %get-tuple-element.59.refs_0_, ...), custom_call_target="tpu_custom_call" | custom-call | bytes 10800000 | tf_op jit(solution)/shard_map/pallas_call | solution.py:59
  31.3 9.4 %all_to_all.15.refs_1_ = f32[32,1,256]{2,1,0:T(1,128)S(1)} all-to-all(f32[32,1,256]{2,1,0:T(1,128)S(1)} %get-tuple-element.71), channel_id=1, replica_groups=mesh['gx'=4,'gy'=8] {'gx','gy'}, dimensions={0} | all-to-all | bytes 65536 | tf_op jit(solution)/shard_map/all_to_all | solution.py:612
  40.7 0.9 %shard_map.65 = (f32[8,16,256]{2,1,0:T(8,128)S(1)}, f32[8,16,256]{2,1,0:T(8,128)S(1)}, f32[8,16,256]{2,1,0:T(8,128)S(1)}, f32[8,128]{1,0:T(8,128)S(1)}, f32[12,4...) custom-call(f32[32,1,256]{2,1,0:T(1,128)S(1)} %all-to-all-done.refs_0_, ...), custom_call_target="tpu_custom_call" | custom-call | bytes 5040000 | tf_op jit(solution)/shard_map/pallas_call | solution.py:59
  41.6 0.2 collective-permute-start.8
  41.8 1.8 %collective-permute-start.9 = (f32[12,4,256]{2,1,0:T(4,128)S(1)}, f32[12,4,256]{2,1,0:T(4,128)S(1)}, u32[]{:S(2)}, u32[]{:S(2)}) collective-permute-start(f32[12,4,256]{2,1,0:T(4,128)S(1)} %get-tuple-element.76), channel_id=1, source_target_pairs={{0,1},{1,0},{2,3},{3,2},{4,5},{5,4},{6,7},{7,6},{8,9},{9,8},{10,11... | collective-permute-start | bytes 147464 | tf_op jit(solution)/shard_map/ppermute | solution.py:609
  43.6 0.2 collective-permute-start.12
  43.8 0.5 collective-permute-start.13
  44.3 0.0 collective-permute-done.8.refs_2_
  44.3 1.5 %collective-permute-done.9.refs_3_ = f32[12,4,256]{2,1,0:T(4,128)S(1)} collective-permute-done((f32[12,4,256]{2,1,0:T(4,128)S(1)}, f32[12,4,256]{2,1,0:T(4,128)S(1)}, u32[]{:S(2)}, u32[]{:S(2)}) %collective-permute-start.9) | collective-permute-done | bytes 49184 | tf_op jit(solution)/shard_map/ppermute | solution.py:609
  45.9 0.1 shard_map.66
  46.0 2.2 %collective-permute-start.10 = (f32[6,8,256]{2,1,0:T(8,128)S(1)}, f32[6,8,256]{2,1,0:T(8,128)S(1)}, u32[]{:S(2)}, u32[]{:S(2)}) collective-permute-start(f32[6,8,256]{2,1,0:T(8,128)S(1)} %get-tuple-element.80), channel_id=1, source_target_pairs={{0,1},{1,0},{2,3},{3,2},{4,5},{5,4},{6,7},{7,6},{8,16},{9,17},{10,... | collective-permute-start | bytes 147464 | tf_op jit(solution)/shard_map/ppermute | solution.py:608
  48.2 0.0 collective-permute-start.11
  48.2 0.0 collective-permute-done.12.refs_11_
  48.2 0.0 collective-permute-done.13.refs_12_
  48.2 2.1 %collective-permute-done.10.refs_3_ = f32[6,8,256]{2,1,0:T(8,128)S(1)} collective-permute-done((f32[6,8,256]{2,1,0:T(8,128)S(1)}, f32[6,8,256]{2,1,0:T(8,128)S(1)}, u32[]{:S(2)}, u32[]{:S(2)}) %collective-permute-start.10) | collective-permute-done | bytes 49184 | tf_op jit(solution)/shard_map/ppermute | solution.py:608
  50.3 0.0 collective-permute-done.11.refs_4_
  50.3 1.7 %shard_map.67 = (f32[8,16,256]{2,1,0:T(8,128)S(1)}, f32[8,16,256]{2,1,0:T(8,128)S(1)}, f32[32,1,256]{2,1,0:T(1,128)S(1)}) custom-call(f32[8,24,256]{2,1,0:T(8,128)S(1)} %get-tuple-element.77.refs_0_, f32[2,24,256]{2,1,0:T(8,128)S(1)} %get-tuple-element.78.refs_1_, f32[2,8,256]{2,1,0:T(8,128)S(1)} %get-tuple-element.79.refs_2_, ...), custom_call_target="tpu_custom_call" | custom-call | bytes 9000000 | tf_op jit(solution)/shard_map/pallas_call | solution.py:59
  52.0 9.4 %all_to_all.16.refs_0_ = f32[32,1,256]{2,1,0:T(1,128)S(1)} all-to-all(f32[32,1,256]{2,1,0:T(1,128)S(1)} %get-tuple-element.89), channel_id=1, replica_groups=mesh['gx'=4,'gy'=8] {'gx','gy'}, dimensions={0} | all-to-all | bytes 65536 | tf_op jit(solution)/shard_map/all_to_all | solution.py:612
  61.4 0.9 %shard_map.68 = (f32[8,16,256]{2,1,0:T(8,128)}, f32[8,16,256]{2,1,0:T(8,128)}) custom-call(f32[32,1,256]{2,1,0:T(1,128)S(1)} %all_to_all.16.refs_0_, f32[8,128]{1,0:T(8,128)S(1)} %get-tuple-element.90.refs_1_, f32[8,16,256]{2,1,0:T(8,128)S(1)} %get-tuple-element.91.refs_2_, f32[8,16,256]{2,1,0:T(8,128)S(1)} %get-tuple-element.92.refs_3_, ...), custom_call_target="tpu_custom_call" | custom-call | bytes 5040000 | tf_op jit(solution)/shard_map/pallas_call | solution.py:59
  (1 shorter events, 0.0 us)
Async XLA Ops:
  3.2 14.5 %all-to-all-start = ((f32[32,1,256]{2,1,0:T(1,128)}), f32[32,1,256]{2,1,0:T(1,128)S(1)}, u32[]{:S(2)}, u32[]{:S(2)}) async-start(f32[32,1,256]{2,1,0:T(1,128)} %get-tuple-element.48), calls=%async_computation | async-start | bytes 65536 | tf_op jit(solution)/shard_map/all_to_all | solution.py:612
  10.6 10.1 %collective-permute-start.3 = (f32[3,8,4,256]{3,2,1,0:T(4,128)S(1)}, f32[3,8,4,256]{3,2,1,0:T(4,128)S(1)}, u32[]{:S(2)}, u32[]{:S(2)}) collective-permute-start(f32[3,8,4,256]{3,2,1,0:T(4,128)S(1)} %get-tuple-element.58), channel_id=1, source_target_pairs={{0,8},{1,2},{2,1},{3,4},{4,3},{5,6},{6,5},{7,15},{8,0},{9,10},{10,... | collective-permute-start | bytes 294920 | tf_op jit(solution)/shard_map/ppermute | solution.py:608
  10.9 10.5 %collective-permute-start.2 = (f32[3,8,4,256]{3,2,1,0:T(4,128)S(1)}, f32[3,8,4,256]{3,2,1,0:T(4,128)S(1)}, u32[]{:S(2)}, u32[]{:S(2)}) collective-permute-start(f32[3,8,4,256]{3,2,1,0:T(4,128)S(1)} %get-tuple-element.53.refs_5_), channel_id=1, source_target_pairs={{0,1},{1,0},{2,3},{3,2},{4,5},{5,4},{6,7},{7,6},{8,9},{9,8},{10,11... | collective-permute-start | bytes 294920 | tf_op jit(solution)/shard_map/ppermute | solution.py:609
  18.4 2.9 %collective-permute-start = (f32[12,4,256]{2,1,0:T(4,128)S(1)}, f32[12,4,256]{2,1,0:T(4,128)S(1)}, u32[]{:S(2)}, u32[]{:S(2)}) collective-permute-start(f32[12,4,256]{2,1,0:T(4,128)S(1)} %get-tuple-element.56), channel_id=1, source_target_pairs={{0,8},{1,2},{2,1},{3,4},{4,3},{5,6},{6,5},{7,15},{8,0},{9,10},{10,... | collective-permute-start | bytes 147464 | tf_op jit(solution)/shard_map/ppermute | solution.py:608
  18.6 4.1 %collective-permute-start.1 = (f32[12,4,256]{2,1,0:T(4,128)S(1)}, f32[12,4,256]{2,1,0:T(4,128)S(1)}, u32[]{:S(2)}, u32[]{:S(2)}) collective-permute-start(f32[12,4,256]{2,1,0:T(4,128)S(1)} %get-tuple-element.57), channel_id=1, source_target_pairs={{0,1},{1,0},{2,3},{3,2},{4,5},{5,4},{6,7},{7,6},{8,9},{9,8},{10,11... | collective-permute-start | bytes 147464 | tf_op jit(solution)/shard_map/ppermute | solution.py:609
  20.6 5.8 %collective-permute-start.6 = (f32[13,16,256]{2,1,0:T(8,128)S(1)}, f32[13,16,256]{2,1,0:T(8,128)S(1)}, u32[]{:S(2)}, u32[]{:S(2)}) collective-permute-start(f32[13,16,256]{2,1,0:T(8,128)S(1)} %get-tuple-element.69), channel_id=1, source_target_pairs={{0,1},{1,0},{2,3},{3,2},{4,5},{5,4},{6,7},{7,6},{8,16},{9,17},{10,... | collective-permute-start | bytes 638984 | tf_op jit(solution)/shard_map/ppermute | solution.py:608
  20.6 5.8 %collective-permute-start.7 = (f32[13,16,256]{2,1,0:T(8,128)S(1)}, f32[13,16,256]{2,1,0:T(8,128)S(1)}, u32[]{:S(2)}, u32[]{:S(2)}) collective-permute-start(f32[13,16,256]{2,1,0:T(8,128)S(1)} %get-tuple-element.70), channel_id=1, source_target_pairs={{0,8},{1,9},{2,10},{3,11},{4,12},{5,13},{6,14},{7,15},{8,0},{9,1},... | collective-permute-start | bytes 638984 | tf_op jit(solution)/shard_map/ppermute | solution.py:609
  22.8 6.1 %collective-permute-start.4 = (f32[26,8,256]{2,1,0:T(8,128)S(1)}, f32[26,8,256]{2,1,0:T(8,128)S(1)}, u32[]{:S(2)}, u32[]{:S(2)}) collective-permute-start(f32[26,8,256]{2,1,0:T(8,128)S(1)} %get-tuple-element.62), channel_id=1, source_target_pairs={{0,1},{1,0},{2,3},{3,2},{4,5},{5,4},{6,7},{7,6},{8,16},{9,17},{10,... | collective-permute-start | bytes 638984 | tf_op jit(solution)/shard_map/ppermute | solution.py:608
  25.1 3.8 %collective-permute-start.5 = (f32[26,8,256]{2,1,0:T(8,128)S(1)}, f32[26,8,256]{2,1,0:T(8,128)S(1)}, u32[]{:S(2)}, u32[]{:S(2)}) collective-permute-start(f32[26,8,256]{2,1,0:T(8,128)S(1)} %get-tuple-element.63), channel_id=1, source_target_pairs={{0,8},{1,9},{2,10},{3,11},{4,12},{5,13},{6,14},{7,15},{8,0},{9,1},... | collective-permute-start | bytes 638984 | tf_op jit(solution)/shard_map/ppermute | solution.py:609
  41.6 2.8 %collective-permute-start.8 = (f32[12,4,256]{2,1,0:T(4,128)S(1)}, f32[12,4,256]{2,1,0:T(4,128)S(1)}, u32[]{:S(2)}, u32[]{:S(2)}) collective-permute-start(f32[12,4,256]{2,1,0:T(4,128)S(1)} %get-tuple-element.75), channel_id=1, source_target_pairs={{0,8},{1,2},{2,1},{3,4},{4,3},{5,6},{6,5},{7,15},{8,0},{9,10},{10,... | collective-permute-start | bytes 147464 | tf_op jit(solution)/shard_map/ppermute | solution.py:608
  41.8 4.1 %collective-permute-start.9 = (f32[12,4,256]{2,1,0:T(4,128)S(1)}, f32[12,4,256]{2,1,0:T(4,128)S(1)}, u32[]{:S(2)}, u32[]{:S(2)}) collective-permute-start(f32[12,4,256]{2,1,0:T(4,128)S(1)} %get-tuple-element.76), channel_id=1, source_target_pairs={{0,1},{1,0},{2,3},{3,2},{4,5},{5,4},{6,7},{7,6},{8,9},{9,8},{10,11... | collective-permute-start | bytes 147464 | tf_op jit(solution)/shard_map/ppermute | solution.py:609
  43.6 4.6 %collective-permute-start.12 = (f32[5,16,256]{2,1,0:T(8,128)S(1)}, f32[5,16,256]{2,1,0:T(8,128)S(1)}, u32[]{:S(2)}, u32[]{:S(2)}) collective-permute-start(f32[5,16,256]{2,1,0:T(8,128)S(1)} %get-tuple-element.82), channel_id=1, source_target_pairs={{0,1},{1,0},{2,3},{3,2},{4,5},{5,4},{6,7},{7,6},{8,16},{9,17},{10,... | collective-permute-start | bytes 245768 | tf_op jit(solution)/shard_map/ppermute | solution.py:608
  43.8 4.4 %collective-permute-start.13 = (f32[5,16,256]{2,1,0:T(8,128)S(1)}, f32[5,16,256]{2,1,0:T(8,128)S(1)}, u32[]{:S(2)}, u32[]{:S(2)}) collective-permute-start(f32[5,16,256]{2,1,0:T(8,128)S(1)} %get-tuple-element.83), channel_id=1, source_target_pairs={{0,8},{1,9},{2,10},{3,11},{4,12},{5,13},{6,14},{7,15},{8,0},{9,1},... | collective-permute-start | bytes 245768 | tf_op jit(solution)/shard_map/ppermute | solution.py:609
  46.0 4.3 %collective-permute-start.10 = (f32[6,8,256]{2,1,0:T(8,128)S(1)}, f32[6,8,256]{2,1,0:T(8,128)S(1)}, u32[]{:S(2)}, u32[]{:S(2)}) collective-permute-start(f32[6,8,256]{2,1,0:T(8,128)S(1)} %get-tuple-element.80), channel_id=1, source_target_pairs={{0,1},{1,0},{2,3},{3,2},{4,5},{5,4},{6,7},{7,6},{8,16},{9,17},{10,... | collective-permute-start | bytes 147464 | tf_op jit(solution)/shard_map/ppermute | solution.py:608
  48.2 2.1 %collective-permute-start.11 = (f32[6,8,256]{2,1,0:T(8,128)S(1)}, f32[6,8,256]{2,1,0:T(8,128)S(1)}, u32[]{:S(2)}, u32[]{:S(2)}) collective-permute-start(f32[6,8,256]{2,1,0:T(8,128)S(1)} %get-tuple-element.81), channel_id=1, source_target_pairs={{0,8},{1,9},{2,10},{3,11},{4,12},{5,13},{6,14},{7,15},{8,0},{9,1},... | collective-permute-start | bytes 147464 | tf_op jit(solution)/shard_map/ppermute | solution.py:609

commit v8 on v7

--- a/solution.py
+++ b/solution.py
@@ -76,9 +76,9 @@
     return jnp.concatenate([jnp.where(lane == edge, far, near) for near, far in zip(turned, beside)], axis=1)
 
 
-def restrict(vectors, field, sums, flags, send, copies=()):
+def restrict(vectors, fields, sums, flags, send, copies=()):
     count, size_x, size_y, size_z = vectors.shape
-    stage = send[1]
+    out, stage = send
     stage[...] = jnp.zeros_like(stage)
 
     def lanes_of(total):
@@ -89,13 +89,15 @@
     for j in range(count):
         if copies and j % (count // len(copies)) == 0:
             copies[j // (count // len(copies))].wait()
-        total = vectors[j, 0].astype(F32) * field[0]
-        for x in range(1, size_x):
-            total = total + vectors[j, x].astype(F32) * field[x]
-        stage[pl.ds(offset + j, 1), :] = lanes_of(total)
+        totals = [0.0] * len(fields)
+        for x in range(size_x):
+            plane = vectors[j, x].astype(F32)
+            totals = [total + plane * field[x] for total, field in zip(totals, fields)]
+        for k, total in enumerate(totals):
+            stage[pl.ds(k * LANES + offset + j, 1), :] = lanes_of(total)
     for k, total in enumerate(sums):
         stage[LANES + k : LANES + k + 1, :] = lanes_of(total)
-    write_row(stage, send[0])
+    write_row(stage, out)
 
 
 def write_row(stage, out):
@@ -106,10 +108,10 @@
         out[k] = row[0:1]
 
 
-def gathered(received, vectors):
+def gathered(received, vectors, part=0):
     share = LANES // vectors.shape[0]
     return [
-        functools.reduce(jnp.add, [received[k + i, :, :LANES] for i in range(share)])
+        functools.reduce(jnp.add, [received[k + i, :, part * LANES : (part + 1) * LANES] for i in range(share)])
         for k in range(0, received.shape[0], share)
     ]
 
@@ -190,7 +192,7 @@
         copy.start()
     copies[0].wait()
     rounded = [held_field[x].astype(jnp.bfloat16).astype(F32) for x in range(field.shape[0])]
-    restrict(held_vectors, rounded, [], flags, (out, stage), copies[1 : 1 + parts])
+    restrict(held_vectors, [rounded, held_field], [], flags, (out, stage), copies[1 : 1 + parts])
     for copy in copies[1 + parts :]:
         copy.wait()
 
@@ -325,7 +327,7 @@
     step = step[0:1, 0:1]
     for x in range(field.shape[0]):
         middle[x] = field[x] - step * image[x]
-    pairs = zip(gathered(received, vectors), gathered(second, vectors))
+    pairs = zip(gathered(received, vectors, 1), gathered(second, vectors))
     prolong(solve([coarse - step * of_image for coarse, of_image in pairs], inverse), vectors, corr)
     subtract_own(middle, corr, velocity, rest)
     by_parity(flags[ODD_Y], lambda out, high: write_y_message(out, rest, corr, high), even_out, odd_out)
@@ -566,7 +568,7 @@
     coefs = [Region(*pair) for pair in zip((own0, own1, own2, own3), halos)]
     smooth(flags, EARLY_FIRST, wide, sides, past, early, late, diagonal, coefs, corr, search, image, scratch)
     products = [dot_planes(right_side, right_side), dot_planes(right_side, image)]
-    restrict(vectors, image, products, flags, (out, stage))
+    restrict(vectors, [image], products, flags, (out, stage))
 
 
 def smoothed_kernel(

time: 62.5 us -> 62.8 us (level)
  no operation moved by 1% of the time
where the time goes in v8:
time: 62.8 us; the launch traced here: 62.6 us
  starting transfers between devices  20.7 us (33%)
  blocking collectives  18.8 us (30%)
  waiting for transfers between devices  12.5 us (20%)
  Pallas kernels  9.87 us (16%)
  between operations  0.73 us (1%)
    all_to_all x2, blocking collectives, share(): return lax.all_to_all(row, AXES, 0, 0)  18.8 us
    pallas_call x10, Pallas kernels, call(): pl.pallas_call(kernel, out_shape=[jax.ShapeDtypeStruct(kind, F32) if isin...  9.87 us
    ppermute x7, starting transfers between devices, swap(): return [lax.ppermute(messages[0], AXES, pairs[0]), odd]  8.04 us
    all_to_all x1, starting transfers between devices, share(): return lax.all_to_all(row, AXES, 0, 0)  7.3 us
    ppermute x7, waiting for transfers between devices, swap(): odd = lax.ppermute(messages[1], AXES, pairs[1])  5.73 us
    ppermute x7, starting transfers between devices, swap(): odd = lax.ppermute(messages[1], AXES, pairs[1])  5.39 us
    all_to_all x1, waiting for transfers between devices, share(): return lax.all_to_all(row, AXES, 0, 0)  3.85 us
    ppermute x7, waiting for transfers between devices, swap(): return [lax.ppermute(messages[0], AXES, pairs[0]), odd]  2.9 us
  transfers between devices with their start and end apart: 15, of which 6 were waited for; matrix products, arithmetic and copies ran while one was open for 0% of the time, Pallas kernels for 2%

profile of v8, /device:TPU:0, one launch (start us, length us, event | category | flops | bytes accessed | tf_op | source)
XLA Modules:
  0.0 62.6 jit_solution(2054125047406844924)
XLA Ops:
  0.6 2.9 %shard_map.59 = (f32[32,1,256]{2,1,0:T(1,128)}, f32[8,16,256]{2,1,0:T(8,128)S(1)}, bf16[32,8,16,256]{3,2,1,0:T(8,128)(2,1)S(1)}, f32[3,8,16,256]{3,2,1,0:T(8,128)S(1)}, f32[32,1024]{1,0:T(8,128)S(1)}) custom-call(f32[8,16,256]{2,1,0:T(8,128)} %refs_0_.1, bf16[32,8,16,256]{3,2,1,0:T(8,128)(2,1)} %refs_1_.1, f32[3,8,16,256]{3,2,1,0:T(8,128)} %refs_2_.1, ...), custom_call_target="tpu_custom_call" | custom-call | bytes 7200000 | tf_op jit(solution)/shard_map/pallas_call | solution.py:59
  3.6 7.3 %all-to-all-start = ((f32[32,1,256]{2,1,0:T(1,128)}), f32[32,1,256]{2,1,0:T(1,128)S(1)}, u32[]{:S(2)}, u32[]{:S(2)}) async-start(f32[32,1,256]{2,1,0:T(1,128)} %get-tuple-element.48), calls=%async_computation | async-start | bytes 65536 | tf_op jit(solution)/shard_map/all_to_all | solution.py:614
  10.9 0.3 collective-permute-start.3
  11.2 3.0 %collective-permute-start.2 = (f32[3,8,4,256]{3,2,1,0:T(4,128)S(1)}, f32[3,8,4,256]{3,2,1,0:T(4,128)S(1)}, u32[]{:S(2)}, u32[]{:S(2)}) collective-permute-start(f32[3,8,4,256]{3,2,1,0:T(4,128)S(1)} %get-tuple-element.53.refs_5_), channel_id=1, source_target_pairs={{0,1},{1,0},{2,3},{3,2},{4,5},{5,4},{6,7},{7,6},{8,9},{9,8},{10,11... | collective-permute-start | bytes 294920 | tf_op jit(solution)/shard_map/ppermute | solution.py:611
  14.2 3.8 %all-to-all-done.refs_0_ = f32[32,1,256]{2,1,0:T(1,128)S(1)} async-done(((f32[32,1,256]{2,1,0:T(1,128)}), f32[32,1,256]{2,1,0:T(1,128)S(1)}, u32[]{:S(2)}, u32[]{:S(2)}) %all-to-all-start) | async-done | bytes 32800 | tf_op jit(solution)/shard_map/all_to_all | solution.py:614
  18.1 0.7 %shard_map.61 = (f32[8,16,256]{2,1,0:T(8,128)S(1)}, f32[8,16,256]{2,1,0:T(8,128)S(1)}, f32[12,4,256]{2,1,0:T(4,128)S(1)}, f32[12,4,256]{2,1,0:T(4,128)S(1)}, f32...) custom-call(f32[32,1,256]{2,1,0:T(1,128)S(1)} %all-to-all-done.refs_0_, ...), custom_call_target="tpu_custom_call" | custom-call | bytes 5040000 | tf_op jit(solution)/shard_map/pallas_call | solution.py:59
  18.8 0.2 collective-permute-start
  19.0 2.0 %collective-permute-start.1 = (f32[12,4,256]{2,1,0:T(4,128)S(1)}, f32[12,4,256]{2,1,0:T(4,128)S(1)}, u32[]{:S(2)}, u32[]{:S(2)}) collective-permute-start(f32[12,4,256]{2,1,0:T(4,128)S(1)} %get-tuple-element.57), channel_id=1, source_target_pairs={{0,1},{1,0},{2,3},{3,2},{4,5},{5,4},{6,7},{7,6},{8,9},{9,8},{10,11... | collective-permute-start | bytes 147464 | tf_op jit(solution)/shard_map/ppermute | solution.py:611
  20.9 0.0 collective-permute-start.6
  21.0 0.0 collective-permute-done.3.refs_6_.refs_2_
  21.0 0.7 %collective-permute-start.7 = (f32[13,16,256]{2,1,0:T(8,128)S(1)}, f32[13,16,256]{2,1,0:T(8,128)S(1)}, u32[]{:S(2)}, u32[]{:S(2)}) collective-permute-start(f32[13,16,256]{2,1,0:T(8,128)S(1)} %get-tuple-element.70), channel_id=1, source_target_pairs={{0,8},{1,9},{2,10},{3,11},{4,12},{5,13},{6,14},{7,15},{8,0},{9,1},... | collective-permute-start | bytes 638984 | tf_op jit(solution)/shard_map/ppermute | solution.py:611
  21.7 0.0 collective-permute-done.2.refs_5_.refs_1_
  21.7 0.0 collective-permute-done.refs_2_
  21.7 1.3 %collective-permute-done.1.refs_3_ = f32[12,4,256]{2,1,0:T(4,128)S(1)} collective-permute-done((f32[12,4,256]{2,1,0:T(4,128)S(1)}, f32[12,4,256]{2,1,0:T(4,128)S(1)}, u32[]{:S(2)}, u32[]{:S(2)}) %collective-permute-start.1) | collective-permute-done | bytes 49184 | tf_op jit(solution)/shard_map/ppermute | solution.py:611
  23.1 0.1 shard_map.62
  23.2 2.2 %collective-permute-start.4 = (f32[26,8,256]{2,1,0:T(8,128)S(1)}, f32[26,8,256]{2,1,0:T(8,128)S(1)}, u32[]{:S(2)}, u32[]{:S(2)}) collective-permute-start(f32[26,8,256]{2,1,0:T(8,128)S(1)} %get-tuple-element.62), channel_id=1, source_target_pairs={{0,1},{1,0},{2,3},{3,2},{4,5},{5,4},{6,7},{7,6},{8,16},{9,17},{10,... | collective-permute-start | bytes 638984 | tf_op jit(solution)/shard_map/ppermute | solution.py:610
  25.4 0.0 collective-permute-start.5
  25.4 0.1 shard_map.63
  25.6 1.2 %collective-permute-done.6.refs_11_ = f32[13,16,256]{2,1,0:T(8,128)S(1)} collective-permute-done((f32[13,16,256]{2,1,0:T(8,128)S(1)}, f32[13,16,256]{2,1,0:T(8,128)S(1)}, u32[]{:S(2)}, u32[]{:S(2)}) %collective-permute-start.6) | collective-permute-done | bytes 213024 | tf_op jit(solution)/shard_map/ppermute | solution.py:610
  26.8 0.0 collective-permute-done.7.refs_12_
  26.8 2.5 %collective-permute-done.4.refs_3_ = f32[26,8,256]{2,1,0:T(8,128)S(1)} collective-permute-done((f32[26,8,256]{2,1,0:T(8,128)S(1)}, f32[26,8,256]{2,1,0:T(8,128)S(1)}, u32[]{:S(2)}, u32[]{:S(2)}) %collective-permute-start.4) | collective-permute-done | bytes 213024 | tf_op jit(solution)/shard_map/ppermute | solution.py:610
  29.3 0.0 collective-permute-done.5.refs_4_
  29.3 2.4 %shard_map.64 = (f32[8,16,256]{2,1,0:T(8,128)S(1)}, f32[8,16,256]{2,1,0:T(8,128)S(1)}, f32[32,1,256]{2,1,0:T(1,128)S(1)}, f32[8,24,256]{2,1,0:T(8,128)S(1)}, f32...) custom-call(f32[8,24,256]{2,1,0:T(8,128)S(1)} %get-tuple-element.59.refs_0_, ...), custom_call_target="tpu_custom_call" | custom-call | bytes 10800000 | tf_op jit(solution)/shard_map/pallas_call | solution.py:59
  31.6 9.4 %all_to_all.15.refs_1_ = f32[32,1,256]{2,1,0:T(1,128)S(1)} all-to-all(f32[32,1,256]{2,1,0:T(1,128)S(1)} %get-tuple-element.71), channel_id=1, replica_groups=mesh['gx'=4,'gy'=8] {'gx','gy'}, dimensions={0} | all-to-all | bytes 65536 | tf_op jit(solution)/shard_map/all_to_all | solution.py:614
  41.0 0.9 %shard_map.65 = (f32[8,16,256]{2,1,0:T(8,128)S(1)}, f32[8,16,256]{2,1,0:T(8,128)S(1)}, f32[8,16,256]{2,1,0:T(8,128)S(1)}, f32[8,128]{1,0:T(8,128)S(1)}, f32[12,4...) custom-call(f32[32,1,256]{2,1,0:T(1,128)S(1)} %all-to-all-done.refs_0_, ...), custom_call_target="tpu_custom_call" | custom-call | bytes 5040000 | tf_op jit(solution)/shard_map/pallas_call | solution.py:59
  41.9 0.2 collective-permute-start.8
  42.1 1.8 %collective-permute-start.9 = (f32[12,4,256]{2,1,0:T(4,128)S(1)}, f32[12,4,256]{2,1,0:T(4,128)S(1)}, u32[]{:S(2)}, u32[]{:S(2)}) collective-permute-start(f32[12,4,256]{2,1,0:T(4,128)S(1)} %get-tuple-element.76), channel_id=1, source_target_pairs={{0,1},{1,0},{2,3},{3,2},{4,5},{5,4},{6,7},{7,6},{8,9},{9,8},{10,11... | collective-permute-start | bytes 147464 | tf_op jit(solution)/shard_map/ppermute | solution.py:611
  44.0 0.2 collective-permute-start.12
  44.2 0.5 collective-permute-start.13
  44.7 0.0 collective-permute-done.8.refs_2_
  44.7 1.5 %collective-permute-done.9.refs_3_ = f32[12,4,256]{2,1,0:T(4,128)S(1)} collective-permute-done((f32[12,4,256]{2,1,0:T(4,128)S(1)}, f32[12,4,256]{2,1,0:T(4,128)S(1)}, u32[]{:S(2)}, u32[]{:S(2)}) %collective-permute-start.9) | collective-permute-done | bytes 49184 | tf_op jit(solution)/shard_map/ppermute | solution.py:611
  46.2 0.1 shard_map.66
  46.3 2.2 %collective-permute-start.10 = (f32[6,8,256]{2,1,0:T(8,128)S(1)}, f32[6,8,256]{2,1,0:T(8,128)S(1)}, u32[]{:S(2)}, u32[]{:S(2)}) collective-permute-start(f32[6,8,256]{2,1,0:T(8,128)S(1)} %get-tuple-element.80), channel_id=1, source_target_pairs={{0,1},{1,0},{2,3},{3,2},{4,5},{5,4},{6,7},{7,6},{8,16},{9,17},{10,... | collective-permute-start | bytes 147464 | tf_op jit(solution)/shard_map/ppermute | solution.py:610
  48.5 0.0 collective-permute-start.11
  48.5 0.0 collective-permute-done.12.refs_11_
  48.5 0.0 collective-permute-done.13.refs_12_
  48.6 2.1 %collective-permute-done.10.refs_3_ = f32[6,8,256]{2,1,0:T(8,128)S(1)} collective-permute-done((f32[6,8,256]{2,1,0:T(8,128)S(1)}, f32[6,8,256]{2,1,0:T(8,128)S(1)}, u32[]{:S(2)}, u32[]{:S(2)}) %collective-permute-start.10) | collective-permute-done | bytes 49184 | tf_op jit(solution)/shard_map/ppermute | solution.py:610
  50.6 0.0 collective-permute-done.11.refs_4_
  50.6 1.7 %shard_map.67 = (f32[8,16,256]{2,1,0:T(8,128)S(1)}, f32[8,16,256]{2,1,0:T(8,128)S(1)}, f32[32,1,256]{2,1,0:T(1,128)S(1)}) custom-call(f32[8,24,256]{2,1,0:T(8,128)S(1)} %get-tuple-element.77.refs_0_, f32[2,24,256]{2,1,0:T(8,128)S(1)} %get-tuple-element.78.refs_1_, f32[2,8,256]{2,1,0:T(8,128)S(1)} %get-tuple-element.79.refs_2_, ...), custom_call_target="tpu_custom_call" | custom-call | bytes 9000000 | tf_op jit(solution)/shard_map/pallas_call | solution.py:59
  52.3 9.4 %all_to_all.16.refs_0_ = f32[32,1,256]{2,1,0:T(1,128)S(1)} all-to-all(f32[32,1,256]{2,1,0:T(1,128)S(1)} %get-tuple-element.89), channel_id=1, replica_groups=mesh['gx'=4,'gy'=8] {'gx','gy'}, dimensions={0} | all-to-all | bytes 65536 | tf_op jit(solution)/shard_map/all_to_all | solution.py:614
  61.7 0.9 %shard_map.68 = (f32[8,16,256]{2,1,0:T(8,128)}, f32[8,16,256]{2,1,0:T(8,128)}) custom-call(f32[32,1,256]{2,1,0:T(1,128)S(1)} %all_to_all.16.refs_0_, f32[8,128]{1,0:T(8,128)S(1)} %get-tuple-element.90.refs_1_, f32[8,16,256]{2,1,0:T(8,128)S(1)} %get-tuple-element.91.refs_2_, f32[8,16,256]{2,1,0:T(8,128)S(1)} %get-tuple-element.92.refs_3_, ...), custom_call_target="tpu_custom_call" | custom-call | bytes 5040000 | tf_op jit(solution)/shard_map/pallas_call | solution.py:59
  (1 shorter events, 0.0 us)
Async XLA Ops:
  3.6 14.5 %all-to-all-start = ((f32[32,1,256]{2,1,0:T(1,128)}), f32[32,1,256]{2,1,0:T(1,128)S(1)}, u32[]{:S(2)}, u32[]{:S(2)}) async-start(f32[32,1,256]{2,1,0:T(1,128)} %get-tuple-element.48), calls=%async_computation | async-start | bytes 65536 | tf_op jit(solution)/shard_map/all_to_all | solution.py:614
  10.9 10.1 %collective-permute-start.3 = (f32[3,8,4,256]{3,2,1,0:T(4,128)S(1)}, f32[3,8,4,256]{3,2,1,0:T(4,128)S(1)}, u32[]{:S(2)}, u32[]{:S(2)}) collective-permute-start(f32[3,8,4,256]{3,2,1,0:T(4,128)S(1)} %get-tuple-element.58), channel_id=1, source_target_pairs={{0,8},{1,2},{2,1},{3,4},{4,3},{5,6},{6,5},{7,15},{8,0},{9,10},{10,... | collective-permute-start | bytes 294920 | tf_op jit(solution)/shard_map/ppermute | solution.py:610
  11.2 10.5 %collective-permute-start.2 = (f32[3,8,4,256]{3,2,1,0:T(4,128)S(1)}, f32[3,8,4,256]{3,2,1,0:T(4,128)S(1)}, u32[]{:S(2)}, u32[]{:S(2)}) collective-permute-start(f32[3,8,4,256]{3,2,1,0:T(4,128)S(1)} %get-tuple-element.53.refs_5_), channel_id=1, source_target_pairs={{0,1},{1,0},{2,3},{3,2},{4,5},{5,4},{6,7},{7,6},{8,9},{9,8},{10,11... | collective-permute-start | bytes 294920 | tf_op jit(solution)/shard_map/ppermute | solution.py:611
  18.8 2.9 %collective-permute-start = (f32[12,4,256]{2,1,0:T(4,128)S(1)}, f32[12,4,256]{2,1,0:T(4,128)S(1)}, u32[]{:S(2)}, u32[]{:S(2)}) collective-permute-start(f32[12,4,256]{2,1,0:T(4,128)S(1)} %get-tuple-element.56), channel_id=1, source_target_pairs={{0,8},{1,2},{2,1},{3,4},{4,3},{5,6},{6,5},{7,15},{8,0},{9,10},{10,... | collective-permute-start | bytes 147464 | tf_op jit(solution)/shard_map/ppermute | solution.py:610
  19.0 4.1 %collective-permute-start.1 = (f32[12,4,256]{2,1,0:T(4,128)S(1)}, f32[12,4,256]{2,1,0:T(4,128)S(1)}, u32[]{:S(2)}, u32[]{:S(2)}) collective-permute-start(f32[12,4,256]{2,1,0:T(4,128)S(1)} %get-tuple-element.57), channel_id=1, source_target_pairs={{0,1},{1,0},{2,3},{3,2},{4,5},{5,4},{6,7},{7,6},{8,9},{9,8},{10,11... | collective-permute-start | bytes 147464 | tf_op jit(solution)/shard_map/ppermute | solution.py:611
  20.9 5.8 %collective-permute-start.6 = (f32[13,16,256]{2,1,0:T(8,128)S(1)}, f32[13,16,256]{2,1,0:T(8,128)S(1)}, u32[]{:S(2)}, u32[]{:S(2)}) collective-permute-start(f32[13,16,256]{2,1,0:T(8,128)S(1)} %get-tuple-element.69), channel_id=1, source_target_pairs={{0,1},{1,0},{2,3},{3,2},{4,5},{5,4},{6,7},{7,6},{8,16},{9,17},{10,... | collective-permute-start | bytes 638984 | tf_op jit(solution)/shard_map/ppermute | solution.py:610
  21.0 5.8 %collective-permute-start.7 = (f32[13,16,256]{2,1,0:T(8,128)S(1)}, f32[13,16,256]{2,1,0:T(8,128)S(1)}, u32[]{:S(2)}, u32[]{:S(2)}) collective-permute-start(f32[13,16,256]{2,1,0:T(8,128)S(1)} %get-tuple-element.70), channel_id=1, source_target_pairs={{0,8},{1,9},{2,10},{3,11},{4,12},{5,13},{6,14},{7,15},{8,0},{9,1},... | collective-permute-start | bytes 638984 | tf_op jit(solution)/shard_map/ppermute | solution.py:611
  23.2 6.1 %collective-permute-start.4 = (f32[26,8,256]{2,1,0:T(8,128)S(1)}, f32[26,8,256]{2,1,0:T(8,128)S(1)}, u32[]{:S(2)}, u32[]{:S(2)}) collective-permute-start(f32[26,8,256]{2,1,0:T(8,128)S(1)} %get-tuple-element.62), channel_id=1, source_target_pairs={{0,1},{1,0},{2,3},{3,2},{4,5},{5,4},{6,7},{7,6},{8,16},{9,17},{10,... | collective-permute-start | bytes 638984 | tf_op jit(solution)/shard_map/ppermute | solution.py:610
  25.4 3.8 %collective-permute-start.5 = (f32[26,8,256]{2,1,0:T(8,128)S(1)}, f32[26,8,256]{2,1,0:T(8,128)S(1)}, u32[]{:S(2)}, u32[]{:S(2)}) collective-permute-start(f32[26,8,256]{2,1,0:T(8,128)S(1)} %get-tuple-element.63), channel_id=1, source_target_pairs={{0,8},{1,9},{2,10},{3,11},{4,12},{5,13},{6,14},{7,15},{8,0},{9,1},... | collective-permute-start | bytes 638984 | tf_op jit(solution)/shard_map/ppermute | solution.py:611
  41.9 2.8 %collective-permute-start.8 = (f32[12,4,256]{2,1,0:T(4,128)S(1)}, f32[12,4,256]{2,1,0:T(4,128)S(1)}, u32[]{:S(2)}, u32[]{:S(2)}) collective-permute-start(f32[12,4,256]{2,1,0:T(4,128)S(1)} %get-tuple-element.75), channel_id=1, source_target_pairs={{0,8},{1,2},{2,1},{3,4},{4,3},{5,6},{6,5},{7,15},{8,0},{9,10},{10,... | collective-permute-start | bytes 147464 | tf_op jit(solution)/shard_map/ppermute | solution.py:610
  42.1 4.1 %collective-permute-start.9 = (f32[12,4,256]{2,1,0:T(4,128)S(1)}, f32[12,4,256]{2,1,0:T(4,128)S(1)}, u32[]{:S(2)}, u32[]{:S(2)}) collective-permute-start(f32[12,4,256]{2,1,0:T(4,128)S(1)} %get-tuple-element.76), channel_id=1, source_target_pairs={{0,1},{1,0},{2,3},{3,2},{4,5},{5,4},{6,7},{7,6},{8,9},{9,8},{10,11... | collective-permute-start | bytes 147464 | tf_op jit(solution)/shard_map/ppermute | solution.py:611
  44.0 4.6 %collective-permute-start.12 = (f32[5,16,256]{2,1,0:T(8,128)S(1)}, f32[5,16,256]{2,1,0:T(8,128)S(1)}, u32[]{:S(2)}, u32[]{:S(2)}) collective-permute-start(f32[5,16,256]{2,1,0:T(8,128)S(1)} %get-tuple-element.82), channel_id=1, source_target_pairs={{0,1},{1,0},{2,3},{3,2},{4,5},{5,4},{6,7},{7,6},{8,16},{9,17},{10,... | collective-permute-start | bytes 245768 | tf_op jit(solution)/shard_map/ppermute | solution.py:610
  44.2 4.4 %collective-permute-start.13 = (f32[5,16,256]{2,1,0:T(8,128)S(1)}, f32[5,16,256]{2,1,0:T(8,128)S(1)}, u32[]{:S(2)}, u32[]{:S(2)}) collective-permute-start(f32[5,16,256]{2,1,0:T(8,128)S(1)} %get-tuple-element.83), channel_id=1, source_target_pairs={{0,8},{1,9},{2,10},{3,11},{4,12},{5,13},{6,14},{7,15},{8,0},{9,1},... | collective-permute-start | bytes 245768 | tf_op jit(solution)/shard_map/ppermute | solution.py:611
  46.3 4.3 %collective-permute-start.10 = (f32[6,8,256]{2,1,0:T(8,128)S(1)}, f32[6,8,256]{2,1,0:T(8,128)S(1)}, u32[]{:S(2)}, u32[]{:S(2)}) collective-permute-start(f32[6,8,256]{2,1,0:T(8,128)S(1)} %get-tuple-element.80), channel_id=1, source_target_pairs={{0,1},{1,0},{2,3},{3,2},{4,5},{5,4},{6,7},{7,6},{8,16},{9,17},{10,... | collective-permute-start | bytes 147464 | tf_op jit(solution)/shard_map/ppermute | solution.py:610
  48.5 2.1 %collective-permute-start.11 = (f32[6,8,256]{2,1,0:T(8,128)S(1)}, f32[6,8,256]{2,1,0:T(8,128)S(1)}, u32[]{:S(2)}, u32[]{:S(2)}) collective-permute-start(f32[6,8,256]{2,1,0:T(8,128)S(1)} %get-tuple-element.81), channel_id=1, source_target_pairs={{0,8},{1,9},{2,10},{3,11},{4,12},{5,13},{6,14},{7,15},{8,0},{9,1},... | collective-permute-start | bytes 147464 | tf_op jit(solution)/shard_map/ppermute | solution.py:611

commit v9 on v8

--- a/solution.py
+++ b/solution.py
@@ -404,6 +404,14 @@
         by_parity(flags[ODD_X], write, even_out, odd_out)
 
     by_side(flags[ODD_Y], write_corners, (even_vel, odd_vel))
+
+
+def ready_kernel(flags, wide, inverse, corr, source, placed):
+    size_x, size_y, size_z = corr.shape
+    for k in range(size_x):
+        source[k] = inverse[k] * wide[k]
+        placed[k] = jnp.zeros(placed.shape[1:], F32)
+        placed[k, WIDE : WIDE + size_y, :] = corr[k]
 
 
 def beside_terms(before, here, after, x, tile, coefs):
@@ -454,8 +462,8 @@
 ):
     source, left, update, whole = scratch
     inverse, b0, b1, _ = coefs
-    size_x, size_y, size_z = corr.shape
-    rows = size_y + 2 * WIDE
+    size_x, rows, size_z = corr.shape
+    size_y = rows - 2 * WIDE
     span = size_x + 2 * WIDE
     row = lax.broadcasted_iota(jnp.int32, (rows, size_z), 0)
     has_low_x, has_high_x = flags[LOW_X] != 0, flags[HIGH_X] != 0
@@ -494,7 +502,7 @@
     by_side(flags[ODD_X], halos, early, late)
 
     for k in range(size_x):
-        source[WIDE + k] = inverse[WIDE + k] * wide[k]
+        source[WIDE + k] = wide[k]
 
     low_in, high_in = WIDE, WIDE + size_x - 1
     source[low_in - 1] = source[low_in - 1] + inverse[low_in - 1] * sides[0]
@@ -527,10 +535,8 @@
     whole[size_x + 1] = jnp.where(has_high_x & inner, whole[size_x + 1] + beside, 0.0)
 
     own = run(box_planes, everything, box_rows, tuple(own_planes))
-    zeros = jnp.zeros((rows - size_y, size_z), F32)
     for k in range(size_x):
-        placed = pltpu.roll(jnp.concatenate([corr[k], zeros], axis=0), WIDE, 0)
-        whole[k + 1] = jnp.where(inner, placed + own[WIDE + k], 0.0)
+        whole[k + 1] = jnp.where(inner, corr[k] + own[WIDE + k], 0.0)
 
     beside = run(box_planes, lowest, tile_row < WIDE + DEPTH, tuple(own_planes))
     for k in range(size_x):
@@ -657,7 +663,9 @@
             *velocity_y,
             micros=0.01,
         )
-        return (*own, *swap((even, odd), x_pairs)[::-1], *coefs, corr, *early[::-1])
+        wide, *rest_own = own
+        source, placed = kernel_call(ready_kernel, [wide_own] * 2, [], wide, coefs[1], corr, micros=0.01)
+        return (source, *rest_own, *swap((even, odd), x_pairs)[::-1], *coefs, placed, *early[::-1])
 
     corr, rest, *messages = kernel_call(
         coarse_kernel,

time: 62.8 us -> 62.8 us (level)
    pallas_call x10 -> x12, Pallas kernels: 9.87 us -> 9.91 us  [call(): pl.pallas_call(kernel, out_shape=[jax.ShapeDtypeStruct(kind, F32) if isin...]
where the time goes in v9:
time: 62.8 us; the launch traced here: 62.6 us
  starting transfers between devices  20.7 us (33%)
  blocking collectives  18.8 us (30%)
  waiting for transfers between devices  12.4 us (20%)
  Pallas kernels  9.91 us (16%)
  between operations  0.75 us (1%)
    all_to_all x2, blocking collectives, share(): return lax.all_to_all(row, AXES, 0, 0)  18.8 us
    pallas_call x12, Pallas kernels, call(): pl.pallas_call(kernel, out_shape=[jax.ShapeDtypeStruct(kind, F32) if isin...  9.91 us
    ppermute x7, starting transfers between devices, swap(): return [lax.ppermute(messages[0], AXES, pairs[0]), odd]  8.04 us
    all_to_all x1, starting transfers between devices, share(): return lax.all_to_all(row, AXES, 0, 0)  7.3 us
    ppermute x7, waiting for transfers between devices, swap(): odd = lax.ppermute(messages[1], AXES, pairs[1])  5.63 us
    ppermute x7, starting transfers between devices, swap(): odd = lax.ppermute(messages[1], AXES, pairs[1])  5.39 us
    all_to_all x1, waiting for transfers between devices, share(): return lax.all_to_all(row, AXES, 0, 0)  3.85 us
    ppermute x7, waiting for transfers between devices, swap(): return [lax.ppermute(messages[0], AXES, pairs[0]), odd]  2.9 us
  transfers between devices with their start and end apart: 15, of which 6 were waited for; matrix products, arithmetic and copies ran while one was open for 0% of the time, Pallas kernels for 2%

profile of v9, /device:TPU:0, one launch (start us, length us, event | category | flops | bytes accessed | tf_op | source)
XLA Modules:
  0.0 62.6 jit_solution(9215395553810431519)
XLA Ops:
  0.6 2.9 %shard_map.59 = (f32[32,1,256]{2,1,0:T(1,128)}, f32[8,16,256]{2,1,0:T(8,128)S(1)}, bf16[32,8,16,256]{3,2,1,0:T(8,128)(2,1)S(1)}, f32[3,8,16,256]{3,2,1,0:T(8,128)S(1)}, f32[32,1024]{1,0:T(8,128)S(1)}) custom-call(f32[8,16,256]{2,1,0:T(8,128)} %refs_0_.1, bf16[32,8,16,256]{3,2,1,0:T(8,128)(2,1)} %refs_1_.1, f32[3,8,16,256]{3,2,1,0:T(8,128)} %refs_2_.1, ...), custom_call_target="tpu_custom_call" | custom-call | bytes 7200000 | tf_op jit(solution)/shard_map/pallas_call | solution.py:59
  3.6 7.3 %all-to-all-start = ((f32[32,1,256]{2,1,0:T(1,128)}), f32[32,1,256]{2,1,0:T(1,128)S(1)}, u32[]{:S(2)}, u32[]{:S(2)}) async-start(f32[32,1,256]{2,1,0:T(1,128)} %get-tuple-element.52), calls=%async_computation | async-start | bytes 65536 | tf_op jit(solution)/shard_map/all_to_all | solution.py:620
  10.9 0.3 collective-permute-start.3
  11.2 3.0 %collective-permute-start.2 = (f32[3,8,4,256]{3,2,1,0:T(4,128)S(1)}, f32[3,8,4,256]{3,2,1,0:T(4,128)S(1)}, u32[]{:S(2)}, u32[]{:S(2)}) collective-permute-start(f32[3,8,4,256]{3,2,1,0:T(4,128)S(1)} %get-tuple-element.57.refs_5_), channel_id=1, source_target_pairs={{0,1},{1,0},{2,3},{3,2},{4,5},{5,4},{6,7},{7,6},{8,9},{9,8},{10,11... | collective-permute-start | bytes 294920 | tf_op jit(solution)/shard_map/ppermute | solution.py:617
  14.2 3.8 %all-to-all-done.refs_0_ = f32[32,1,256]{2,1,0:T(1,128)S(1)} async-done(((f32[32,1,256]{2,1,0:T(1,128)}), f32[32,1,256]{2,1,0:T(1,128)S(1)}, u32[]{:S(2)}, u32[]{:S(2)}) %all-to-all-start) | async-done | bytes 32800 | tf_op jit(solution)/shard_map/all_to_all | solution.py:620
  18.1 0.7 %shard_map.61 = (f32[8,16,256]{2,1,0:T(8,128)S(1)}, f32[8,16,256]{2,1,0:T(8,128)S(1)}, f32[12,4,256]{2,1,0:T(4,128)S(1)}, f32[12,4,256]{2,1,0:T(4,128)S(1)}, f32...) custom-call(f32[32,1,256]{2,1,0:T(1,128)S(1)} %all-to-all-done.refs_0_, ...), custom_call_target="tpu_custom_call" | custom-call | bytes 5040000 | tf_op jit(solution)/shard_map/pallas_call | solution.py:59
  18.8 0.2 collective-permute-start
  19.0 2.0 %collective-permute-start.1 = (f32[12,4,256]{2,1,0:T(4,128)S(1)}, f32[12,4,256]{2,1,0:T(4,128)S(1)}, u32[]{:S(2)}, u32[]{:S(2)}) collective-permute-start(f32[12,4,256]{2,1,0:T(4,128)S(1)} %get-tuple-element.61), channel_id=1, source_target_pairs={{0,1},{1,0},{2,3},{3,2},{4,5},{5,4},{6,7},{7,6},{8,9},{9,8},{10,11... | collective-permute-start | bytes 147464 | tf_op jit(solution)/shard_map/ppermute | solution.py:617
  20.9 0.0 collective-permute-start.6
  21.0 0.0 collective-permute-done.3.refs_6_.refs_2_
  21.0 0.7 %collective-permute-start.7 = (f32[13,16,256]{2,1,0:T(8,128)S(1)}, f32[13,16,256]{2,1,0:T(8,128)S(1)}, u32[]{:S(2)}, u32[]{:S(2)}) collective-permute-start(f32[13,16,256]{2,1,0:T(8,128)S(1)} %get-tuple-element.76), channel_id=1, source_target_pairs={{0,8},{1,9},{2,10},{3,11},{4,12},{5,13},{6,14},{7,15},{8,0},{9,1},... | collective-permute-start | bytes 638984 | tf_op jit(solution)/shard_map/ppermute | solution.py:617
  21.7 0.0 collective-permute-done.2.refs_5_.refs_1_
  21.7 0.0 collective-permute-done.refs_2_
  21.7 1.3 %collective-permute-done.1.refs_3_ = f32[12,4,256]{2,1,0:T(4,128)S(1)} collective-permute-done((f32[12,4,256]{2,1,0:T(4,128)S(1)}, f32[12,4,256]{2,1,0:T(4,128)S(1)}, u32[]{:S(2)}, u32[]{:S(2)}) %collective-permute-start.1) | collective-permute-done | bytes 49184 | tf_op jit(solution)/shard_map/ppermute | solution.py:617
  23.1 0.1 shard_map.62
  23.2 2.2 %collective-permute-start.4 = (f32[26,8,256]{2,1,0:T(8,128)S(1)}, f32[26,8,256]{2,1,0:T(8,128)S(1)}, u32[]{:S(2)}, u32[]{:S(2)}) collective-permute-start(f32[26,8,256]{2,1,0:T(8,128)S(1)} %get-tuple-element.68), channel_id=1, source_target_pairs={{0,1},{1,0},{2,3},{3,2},{4,5},{5,4},{6,7},{7,6},{8,16},{9,17},{10,... | collective-permute-start | bytes 638984 | tf_op jit(solution)/shard_map/ppermute | solution.py:616
  25.4 0.0 collective-permute-start.5
  25.4 0.1 shard_map.63
  25.6 1.1 %collective-permute-done.6.refs_11_ = f32[13,16,256]{2,1,0:T(8,128)S(1)} collective-permute-done((f32[13,16,256]{2,1,0:T(8,128)S(1)}, f32[13,16,256]{2,1,0:T(8,128)S(1)}, u32[]{:S(2)}, u32[]{:S(2)}) %collective-permute-start.6) | collective-permute-done | bytes 213024 | tf_op jit(solution)/shard_map/ppermute | solution.py:616
  26.8 0.0 collective-permute-done.7.refs_12_
  26.8 2.5 %collective-permute-done.4.refs_3_ = f32[26,8,256]{2,1,0:T(8,128)S(1)} collective-permute-done((f32[26,8,256]{2,1,0:T(8,128)S(1)}, f32[26,8,256]{2,1,0:T(8,128)S(1)}, u32[]{:S(2)}, u32[]{:S(2)}) %collective-permute-start.4) | collective-permute-done | bytes 213024 | tf_op jit(solution)/shard_map/ppermute | solution.py:616
  29.3 0.0 collective-permute-done.5.refs_4_
  29.3 2.3 %shard_map.65 = (f32[8,16,256]{2,1,0:T(8,128)S(1)}, f32[8,16,256]{2,1,0:T(8,128)S(1)}, f32[32,1,256]{2,1,0:T(1,128)S(1)}, f32[8,24,256]{2,1,0:T(8,128)S(1)}, f32...) custom-call(f32[8,24,256]{2,1,0:T(8,128)S(1)} %get-tuple-element.65.refs_0_, ...), custom_call_target="tpu_custom_call" | custom-call | bytes 10800000 | tf_op jit(solution)/shard_map/pallas_call | solution.py:59
  31.6 9.4 %all_to_all.15.refs_1_ = f32[32,1,256]{2,1,0:T(1,128)S(1)} all-to-all(f32[32,1,256]{2,1,0:T(1,128)S(1)} %get-tuple-element.77), channel_id=1, replica_groups=mesh['gx'=4,'gy'=8] {'gx','gy'}, dimensions={0} | all-to-all | bytes 65536 | tf_op jit(solution)/shard_map/all_to_all | solution.py:620
  41.0 0.9 %shard_map.66 = (f32[8,16,256]{2,1,0:T(8,128)S(1)}, f32[8,16,256]{2,1,0:T(8,128)S(1)}, f32[8,16,256]{2,1,0:T(8,128)S(1)}, f32[8,128]{1,0:T(8,128)S(1)}, f32[12,4...) custom-call(f32[32,1,256]{2,1,0:T(1,128)S(1)} %all-to-all-done.refs_0_, ...), custom_call_target="tpu_custom_call" | custom-call | bytes 5040000 | tf_op jit(solution)/shard_map/pallas_call | solution.py:59
  41.9 0.2 collective-permute-start.8
  42.1 1.8 %collective-permute-start.9 = (f32[12,4,256]{2,1,0:T(4,128)S(1)}, f32[12,4,256]{2,1,0:T(4,128)S(1)}, u32[]{:S(2)}, u32[]{:S(2)}) collective-permute-start(f32[12,4,256]{2,1,0:T(4,128)S(1)} %get-tuple-element.82), channel_id=1, source_target_pairs={{0,1},{1,0},{2,3},{3,2},{4,5},{5,4},{6,7},{7,6},{8,9},{9,8},{10,11... | collective-permute-start | bytes 147464 | tf_op jit(solution)/shard_map/ppermute | solution.py:617
  43.9 0.2 collective-permute-start.12
  44.1 0.5 collective-permute-start.13
  44.7 0.0 collective-permute-done.8.refs_2_
  44.7 1.5 %collective-permute-done.9.refs_3_ = f32[12,4,256]{2,1,0:T(4,128)S(1)} collective-permute-done((f32[12,4,256]{2,1,0:T(4,128)S(1)}, f32[12,4,256]{2,1,0:T(4,128)S(1)}, u32[]{:S(2)}, u32[]{:S(2)}) %collective-permute-start.9) | collective-permute-done | bytes 49184 | tf_op jit(solution)/shard_map/ppermute | solution.py:617
  46.2 0.1 shard_map.67
  46.3 2.2 %collective-permute-start.10 = (f32[6,8,256]{2,1,0:T(8,128)S(1)}, f32[6,8,256]{2,1,0:T(8,128)S(1)}, u32[]{:S(2)}, u32[]{:S(2)}) collective-permute-start(f32[6,8,256]{2,1,0:T(8,128)S(1)} %get-tuple-element.87), channel_id=1, source_target_pairs={{0,1},{1,0},{2,3},{3,2},{4,5},{5,4},{6,7},{7,6},{8,16},{9,17},{10,... | collective-permute-start | bytes 147464 | tf_op jit(solution)/shard_map/ppermute | solution.py:616
  48.5 0.0 collective-permute-start.11
  48.6 0.0 collective-permute-done.12.refs_11_
  48.6 0.0 collective-permute-done.13.refs_12_
  48.6 2.0 %collective-permute-done.10.refs_3_ = f32[6,8,256]{2,1,0:T(8,128)S(1)} collective-permute-done((f32[6,8,256]{2,1,0:T(8,128)S(1)}, f32[6,8,256]{2,1,0:T(8,128)S(1)}, u32[]{:S(2)}, u32[]{:S(2)}) %collective-permute-start.10) | collective-permute-done | bytes 49184 | tf_op jit(solution)/shard_map/ppermute | solution.py:616
  50.6 0.0 collective-permute-done.11.refs_4_
  50.6 1.7 %shard_map.69 = (f32[8,16,256]{2,1,0:T(8,128)S(1)}, f32[8,16,256]{2,1,0:T(8,128)S(1)}, f32[32,1,256]{2,1,0:T(1,128)S(1)}) custom-call(f32[8,24,256]{2,1,0:T(8,128)S(1)} %get-tuple-element.84.refs_0_, f32[2,24,256]{2,1,0:T(8,128)S(1)} %get-tuple-element.85.refs_1_, f32[2,8,256]{2,1,0:T(8,128)S(1)} %get-tuple-element.86.refs_2_, ...), custom_call_target="tpu_custom_call" | custom-call | bytes 9000000 | tf_op jit(solution)/shard_map/pallas_call | solution.py:59
  52.3 9.4 %all_to_all.16.refs_0_ = f32[32,1,256]{2,1,0:T(1,128)S(1)} all-to-all(f32[32,1,256]{2,1,0:T(1,128)S(1)} %get-tuple-element.97), channel_id=1, replica_groups=mesh['gx'=4,'gy'=8] {'gx','gy'}, dimensions={0} | all-to-all | bytes 65536 | tf_op jit(solution)/shard_map/all_to_all | solution.py:620
  61.7 0.9 %shard_map.70 = (f32[8,16,256]{2,1,0:T(8,128)}, f32[8,16,256]{2,1,0:T(8,128)}) custom-call(f32[32,1,256]{2,1,0:T(1,128)S(1)} %all_to_all.16.refs_0_, f32[8,128]{1,0:T(8,128)S(1)} %get-tuple-element.98.refs_1_, f32[8,16,256]{2,1,0:T(8,128)S(1)} %get-tuple-element.99.refs_2_, f32[8,16,256]{2,1,0:T(8,128)S(1)} %get-tuple-element.100.refs_3_, ...), custom_call_target="tpu_custom_call" | custom-call | bytes 5040000 | tf_op jit(solution)/shard_map/pallas_call | solution.py:59
  (3 shorter events, 0.1 us)
Async XLA Ops:
  3.6 14.5 %all-to-all-start = ((f32[32,1,256]{2,1,0:T(1,128)}), f32[32,1,256]{2,1,0:T(1,128)S(1)}, u32[]{:S(2)}, u32[]{:S(2)}) async-start(f32[32,1,256]{2,1,0:T(1,128)} %get-tuple-element.52), calls=%async_computation | async-start | bytes 65536 | tf_op jit(solution)/shard_map/all_to_all | solution.py:620
  10.9 10.1 %collective-permute-start.3 = (f32[3,8,4,256]{3,2,1,0:T(4,128)S(1)}, f32[3,8,4,256]{3,2,1,0:T(4,128)S(1)}, u32[]{:S(2)}, u32[]{:S(2)}) collective-permute-start(f32[3,8,4,256]{3,2,1,0:T(4,128)S(1)} %get-tuple-element.62), channel_id=1, source_target_pairs={{0,8},{1,2},{2,1},{3,4},{4,3},{5,6},{6,5},{7,15},{8,0},{9,10},{10,... | collective-permute-start | bytes 294920 | tf_op jit(solution)/shard_map/ppermute | solution.py:616
  11.2 10.5 %collective-permute-start.2 = (f32[3,8,4,256]{3,2,1,0:T(4,128)S(1)}, f32[3,8,4,256]{3,2,1,0:T(4,128)S(1)}, u32[]{:S(2)}, u32[]{:S(2)}) collective-permute-start(f32[3,8,4,256]{3,2,1,0:T(4,128)S(1)} %get-tuple-element.57.refs_5_), channel_id=1, source_target_pairs={{0,1},{1,0},{2,3},{3,2},{4,5},{5,4},{6,7},{7,6},{8,9},{9,8},{10,11... | collective-permute-start | bytes 294920 | tf_op jit(solution)/shard_map/ppermute | solution.py:617
  18.8 2.9 %collective-permute-start = (f32[12,4,256]{2,1,0:T(4,128)S(1)}, f32[12,4,256]{2,1,0:T(4,128)S(1)}, u32[]{:S(2)}, u32[]{:S(2)}) collective-permute-start(f32[12,4,256]{2,1,0:T(4,128)S(1)} %get-tuple-element.60), channel_id=1, source_target_pairs={{0,8},{1,2},{2,1},{3,4},{4,3},{5,6},{6,5},{7,15},{8,0},{9,10},{10,... | collective-permute-start | bytes 147464 | tf_op jit(solution)/shard_map/ppermute | solution.py:616
  19.0 4.1 %collective-permute-start.1 = (f32[12,4,256]{2,1,0:T(4,128)S(1)}, f32[12,4,256]{2,1,0:T(4,128)S(1)}, u32[]{:S(2)}, u32[]{:S(2)}) collective-permute-start(f32[12,4,256]{2,1,0:T(4,128)S(1)} %get-tuple-element.61), channel_id=1, source_target_pairs={{0,1},{1,0},{2,3},{3,2},{4,5},{5,4},{6,7},{7,6},{8,9},{9,8},{10,11... | collective-permute-start | bytes 147464 | tf_op jit(solution)/shard_map/ppermute | solution.py:617
  20.9 5.8 %collective-permute-start.6 = (f32[13,16,256]{2,1,0:T(8,128)S(1)}, f32[13,16,256]{2,1,0:T(8,128)S(1)}, u32[]{:S(2)}, u32[]{:S(2)}) collective-permute-start(f32[13,16,256]{2,1,0:T(8,128)S(1)} %get-tuple-element.75), channel_id=1, source_target_pairs={{0,1},{1,0},{2,3},{3,2},{4,5},{5,4},{6,7},{7,6},{8,16},{9,17},{10,... | collective-permute-start | bytes 638984 | tf_op jit(solution)/shard_map/ppermute | solution.py:616
  21.0 5.8 %collective-permute-start.7 = (f32[13,16,256]{2,1,0:T(8,128)S(1)}, f32[13,16,256]{2,1,0:T(8,128)S(1)}, u32[]{:S(2)}, u32[]{:S(2)}) collective-permute-start(f32[13,16,256]{2,1,0:T(8,128)S(1)} %get-tuple-element.76), channel_id=1, source_target_pairs={{0,8},{1,9},{2,10},{3,11},{4,12},{5,13},{6,14},{7,15},{8,0},{9,1},... | collective-permute-start | bytes 638984 | tf_op jit(solution)/shard_map/ppermute | solution.py:617
  23.2 6.1 %collective-permute-start.4 = (f32[26,8,256]{2,1,0:T(8,128)S(1)}, f32[26,8,256]{2,1,0:T(8,128)S(1)}, u32[]{:S(2)}, u32[]{:S(2)}) collective-permute-start(f32[26,8,256]{2,1,0:T(8,128)S(1)} %get-tuple-element.68), channel_id=1, source_target_pairs={{0,1},{1,0},{2,3},{3,2},{4,5},{5,4},{6,7},{7,6},{8,16},{9,17},{10,... | collective-permute-start | bytes 638984 | tf_op jit(solution)/shard_map/ppermute | solution.py:616
  25.4 3.8 %collective-permute-start.5 = (f32[26,8,256]{2,1,0:T(8,128)S(1)}, f32[26,8,256]{2,1,0:T(8,128)S(1)}, u32[]{:S(2)}, u32[]{:S(2)}) collective-permute-start(f32[26,8,256]{2,1,0:T(8,128)S(1)} %get-tuple-element.69), channel_id=1, source_target_pairs={{0,8},{1,9},{2,10},{3,11},{4,12},{5,13},{6,14},{7,15},{8,0},{9,1},... | collective-permute-start | bytes 638984 | tf_op jit(solution)/shard_map/ppermute | solution.py:617
  41.9 2.8 %collective-permute-start.8 = (f32[12,4,256]{2,1,0:T(4,128)S(1)}, f32[12,4,256]{2,1,0:T(4,128)S(1)}, u32[]{:S(2)}, u32[]{:S(2)}) collective-permute-start(f32[12,4,256]{2,1,0:T(4,128)S(1)} %get-tuple-element.81), channel_id=1, source_target_pairs={{0,8},{1,2},{2,1},{3,4},{4,3},{5,6},{6,5},{7,15},{8,0},{9,10},{10,... | collective-permute-start | bytes 147464 | tf_op jit(solution)/shard_map/ppermute | solution.py:616
  42.1 4.1 %collective-permute-start.9 = (f32[12,4,256]{2,1,0:T(4,128)S(1)}, f32[12,4,256]{2,1,0:T(4,128)S(1)}, u32[]{:S(2)}, u32[]{:S(2)}) collective-permute-start(f32[12,4,256]{2,1,0:T(4,128)S(1)} %get-tuple-element.82), channel_id=1, source_target_pairs={{0,1},{1,0},{2,3},{3,2},{4,5},{5,4},{6,7},{7,6},{8,9},{9,8},{10,11... | collective-permute-start | bytes 147464 | tf_op jit(solution)/shard_map/ppermute | solution.py:617
  43.9 4.6 %collective-permute-start.12 = (f32[5,16,256]{2,1,0:T(8,128)S(1)}, f32[5,16,256]{2,1,0:T(8,128)S(1)}, u32[]{:S(2)}, u32[]{:S(2)}) collective-permute-start(f32[5,16,256]{2,1,0:T(8,128)S(1)} %get-tuple-element.90), channel_id=1, source_target_pairs={{0,1},{1,0},{2,3},{3,2},{4,5},{5,4},{6,7},{7,6},{8,16},{9,17},{10,... | collective-permute-start | bytes 245768 | tf_op jit(solution)/shard_map/ppermute | solution.py:616
  44.1 4.4 %collective-permute-start.13 = (f32[5,16,256]{2,1,0:T(8,128)S(1)}, f32[5,16,256]{2,1,0:T(8,128)S(1)}, u32[]{:S(2)}, u32[]{:S(2)}) collective-permute-start(f32[5,16,256]{2,1,0:T(8,128)S(1)} %get-tuple-element.91), channel_id=1, source_target_pairs={{0,8},{1,9},{2,10},{3,11},{4,12},{5,13},{6,14},{7,15},{8,0},{9,1},... | collective-permute-start | bytes 245768 | tf_op jit(solution)/shard_map/ppermute | solution.py:617
  46.3 4.3 %collective-permute-start.10 = (f32[6,8,256]{2,1,0:T(8,128)S(1)}, f32[6,8,256]{2,1,0:T(8,128)S(1)}, u32[]{:S(2)}, u32[]{:S(2)}) collective-permute-start(f32[6,8,256]{2,1,0:T(8,128)S(1)} %get-tuple-element.87), channel_id=1, source_target_pairs={{0,1},{1,0},{2,3},{3,2},{4,5},{5,4},{6,7},{7,6},{8,16},{9,17},{10,... | collective-permute-start | bytes 147464 | tf_op jit(solution)/shard_map/ppermute | solution.py:616
  48.5 2.1 %collective-permute-start.11 = (f32[6,8,256]{2,1,0:T(8,128)S(1)}, f32[6,8,256]{2,1,0:T(8,128)S(1)}, u32[]{:S(2)}, u32[]{:S(2)}) collective-permute-start(f32[6,8,256]{2,1,0:T(8,128)S(1)} %get-tuple-element.88), channel_id=1, source_target_pairs={{0,8},{1,9},{2,10},{3,11},{4,12},{5,13},{6,14},{7,15},{8,0},{9,1},... | collective-permute-start | bytes 147464 | tf_op jit(solution)/shard_map/ppermute | solution.py:617

commit v10 on v9

--- a/solution.py
+++ b/solution.py
@@ -565,7 +565,7 @@
 
 
 def search_kernel(
-    flags, wide, sides, past, odd_late, even_late, diagonal, own0, own1, own2, own3, corr, odd_early, even_early, vectors,
+    flags, wide, sides, past, odd_late, even_late, diagonal, own0, own1, own2, own3, corr, even_early, odd_early, vectors,
     right_side, search, image, out, halo0, halo1, halo2, halo3, stage, wide_vel, *scratch
 ):
     halos = (halo0, halo1, halo2, halo3)
@@ -578,7 +578,7 @@
 
 
 def smoothed_kernel(
-    flags, wide, sides, past, odd_late, even_late, diagonal, own0, own1, own2, own3, corr, odd_early, even_early, halo0,
+    flags, wide, sides, past, odd_late, even_late, diagonal, own0, own1, own2, own3, corr, even_early, odd_early, halo0,
     halo1, halo2, halo3, middle, smoothed, turned, out, *scratch
 ):
     early, late = (even_early, odd_early), (even_late, odd_late)
@@ -665,7 +665,7 @@
         )
         wide, *rest_own = own
         source, placed = kernel_call(ready_kernel, [wide_own] * 2, [], wide, coefs[1], corr, micros=0.01)
-        return (source, *rest_own, *swap((even, odd), x_pairs)[::-1], *coefs, placed, *early[::-1])
+        return (source, *rest_own, *swap((even, odd), x_pairs)[::-1], *coefs, placed, *early)
 
     corr, rest, *messages = kernel_call(
         coarse_kernel,

time: 62.8 us -> 62.8 us (level)
  starting transfers between devices: 20.7 us -> 19.7 us
  waiting for transfers between devices: 12.4 us -> 13.4 us
    ppermute x7, starting transfers between devices: 8.04 us -> 6.82 us  [swap(): return [lax.ppermute(messages[0], AXES, pairs[0]), odd]]
    ppermute x7, waiting for transfers between devices: 2.9 us -> 3.89 us  [swap(): return [lax.ppermute(messages[0], AXES, pairs[0]), odd]]
where the time goes in v10:
time: 62.8 us; the launch traced here: 62.6 us
  starting transfers between devices  19.7 us (31%)
  blocking collectives  18.8 us (30%)
  waiting for transfers between devices  13.4 us (21%)
  Pallas kernels  9.91 us (16%)
  between operations  0.76 us (1%)
    all_to_all x2, blocking collectives, share(): return lax.all_to_all(row, AXES, 0, 0)  18.8 us
    pallas_call x12, Pallas kernels, call(): pl.pallas_call(kernel, out_shape=[jax.ShapeDtypeStruct(kind, F32) if isin...  9.91 us
    all_to_all x1, starting transfers between devices, share(): return lax.all_to_all(row, AXES, 0, 0)  7.3 us
    ppermute x7, starting transfers between devices, swap(): return [lax.ppermute(messages[0], AXES, pairs[0]), odd]  6.82 us
    ppermute x7, waiting for transfers between devices, swap(): odd = lax.ppermute(messages[1], AXES, pairs[1])  5.63 us
    ppermute x7, starting transfers between devices, swap(): odd = lax.ppermute(messages[1], AXES, pairs[1])  5.62 us
    ppermute x7, waiting for transfers between devices, swap(): return [lax.ppermute(messages[0], AXES, pairs[0]), odd]  3.89 us
    all_to_all x1, waiting for transfers between devices, share(): return lax.all_to_all(row, AXES, 0, 0)  3.85 us
  transfers between devices with their start and end apart: 15, of which 6 were waited for; matrix products, arithmetic and copies ran while one was open for 0% of the time, Pallas kernels for 2%

profile of v10, /device:TPU:0, one launch (start us, length us, event | category | flops | bytes accessed | tf_op | source)
XLA Modules:
  0.0 62.6 jit_solution(2305729122531533879)
XLA Ops:
  0.6 2.9 %shard_map.59 = (f32[32,1,256]{2,1,0:T(1,128)}, f32[8,16,256]{2,1,0:T(8,128)S(1)}, bf16[32,8,16,256]{3,2,1,0:T(8,128)(2,1)S(1)}, f32[3,8,16,256]{3,2,1,0:T(8,128)S(1)}, f32[32,1024]{1,0:T(8,128)S(1)}) custom-call(f32[8,16,256]{2,1,0:T(8,128)} %refs_0_.1, bf16[32,8,16,256]{3,2,1,0:T(8,128)(2,1)} %refs_1_.1, f32[3,8,16,256]{3,2,1,0:T(8,128)} %refs_2_.1, ...), custom_call_target="tpu_custom_call" | custom-call | bytes 7200000 | tf_op jit(solution)/shard_map/pallas_call | solution.py:59
  3.6 7.3 %all-to-all-start = ((f32[32,1,256]{2,1,0:T(1,128)}), f32[32,1,256]{2,1,0:T(1,128)S(1)}, u32[]{:S(2)}, u32[]{:S(2)}) async-start(f32[32,1,256]{2,1,0:T(1,128)} %get-tuple-element.52), calls=%async_computation | async-start | bytes 65536 | tf_op jit(solution)/shard_map/all_to_all | solution.py:620
  10.9 0.3 collective-permute-start.3
  11.2 3.0 %collective-permute-start.2 = (f32[3,8,4,256]{3,2,1,0:T(4,128)S(1)}, f32[3,8,4,256]{3,2,1,0:T(4,128)S(1)}, u32[]{:S(2)}, u32[]{:S(2)}) collective-permute-start(f32[3,8,4,256]{3,2,1,0:T(4,128)S(1)} %get-tuple-element.57.refs_5_), channel_id=1, source_target_pairs={{0,1},{1,0},{2,3},{3,2},{4,5},{5,4},{6,7},{7,6},{8,9},{9,8},{10,11... | collective-permute-start | bytes 294920 | tf_op jit(solution)/shard_map/ppermute | solution.py:617
  14.2 3.8 %all-to-all-done.refs_0_ = f32[32,1,256]{2,1,0:T(1,128)S(1)} async-done(((f32[32,1,256]{2,1,0:T(1,128)}), f32[32,1,256]{2,1,0:T(1,128)S(1)}, u32[]{:S(2)}, u32[]{:S(2)}) %all-to-all-start) | async-done | bytes 32800 | tf_op jit(solution)/shard_map/all_to_all | solution.py:620
  18.1 0.7 %shard_map.61 = (f32[8,16,256]{2,1,0:T(8,128)S(1)}, f32[8,16,256]{2,1,0:T(8,128)S(1)}, f32[12,4,256]{2,1,0:T(4,128)S(1)}, f32[12,4,256]{2,1,0:T(4,128)S(1)}, f32...) custom-call(f32[32,1,256]{2,1,0:T(1,128)S(1)} %all-to-all-done.refs_0_, ...), custom_call_target="tpu_custom_call" | custom-call | bytes 5040000 | tf_op jit(solution)/shard_map/pallas_call | solution.py:59
  18.8 0.2 collective-permute-start
  19.0 2.0 %collective-permute-start.1 = (f32[12,4,256]{2,1,0:T(4,128)S(1)}, f32[12,4,256]{2,1,0:T(4,128)S(1)}, u32[]{:S(2)}, u32[]{:S(2)}) collective-permute-start(f32[12,4,256]{2,1,0:T(4,128)S(1)} %get-tuple-element.61), channel_id=1, source_target_pairs={{0,1},{1,0},{2,3},{3,2},{4,5},{5,4},{6,7},{7,6},{8,9},{9,8},{10,11... | collective-permute-start | bytes 147464 | tf_op jit(solution)/shard_map/ppermute | solution.py:617
  20.9 0.0 collective-permute-start.6
  20.9 0.0 collective-permute-done.3.refs_6_.refs_2_
  20.9 0.2 collective-permute-start.7
  21.1 0.0 collective-permute-done.2.refs_5_.refs_1_
  21.1 0.0 collective-permute-done.refs_2_
  21.1 1.9 %collective-permute-done.1.refs_3_ = f32[12,4,256]{2,1,0:T(4,128)S(1)} collective-permute-done((f32[12,4,256]{2,1,0:T(4,128)S(1)}, f32[12,4,256]{2,1,0:T(4,128)S(1)}, u32[]{:S(2)}, u32[]{:S(2)}) %collective-permute-start.1) | collective-permute-done | bytes 49184 | tf_op jit(solution)/shard_map/ppermute | solution.py:617
  23.1 0.1 shard_map.62
  23.2 2.2 %collective-permute-start.4 = (f32[26,8,256]{2,1,0:T(8,128)S(1)}, f32[26,8,256]{2,1,0:T(8,128)S(1)}, u32[]{:S(2)}, u32[]{:S(2)}) collective-permute-start(f32[26,8,256]{2,1,0:T(8,128)S(1)} %get-tuple-element.68), channel_id=1, source_target_pairs={{0,1},{1,0},{2,3},{3,2},{4,5},{5,4},{6,7},{7,6},{8,16},{9,17},{10,... | collective-permute-start | bytes 638984 | tf_op jit(solution)/shard_map/ppermute | solution.py:616
  25.4 0.0 collective-permute-start.5
  25.4 0.1 shard_map.63
  25.6 0.0 collective-permute-done.6.refs_11_
  25.6 1.1 %collective-permute-done.7.refs_12_ = f32[13,16,256]{2,1,0:T(8,128)S(1)} collective-permute-done((f32[13,16,256]{2,1,0:T(8,128)S(1)}, f32[13,16,256]{2,1,0:T(8,128)S(1)}, u32[]{:S(2)}, u32[]{:S(2)}) %collective-permute-start.7) | collective-permute-done | bytes 213024 | tf_op jit(solution)/shard_map/ppermute | solution.py:616
  26.8 2.5 %collective-permute-done.4.refs_3_ = f32[26,8,256]{2,1,0:T(8,128)S(1)} collective-permute-done((f32[26,8,256]{2,1,0:T(8,128)S(1)}, f32[26,8,256]{2,1,0:T(8,128)S(1)}, u32[]{:S(2)}, u32[]{:S(2)}) %collective-permute-start.4) | collective-permute-done | bytes 213024 | tf_op jit(solution)/shard_map/ppermute | solution.py:616
  29.3 0.0 collective-permute-done.5.refs_4_
  29.3 2.3 %shard_map.65 = (f32[8,16,256]{2,1,0:T(8,128)S(1)}, f32[8,16,256]{2,1,0:T(8,128)S(1)}, f32[32,1,256]{2,1,0:T(1,128)S(1)}, f32[8,24,256]{2,1,0:T(8,128)S(1)}, f32...) custom-call(f32[8,24,256]{2,1,0:T(8,128)S(1)} %get-tuple-element.65.refs_0_, ...), custom_call_target="tpu_custom_call" | custom-call | bytes 10800000 | tf_op jit(solution)/shard_map/pallas_call | solution.py:59
  31.6 9.4 %all_to_all.15.refs_1_ = f32[32,1,256]{2,1,0:T(1,128)S(1)} all-to-all(f32[32,1,256]{2,1,0:T(1,128)S(1)} %get-tuple-element.77), channel_id=1, replica_groups=mesh['gx'=4,'gy'=8] {'gx','gy'}, dimensions={0} | all-to-all | bytes 65536 | tf_op jit(solution)/shard_map/all_to_all | solution.py:620
  41.0 0.9 %shard_map.66 = (f32[8,16,256]{2,1,0:T(8,128)S(1)}, f32[8,16,256]{2,1,0:T(8,128)S(1)}, f32[8,16,256]{2,1,0:T(8,128)S(1)}, f32[8,128]{1,0:T(8,128)S(1)}, f32[12,4...) custom-call(f32[32,1,256]{2,1,0:T(1,128)S(1)} %all-to-all-done.refs_0_, ...), custom_call_target="tpu_custom_call" | custom-call | bytes 5040000 | tf_op jit(solution)/shard_map/pallas_call | solution.py:59
  41.9 0.2 collective-permute-start.8
  42.1 1.8 %collective-permute-start.9 = (f32[12,4,256]{2,1,0:T(4,128)S(1)}, f32[12,4,256]{2,1,0:T(4,128)S(1)}, u32[]{:S(2)}, u32[]{:S(2)}) collective-permute-start(f32[12,4,256]{2,1,0:T(4,128)S(1)} %get-tuple-element.82), channel_id=1, source_target_pairs={{0,1},{1,0},{2,3},{3,2},{4,5},{5,4},{6,7},{7,6},{8,9},{9,8},{10,11... | collective-permute-start | bytes 147464 | tf_op jit(solution)/shard_map/ppermute | solution.py:617
  43.9 0.0 collective-permute-start.12
  43.9 0.3 collective-permute-start.13
  44.2 0.0 collective-permute-done.8.refs_2_
  44.2 2.0 %collective-permute-done.9.refs_3_ = f32[12,4,256]{2,1,0:T(4,128)S(1)} collective-permute-done((f32[12,4,256]{2,1,0:T(4,128)S(1)}, f32[12,4,256]{2,1,0:T(4,128)S(1)}, u32[]{:S(2)}, u32[]{:S(2)}) %collective-permute-start.9) | collective-permute-done | bytes 49184 | tf_op jit(solution)/shard_map/ppermute | solution.py:617
  46.2 0.1 shard_map.67
  46.3 2.2 %collective-permute-start.10 = (f32[6,8,256]{2,1,0:T(8,128)S(1)}, f32[6,8,256]{2,1,0:T(8,128)S(1)}, u32[]{:S(2)}, u32[]{:S(2)}) collective-permute-start(f32[6,8,256]{2,1,0:T(8,128)S(1)} %get-tuple-element.87), channel_id=1, source_target_pairs={{0,1},{1,0},{2,3},{3,2},{4,5},{5,4},{6,7},{7,6},{8,16},{9,17},{10,... | collective-permute-start | bytes 147464 | tf_op jit(solution)/shard_map/ppermute | solution.py:616
  48.5 0.0 collective-permute-start.11
  48.6 0.0 collective-permute-done.12.refs_11_
  48.6 0.0 collective-permute-done.13.refs_12_
  48.6 2.0 %collective-permute-done.10.refs_3_ = f32[6,8,256]{2,1,0:T(8,128)S(1)} collective-permute-done((f32[6,8,256]{2,1,0:T(8,128)S(1)}, f32[6,8,256]{2,1,0:T(8,128)S(1)}, u32[]{:S(2)}, u32[]{:S(2)}) %collective-permute-start.10) | collective-permute-done | bytes 49184 | tf_op jit(solution)/shard_map/ppermute | solution.py:616
  50.6 0.0 collective-permute-done.11.refs_4_
  50.6 1.7 %shard_map.69 = (f32[8,16,256]{2,1,0:T(8,128)S(1)}, f32[8,16,256]{2,1,0:T(8,128)S(1)}, f32[32,1,256]{2,1,0:T(1,128)S(1)}) custom-call(f32[8,24,256]{2,1,0:T(8,128)S(1)} %get-tuple-element.84.refs_0_, f32[2,24,256]{2,1,0:T(8,128)S(1)} %get-tuple-element.85.refs_1_, f32[2,8,256]{2,1,0:T(8,128)S(1)} %get-tuple-element.86.refs_2_, ...), custom_call_target="tpu_custom_call" | custom-call | bytes 9000000 | tf_op jit(solution)/shard_map/pallas_call | solution.py:59
  52.3 9.4 %all_to_all.16.refs_0_ = f32[32,1,256]{2,1,0:T(1,128)S(1)} all-to-all(f32[32,1,256]{2,1,0:T(1,128)S(1)} %get-tuple-element.97), channel_id=1, replica_groups=mesh['gx'=4,'gy'=8] {'gx','gy'}, dimensions={0} | all-to-all | bytes 65536 | tf_op jit(solution)/shard_map/all_to_all | solution.py:620
  61.7 0.9 %shard_map.70 = (f32[8,16,256]{2,1,0:T(8,128)}, f32[8,16,256]{2,1,0:T(8,128)}) custom-call(f32[32,1,256]{2,1,0:T(1,128)S(1)} %all_to_all.16.refs_0_, f32[8,128]{1,0:T(8,128)S(1)} %get-tuple-element.98.refs_1_, f32[8,16,256]{2,1,0:T(8,128)S(1)} %get-tuple-element.99.refs_2_, f32[8,16,256]{2,1,0:T(8,128)S(1)} %get-tuple-element.100.refs_3_, ...), custom_call_target="tpu_custom_call" | custom-call | bytes 5040000 | tf_op jit(solution)/shard_map/pallas_call | solution.py:59
  (3 shorter events, 0.1 us)
Async XLA Ops:
  3.6 14.5 %all-to-all-start = ((f32[32,1,256]{2,1,0:T(1,128)}), f32[32,1,256]{2,1,0:T(1,128)S(1)}, u32[]{:S(2)}, u32[]{:S(2)}) async-start(f32[32,1,256]{2,1,0:T(1,128)} %get-tuple-element.52), calls=%async_computation | async-start | bytes 65536 | tf_op jit(solution)/shard_map/all_to_all | solution.py:620
  10.9 10.0 %collective-permute-start.3 = (f32[3,8,4,256]{3,2,1,0:T(4,128)S(1)}, f32[3,8,4,256]{3,2,1,0:T(4,128)S(1)}, u32[]{:S(2)}, u32[]{:S(2)}) collective-permute-start(f32[3,8,4,256]{3,2,1,0:T(4,128)S(1)} %get-tuple-element.62), channel_id=1, source_target_pairs={{0,8},{1,2},{2,1},{3,4},{4,3},{5,6},{6,5},{7,15},{8,0},{9,10},{10,... | collective-permute-start | bytes 294920 | tf_op jit(solution)/shard_map/ppermute | solution.py:616
  11.2 9.9 %collective-permute-start.2 = (f32[3,8,4,256]{3,2,1,0:T(4,128)S(1)}, f32[3,8,4,256]{3,2,1,0:T(4,128)S(1)}, u32[]{:S(2)}, u32[]{:S(2)}) collective-permute-start(f32[3,8,4,256]{3,2,1,0:T(4,128)S(1)} %get-tuple-element.57.refs_5_), channel_id=1, source_target_pairs={{0,1},{1,0},{2,3},{3,2},{4,5},{5,4},{6,7},{7,6},{8,9},{9,8},{10,11... | collective-permute-start | bytes 294920 | tf_op jit(solution)/shard_map/ppermute | solution.py:617
  18.8 2.4 %collective-permute-start = (f32[12,4,256]{2,1,0:T(4,128)S(1)}, f32[12,4,256]{2,1,0:T(4,128)S(1)}, u32[]{:S(2)}, u32[]{:S(2)}) collective-permute-start(f32[12,4,256]{2,1,0:T(4,128)S(1)} %get-tuple-element.60), channel_id=1, source_target_pairs={{0,8},{1,2},{2,1},{3,4},{4,3},{5,6},{6,5},{7,15},{8,0},{9,10},{10,... | collective-permute-start | bytes 147464 | tf_op jit(solution)/shard_map/ppermute | solution.py:616
  19.0 4.1 %collective-permute-start.1 = (f32[12,4,256]{2,1,0:T(4,128)S(1)}, f32[12,4,256]{2,1,0:T(4,128)S(1)}, u32[]{:S(2)}, u32[]{:S(2)}) collective-permute-start(f32[12,4,256]{2,1,0:T(4,128)S(1)} %get-tuple-element.61), channel_id=1, source_target_pairs={{0,1},{1,0},{2,3},{3,2},{4,5},{5,4},{6,7},{7,6},{8,9},{9,8},{10,11... | collective-permute-start | bytes 147464 | tf_op jit(solution)/shard_map/ppermute | solution.py:617
  20.9 4.7 %collective-permute-start.6 = (f32[13,16,256]{2,1,0:T(8,128)S(1)}, f32[13,16,256]{2,1,0:T(8,128)S(1)}, u32[]{:S(2)}, u32[]{:S(2)}) collective-permute-start(f32[13,16,256]{2,1,0:T(8,128)S(1)} %get-tuple-element.75), channel_id=1, source_target_pairs={{0,8},{1,9},{2,10},{3,11},{4,12},{5,13},{6,14},{7,15},{8,0},{9,1},... | collective-permute-start | bytes 638984 | tf_op jit(solution)/shard_map/ppermute | solution.py:617
  20.9 5.8 %collective-permute-start.7 = (f32[13,16,256]{2,1,0:T(8,128)S(1)}, f32[13,16,256]{2,1,0:T(8,128)S(1)}, u32[]{:S(2)}, u32[]{:S(2)}) collective-permute-start(f32[13,16,256]{2,1,0:T(8,128)S(1)} %get-tuple-element.76), channel_id=1, source_target_pairs={{0,1},{1,0},{2,3},{3,2},{4,5},{5,4},{6,7},{7,6},{8,16},{9,17},{10,... | collective-permute-start | bytes 638984 | tf_op jit(solution)/shard_map/ppermute | solution.py:616
  23.2 6.1 %collective-permute-start.4 = (f32[26,8,256]{2,1,0:T(8,128)S(1)}, f32[26,8,256]{2,1,0:T(8,128)S(1)}, u32[]{:S(2)}, u32[]{:S(2)}) collective-permute-start(f32[26,8,256]{2,1,0:T(8,128)S(1)} %get-tuple-element.68), channel_id=1, source_target_pairs={{0,1},{1,0},{2,3},{3,2},{4,5},{5,4},{6,7},{7,6},{8,16},{9,17},{10,... | collective-permute-start | bytes 638984 | tf_op jit(solution)/shard_map/ppermute | solution.py:616
  25.4 3.8 %collective-permute-start.5 = (f32[26,8,256]{2,1,0:T(8,128)S(1)}, f32[26,8,256]{2,1,0:T(8,128)S(1)}, u32[]{:S(2)}, u32[]{:S(2)}) collective-permute-start(f32[26,8,256]{2,1,0:T(8,128)S(1)} %get-tuple-element.69), channel_id=1, source_target_pairs={{0,8},{1,9},{2,10},{3,11},{4,12},{5,13},{6,14},{7,15},{8,0},{9,1},... | collective-permute-start | bytes 638984 | tf_op jit(solution)/shard_map/ppermute | solution.py:617
  41.9 2.3 %collective-permute-start.8 = (f32[12,4,256]{2,1,0:T(4,128)S(1)}, f32[12,4,256]{2,1,0:T(4,128)S(1)}, u32[]{:S(2)}, u32[]{:S(2)}) collective-permute-start(f32[12,4,256]{2,1,0:T(4,128)S(1)} %get-tuple-element.81), channel_id=1, source_target_pairs={{0,8},{1,2},{2,1},{3,4},{4,3},{5,6},{6,5},{7,15},{8,0},{9,10},{10,... | collective-permute-start | bytes 147464 | tf_op jit(solution)/shard_map/ppermute | solution.py:616
  42.1 4.1 %collective-permute-start.9 = (f32[12,4,256]{2,1,0:T(4,128)S(1)}, f32[12,4,256]{2,1,0:T(4,128)S(1)}, u32[]{:S(2)}, u32[]{:S(2)}) collective-permute-start(f32[12,4,256]{2,1,0:T(4,128)S(1)} %get-tuple-element.82), channel_id=1, source_target_pairs={{0,1},{1,0},{2,3},{3,2},{4,5},{5,4},{6,7},{7,6},{8,9},{9,8},{10,11... | collective-permute-start | bytes 147464 | tf_op jit(solution)/shard_map/ppermute | solution.py:617
  43.9 4.6 %collective-permute-start.12 = (f32[5,16,256]{2,1,0:T(8,128)S(1)}, f32[5,16,256]{2,1,0:T(8,128)S(1)}, u32[]{:S(2)}, u32[]{:S(2)}) collective-permute-start(f32[5,16,256]{2,1,0:T(8,128)S(1)} %get-tuple-element.90), channel_id=1, source_target_pairs={{0,8},{1,9},{2,10},{3,11},{4,12},{5,13},{6,14},{7,15},{8,0},{9,1},... | collective-permute-start | bytes 245768 | tf_op jit(solution)/shard_map/ppermute | solution.py:617
  43.9 4.6 %collective-permute-start.13 = (f32[5,16,256]{2,1,0:T(8,128)S(1)}, f32[5,16,256]{2,1,0:T(8,128)S(1)}, u32[]{:S(2)}, u32[]{:S(2)}) collective-permute-start(f32[5,16,256]{2,1,0:T(8,128)S(1)} %get-tuple-element.91), channel_id=1, source_target_pairs={{0,1},{1,0},{2,3},{3,2},{4,5},{5,4},{6,7},{7,6},{8,16},{9,17},{10,... | collective-permute-start | bytes 245768 | tf_op jit(solution)/shard_map/ppermute | solution.py:616
  46.3 4.3 %collective-permute-start.10 = (f32[6,8,256]{2,1,0:T(8,128)S(1)}, f32[6,8,256]{2,1,0:T(8,128)S(1)}, u32[]{:S(2)}, u32[]{:S(2)}) collective-permute-start(f32[6,8,256]{2,1,0:T(8,128)S(1)} %get-tuple-element.87), channel_id=1, source_target_pairs={{0,1},{1,0},{2,3},{3,2},{4,5},{5,4},{6,7},{7,6},{8,16},{9,17},{10,... | collective-permute-start | bytes 147464 | tf_op jit(solution)/shard_map/ppermute | solution.py:616
  48.5 2.1 %collective-permute-start.11 = (f32[6,8,256]{2,1,0:T(8,128)S(1)}, f32[6,8,256]{2,1,0:T(8,128)S(1)}, u32[]{:S(2)}, u32[]{:S(2)}) collective-permute-start(f32[6,8,256]{2,1,0:T(8,128)S(1)} %get-tuple-element.88), channel_id=1, source_target_pairs={{0,8},{1,9},{2,10},{3,11},{4,12},{5,13},{6,14},{7,15},{8,0},{9,1},... | collective-permute-start | bytes 147464 | tf_op jit(solution)/shard_map/ppermute | solution.py:617
